TPU v7x, 32 devices: a whole 2x2x4 slice. The times are simulated.
32 devices in a mesh: section: 4 (over x, core), mp: 8 (over z, y).
Axes of the slice: x: 2, y: 2, z: 4, core: 2. Of those that a mesh axis runs over, the one named last changes fastest.
Arguments:
- queries: bfloat16 [4096, 4096], P(('section', 'mp')), may hold values from -6 to 6
- keys: bfloat16 [1024, 512], P(('section', 'mp')), may hold values from -6 to 6
- values: bfloat16 [1024, 512], P(('section', 'mp')), may hold values from -6 to 6
- seg_image: int32 [4096], P(('section', 'mp')), may hold values from 0 to 3, as said below
- tile_counts: int32 [4], replicated, may hold values from 1 to 4, as said below
- gate: float32 [1], replicated, may hold values from 0.4 to 1.5
- cotangent: bfloat16 [4096, 4096], P(('section', 'mp')), may hold values from -6 to 6
Outputs:
- gated: bfloat16 [4096, 4096], P(('section', 'mp'))
- grad_queries: bfloat16 [4096, 4096], P(('section', 'mp'))
- grad_keys: float32 [1024, 512], P(('section', 'mp'))
- grad_values: float32 [1024, 512], P(('section', 'mp'))
- grad_gate: float32 [1], replicated
Inputs may be any that keep to these rules, and one draw needn't show every extreme that they name: `seg_image`: within the 128 tokens of one device, a leading run attends one image and the rest attend one image, possibly the same. Image i holds 64 * tile_counts[i] real tokens at the start of its 256 slots.
All inputs are finite; a program needn't handle non-finite values.
Results may differ from a plain program's by a relative error of at most 0.029.
Values may be sent and summed in bfloat16 or wider, within the bound.
No kernel may reach another device: no remote copies, remote signals or barrier semaphores. Data moves between devices by JAX's collectives and lax.ppermute only.
A program may use at most 64 MiB of HBM per device.

v0:
```python
import jax
import jax.numpy as jnp
from jax import lax
from jax.sharding import PartitionSpec as P

KV_HEADS = 4
TILE_TOK = 64
NIMG = 4
IMG_TOK = 256


def one_head(operands, valid, tg, scale):
    q, k, v, dy = operands
    s = jnp.einsum("tgd,nd->gtn", q, k, preferred_element_type=jnp.float32) * scale
    s = jnp.where(valid[None], s, -1e30)
    top = jnp.max(s, axis=-1, keepdims=True)
    e = jnp.where(valid[None], jnp.exp(s - top), 0.0)
    p = e / jnp.sum(e, axis=-1, keepdims=True)
    p16 = p.astype(jnp.bfloat16)
    o = jnp.einsum("gtn,nd->tgd", p16, v, preferred_element_type=jnp.float32)
    y = (tg * o).astype(jnp.bfloat16)
    do16 = (tg * dy.astype(jnp.float32)).astype(jnp.bfloat16)
    dp = jnp.einsum("tgd,nd->gtn", do16, v, preferred_element_type=jnp.float32)
    delta = jnp.einsum("tgd,tgd->gt", do16.astype(jnp.float32), o)
    ds16 = (scale * p * (dp - delta[..., None])).astype(jnp.bfloat16)
    dq = jnp.einsum("gtn,nd->tgd", ds16, k, preferred_element_type=jnp.float32).astype(jnp.bfloat16)
    dk = jnp.einsum("gtn,tgd->nd", ds16, q, preferred_element_type=jnp.float32)
    dv = jnp.einsum("gtn,tgd->nd", p16, do16, preferred_element_type=jnp.float32)
    gterm = jnp.sum(dy.astype(jnp.float32) * o)
    return (y, dq, dk, dv, gterm)


def local(queries, keys, values, seg_image, tile_counts, gate, cotangent):
    tokens = queries.shape[0]
    width = keys.shape[1]
    kv_count = KV_HEADS
    head_size = width // kv_count
    group = queries.shape[1] // width
    tg = jnp.tanh(gate[0])
    scale = 1.0 / head_size**0.5
    all_keys, all_values = (
        lax.all_gather(keys, ("section", "mp"), axis=0, tiled=True),
        lax.all_gather(values, ("section", "mp"), axis=0, tiled=True),
    )
    total = all_keys.shape[0]
    slots = jnp.arange(total, dtype=jnp.int32)
    key_image = slots // IMG_TOK
    key_pos = slots % IMG_TOK
    keep = jnp.ones((total,), bool)
    count = all_keys.shape[0]
    image_ids = jnp.arange(NIMG, dtype=jnp.int32)
    limit = (
        jnp.sum(
            jnp.where(key_image[:, None] == image_ids[None, :], tile_counts[None, :], 0), axis=1
        )
        * TILE_TOK
    )
    valid = (key_image[None, :] == seg_image[:, None]) & (key_pos < limit)[None, :] & keep[None, :]
    q_heads = jnp.moveaxis(queries.reshape(tokens, kv_count, group, head_size), 1, 0)
    dy_heads = jnp.moveaxis(cotangent.reshape(tokens, kv_count, group, head_size), 1, 0)
    k_heads = jnp.moveaxis(all_keys.reshape(count, kv_count, head_size), 1, 0)
    v_heads = jnp.moveaxis(all_values.reshape(count, kv_count, head_size), 1, 0)
    y_all, dq_all, dk_all, dv_all, gterms = lax.map(
        lambda ops: one_head(ops, valid, tg, scale), (q_heads, k_heads, v_heads, dy_heads)
    )
    gated = jnp.moveaxis(y_all, 0, 1).reshape(tokens, group * width)
    grad_queries = jnp.moveaxis(dq_all, 0, 1).reshape(tokens, group * width)
    term = jnp.concatenate(
        [
            jnp.moveaxis(dk_all, 0, 1).reshape(count, width),
            jnp.moveaxis(dv_all, 0, 1).reshape(count, width),
        ],
        1,
    )
    owned = lax.psum_scatter(term, ("section", "mp"), scatter_dimension=0, tiled=True)
    gate_total = lax.psum(jnp.sum(gterms), ("section", "mp"))
    grad_gate = ((1.0 - tg * tg) * gate_total).reshape(1)
    return (gated, grad_queries, owned[:, :width], owned[:, width:], grad_gate)


def solution(mesh):
    return jax.shard_map(
        local,
        mesh=mesh,
        in_specs=(
            P(("section", "mp"), None),
            P(("section", "mp"), None),
            P(("section", "mp"), None),
            P(("section", "mp")),
            P(),
            P(),
            P(("section", "mp"), None),
        ),
        out_specs=(
            P(("section", "mp"), None),
            P(("section", "mp"), None),
            P(("section", "mp"), None),
            P(("section", "mp"), None),
            P(),
        ),
        check_vma=False,
    )
```

profile of v0, /device:TPU:0, one launch (start us, length us, event | category | flops | bytes accessed | tf_op | source)
XLA Modules:
  0.0 362.6 jit_solution(17325517439164506308)
XLA Ops:
  9.5 1.6 copy.64
  11.1 1.4 copy.65
  12.6 55.0 %all-gather.5.cloned.1.call-done = bf16[1024,512]{1,0:T(8,128)(2,1)} async-done(((bf16[32,512]{1,0:T(8,128)(2,1)}), bf16[1024,512]{1,0:T(8,128)(2,1)}) %all-gather.5.cloned.1.call-update) | async-done | bytes 1048592 | tf_op jit(solution)/shard_map/all_gather | solution.py:42
  67.6 1.5 copy.63
  69.1 54.2 %all-gather.3.cloned.1.call-done = bf16[1024,512]{1,0:T(8,128)(2,1)} async-done(((bf16[32,512]{1,0:T(8,128)(2,1)}), bf16[1024,512]{1,0:T(8,128)(2,1)}) %all-gather.3.cloned.1.call-update) | async-done | bytes 1048592 | tf_op jit(solution)/shard_map/all_gather | solution.py:43
  123.3 2.3 copy.62
  125.6 79.2 %while.19 = (s32[]{:T(128)}, bf16[4,128,8,128]{1,3,2,0:T(8,128)(2,1)}, bf16[4,128,8,128]{1,3,2,0:T(8,128)(2,1)}, f32[4,1024,128]{2,1,0:T(8,128)}, f32[4,1024,128...) while((s32[]{:T(128)}, ...), condition=%wide.region_5.6_spmd.clone, body=%wide.region_1.5_spmd.clone.sunk | while | flops 1625817088 | bytes 52331836 | solution.py:63
  125.9 3.6 %fusion.125 = (f32[8,128]{1,0:T(8,128)S(1)}, f32[8,128,1024]{1,2,0:T(8,128)}) fusion(pred[128,1024]{0,1:T(8,128)(4,1)S(1)} %compare_and_fusion.2, bf16[4,128,8,128]{1,3,2,0:T(8,128)(2,1)S(1)} %get-tuple-element.319, s32[]{:T(128)S(6)} %copy.106, bf16[4,1024,128]{1,2,0:T(8,128)(2,1)S(1)} %get-tuple-element.318), kind=kOutput, calls=%fused_computation.83.clone.1 | convolution fusion | flops 273679360 | bytes 4985856 | tf_op jit(solution)/shard_map/while/body/eval_jaxpr/sub | solution.py:17
  129.6 2.5 fusion.126
  132.1 2.1 fusion.127
  134.2 1.7 fusion.133
  135.9 0.8 dynamic_update_slice.36
  136.7 2.6 fusion.132
  139.4 3.3 fusion.129
  142.7 1.2 fusion.130
  143.9 1.5 fusion.131
  145.7 3.6 %fusion.125 = (f32[8,128]{1,0:T(8,128)S(1)}, f32[8,128,1024]{1,2,0:T(8,128)}) fusion(pred[128,1024]{0,1:T(8,128)(4,1)S(1)} %compare_and_fusion.2, bf16[4,128,8,128]{1,3,2,0:T(8,128)(2,1)S(1)} %get-tuple-element.319, s32[]{:T(128)S(6)} %copy.106, bf16[4,1024,128]{1,2,0:T(8,128)(2,1)S(1)} %get-tuple-element.318), kind=kOutput, calls=%fused_computation.83.clone.1 | convolution fusion | flops 273679360 | bytes 4985856 | tf_op jit(solution)/shard_map/while/body/eval_jaxpr/sub | solution.py:17
  149.4 2.5 fusion.126
  151.9 2.1 fusion.127
  154.0 1.7 fusion.133
  156.5 2.6 fusion.132
  159.2 3.3 fusion.129
  162.5 1.2 fusion.130
  163.7 1.5 fusion.131
  165.5 3.6 %fusion.125 = (f32[8,128]{1,0:T(8,128)S(1)}, f32[8,128,1024]{1,2,0:T(8,128)}) fusion(pred[128,1024]{0,1:T(8,128)(4,1)S(1)} %compare_and_fusion.2, bf16[4,128,8,128]{1,3,2,0:T(8,128)(2,1)S(1)} %get-tuple-element.319, s32[]{:T(128)S(6)} %copy.106, bf16[4,1024,128]{1,2,0:T(8,128)(2,1)S(1)} %get-tuple-element.318), kind=kOutput, calls=%fused_computation.83.clone.1 | convolution fusion | flops 273679360 | bytes 4985856 | tf_op jit(solution)/shard_map/while/body/eval_jaxpr/sub | solution.py:17
  169.2 2.5 fusion.126
  171.7 2.1 fusion.127
  173.9 1.7 fusion.133
  175.5 0.8 dynamic_update_slice.36
  176.3 2.5 fusion.132
  178.9 3.3 fusion.129
  182.2 1.2 fusion.130
  183.5 1.5 fusion.131
  185.3 3.7 %fusion.125 = (f32[8,128]{1,0:T(8,128)S(1)}, f32[8,128,1024]{1,2,0:T(8,128)}) fusion(pred[128,1024]{0,1:T(8,128)(4,1)S(1)} %compare_and_fusion.2, bf16[4,128,8,128]{1,3,2,0:T(8,128)(2,1)S(1)} %get-tuple-element.319, s32[]{:T(128)S(6)} %copy.106, bf16[4,1024,128]{1,2,0:T(8,128)(2,1)S(1)} %get-tuple-element.318), kind=kOutput, calls=%fused_computation.83.clone.1 | convolution fusion | flops 273679360 | bytes 4985856 | tf_op jit(solution)/shard_map/while/body/eval_jaxpr/sub | solution.py:17
  189.0 2.5 fusion.126
  191.5 2.1 fusion.127
  193.6 1.7 fusion.133
  196.1 2.6 fusion.132
  198.7 3.3 fusion.129
  202.0 1.2 fusion.130
  203.3 1.5 fusion.131
  204.8 2.8 copy_bitcast_fusion
  207.6 2.3 pad_maximum_fusion
  210.6 40.9 %psum.7 = f32[]{:T(128)} all-reduce(f32[]{:T(128)} %reduce_sum.37), channel_id=1, replica_groups=mesh['section'=4,'mp'=8] {'section','mp'}, use_global_device_ids=true, to_apply=%region_8.9 | all-reduce | flops 1 | bytes 8 | tf_op jit(solution)/shard_map/psum | solution.py:76
  251.5 2.3 copy.84
  253.8 1.3 copy.85
  255.7 97.7 %reduce-scatter.2.cloned.1.call-done = f32[32,1024]{1,0:T(8,128)} async-done(((f32[1024,1024]{1,0:T(8,128)}), f32[32,1024]{1,0:T(8,128)}) %reduce-scatter.2.cloned.1.call-update) | async-done | bytes 131088 | tf_op jit(solution)/shard_map/reduce_scatter | solution.py:75
  353.4 1.5 fusion.87
  (73 shorter events, 5.7 us)
Async XLA Ops:
  7.2 3.9 %copy-start.5 = (bf16[128,4096]{1,0:T(8,128)(2,1)S(1)}, bf16[128,4096]{1,0:T(8,128)(2,1)}, u32[]{:S(2)}) copy-start(bf16[128,4096]{1,0:T(8,128)(2,1)} %param.15) | copy-start | bytes 3145732
  7.2 60.5 %all-gather.5.cloned.1.call-start = ((), (), s32[]{:S(2)}) async-start(), calls=%async_computation.2 | async-start | bytes 1081344 | tf_op jit(solution)/shard_map/all_gather | solution.py:42
  7.9 115.4 %all-gather.3.cloned.1.call-start = ((), (), s32[]{:S(2)}) async-start(), calls=%async_computation.1 | async-start | bytes 1081344 | tf_op jit(solution)/shard_map/all_gather | solution.py:43
  8.7 344.8 %reduce-scatter.2.cloned.1.call-start = ((), (), s32[]{:S(2)}) async-start(), calls=%async_computation.3 | async-start | bytes 4325376 | tf_op jit(solution)/shard_map/reduce_scatter | solution.py:75
  9.4 3.0 copy-start.8
  12.6 113.0 %copy-start.7 = (s32[128]{0:T(128)S(1)}, s32[128]{0:T(128)}, u32[]{:S(2)}) copy-start(s32[128]{0:T(128)} %param.12) | copy-start | bytes 1540
  125.6 4.0 %copy-start.1 = (bf16[4,1024,128]{1,2,0:T(8,128)(2,1)}, bf16[4,1024,128]{1,2,0:T(8,128)(2,1)S(1)}, u32[]{:S(2)}) copy-start(bf16[4,1024,128]{1,2,0:T(8,128)(2,1)S(1)} %get-tuple-element.318) | copy-start | bytes 3145732 | tf_op jit(solution)/shard_map/while
  125.6 4.0 %copy-start.3 = (bf16[4,128,8,128]{1,3,2,0:T(8,128)(2,1)}, bf16[4,128,8,128]{1,3,2,0:T(8,128)(2,1)S(1)}, u32[]{:S(2)}) copy-start(bf16[4,128,8,128]{1,3,2,0:T(8,128)(2,1)S(1)} %get-tuple-element.319) | copy-start | bytes 3145732 | tf_op jit(solution)/shard_map/while
  136.7 2.6 copy-start
  139.4 3.3 copy-start.2
  142.7 1.2 copy-start.4
  145.4 4.0 %copy-start.1 = (bf16[4,1024,128]{1,2,0:T(8,128)(2,1)}, bf16[4,1024,128]{1,2,0:T(8,128)(2,1)S(1)}, u32[]{:S(2)}) copy-start(bf16[4,1024,128]{1,2,0:T(8,128)(2,1)S(1)} %get-tuple-element.318) | copy-start | bytes 3145732 | tf_op jit(solution)/shard_map/while
  145.4 4.0 %copy-start.3 = (bf16[4,128,8,128]{1,3,2,0:T(8,128)(2,1)}, bf16[4,128,8,128]{1,3,2,0:T(8,128)(2,1)S(1)}, u32[]{:S(2)}) copy-start(bf16[4,128,8,128]{1,3,2,0:T(8,128)(2,1)S(1)} %get-tuple-element.319) | copy-start | bytes 3145732 | tf_op jit(solution)/shard_map/while
  156.5 2.6 copy-start
  159.1 3.3 copy-start.2
  162.4 1.2 copy-start.4
  165.2 4.0 %copy-start.1 = (bf16[4,1024,128]{1,2,0:T(8,128)(2,1)}, bf16[4,1024,128]{1,2,0:T(8,128)(2,1)S(1)}, u32[]{:S(2)}) copy-start(bf16[4,1024,128]{1,2,0:T(8,128)(2,1)S(1)} %get-tuple-element.318) | copy-start | bytes 3145732 | tf_op jit(solution)/shard_map/while
  165.2 4.0 %copy-start.3 = (bf16[4,128,8,128]{1,3,2,0:T(8,128)(2,1)}, bf16[4,128,8,128]{1,3,2,0:T(8,128)(2,1)S(1)}, u32[]{:S(2)}) copy-start(bf16[4,128,8,128]{1,3,2,0:T(8,128)(2,1)S(1)} %get-tuple-element.319) | copy-start | bytes 3145732 | tf_op jit(solution)/shard_map/while
  176.3 2.5 copy-start
  178.9 3.3 copy-start.2
  182.2 1.2 copy-start.4
  185.0 4.0 %copy-start.1 = (bf16[4,1024,128]{1,2,0:T(8,128)(2,1)}, bf16[4,1024,128]{1,2,0:T(8,128)(2,1)S(1)}, u32[]{:S(2)}) copy-start(bf16[4,1024,128]{1,2,0:T(8,128)(2,1)S(1)} %get-tuple-element.318) | copy-start | bytes 3145732 | tf_op jit(solution)/shard_map/while
  185.0 4.0 %copy-start.3 = (bf16[4,128,8,128]{1,3,2,0:T(8,128)(2,1)}, bf16[4,128,8,128]{1,3,2,0:T(8,128)(2,1)S(1)}, u32[]{:S(2)}) copy-start(bf16[4,128,8,128]{1,3,2,0:T(8,128)(2,1)S(1)} %get-tuple-element.319) | copy-start | bytes 3145732 | tf_op jit(solution)/shard_map/while
  196.1 2.6 copy-start
  198.7 3.3 copy-start.2
  202.0 1.2 copy-start.4
  210.0 43.8 %copy-start.6 = (bf16[4,128,8,128]{1,3,2,0:T(8,128)(2,1)S(1)}, bf16[4,128,8,128]{1,3,2,0:T(8,128)(2,1)}, u32[]{:S(2)}) copy-start(bf16[4,128,8,128]{1,3,2,0:T(8,128)(2,1)} %get-tuple-element.72) | copy-start | bytes 3145732
Sparse Core Ops, SparseCore 0:
  11.1 56.5 all-gather.4
  70.7 52.5 all-gather.2
  210.1 143.2 reduce-scatter.1
where the time goes:
time: 364 us; the launch traced here: 363 us
  waiting for transfers between devices  208 us (57%)
  matrix products  57.1 us (16%)
  blocking collectives  40.9 us (11%)
  other arithmetic  21.7 us (6%)
  local copies, waits for them, and re-layouts  17.9 us (5%)
  between operations  16.3 us (4%)
    reduce_scatter x1, waiting for transfers between devices, local(): lax.psum_scatter(term, ('section', 'mp'), scatter_dimension=0, tiled=True)  97.7 us
    all_gather x1, waiting for transfers between devices, local(): lax.all_gather(keys, ('section', 'mp'), axis=0, tiled=True)  55 us
    all_gather x1, waiting for transfers between devices, local(): lax.all_gather(values, ('section', 'mp'), axis=0, tiled=True)  54.2 us
    psum x1, blocking collectives, local(): gate_total = lax.psum(jnp.sum(gterms), ('section', 'mp'))  40.9 us
    sub x4, matrix products, one_head(): e = jnp.where(valid[None], jnp.exp(s - top), 0.0)  14.6 us
    dot_general x4, matrix products, one_head(): dp = jnp.einsum('tgd,nd->gtn', do16, v, preferred_element_type=jnp.float32)  13.1 us
    dot_general x4, matrix products, one_head(): jnp.einsum('gtn,tgd->nd', p16, do16, preferred_element_type=jnp.float32)  10.2 us
    convert_element_type x4, other arithmetic, one_head(): p16 = p.astype(jnp.bfloat16)  10.1 us
  transfers between devices with their start and end apart: 3, of which 3 were waited for; matrix products, arithmetic and copies ran while one was open for 2% of the time, Pallas kernels for 0%

commit v1 on v0

v1 whole, which is shorter than its diff:
```python
import functools

import jax
import jax.numpy as jnp
from jax import lax
from jax.experimental import pallas as pl
from jax.experimental.pallas import tpu as pltpu
from jax.sharding import PartitionSpec as P

KV_HEADS = 4
TILE_TOK = 64
IMG_TOK = 256
AXES = ("section", "mp")
NEG = -1e30
LOG2E = 1.4426950408889634

NT = (((1,), (1,)), ((), ()))
NN = (((1,), (0,)), ((), ()))
TN = (((0,), (0,)), ((), ()))


def mm(a, b, dims):
    return lax.dot_general(a, b, dims, preferred_element_type=jnp.float32)


def attend_kernel(
    folded,
    seg_s,
    cnt_s,
    gate_s,
    seg_v,
    q_ref,
    dy_ref,
    own,
    other,
    y_ref,
    dq_ref,
    part_own,
    part_other,
    g_ref,
    kv,
    acc,
    qc,
    dc,
    p16,
    ds16,
    bias,
    rowsel,
    sems,
):
    step = pl.program_id(0)
    last = pl.num_programs(0) - 1
    tokens = q_ref.shape[0]
    slots, width = kv.shape[1], kv.shape[2] // 2
    hd = width // KV_HEADS
    group = q_ref.shape[1] // hd
    scale = 1.0 / hd**0.5
    section = lax.axis_index("section")
    core, xpos = section % 2, section // 2
    img_a, img_b = seg_s[0], seg_s[tokens - 1]

    def place(img):
        return ((img % 2) ^ core), ((img // 2) ^ xpos)

    def fetch(i, img, start):
        par, dx = place(img)

        @pl.when(par == 0)
        def _():
            c = pltpu.make_async_copy(own.at[dx], kv.at[i], sems.at[i])
            c.start() if start else c.wait()

        @pl.when(par != 0)
        def _():
            c = pltpu.make_async_copy(other.at[dx], kv.at[i], sems.at[i])
            c.start() if start else c.wait()

    in_a = seg_v[...] == img_a
    tg = jnp.tanh(jnp.full((1, hd), gate_s[0], jnp.float32))

    @pl.when(step == 0)
    def _():
        fetch(0, img_a, True)
        fetch(1, img_b, True)
        acc[...] = jnp.zeros_like(acc)
        g_ref[...] = jnp.zeros_like(g_ref)
        n = lax.broadcasted_iota(jnp.int32, (slots, tokens), 0)
        if folded:
            zpos = lax.axis_index("mp") // 2
            per = slots // 8
            tile = ((n // per) % 4) ^ zpos
        else:
            tile = n // TILE_TOK
        limit = jnp.where(in_a, cnt_s[img_a], cnt_s[img_b])
        bias[...] = jnp.where(tile < limit, 0.0, NEG)
        rowsel[...] = jnp.broadcast_to(in_a.astype(jnp.float32), (hd, tokens)).T
        fetch(0, img_a, False)
        fetch(1, img_b, False)

    rows_a = rowsel[...] > 0.5
    kcols = pl.ds(pl.multiple_of(step * hd, hd), hd)
    vcols = pl.ds(pl.multiple_of(width + step * hd, hd), hd)
    kcat = jnp.concatenate([kv[0, :, kcols], kv[1, :, kcols]], axis=1)
    vcat = jnp.concatenate([kv[0, :, vcols], kv[1, :, vcols]], axis=1)
    kcat_t = kcat.astype(jnp.float32).T.astype(jnp.bfloat16)
    vcat_t = vcat.astype(jnp.float32).T.astype(jnp.bfloat16)
    zero = jnp.zeros((tokens, hd), jnp.bfloat16)
    for g in range(group):
        cols = slice(g * hd, (g + 1) * hd)
        rows = slice(g * tokens, (g + 1) * tokens)
        q = q_ref[:, cols]
        dy = dy_ref[:, cols].astype(jnp.float32)
        do = (tg * dy).astype(jnp.bfloat16)
        qc[rows, :hd] = jnp.where(rows_a, q, zero)
        qc[rows, hd:] = jnp.where(rows_a, zero, q)
        dc[rows, :hd] = jnp.where(rows_a, do, zero)
        dc[rows, hd:] = jnp.where(rows_a, zero, do)

    pair = 2
    gsum = jnp.zeros((tokens, hd), jnp.float32)
    in_a2 = jnp.concatenate([in_a] * pair, axis=1)
    for h in range(0, group, pair):
        rows = slice(h * tokens, (h + pair) * tokens)
        s = mm(kcat, qc[rows, :], NT)
        s = s + jnp.concatenate([bias[...]] * pair, axis=1)
        top = jnp.max(s, axis=0, keepdims=True)
        e = jnp.exp2((s - top) * (scale * LOG2E))
        p = e * (1.0 / jnp.sum(e, axis=0, keepdims=True))
        ph = p.astype(jnp.bfloat16)
        p16[:, rows] = ph
        dp = mm(vcat, dc[rows, :], NT)
        delta = jnp.sum(ph.astype(jnp.float32) * dp, axis=0, keepdims=True)
        dsh = (scale * p * (dp - delta)).astype(jnp.bfloat16)
        ds16[:, rows] = dsh
        o = mm(vcat_t, ph, NN)
        o = jnp.where(in_a2, o[:hd], o[hd:])
        dq = mm(kcat_t, dsh, NN)
        dq = jnp.where(in_a2, dq[:hd], dq[hd:])
        for j in range(pair):
            cols = slice((h + j) * hd, (h + j + 1) * hd)
            toks = slice(j * tokens, (j + 1) * tokens)
            ot = o[:, toks].T
            y_ref[:, cols] = (tg * ot).astype(jnp.bfloat16)
            gsum = gsum + dy_ref[:, cols].astype(jnp.float32) * ot
            dq_ref[:, cols] = dq[:, toks].T.astype(jnp.bfloat16)
    g_ref[...] += jnp.sum(gsum.reshape(tokens // 8, 8, hd), axis=0)
    dk = mm(ds16[...], qc[...], NN)
    dv = mm(p16[...], dc[...], NN)
    par_a, dx_a = place(img_a)
    par_b, dx_b = place(img_b)
    at_a, at_b = par_a * 2 + dx_a, par_b * 2 + dx_b
    acc[at_b, :, kcols] = dk[:, hd:].astype(jnp.bfloat16)
    acc[at_b, :, vcols] = dv[:, hd:].astype(jnp.bfloat16)
    acc[at_a, :, kcols] = dk[:, :hd].astype(jnp.bfloat16)
    acc[at_a, :, vcols] = dv[:, :hd].astype(jnp.bfloat16)

    @pl.when(step == last)
    def _():
        c1 = pltpu.make_async_copy(acc.at[pl.ds(2, 2)], part_other, sems.at[2])
        c0 = pltpu.make_async_copy(acc.at[pl.ds(0, 2)], part_own, sems.at[3])
        c1.start()
        c0.start()
        c1.wait()
        c0.wait()


def attend(folded, seg, counts, gate, q, dy, own, other):
    tokens, feats = q.shape
    slots, width2 = own.shape[1], own.shape[2]
    hd = width2 // 2 // KV_HEADS
    block = feats // KV_HEADS
    rows = block // hd * tokens
    smem = pl.BlockSpec(memory_space=pltpu.SMEM)
    hbm = pl.BlockSpec(memory_space=pl.ANY)
    cut = pl.BlockSpec((tokens, block), lambda i: (0, i))
    flops = 12 * KV_HEADS * rows * slots * hd * 2
    return pl.pallas_call(
        functools.partial(attend_kernel, folded),
        grid=(KV_HEADS,),
        in_specs=[
            smem,
            smem,
            smem,
            pl.BlockSpec((1, tokens), lambda i: (0, 0)),
            cut,
            cut,
            hbm,
            hbm,
        ],
        out_specs=[cut, cut, hbm, hbm, pl.BlockSpec((8, hd), lambda i: (0, 0))],
        out_shape=[
            jax.ShapeDtypeStruct(q.shape, jnp.bfloat16),
            jax.ShapeDtypeStruct(q.shape, jnp.bfloat16),
            jax.ShapeDtypeStruct(own.shape, jnp.bfloat16),
            jax.ShapeDtypeStruct(own.shape, jnp.bfloat16),
            jax.ShapeDtypeStruct((8, hd), jnp.float32),
        ],
        scratch_shapes=[
            pltpu.VMEM((2, slots, width2), jnp.bfloat16),
            pltpu.VMEM((4, slots, width2), jnp.bfloat16),
            pltpu.VMEM((rows, 2 * hd), jnp.bfloat16),
            pltpu.VMEM((rows, 2 * hd), jnp.bfloat16),
            pltpu.VMEM((slots, rows), jnp.bfloat16),
            pltpu.VMEM((slots, rows), jnp.bfloat16),
            pltpu.VMEM((slots, tokens), jnp.float32),
            pltpu.VMEM((tokens, hd), jnp.float32),
            pltpu.SemaphoreType.DMA((4,)),
        ],
        compiler_params=pltpu.CompilerParams(
            dimension_semantics=("arbitrary",), vmem_limit_bytes=32 * 1024 * 1024
        ),
        cost_estimate=pl.CostEstimate(
            flops=flops,
            bytes_accessed=8 * q.size + 8 * own.size,
            transcendentals=KV_HEADS * rows * slots,
        ),
    )(seg, counts, gate, seg.reshape(1, tokens), q, dy, own, other)


def local(mp, queries, keys, values, seg_image, tile_counts, gate, cotangent):
    f32, bf16 = jnp.float32, jnp.bfloat16
    width = keys.shape[1]
    mine = keys.shape[0]
    folded = mp == 8

    def send_z(x, k):
        perm = [(m, ((m // 2) ^ k) * 2 + m % 2) for m in range(mp)]
        return lax.ppermute(x, "mp", perm)

    def send_xy(x, dx, dy):
        perm = []
        for s in range(4):
            for m in range(mp):
                perm.append((s * mp + m, (s ^ (2 * dx)) * mp + (m ^ dy)))
        return lax.ppermute(x, AXES, perm)

    def send_core(x):
        return lax.ppermute(x, "section", [(s, s ^ 1) for s in range(4)])

    kv = jnp.concatenate([keys, values], axis=1)
    if folded:
        col = jnp.concatenate([kv] + [send_z(kv, k) for k in (1, 2, 3)], axis=0)
        parts = [col] + [send_xy(col, dx, dy) for dx, dy in ((0, 1), (1, 0), (1, 1))]
        own = jnp.concatenate(parts, axis=0)
    else:
        col = lax.all_gather(kv, "mp", axis=0, tiled=True)
        own = jnp.concatenate([col, send_xy(col, 1, 0)], axis=0)
    own = own.reshape(2, IMG_TOK, 2 * width)
    other = send_core(own)

    y, dq, part_own, part_other, gpart = attend(
        folded, seg_image, tile_counts, gate, queries, cotangent, own, other
    )

    got = send_core(part_other)
    gsum = gpart + send_core(gpart)
    both = (part_own.astype(f32) + got.astype(f32)).astype(bf16)
    if folded:
        cut = both.reshape(4, 4 * mine, 2 * width)
        order = ((0, 1), (1, 0), (1, 1))
        recv = [send_xy(cut[2 * dx + dy], dx, dy) for dx, dy in order]
        total = cut[0].astype(f32)
        for r in recv:
            total = total + r.astype(f32)
        gsum = gsum + sum(send_xy(gsum, dx, dy) for dx, dy in order)
        cut = total.astype(bf16).reshape(4, mine, 2 * width)
        recv = [send_z(cut[k], k) for k in (1, 2, 3)]
        owned = cut[0].astype(f32)
        for r in recv:
            owned = owned + r.astype(f32)
        gsum = gsum + sum(send_z(gsum, k) for k in (1, 2, 3))
    else:
        total = both[0].astype(f32) + send_xy(both[1], 1, 0).astype(f32)
        owned = lax.psum_scatter(total, "mp", scatter_dimension=0, tiled=True)
        gsum = lax.psum(gsum + send_xy(gsum, 1, 0), "mp")
    tg = jnp.tanh(gate[0])
    grad_gate = ((1.0 - tg * tg) * jnp.sum(gsum)).reshape(1)
    return (y, dq, owned[:, :width], owned[:, width:], grad_gate)


def solution(mesh):
    rows = P(AXES, None)
    return jax.shard_map(
        functools.partial(local, mesh.shape["mp"]),
        mesh=mesh,
        in_specs=(rows, rows, rows, P(AXES), P(), P(), rows),
        out_specs=(rows, rows, rows, rows, P()),
        check_vma=False,
    )
```

time: 364 us -> 78.5 us (0.22)
  waiting for transfers between devices: 208 us -> 33.9 us
  matrix products: 57.1 us -> 0 us
  blocking collectives: 40.9 us -> 0 us
  starting transfers between devices: 0.11 us -> 26.6 us
  other arithmetic: 21.7 us -> 1.24 us
  local copies, waits for them, and re-layouts: 17.9 us -> 2.35 us
  between operations: 16.3 us -> 3.27 us
  Pallas kernels: 0 us -> 10.8 us
    all_gather x2 -> x0, waiting for transfers between devices: 109 us -> none  [the longest x1 55 us: local(): lax.all_gather(keys, ('section', 'mp'), axis=0, tiled=True)]
    reduce_scatter x1 -> x0, waiting for transfers between devices: 97.7 us -> none  [local(): lax.psum_scatter(term, ('section', 'mp'), scatter_dimension=0, tiled=True)]
    dot_general x20 -> x0, matrix products: 42.5 us -> none  [the longest x4 13.1 us: one_head(): dp = jnp.einsum('tgd,nd->gtn', do16, v, preferred_element_type=jnp.float32)]
    psum x1 -> x0, blocking collectives: 40.9 us -> none  [local(): gate_total = lax.psum(jnp.sum(gterms), ('section', 'mp'))]
    ppermute x0 -> x21, waiting for transfers between devices: none -> 33.9 us  [the longest x9 19.7 us: send_xy(): return lax.ppermute(x, AXES, perm)]
    ppermute x0 -> x21, starting transfers between devices: none -> 26.6 us  [the longest x9 14.4 us: send_z(): return lax.ppermute(x, 'mp', perm)]
    sub x4 -> x0, matrix products: 14.6 us -> none  [one_head(): e = jnp.where(valid[None], jnp.exp(s - top), 0.0)]
    pallas_call x0 -> x1, Pallas kernels: none -> 10.8 us  [attend(): pl.pallas_call(functools.partial(attend_kernel, folded), grid=(KV_HEADS,)...]
  transfers between devices with their start and end apart: 3 -> 21, of which waited for: 3 -> 12; matrix products, arithmetic and copies ran while one was open for 2% -> 1% of each run, Pallas kernels for 0% -> 0%
where the time goes in v1:
time: 78.5 us; the launch traced here: 78.2 us
  waiting for transfers between devices  33.9 us (43%)
  starting transfers between devices  26.6 us (34%)
  Pallas kernels  10.8 us (14%)
  between operations  3.27 us (4%)
  local copies, waits for them, and re-layouts  2.35 us (3%)
  other arithmetic  1.24 us (2%)
    ppermute x9, waiting for transfers between devices, send_xy(): return lax.ppermute(x, AXES, perm)  19.7 us
    ppermute x9, starting transfers between devices, send_z(): return lax.ppermute(x, 'mp', perm)  14.4 us
    ppermute x9, starting transfers between devices, send_xy(): return lax.ppermute(x, AXES, perm)  11.9 us
    pallas_call x1, Pallas kernels, attend(): pl.pallas_call(functools.partial(attend_kernel, folded), grid=(KV_HEADS,)...  10.8 us
    ppermute x9, waiting for transfers between devices, send_z(): return lax.ppermute(x, 'mp', perm)  8.57 us
    ppermute x3, waiting for transfers between devices, send_core(): return lax.ppermute(x, 'section', [(s, s ^ 1) for s in range(4)])  5.7 us
  transfers between devices with their start and end apart: 21, of which 12 were waited for; matrix products, arithmetic and copies ran while one was open for 1% of the time, Pallas kernels for 0%

profile of v1, /device:TPU:0, one launch (start us, length us, event | category | flops | bytes accessed | tf_op | source)
XLA Modules:
  0.0 78.2 jit_solution(15707141413392976106)
XLA Ops:
  0.6 0.8 constant_dynamic-update-slice_fusion.1
  1.4 0.8 constant_dynamic-update-slice_fusion
  2.2 3.0 %collective-permute-start = (bf16[32,1024]{1,0:T(8,128)(2,1)S(1)}, bf16[32,1024]{1,0:T(8,128)(2,1)S(1)}, u32[]{:S(2)}, u32[]{:S(2)}) collective-permute-start(bf16[32,1024]{1,0:T(8,128)(2,1)S(1)} %get-tuple-element.23), channel_id=1, source_target_pairs={{0,2},{1,3},{2,0},{3,1},{4,6},{5,7},{6,4},{7,5},{8,10},{9,11},{10,... | collective-permute-start | bytes 196616 | tf_op jit(solution)/shard_map/ppermute | solution.py:228
  5.2 2.6 %collective-permute-start.1 = (bf16[32,1024]{1,0:T(8,128)(2,1)S(1)}, bf16[32,1024]{1,0:T(8,128)(2,1)S(1)}, u32[]{:S(2)}, u32[]{:S(2)}) collective-permute-start(bf16[32,1024]{1,0:T(8,128)(2,1)S(1)} %get-tuple-element.23), channel_id=1, source_target_pairs={{0,4},{1,5},{2,6},{3,7},{4,0},{5,1},{6,2},{7,3},{8,12},{9,13},{10,... | collective-permute-start | bytes 196616 | tf_op jit(solution)/shard_map/ppermute | solution.py:228
  7.8 0.0 collective-permute-start.2
  7.8 0.0 collective-permute-done
  7.8 4.7 %collective-permute-done.1 = bf16[32,1024]{1,0:T(8,128)(2,1)S(1)} collective-permute-done((bf16[32,1024]{1,0:T(8,128)(2,1)S(1)}, bf16[32,1024]{1,0:T(8,128)(2,1)S(1)}, u32[]{:S(2)}, u32[]{:S(2)}) %collective-permute-start.1) | collective-permute-done | bytes 65568 | tf_op jit(solution)/shard_map/ppermute | solution.py:228
  12.4 1.4 %collective-permute-done.2 = bf16[32,1024]{1,0:T(8,128)(2,1)S(1)} collective-permute-done((bf16[32,1024]{1,0:T(8,128)(2,1)S(1)}, bf16[32,1024]{1,0:T(8,128)(2,1)S(1)}, u32[]{:S(2)}, u32[]{:S(2)}) %collective-permute-start.2) | collective-permute-done | bytes 65568 | tf_op jit(solution)/shard_map/ppermute | solution.py:228
  13.9 0.0 copy-start
  13.9 0.0 copy-start.2
  13.9 0.0 copy-start.3
  13.9 1.6 %collective-permute-start.3 = (bf16[128,1024]{1,0:T(8,128)(2,1)S(1)}, bf16[128,1024]{1,0:T(8,128)(2,1)S(1)}, u32[]{:S(2)}, u32[]{:S(2)}) collective-permute-start(bf16[128,1024]{1,0:T(8,128)(2,1)S(1)} %pad_maximum_fusion), channel_id=1, source_target_pairs={{0,1},{1,0},{2,3},{3,2},{4,5},{5,4},{6,7},{7,6},{8,9},{9,8},{10,11... | collective-permute-start | bytes 786440 | tf_op jit(solution)/shard_map/ppermute | solution.py:235
  15.5 1.5 %collective-permute-start.4 = (bf16[128,1024]{1,0:T(8,128)(2,1)S(1)}, bf16[128,1024]{1,0:T(8,128)(2,1)S(1)}, u32[]{:S(2)}, u32[]{:S(2)}) collective-permute-start(bf16[128,1024]{1,0:T(8,128)(2,1)S(1)} %pad_maximum_fusion), channel_id=1, source_target_pairs={{0,16},{1,17},{2,18},{3,19},{4,20},{5,21},{6,22},{7,23},{8,24},{9,... | collective-permute-start | bytes 786440 | tf_op jit(solution)/shard_map/ppermute | solution.py:235
  17.0 0.5 collective-permute-start.5
  17.5 4.8 %collective-permute-done.3 = bf16[128,1024]{1,0:T(8,128)(2,1)S(1)} collective-permute-done((bf16[128,1024]{1,0:T(8,128)(2,1)S(1)}, bf16[128,1024]{1,0:T(8,128)(2,1)S(1)}, u32[]{:S(2)}, u32[]{:S(2)}) %collective-permute-start.3) | collective-permute-done | bytes 262176 | tf_op jit(solution)/shard_map/ppermute | solution.py:235
  22.3 2.1 %collective-permute-done.4 = bf16[128,1024]{1,0:T(8,128)(2,1)S(1)} collective-permute-done((bf16[128,1024]{1,0:T(8,128)(2,1)S(1)}, bf16[128,1024]{1,0:T(8,128)(2,1)S(1)}, u32[]{:S(2)}, u32[]{:S(2)}) %collective-permute-start.4) | collective-permute-done | bytes 262176 | tf_op jit(solution)/shard_map/ppermute | solution.py:235
  24.5 2.7 %collective-permute-done.5 = bf16[128,1024]{1,0:T(8,128)(2,1)S(1)} collective-permute-done((bf16[128,1024]{1,0:T(8,128)(2,1)S(1)}, bf16[128,1024]{1,0:T(8,128)(2,1)S(1)}, u32[]{:S(2)}, u32[]{:S(2)}) %collective-permute-start.5) | collective-permute-done | bytes 262176 | tf_op jit(solution)/shard_map/ppermute | solution.py:235
  27.2 0.1 collective-permute-start.6
  27.9 2.0 %collective-permute-done.6.other = bf16[2,256,1024]{2,1,0:T(8,128)(2,1)S(1)} collective-permute-done((bf16[2,256,1024]{2,1,0:T(8,128)(2,1)S(1)}, bf16[2,256,1024]{2,1,0:T(8,128)(2,1)S(1)}, u32[]{:S(2)}, u32[]{:S(2)}) %collective-permute-start.6) | collective-permute-done | bytes 1048608 | tf_op jit(solution)/shard_map/ppermute | solution.py:238
  30.0 10.8 %shard_map.110 = (bf16[128,4096]{1,0:T(8,128)(2,1)}, bf16[128,4096]{1,0:T(8,128)(2,1)}, bf16[2,256,1024]{2,1,0:T(8,128)(2,1)S(1)}, bf16[2,256,1024]{2,1,0:T(8,128)(2,1)S(1)}, f32[8,128]{1,0:T(8,128)S(1)}) custom-call(s32[128]{0:T(128)S(1)} %copy-done.2, s32[4]{0:T(128)S(1)} %copy-done.3, f32[1]{0:T(128)S(6)} %copy.20.gate_s, s32[1,128]{1,0:T(1,128)S(1)} %bitcast.18, ...), custom_call_target="tpu_custom_call" | custom-call | flops 3221225472 | bytes 8388608 | tf_op jit(solution)/shard_map/pallas_call | solution.py:177
  40.8 0.2 collective-permute-start.7
  41.0 2.5 %collective-permute-done.7 = bf16[2,256,1024]{2,1,0:T(8,128)(2,1)S(1)} collective-permute-done((bf16[2,256,1024]{2,1,0:T(8,128)(2,1)S(1)}, bf16[2,256,1024]{2,1,0:T(8,128)(2,1)S(1)}, u32[]{:S(2)}, u32[]{:S(2)}) %collective-permute-start.7) | collective-permute-done | bytes 1048608 | tf_op jit(solution)/shard_map/ppermute | solution.py:238
  43.5 0.4 add_convert_fusion
  43.9 0.1 slice_bitcast_fusion.2
  44.0 2.5 %collective-permute-start.10 = (bf16[128,1024]{1,0:T(8,128)(2,1)S(1)}, bf16[128,1024]{1,0:T(8,128)(2,1)S(1)}, u32[]{:S(2)}, u32[]{:S(2)}) collective-permute-start(bf16[128,1024]{1,0:T(8,128)(2,1)S(1)} %get-tuple-element.16), channel_id=1, source_target_pairs={{0,17},{1,16},{2,19},{3,18},{4,21},{5,20},{6,23},{7,22},{8,25},{9,... | collective-permute-start | bytes 786440 | tf_op jit(solution)/shard_map/ppermute | solution.py:235
  46.5 0.5 collective-permute-start.8
  47.0 0.5 collective-permute-start.9
  47.6 0.0 collective-permute-start.14
  47.6 1.2 %collective-permute-done.14 = f32[8,128]{1,0:T(8,128)S(1)} collective-permute-done((f32[8,128]{1,0:T(8,128)S(1)}, f32[8,128]{1,0:T(8,128)S(1)}, u32[]{:S(2)}, u32[]{:S(2)}) %collective-permute-start.14) | collective-permute-done | bytes 4128 | tf_op jit(solution)/shard_map/ppermute | solution.py:238
  48.7 1.5 %collective-permute-start.15 = (f32[8,128]{1,0:T(8,128)S(1)}, f32[8,128]{1,0:T(8,128)S(1)}, u32[]{:S(2)}, u32[]{:S(2)}) collective-permute-start(f32[8,128]{1,0:T(8,128)S(1)} %add.49), channel_id=1, source_target_pairs={{0,1},{1,0},{2,3},{3,2},{4,5},{5,4},{6,7},{7,6},{8,9},{9,8},{10,11... | collective-permute-start | bytes 12296 | tf_op jit(solution)/shard_map/ppermute | solution.py:235
  50.2 1.5 %collective-permute-start.16 = (f32[8,128]{1,0:T(8,128)S(1)}, f32[8,128]{1,0:T(8,128)S(1)}, u32[]{:S(2)}, u32[]{:S(2)}) collective-permute-start(f32[8,128]{1,0:T(8,128)S(1)} %add.49), channel_id=1, source_target_pairs={{0,16},{1,17},{2,18},{3,19},{4,20},{5,21},{6,22},{7,23},{8,24},{9,... | collective-permute-start | bytes 12296 | tf_op jit(solution)/shard_map/ppermute | solution.py:235
  51.7 7.3 %collective-permute-done.15 = f32[8,128]{1,0:T(8,128)S(1)} collective-permute-done((f32[8,128]{1,0:T(8,128)S(1)}, f32[8,128]{1,0:T(8,128)S(1)}, u32[]{:S(2)}, u32[]{:S(2)}) %collective-permute-start.15) | collective-permute-done | bytes 4128 | tf_op jit(solution)/shard_map/ppermute | solution.py:235
  59.0 1.7 %collective-permute-start.17 = (f32[8,128]{1,0:T(8,128)S(1)}, f32[8,128]{1,0:T(8,128)S(1)}, u32[]{:S(2)}, u32[]{:S(2)}) collective-permute-start(f32[8,128]{1,0:T(8,128)S(1)} %add.49), channel_id=1, source_target_pairs={{0,17},{1,16},{2,19},{3,18},{4,21},{5,20},{6,23},{7,22},{8,25},{9,... | collective-permute-start | bytes 12296 | tf_op jit(solution)/shard_map/ppermute | solution.py:235
  60.8 2.7 %collective-permute-done.17 = f32[8,128]{1,0:T(8,128)S(1)} collective-permute-done((f32[8,128]{1,0:T(8,128)S(1)}, f32[8,128]{1,0:T(8,128)S(1)}, u32[]{:S(2)}, u32[]{:S(2)}) %collective-permute-start.17) | collective-permute-done | bytes 4128 | tf_op jit(solution)/shard_map/ppermute | solution.py:235
  63.5 0.7 collective-permute-start.18
  64.2 1.4 %collective-permute-start.19 = (f32[8,128]{1,0:T(8,128)S(1)}, f32[8,128]{1,0:T(8,128)S(1)}, u32[]{:S(2)}, u32[]{:S(2)}) collective-permute-start(f32[8,128]{1,0:T(8,128)S(1)} %add_add_fusion), channel_id=1, source_target_pairs={{0,4},{1,5},{2,6},{3,7},{4,0},{5,1},{6,2},{7,3},{8,12},{9,13},{10,... | collective-permute-start | bytes 12296 | tf_op jit(solution)/shard_map/ppermute | solution.py:228
  65.6 0.0 collective-permute-done.10
  65.6 2.3 %collective-permute-start.20 = (f32[8,128]{1,0:T(8,128)S(1)}, f32[8,128]{1,0:T(8,128)S(1)}, u32[]{:S(2)}, u32[]{:S(2)}) collective-permute-start(f32[8,128]{1,0:T(8,128)S(1)} %add_add_fusion), channel_id=1, source_target_pairs={{0,6},{1,7},{2,4},{3,5},{4,2},{5,3},{6,0},{7,1},{8,14},{9,15},{10,... | collective-permute-start | bytes 12296 | tf_op jit(solution)/shard_map/ppermute | solution.py:228
  67.9 0.0 collective-permute-done.8
  67.9 0.2 fusion.2
  68.1 0.1 collective-permute-start.11
  68.2 2.1 %collective-permute-start.12 = (bf16[32,1024]{1,0:T(8,128)(2,1)S(1)}, bf16[32,1024]{1,0:T(8,128)(2,1)S(1)}, u32[]{:S(2)}, u32[]{:S(2)}) collective-permute-start(bf16[32,1024]{1,0:T(8,128)(2,1)S(1)} %get-tuple-element.20), channel_id=1, source_target_pairs={{0,4},{1,5},{2,6},{3,7},{4,0},{5,1},{6,2},{7,3},{8,12},{9,13},{10,... | collective-permute-start | bytes 196616 | tf_op jit(solution)/shard_map/ppermute | solution.py:228
  70.3 0.0 collective-permute-done.18
  70.3 2.3 %collective-permute-start.13 = (bf16[32,1024]{1,0:T(8,128)(2,1)S(1)}, bf16[32,1024]{1,0:T(8,128)(2,1)S(1)}, u32[]{:S(2)}, u32[]{:S(2)}) collective-permute-start(bf16[32,1024]{1,0:T(8,128)(2,1)S(1)} %get-tuple-element.19), channel_id=1, source_target_pairs={{0,6},{1,7},{2,4},{3,5},{4,2},{5,3},{6,0},{7,1},{8,14},{9,15},{10,... | collective-permute-start | bytes 196616 | tf_op jit(solution)/shard_map/ppermute | solution.py:228
  72.6 0.6 add_reduce_fusion
  73.9 0.1 collective-permute-done.12
  74.0 2.4 %collective-permute-done.13 = bf16[32,1024]{1,0:T(8,128)(2,1)S(1)} collective-permute-done((bf16[32,1024]{1,0:T(8,128)(2,1)S(1)}, bf16[32,1024]{1,0:T(8,128)(2,1)S(1)}, u32[]{:S(2)}, u32[]{:S(2)}) %collective-permute-start.13) | collective-permute-done | bytes 65568 | tf_op jit(solution)/shard_map/ppermute | solution.py:228
  76.4 0.7 fusion.4
  (21 shorter events, 0.2 us)
Async XLA Ops:
  2.2 5.6 %collective-permute-start = (bf16[32,1024]{1,0:T(8,128)(2,1)S(1)}, bf16[32,1024]{1,0:T(8,128)(2,1)S(1)}, u32[]{:S(2)}, u32[]{:S(2)}) collective-permute-start(bf16[32,1024]{1,0:T(8,128)(2,1)S(1)} %get-tuple-element.23), channel_id=1, source_target_pairs={{0,2},{1,3},{2,0},{3,1},{4,6},{5,7},{6,4},{7,5},{8,10},{9,11},{10,... | collective-permute-start | bytes 196616 | tf_op jit(solution)/shard_map/ppermute | solution.py:228
  5.2 7.3 %collective-permute-start.1 = (bf16[32,1024]{1,0:T(8,128)(2,1)S(1)}, bf16[32,1024]{1,0:T(8,128)(2,1)S(1)}, u32[]{:S(2)}, u32[]{:S(2)}) collective-permute-start(bf16[32,1024]{1,0:T(8,128)(2,1)S(1)} %get-tuple-element.23), channel_id=1, source_target_pairs={{0,4},{1,5},{2,6},{3,7},{4,0},{5,1},{6,2},{7,3},{8,12},{9,13},{10,... | collective-permute-start | bytes 196616 | tf_op jit(solution)/shard_map/ppermute | solution.py:228
  7.8 6.1 %collective-permute-start.2 = (bf16[32,1024]{1,0:T(8,128)(2,1)S(1)}, bf16[32,1024]{1,0:T(8,128)(2,1)S(1)}, u32[]{:S(2)}, u32[]{:S(2)}) collective-permute-start(bf16[32,1024]{1,0:T(8,128)(2,1)S(1)} %get-tuple-element.23), channel_id=1, source_target_pairs={{0,6},{1,7},{2,4},{3,5},{4,2},{5,3},{6,0},{7,1},{8,14},{9,15},{10,... | collective-permute-start | bytes 196616 | tf_op jit(solution)/shard_map/ppermute | solution.py:228
  13.8 16.1 %copy-start.1 = (bf16[128,4096]{1,0:T(8,128)(2,1)S(1)}, bf16[128,4096]{1,0:T(8,128)(2,1)}, u32[]{:S(2)}) copy-start(bf16[128,4096]{1,0:T(8,128)(2,1)} %dy_ref.1) | copy-start | bytes 3145732
  13.9 16.1 %copy-start = (bf16[128,4096]{1,0:T(8,128)(2,1)S(1)}, bf16[128,4096]{1,0:T(8,128)(2,1)}, u32[]{:S(2)}) copy-start(bf16[128,4096]{1,0:T(8,128)(2,1)} %q_ref.1) | copy-start | bytes 3145732
  13.9 16.1 %copy-start.2 = (s32[128]{0:T(128)S(1)}, s32[128]{0:T(128)}, u32[]{:S(2)}) copy-start(s32[128]{0:T(128)} %seg_s.1) | copy-start | bytes 1540
  13.9 16.1 %copy-start.3 = (s32[4]{0:T(128)S(1)}, s32[4]{0:T(128)}, u32[]{:S(2)}) copy-start(s32[4]{0:T(128)} %cnt_s.1) | copy-start | bytes 52
  13.9 8.4 %collective-permute-start.3 = (bf16[128,1024]{1,0:T(8,128)(2,1)S(1)}, bf16[128,1024]{1,0:T(8,128)(2,1)S(1)}, u32[]{:S(2)}, u32[]{:S(2)}) collective-permute-start(bf16[128,1024]{1,0:T(8,128)(2,1)S(1)} %pad_maximum_fusion), channel_id=1, source_target_pairs={{0,1},{1,0},{2,3},{3,2},{4,5},{5,4},{6,7},{7,6},{8,9},{9,8},{10,11... | collective-permute-start | bytes 786440 | tf_op jit(solution)/shard_map/ppermute | solution.py:235
  15.5 9.0 %collective-permute-start.4 = (bf16[128,1024]{1,0:T(8,128)(2,1)S(1)}, bf16[128,1024]{1,0:T(8,128)(2,1)S(1)}, u32[]{:S(2)}, u32[]{:S(2)}) collective-permute-start(bf16[128,1024]{1,0:T(8,128)(2,1)S(1)} %pad_maximum_fusion), channel_id=1, source_target_pairs={{0,16},{1,17},{2,18},{3,19},{4,20},{5,21},{6,22},{7,23},{8,24},{9,... | collective-permute-start | bytes 786440 | tf_op jit(solution)/shard_map/ppermute | solution.py:235
  17.0 10.2 %collective-permute-start.5 = (bf16[128,1024]{1,0:T(8,128)(2,1)S(1)}, bf16[128,1024]{1,0:T(8,128)(2,1)S(1)}, u32[]{:S(2)}, u32[]{:S(2)}) collective-permute-start(bf16[128,1024]{1,0:T(8,128)(2,1)S(1)} %pad_maximum_fusion), channel_id=1, source_target_pairs={{0,17},{1,16},{2,19},{3,18},{4,21},{5,20},{6,23},{7,22},{8,25},{9,... | collective-permute-start | bytes 786440 | tf_op jit(solution)/shard_map/ppermute | solution.py:235
  27.2 2.7 %collective-permute-start.6 = (bf16[2,256,1024]{2,1,0:T(8,128)(2,1)S(1)}, bf16[2,256,1024]{2,1,0:T(8,128)(2,1)S(1)}, u32[]{:S(2)}, u32[]{:S(2)}) collective-permute-start(bf16[2,256,1024]{2,1,0:T(8,128)(2,1)S(1)} %bitcast.16), channel_id=1, source_target_pairs={{0,8},{8,0},{16,24},{24,16},{1,9},{9,1},{17,25},{25,17},{2,10},{10... | collective-permute-start | bytes 3145736 | tf_op jit(solution)/shard_map/ppermute | solution.py:238
  40.8 2.7 %collective-permute-start.7 = (bf16[2,256,1024]{2,1,0:T(8,128)(2,1)S(1)}, bf16[2,256,1024]{2,1,0:T(8,128)(2,1)S(1)}, u32[]{:S(2)}, u32[]{:S(2)}) collective-permute-start(bf16[2,256,1024]{2,1,0:T(8,128)(2,1)S(1)} %get-tuple-element.13), channel_id=1, source_target_pairs={{0,8},{8,0},{16,24},{24,16},{1,9},{9,1},{17,25},{25,17},{2,10},{10... | collective-permute-start | bytes 3145736 | tf_op jit(solution)/shard_map/ppermute | solution.py:238
  44.0 21.6 %collective-permute-start.10 = (bf16[128,1024]{1,0:T(8,128)(2,1)S(1)}, bf16[128,1024]{1,0:T(8,128)(2,1)S(1)}, u32[]{:S(2)}, u32[]{:S(2)}) collective-permute-start(bf16[128,1024]{1,0:T(8,128)(2,1)S(1)} %get-tuple-element.16), channel_id=1, source_target_pairs={{0,17},{1,16},{2,19},{3,18},{4,21},{5,20},{6,23},{7,22},{8,25},{9,... | collective-permute-start | bytes 786440 | tf_op jit(solution)/shard_map/ppermute | solution.py:235
  46.5 21.4 %collective-permute-start.8 = (bf16[128,1024]{1,0:T(8,128)(2,1)S(1)}, bf16[128,1024]{1,0:T(8,128)(2,1)S(1)}, u32[]{:S(2)}, u32[]{:S(2)}) collective-permute-start(bf16[128,1024]{1,0:T(8,128)(2,1)S(1)} %get-tuple-element.15), channel_id=1, source_target_pairs={{0,1},{1,0},{2,3},{3,2},{4,5},{5,4},{6,7},{7,6},{8,9},{9,8},{10,11... | collective-permute-start | bytes 786440 | tf_op jit(solution)/shard_map/ppermute | solution.py:235
  47.0 20.9 %collective-permute-start.9 = (bf16[128,1024]{1,0:T(8,128)(2,1)S(1)}, bf16[128,1024]{1,0:T(8,128)(2,1)S(1)}, u32[]{:S(2)}, u32[]{:S(2)}) collective-permute-start(bf16[128,1024]{1,0:T(8,128)(2,1)S(1)} %get-tuple-element.17), channel_id=1, source_target_pairs={{0,16},{1,17},{2,18},{3,19},{4,20},{5,21},{6,22},{7,23},{8,24},{9,... | collective-permute-start | bytes 786440 | tf_op jit(solution)/shard_map/ppermute | solution.py:235
  47.6 1.2 %collective-permute-start.14 = (f32[8,128]{1,0:T(8,128)S(1)}, f32[8,128]{1,0:T(8,128)S(1)}, u32[]{:S(2)}, u32[]{:S(2)}) collective-permute-start(f32[8,128]{1,0:T(8,128)S(1)} %get-tuple-element.14), channel_id=1, source_target_pairs={{0,8},{8,0},{16,24},{24,16},{1,9},{9,1},{17,25},{25,17},{2,10},{10... | collective-permute-start | bytes 12296 | tf_op jit(solution)/shard_map/ppermute | solution.py:238
  48.7 10.3 %collective-permute-start.15 = (f32[8,128]{1,0:T(8,128)S(1)}, f32[8,128]{1,0:T(8,128)S(1)}, u32[]{:S(2)}, u32[]{:S(2)}) collective-permute-start(f32[8,128]{1,0:T(8,128)S(1)} %add.49), channel_id=1, source_target_pairs={{0,1},{1,0},{2,3},{3,2},{4,5},{5,4},{6,7},{7,6},{8,9},{9,8},{10,11... | collective-permute-start | bytes 12296 | tf_op jit(solution)/shard_map/ppermute | solution.py:235
  50.2 10.6 %collective-permute-start.16 = (f32[8,128]{1,0:T(8,128)S(1)}, f32[8,128]{1,0:T(8,128)S(1)}, u32[]{:S(2)}, u32[]{:S(2)}) collective-permute-start(f32[8,128]{1,0:T(8,128)S(1)} %add.49), channel_id=1, source_target_pairs={{0,16},{1,17},{2,18},{3,19},{4,20},{5,21},{6,22},{7,23},{8,24},{9,... | collective-permute-start | bytes 12296 | tf_op jit(solution)/shard_map/ppermute | solution.py:235
  59.0 4.5 %collective-permute-start.17 = (f32[8,128]{1,0:T(8,128)S(1)}, f32[8,128]{1,0:T(8,128)S(1)}, u32[]{:S(2)}, u32[]{:S(2)}) collective-permute-start(f32[8,128]{1,0:T(8,128)S(1)} %add.49), channel_id=1, source_target_pairs={{0,17},{1,16},{2,19},{3,18},{4,21},{5,20},{6,23},{7,22},{8,25},{9,... | collective-permute-start | bytes 12296 | tf_op jit(solution)/shard_map/ppermute | solution.py:235
  63.5 6.8 %collective-permute-start.18 = (f32[8,128]{1,0:T(8,128)S(1)}, f32[8,128]{1,0:T(8,128)S(1)}, u32[]{:S(2)}, u32[]{:S(2)}) collective-permute-start(f32[8,128]{1,0:T(8,128)S(1)} %add_add_fusion), channel_id=1, source_target_pairs={{0,2},{1,3},{2,0},{3,1},{4,6},{5,7},{6,4},{7,5},{8,10},{9,11},{10,... | collective-permute-start | bytes 12296 | tf_op jit(solution)/shard_map/ppermute | solution.py:228
  64.2 8.4 %collective-permute-start.19 = (f32[8,128]{1,0:T(8,128)S(1)}, f32[8,128]{1,0:T(8,128)S(1)}, u32[]{:S(2)}, u32[]{:S(2)}) collective-permute-start(f32[8,128]{1,0:T(8,128)S(1)} %add_add_fusion), channel_id=1, source_target_pairs={{0,4},{1,5},{2,6},{3,7},{4,0},{5,1},{6,2},{7,3},{8,12},{9,13},{10,... | collective-permute-start | bytes 12296 | tf_op jit(solution)/shard_map/ppermute | solution.py:228
  65.6 7.0 %collective-permute-start.20 = (f32[8,128]{1,0:T(8,128)S(1)}, f32[8,128]{1,0:T(8,128)S(1)}, u32[]{:S(2)}, u32[]{:S(2)}) collective-permute-start(f32[8,128]{1,0:T(8,128)S(1)} %add_add_fusion), channel_id=1, source_target_pairs={{0,6},{1,7},{2,4},{3,5},{4,2},{5,3},{6,0},{7,1},{8,14},{9,15},{10,... | collective-permute-start | bytes 12296 | tf_op jit(solution)/shard_map/ppermute | solution.py:228
  68.1 5.7 %collective-permute-start.11 = (bf16[32,1024]{1,0:T(8,128)(2,1)S(1)}, bf16[32,1024]{1,0:T(8,128)(2,1)S(1)}, u32[]{:S(2)}, u32[]{:S(2)}) collective-permute-start(bf16[32,1024]{1,0:T(8,128)(2,1)S(1)} %get-tuple-element.18), channel_id=1, source_target_pairs={{0,2},{1,3},{2,0},{3,1},{4,6},{5,7},{6,4},{7,5},{8,10},{9,11},{10,... | collective-permute-start | bytes 196616 | tf_op jit(solution)/shard_map/ppermute | solution.py:228
  68.2 5.8 %collective-permute-start.12 = (bf16[32,1024]{1,0:T(8,128)(2,1)S(1)}, bf16[32,1024]{1,0:T(8,128)(2,1)S(1)}, u32[]{:S(2)}, u32[]{:S(2)}) collective-permute-start(bf16[32,1024]{1,0:T(8,128)(2,1)S(1)} %get-tuple-element.20), channel_id=1, source_target_pairs={{0,4},{1,5},{2,6},{3,7},{4,0},{5,1},{6,2},{7,3},{8,12},{9,13},{10,... | collective-permute-start | bytes 196616 | tf_op jit(solution)/shard_map/ppermute | solution.py:228
  70.3 6.1 %collective-permute-start.13 = (bf16[32,1024]{1,0:T(8,128)(2,1)S(1)}, bf16[32,1024]{1,0:T(8,128)(2,1)S(1)}, u32[]{:S(2)}, u32[]{:S(2)}) collective-permute-start(bf16[32,1024]{1,0:T(8,128)(2,1)S(1)} %get-tuple-element.19), channel_id=1, source_target_pairs={{0,6},{1,7},{2,4},{3,5},{4,2},{5,3},{6,0},{7,1},{8,14},{9,15},{10,... | collective-permute-start | bytes 196616 | tf_op jit(solution)/shard_map/ppermute | solution.py:228

commit v2 on v1

--- a/solution.py
+++ b/solution.py
@@ -5,12 +5,13 @@
 from jax import lax
 from jax.experimental import pallas as pl
 from jax.experimental.pallas import tpu as pltpu
+from jax.sharding import Mesh
 from jax.sharding import PartitionSpec as P
 
 KV_HEADS = 4
 TILE_TOK = 64
 IMG_TOK = 256
-AXES = ("section", "mp")
+AXES = ("x", "core", "z", "y")
 NEG = -1e30
 LOG2E = 1.4426950408889634
 
@@ -24,7 +25,8 @@
 
 
 def attend_kernel(
-    folded,
+    mine,
+    cols,
     seg_s,
     cnt_s,
     gate_s,
@@ -55,12 +57,11 @@
     hd = width // KV_HEADS
     group = q_ref.shape[1] // hd
     scale = 1.0 / hd**0.5
-    section = lax.axis_index("section")
-    core, xpos = section % 2, section // 2
+    core = lax.axis_index("core")
     img_a, img_b = seg_s[0], seg_s[tokens - 1]
 
     def place(img):
-        return ((img % 2) ^ core), ((img // 2) ^ xpos)
+        return (img % 2) ^ core, img // 2
 
     def fetch(i, img, start):
         par, dx = place(img)
@@ -85,12 +86,9 @@
         acc[...] = jnp.zeros_like(acc)
         g_ref[...] = jnp.zeros_like(g_ref)
         n = lax.broadcasted_iota(jnp.int32, (slots, tokens), 0)
-        if folded:
-            zpos = lax.axis_index("mp") // 2
-            per = slots // 8
-            tile = ((n // per) % 4) ^ zpos
-        else:
-            tile = n // TILE_TOK
+        outer, inner = n // mine, n % mine
+        place_n = (outer % cols) * (2 * mine) + (outer // cols) * mine + inner
+        tile = place_n // TILE_TOK
         limit = jnp.where(in_a, cnt_s[img_a], cnt_s[img_b])
         bias[...] = jnp.where(tile < limit, 0.0, NEG)
         rowsel[...] = jnp.broadcast_to(in_a.astype(jnp.float32), (hd, tokens)).T
@@ -106,10 +104,10 @@
     vcat_t = vcat.astype(jnp.float32).T.astype(jnp.bfloat16)
     zero = jnp.zeros((tokens, hd), jnp.bfloat16)
     for g in range(group):
-        cols = slice(g * hd, (g + 1) * hd)
+        feats = slice(g * hd, (g + 1) * hd)
         rows = slice(g * tokens, (g + 1) * tokens)
-        q = q_ref[:, cols]
-        dy = dy_ref[:, cols].astype(jnp.float32)
+        q = q_ref[:, feats]
+        dy = dy_ref[:, feats].astype(jnp.float32)
         do = (tg * dy).astype(jnp.bfloat16)
         qc[rows, :hd] = jnp.where(rows_a, q, zero)
         qc[rows, hd:] = jnp.where(rows_a, zero, q)
@@ -137,12 +135,12 @@
         dq = mm(kcat_t, dsh, NN)
         dq = jnp.where(in_a2, dq[:hd], dq[hd:])
         for j in range(pair):
-            cols = slice((h + j) * hd, (h + j + 1) * hd)
+            feats = slice((h + j) * hd, (h + j + 1) * hd)
             toks = slice(j * tokens, (j + 1) * tokens)
             ot = o[:, toks].T
-            y_ref[:, cols] = (tg * ot).astype(jnp.bfloat16)
-            gsum = gsum + dy_ref[:, cols].astype(jnp.float32) * ot
-            dq_ref[:, cols] = dq[:, toks].T.astype(jnp.bfloat16)
+            y_ref[:, feats] = (tg * ot).astype(jnp.bfloat16)
+            gsum = gsum + dy_ref[:, feats].astype(jnp.float32) * ot
+            dq_ref[:, feats] = dq[:, toks].T.astype(jnp.bfloat16)
     g_ref[...] += jnp.sum(gsum.reshape(tokens // 8, 8, hd), axis=0)
     dk = mm(ds16[...], qc[...], NN)
     dv = mm(p16[...], dc[...], NN)
@@ -164,7 +162,7 @@
         c0.wait()
 
 
-def attend(folded, seg, counts, gate, q, dy, own, other):
+def attend(mine, cols, seg, counts, gate, q, dy, own, other):
     tokens, feats = q.shape
     slots, width2 = own.shape[1], own.shape[2]
     hd = width2 // 2 // KV_HEADS
@@ -175,7 +173,7 @@
     cut = pl.BlockSpec((tokens, block), lambda i: (0, i))
     flops = 12 * KV_HEADS * rows * slots * hd * 2
     return pl.pallas_call(
-        functools.partial(attend_kernel, folded),
+        functools.partial(attend_kernel, mine, cols),
         grid=(KV_HEADS,),
         in_specs=[
             smem,
@@ -217,72 +215,47 @@
     )(seg, counts, gate, seg.reshape(1, tokens), q, dy, own, other)
 
 
-def local(mp, queries, keys, values, seg_image, tile_counts, gate, cotangent):
+def local(queries, keys, values, seg_image, tile_counts, gate, cotangent):
     f32, bf16 = jnp.float32, jnp.bfloat16
-    width = keys.shape[1]
-    mine = keys.shape[0]
-    folded = mp == 8
-
-    def send_z(x, k):
-        perm = [(m, ((m // 2) ^ k) * 2 + m % 2) for m in range(mp)]
-        return lax.ppermute(x, "mp", perm)
-
-    def send_xy(x, dx, dy):
-        perm = []
-        for s in range(4):
-            for m in range(mp):
-                perm.append((s * mp + m, (s ^ (2 * dx)) * mp + (m ^ dy)))
-        return lax.ppermute(x, AXES, perm)
+    mine, width = keys.shape
+    cols = lax.axis_size("z")
 
     def send_core(x):
-        return lax.ppermute(x, "section", [(s, s ^ 1) for s in range(4)])
+        return lax.ppermute(x, "core", [(0, 1), (1, 0)])
 
     kv = jnp.concatenate([keys, values], axis=1)
-    if folded:
-        col = jnp.concatenate([kv] + [send_z(kv, k) for k in (1, 2, 3)], axis=0)
-        parts = [col] + [send_xy(col, dx, dy) for dx, dy in ((0, 1), (1, 0), (1, 1))]
-        own = jnp.concatenate(parts, axis=0)
-    else:
-        col = lax.all_gather(kv, "mp", axis=0, tiled=True)
-        own = jnp.concatenate([col, send_xy(col, 1, 0)], axis=0)
+    kv = jnp.broadcast_to(kv[None], (cols,) + kv.shape)
+    col = lax.all_to_all(kv, "z", 0, 0, tiled=True)
+    col = jnp.broadcast_to(col[None], (4,) + col.shape)
+    own = lax.all_to_all(col, ("x", "y"), 0, 0, tiled=True)
     own = own.reshape(2, IMG_TOK, 2 * width)
     other = send_core(own)
 
     y, dq, part_own, part_other, gpart = attend(
-        folded, seg_image, tile_counts, gate, queries, cotangent, own, other
+        mine, cols, seg_image, tile_counts, gate, queries, cotangent, own, other
     )
 
     got = send_core(part_other)
-    gsum = gpart + send_core(gpart)
+    gates = jnp.broadcast_to(gpart[None], (4 * 2 * cols,) + gpart.shape)
+    gates = lax.all_to_all(gates, ("x", "core", "z", "y"), 0, 0, tiled=True)
     both = (part_own.astype(f32) + got.astype(f32)).astype(bf16)
-    if folded:
-        cut = both.reshape(4, 4 * mine, 2 * width)
-        order = ((0, 1), (1, 0), (1, 1))
-        recv = [send_xy(cut[2 * dx + dy], dx, dy) for dx, dy in order]
-        total = cut[0].astype(f32)
-        for r in recv:
-            total = total + r.astype(f32)
-        gsum = gsum + sum(send_xy(gsum, dx, dy) for dx, dy in order)
-        cut = total.astype(bf16).reshape(4, mine, 2 * width)
-        recv = [send_z(cut[k], k) for k in (1, 2, 3)]
-        owned = cut[0].astype(f32)
-        for r in recv:
-            owned = owned + r.astype(f32)
-        gsum = gsum + sum(send_z(gsum, k) for k in (1, 2, 3))
-    else:
-        total = both[0].astype(f32) + send_xy(both[1], 1, 0).astype(f32)
-        owned = lax.psum_scatter(total, "mp", scatter_dimension=0, tiled=True)
-        gsum = lax.psum(gsum + send_xy(gsum, 1, 0), "mp")
+    both = both.reshape(4, cols, mine, 2 * width)
+    both = lax.all_to_all(both, ("x", "y"), 0, 0, tiled=True)
+    total = jnp.sum(both.astype(f32), axis=0).astype(bf16)
+    total = lax.all_to_all(total, "z", 0, 0, tiled=True)
+    owned = jnp.sum(total.astype(f32), axis=0)
     tg = jnp.tanh(gate[0])
-    grad_gate = ((1.0 - tg * tg) * jnp.sum(gsum)).reshape(1)
+    grad_gate = ((1.0 - tg * tg) * jnp.sum(gates)).reshape(1)
     return (y, dq, owned[:, :width], owned[:, width:], grad_gate)
 
 
 def solution(mesh):
+    section, mp = mesh.shape["section"], mesh.shape["mp"]
+    fine = Mesh(mesh.devices.reshape(section // 2, 2, mp // 2, 2), AXES)
     rows = P(AXES, None)
     return jax.shard_map(
-        functools.partial(local, mesh.shape["mp"]),
-        mesh=mesh,
+        local,
+        mesh=fine,
         in_specs=(rows, rows, rows, P(AXES), P(), P(), rows),
         out_specs=(rows, rows, rows, rows, P()),
         check_vma=False,

time: 78.5 us -> 93.5 us (1.19)
  blocking collectives: 0 us -> 47.7 us
  starting transfers between devices: 26.6 us -> 7.57 us
  waiting for transfers between devices: 33.9 us -> 19.4 us
  other arithmetic: 1.24 us -> 2.78 us
    all_to_all x0 -> x3, blocking collectives: none -> 47.7 us  [the longest x1 17.1 us: local(): both = lax.all_to_all(both, ('x', 'y'), 0, 0, tiled=True)]
    ppermute x21 -> x2, waiting for transfers between devices: 33.9 us -> 4.54 us  [send_core(): return lax.ppermute(x, 'core', [(0, 1), (1, 0)])]
    ppermute x21 -> x2, starting transfers between devices: 26.6 us -> 0.19 us  [send_core(): return lax.ppermute(x, 'core', [(0, 1), (1, 0)])]
    all_to_all x0 -> x2, waiting for transfers between devices: none -> 14.9 us  [the longest x1 8.06 us: local(): total = lax.all_to_all(total, 'z', 0, 0, tiled=True)]
    all_to_all x0 -> x2, starting transfers between devices: none -> 7.38 us  [the longest x1 3.98 us: local(): gates = lax.all_to_all(gates, ('x', 'core', 'z', 'y'), 0, 0, tiled=True)]
    reduce_sum x1 -> x3, other arithmetic: 0.6 us -> 1.59 us  [the longest x1 0.93 us: local(): total = jnp.sum(both.astype(f32), axis=0).astype(bf16)]
  transfers between devices with their start and end apart: 21 -> 4, of which waited for: 12 -> 4; matrix products, arithmetic and copies ran while one was open for 1% -> 2% of each run, Pallas kernels for 0% -> 0%
where the time goes in v2:
time: 93.5 us; the launch traced here: 93 us
  blocking collectives  47.7 us (51%)
  waiting for transfers between devices  19.4 us (21%)
  Pallas kernels  10.9 us (12%)
  starting transfers between devices  7.57 us (8%)
  between operations  3.21 us (3%)
  other arithmetic  2.78 us (3%)
  local copies, waits for them, and re-layouts  1.48 us (2%)
    all_to_all x1, blocking collectives, local(): both = lax.all_to_all(both, ('x', 'y'), 0, 0, tiled=True)  17.1 us
    all_to_all x1, blocking collectives, local(): own = lax.all_to_all(col, ('x', 'y'), 0, 0, tiled=True)  15.5 us
    all_to_all x1, blocking collectives, local(): col = lax.all_to_all(kv, 'z', 0, 0, tiled=True)  15 us
    pallas_call x1, Pallas kernels, attend(): pl.pallas_call(functools.partial(attend_kernel, mine, cols), grid=(KV_HEA...  10.9 us
    all_to_all x1, waiting for transfers between devices, local(): total = lax.all_to_all(total, 'z', 0, 0, tiled=True)  8.06 us
    all_to_all x1, waiting for transfers between devices, local(): gates = lax.all_to_all(gates, ('x', 'core', 'z', 'y'), 0, 0, tiled=True)  6.81 us
    ppermute x2, waiting for transfers between devices, send_core(): return lax.ppermute(x, 'core', [(0, 1), (1, 0)])  4.54 us
    all_to_all x1, starting transfers between devices, local(): gates = lax.all_to_all(gates, ('x', 'core', 'z', 'y'), 0, 0, tiled=True)  3.98 us
  transfers between devices with their start and end apart: 4, of which 4 were waited for; matrix products, arithmetic and copies ran while one was open for 2% of the time, Pallas kernels for 0%

profile of v2, /device:TPU:0, one launch (start us, length us, event | category | flops | bytes accessed | tf_op | source)
XLA Modules:
  0.0 93.0 jit_solution(14275414920962370254)
XLA Ops:
  0.6 0.8 pad_maximum_fusion
  1.4 15.0 %all_to_all.25 = bf16[4,32,1024]{2,1,0:T(8,128)(2,1)S(1)} all-to-all(bf16[4,32,1024]{2,1,0:T(8,128)(2,1)S(1)} %broadcast_in_dim.6), channel_id=1, replica_groups=mesh['x'=2,'core'=2,'z'=4,'y'=2] {'z'}, dimensions={0} | all-to-all | bytes 524288 | tf_op jit(solution)/shard_map/all_to_all | solution.py:228
  16.4 0.1 broadcast_in_dim.7
  16.6 0.0 copy-start
  16.6 0.0 copy-start.1
  16.6 0.0 copy-start.2
  16.6 0.0 copy-start.3
  16.6 15.5 %all_to_all.26 = bf16[4,4,32,1024]{3,2,1,0:T(8,128)(2,1)S(1)} all-to-all(bf16[4,4,32,1024]{3,2,1,0:T(8,128)(2,1)S(1)} %broadcast_in_dim.7), channel_id=1, replica_groups=mesh['x'=2,'core'=2,'z'=4,'y'=2] {'x','y'}, dimensions={0} | all-to-all | bytes 2097152 | tf_op jit(solution)/shard_map/all_to_all | solution.py:230
  32.1 0.0 collective-permute-start
  32.8 2.0 %collective-permute-done.other = bf16[2,256,1024]{2,1,0:T(8,128)(2,1)S(1)} collective-permute-done((bf16[2,256,1024]{2,1,0:T(8,128)(2,1)S(1)}, bf16[2,256,1024]{2,1,0:T(8,128)(2,1)S(1)}, u32[]{:S(2)}, u32[]{:S(2)}) %collective-permute-start) | collective-permute-done | bytes 1048608 | tf_op jit(solution)/shard_map/ppermute | solution.py:224
  34.8 0.0 copy-done
  34.8 0.0 copy-done.1
  34.8 0.0 copy-done.2
  34.8 0.0 copy-done.3
  34.8 10.9 %shard_map.110 = (bf16[128,4096]{1,0:T(8,128)(2,1)}, bf16[128,4096]{1,0:T(8,128)(2,1)}, bf16[2,256,1024]{2,1,0:T(8,128)(2,1)S(1)}, bf16[2,256,1024]{2,1,0:T(8,128)(2,1)S(1)}, f32[8,128]{1,0:T(8,128)S(1)}) custom-call(s32[128]{0:T(128)S(1)} %copy-done.2, s32[4]{0:T(128)S(1)} %copy-done.3, f32[1]{0:T(128)S(6)} %copy.12.gate_s, s32[1,128]{1,0:T(1,128)S(1)} %bitcast.7, ...), custom_call_target="tpu_custom_call" | custom-call | flops 3221225472 | bytes 8388608 | tf_op jit(solution)/shard_map/pallas_call | solution.py:175
  45.7 0.2 collective-permute-start.1
  45.9 2.5 %collective-permute-done.1 = bf16[2,256,1024]{2,1,0:T(8,128)(2,1)S(1)} collective-permute-done((bf16[2,256,1024]{2,1,0:T(8,128)(2,1)S(1)}, bf16[2,256,1024]{2,1,0:T(8,128)(2,1)S(1)}, u32[]{:S(2)}, u32[]{:S(2)}) %collective-permute-start.1) | collective-permute-done | bytes 1048608 | tf_op jit(solution)/shard_map/ppermute | solution.py:224
  48.5 0.4 add_convert_fusion
  48.9 17.1 %all_to_all.27 = bf16[4,4,32,1024]{3,2,1,0:T(8,128)(2,1)S(1)} all-to-all(bf16[4,4,32,1024]{3,2,1,0:T(8,128)(2,1)S(1)} %bitcast.8), channel_id=1, replica_groups=mesh['x'=2,'core'=2,'z'=4,'y'=2] {'x','y'}, dimensions={0} | all-to-all | bytes 2097152 | tf_op jit(solution)/shard_map/all_to_all | solution.py:243
  66.0 0.7 broadcast_in_dim.8
  66.7 4.0 %all-to-all-start.4 = ((f32[32,8,128]{2,1,0:T(8,128)}), f32[32,8,128]{2,1,0:T(8,128)S(1)}, u32[]{:S(2)}, u32[]{:S(2)}) async-start(f32[32,8,128]{2,1,0:T(8,128)} %broadcast_in_dim.8), calls=%async_computation.4 | async-start | bytes 262144 | tf_op jit(solution)/shard_map/all_to_all | solution.py:240
  70.7 0.9 reduce_sum.30
  71.6 6.8 %all-to-all-done.4 = f32[32,8,128]{2,1,0:T(8,128)S(1)} async-done(((f32[32,8,128]{2,1,0:T(8,128)}), f32[32,8,128]{2,1,0:T(8,128)S(1)}, u32[]{:S(2)}, u32[]{:S(2)}) %all-to-all-start.4) | async-done | bytes 131104 | tf_op jit(solution)/shard_map/all_to_all | solution.py:240
  78.4 3.4 %all-to-all-start.3 = ((bf16[4,32,1024]{2,1,0:T(8,128)(2,1)}), bf16[4,32,1024]{2,1,0:T(8,128)(2,1)S(1)}, u32[]{:S(2)}, u32[]{:S(2)}) async-start(bf16[4,32,1024]{2,1,0:T(8,128)(2,1)} %reduce_sum.30), calls=%async_computation.3 | async-start | bytes 524288 | tf_op jit(solution)/shard_map/all_to_all | solution.py:245
  81.9 0.6 reduce_sum.32
  83.1 8.1 %all-to-all-done.3 = bf16[4,32,1024]{2,1,0:T(8,128)(2,1)S(1)} async-done(((bf16[4,32,1024]{2,1,0:T(8,128)(2,1)}), bf16[4,32,1024]{2,1,0:T(8,128)(2,1)S(1)}, u32[]{:S(2)}, u32[]{:S(2)}) %all-to-all-start.3) | async-done | bytes 262176 | tf_op jit(solution)/shard_map/all_to_all | solution.py:245
  91.2 0.7 fusion
  (2 shorter events, 0.1 us)
Async XLA Ops:
  16.6 18.2 %copy-start = (bf16[128,4096]{1,0:T(8,128)(2,1)S(1)}, bf16[128,4096]{1,0:T(8,128)(2,1)}, u32[]{:S(2)}) copy-start(bf16[128,4096]{1,0:T(8,128)(2,1)} %q_ref.1) | copy-start | bytes 3145732
  16.6 18.2 %copy-start.1 = (bf16[128,4096]{1,0:T(8,128)(2,1)S(1)}, bf16[128,4096]{1,0:T(8,128)(2,1)}, u32[]{:S(2)}) copy-start(bf16[128,4096]{1,0:T(8,128)(2,1)} %dy_ref.1) | copy-start | bytes 3145732
  16.6 18.2 %copy-start.2 = (s32[128]{0:T(128)S(1)}, s32[128]{0:T(128)}, u32[]{:S(2)}) copy-start(s32[128]{0:T(128)} %seg_s.1) | copy-start | bytes 1540
  16.6 18.2 %copy-start.3 = (s32[4]{0:T(128)S(1)}, s32[4]{0:T(128)}, u32[]{:S(2)}) copy-start(s32[4]{0:T(128)} %cnt_s.1) | copy-start | bytes 52
  32.1 2.7 %collective-permute-start = (bf16[2,256,1024]{2,1,0:T(8,128)(2,1)S(1)}, bf16[2,256,1024]{2,1,0:T(8,128)(2,1)S(1)}, u32[]{:S(2)}, u32[]{:S(2)}) collective-permute-start(bf16[2,256,1024]{2,1,0:T(8,128)(2,1)S(1)} %bitcast.5), channel_id=1, source_target_pairs={{0,8},{8,0},{1,9},{9,1},{2,10},{10,2},{3,11},{11,3},{4,12},{12,4},... | collective-permute-start | bytes 3145736 | tf_op jit(solution)/shard_map/ppermute | solution.py:224
  45.7 2.7 %collective-permute-start.1 = (bf16[2,256,1024]{2,1,0:T(8,128)(2,1)S(1)}, bf16[2,256,1024]{2,1,0:T(8,128)(2,1)S(1)}, u32[]{:S(2)}, u32[]{:S(2)}) collective-permute-start(bf16[2,256,1024]{2,1,0:T(8,128)(2,1)S(1)} %get-tuple-element.13), channel_id=1, source_target_pairs={{0,8},{8,0},{1,9},{9,1},{2,10},{10,2},{3,11},{11,3},{4,12},{12,4},... | collective-permute-start | bytes 3145736 | tf_op jit(solution)/shard_map/ppermute | solution.py:224
  66.7 11.7 %all-to-all-start.4 = ((f32[32,8,128]{2,1,0:T(8,128)}), f32[32,8,128]{2,1,0:T(8,128)S(1)}, u32[]{:S(2)}, u32[]{:S(2)}) async-start(f32[32,8,128]{2,1,0:T(8,128)} %broadcast_in_dim.8), calls=%async_computation.4 | async-start | bytes 262144 | tf_op jit(solution)/shard_map/all_to_all | solution.py:240
  78.4 12.8 %all-to-all-start.3 = ((bf16[4,32,1024]{2,1,0:T(8,128)(2,1)}), bf16[4,32,1024]{2,1,0:T(8,128)(2,1)S(1)}, u32[]{:S(2)}, u32[]{:S(2)}) async-start(bf16[4,32,1024]{2,1,0:T(8,128)(2,1)} %reduce_sum.30), calls=%async_computation.3 | async-start | bytes 524288 | tf_op jit(solution)/shard_map/all_to_all | solution.py:245

commit v3 on v2

--- a/solution.py
+++ b/solution.py
@@ -14,10 +14,13 @@
 AXES = ("x", "core", "z", "y")
 NEG = -1e30
 LOG2E = 1.4426950408889634
+CHUNKS = 2
+GROWS = 16
+GTOP = 8
+PEERS = ((0, 1), (1, 0), (1, 1))
 
 NT = (((1,), (1,)), ((), ()))
 NN = (((1,), (0,)), ((), ()))
-TN = (((0,), (0,)), ((), ()))
 
 
 def mm(a, b, dims):
@@ -27,6 +30,8 @@
 def attend_kernel(
     mine,
     cols,
+    folded,
+    first,
     seg_s,
     cnt_s,
     gate_s,
@@ -35,6 +40,9 @@
     dy_ref,
     own,
     other,
+    g_in,
+    y_in,
+    dq_in,
     y_ref,
     dq_ref,
     part_own,
@@ -51,17 +59,19 @@
     sems,
 ):
     step = pl.program_id(0)
-    last = pl.num_programs(0) - 1
+    heads = kv.shape[2] // (2 * q_ref.shape[0])
+    last = heads - 1
     tokens = q_ref.shape[0]
     slots, width = kv.shape[1], kv.shape[2] // 2
-    hd = width // KV_HEADS
+    half = slots // 2
+    hd = width // heads
     group = q_ref.shape[1] // hd
     scale = 1.0 / hd**0.5
-    core = lax.axis_index("core")
+    core, xpos = lax.axis_index("core"), lax.axis_index("x")
     img_a, img_b = seg_s[0], seg_s[tokens - 1]
 
     def place(img):
-        return (img % 2) ^ core, img // 2
+        return (img % 2) ^ core, (img // 2) ^ xpos
 
     def fetch(i, img, start):
         par, dx = place(img)
@@ -84,11 +94,13 @@
         fetch(0, img_a, True)
         fetch(1, img_b, True)
         acc[...] = jnp.zeros_like(acc)
-        g_ref[...] = jnp.zeros_like(g_ref)
+        g_ref[...] = jnp.zeros_like(g_ref) if first else g_in[...]
         n = lax.broadcasted_iota(jnp.int32, (slots, tokens), 0)
-        outer, inner = n // mine, n % mine
-        place_n = (outer % cols) * (2 * mine) + (outer // cols) * mine + inner
-        tile = place_n // TILE_TOK
+        zi = (n // mine) % cols
+        yi = (n // half) ^ lax.axis_index("y")
+        if folded:
+            zi = zi ^ lax.axis_index("z")
+        tile = (zi * (2 * mine) + yi * mine + n % mine) // TILE_TOK
         limit = jnp.where(in_a, cnt_s[img_a], cnt_s[img_b])
         bias[...] = jnp.where(tile < limit, 0.0, NEG)
         rowsel[...] = jnp.broadcast_to(in_a.astype(jnp.float32), (hd, tokens)).T
@@ -142,18 +154,31 @@
             gsum = gsum + dy_ref[:, feats].astype(jnp.float32) * ot
             dq_ref[:, feats] = dq[:, toks].T.astype(jnp.bfloat16)
     g_ref[...] += jnp.sum(gsum.reshape(tokens // 8, 8, hd), axis=0)
-    dk = mm(ds16[...], qc[...], NN)
-    dv = mm(p16[...], dc[...], NN)
+    dk = mm(ds16[...], qc[...], NN).astype(jnp.bfloat16)
+    dv = mm(p16[...], dc[...], NN).astype(jnp.bfloat16)
     par_a, dx_a = place(img_a)
     par_b, dx_b = place(img_b)
-    at_a, at_b = par_a * 2 + dx_a, par_b * 2 + dx_b
-    acc[at_b, :, kcols] = dk[:, hd:].astype(jnp.bfloat16)
-    acc[at_b, :, vcols] = dv[:, hd:].astype(jnp.bfloat16)
-    acc[at_a, :, kcols] = dk[:, :hd].astype(jnp.bfloat16)
-    acc[at_a, :, vcols] = dv[:, :hd].astype(jnp.bfloat16)
+    krows = pl.ds(pl.multiple_of(step * half, half), half)
+    vrows = pl.ds(pl.multiple_of((heads + step) * half, half), half)
+    for at, lanes in ((par_b * 2 + dx_b, slice(hd, 2 * hd)), (par_a * 2 + dx_a, slice(0, hd))):
+        for j in range(2):
+            part = slice(j * half, (j + 1) * half)
+            acc[at, j, krows] = dk[part, lanes]
+            acc[at, j, vrows] = dv[part, lanes]
 
     @pl.when(step == last)
     def _():
+        left = jnp.broadcast_to(jnp.sum(g_ref[...], axis=0, keepdims=True), (GROWS, hd))
+        line = lax.broadcasted_iota(jnp.int32, (GROWS, hd), 0)
+        digits = jnp.zeros((GROWS, hd), jnp.float32)
+        for i in range(GROWS):
+            unit = 4.0 ** (GTOP - i)
+            d = jnp.round(left * (1.0 / unit))
+            left = left - d * unit
+            digits = jnp.where(line == i, d, digits)
+        for i in range(4):
+            for j in range(2):
+                acc[i, j, 2 * heads * half :] = digits.astype(jnp.bfloat16)
         c1 = pltpu.make_async_copy(acc.at[pl.ds(2, 2)], part_other, sems.at[2])
         c0 = pltpu.make_async_copy(acc.at[pl.ds(0, 2)], part_own, sems.at[3])
         c1.start()
@@ -162,19 +187,25 @@
         c0.wait()
 
 
-def attend(mine, cols, seg, counts, gate, q, dy, own, other):
+def attend(chunk, mine, cols, folded, seg, counts, gate, q, dy, own, other, prev):
     tokens, feats = q.shape
     slots, width2 = own.shape[1], own.shape[2]
-    hd = width2 // 2 // KV_HEADS
+    heads = KV_HEADS // CHUNKS
+    hd = width2 // 2 // heads
     block = feats // KV_HEADS
     rows = block // hd * tokens
     smem = pl.BlockSpec(memory_space=pltpu.SMEM)
     hbm = pl.BlockSpec(memory_space=pl.ANY)
-    cut = pl.BlockSpec((tokens, block), lambda i: (0, i))
-    flops = 12 * KV_HEADS * rows * slots * hd * 2
+    cut = pl.BlockSpec((tokens, block), lambda i: (0, i + chunk * heads))
+    gspec = pl.BlockSpec((8, hd), lambda i: (0, 0))
+    flops = 12 * heads * rows * slots * hd * 2
+    first = prev is None
+    if first:
+        prev = (jnp.zeros((8, hd), jnp.float32), q, q)
+    part = (2, 2, heads * slots + GROWS, hd)
     return pl.pallas_call(
-        functools.partial(attend_kernel, mine, cols),
-        grid=(KV_HEADS,),
+        functools.partial(attend_kernel, mine, cols, folded, first),
+        grid=(heads,),
         in_specs=[
             smem,
             smem,
@@ -184,18 +215,22 @@
             cut,
             hbm,
             hbm,
+            gspec,
+            hbm,
+            hbm,
         ],
-        out_specs=[cut, cut, hbm, hbm, pl.BlockSpec((8, hd), lambda i: (0, 0))],
+        out_specs=[cut, cut, hbm, hbm, gspec],
         out_shape=[
             jax.ShapeDtypeStruct(q.shape, jnp.bfloat16),
             jax.ShapeDtypeStruct(q.shape, jnp.bfloat16),
-            jax.ShapeDtypeStruct(own.shape, jnp.bfloat16),
-            jax.ShapeDtypeStruct(own.shape, jnp.bfloat16),
+            jax.ShapeDtypeStruct(part, jnp.bfloat16),
+            jax.ShapeDtypeStruct(part, jnp.bfloat16),
             jax.ShapeDtypeStruct((8, hd), jnp.float32),
         ],
+        input_output_aliases={} if first else {9: 0, 10: 1},
         scratch_shapes=[
             pltpu.VMEM((2, slots, width2), jnp.bfloat16),
-            pltpu.VMEM((4, slots, width2), jnp.bfloat16),
+            pltpu.VMEM((4,) + part[1:], jnp.bfloat16),
             pltpu.VMEM((rows, 2 * hd), jnp.bfloat16),
             pltpu.VMEM((rows, 2 * hd), jnp.bfloat16),
             pltpu.VMEM((slots, rows), jnp.bfloat16),
@@ -209,44 +244,83 @@
         ),
         cost_estimate=pl.CostEstimate(
             flops=flops,
-            bytes_accessed=8 * q.size + 8 * own.size,
-            transcendentals=KV_HEADS * rows * slots,
+            bytes_accessed=4 * q.size + 8 * own.size,
+            transcendentals=heads * rows * slots,
         ),
-    )(seg, counts, gate, seg.reshape(1, tokens), q, dy, own, other)
+    )(seg, counts, gate, seg.reshape(1, tokens), q, dy, own, other, *prev)
 
 
 def local(queries, keys, values, seg_image, tile_counts, gate, cotangent):
     f32, bf16 = jnp.float32, jnp.bfloat16
     mine, width = keys.shape
+    hd = width // KV_HEADS
+    heads = KV_HEADS // CHUNKS
+    wide = width // CHUNKS
     cols = lax.axis_size("z")
+    folded = cols == 4
+    half = cols * mine
+
+    def send_z(x, k):
+        return lax.ppermute(x, "z", [(i, i ^ k) for i in range(cols)])
+
+    def send_xy(x, dx, dy):
+        return lax.ppermute(x, ("x", "y"), [(i, i ^ (2 * dx + dy)) for i in range(4)])
 
     def send_core(x):
         return lax.ppermute(x, "core", [(0, 1), (1, 0)])
 
-    kv = jnp.concatenate([keys, values], axis=1)
-    kv = jnp.broadcast_to(kv[None], (cols,) + kv.shape)
-    col = lax.all_to_all(kv, "z", 0, 0, tiled=True)
-    col = jnp.broadcast_to(col[None], (4,) + col.shape)
-    own = lax.all_to_all(col, ("x", "y"), 0, 0, tiled=True)
-    own = own.reshape(2, IMG_TOK, 2 * width)
-    other = send_core(own)
-
-    y, dq, part_own, part_other, gpart = attend(
-        mine, cols, seg_image, tile_counts, gate, queries, cotangent, own, other
+    kv = jnp.stack(
+        [
+            jnp.concatenate([keys[:, c * wide : (c + 1) * wide], values[:, c * wide : (c + 1) * wide]], axis=1)
+            for c in range(CHUNKS)
+        ]
     )
-
-    got = send_core(part_other)
-    gates = jnp.broadcast_to(gpart[None], (4 * 2 * cols,) + gpart.shape)
-    gates = lax.all_to_all(gates, ("x", "core", "z", "y"), 0, 0, tiled=True)
-    both = (part_own.astype(f32) + got.astype(f32)).astype(bf16)
-    both = both.reshape(4, cols, mine, 2 * width)
-    both = lax.all_to_all(both, ("x", "y"), 0, 0, tiled=True)
-    total = jnp.sum(both.astype(f32), axis=0).astype(bf16)
-    total = lax.all_to_all(total, "z", 0, 0, tiled=True)
-    owned = jnp.sum(total.astype(f32), axis=0)
+    if folded:
+        col = [kv] + [send_z(kv, k) for k in (1, 2, 3)]
+    else:
+        col = [lax.all_gather(kv, "z", axis=1, tiled=True)]
+
+    prev = None
+    reduced = []
+    for c in range(CHUNKS):
+        block = jnp.concatenate([p[c] for p in col], axis=0)
+        own = jnp.concatenate([block] + [send_xy(block, *p) for p in PEERS], axis=0)
+        own = own.reshape(2, 2 * half, 2 * wide)
+        other = send_core(own)
+        y, dq, part_own, part_other, g = attend(
+            c, mine, cols, folded, seg_image, tile_counts, gate, queries, cotangent, own, other, prev
+        )
+        prev = (g, y, dq)
+        got = send_core(part_other)
+        both = (part_own.astype(f32) + got.astype(f32)).astype(bf16)
+        total = both[0, 0].astype(f32)
+        for dx, dy in PEERS:
+            total = total + send_xy(both[dx, dy], dx, dy).astype(f32)
+        grads, gates = total[: 2 * heads * half], total[2 * heads * half :]
+        grads = grads.reshape(2 * heads, cols, mine, hd)
+        if folded:
+            grads, gates = grads.astype(bf16), gates.astype(bf16)
+            cut = [
+                jnp.concatenate([grads[:, k].reshape(2 * heads * mine, hd), gates], axis=0) for k in range(cols)
+            ]
+            total = cut[0].astype(f32)
+            for k in (1, 2, 3):
+                total = total + send_z(cut[k], k).astype(f32)
+            grads, gates = total[: 2 * heads * mine], total[2 * heads * mine :]
+        else:
+            grads = lax.psum_scatter(grads, "z", scatter_dimension=1, tiled=True)
+            gates = lax.psum(gates, "z")
+        reduced.append(grads.reshape(2 * heads, mine, hd))
+
+    def lay(blocks):
+        return jnp.concatenate(blocks, axis=1)
+
+    dk = lay([r[i] for r in reduced for i in range(heads)])
+    dv = lay([r[heads + i] for r in reduced for i in range(heads)])
+    units = 4.0 ** (GTOP - jnp.arange(GROWS, dtype=f32))
     tg = jnp.tanh(gate[0])
-    grad_gate = ((1.0 - tg * tg) * jnp.sum(gates)).reshape(1)
-    return (y, dq, owned[:, :width], owned[:, width:], grad_gate)
+    grad_gate = ((1.0 - tg * tg) * jnp.sum(gates * units[:, None])).reshape(1)
+    return (y, dq, dk, dv, grad_gate)
 
 
 def solution(mesh):

time: 93.5 us -> 79.3 us (0.85)
  blocking collectives: 47.7 us -> 0 us
  starting transfers between devices: 7.57 us -> 30.5 us
  waiting for transfers between devices: 19.4 us -> 28.1 us
  Pallas kernels: 10.9 us -> 12.8 us
    all_to_all x3 -> x0, blocking collectives: 47.7 us -> none  [the longest x1 17.1 us: local(): both = lax.all_to_all(both, ('x', 'y'), 0, 0, tiled=True)]
    ppermute x0 -> x21, starting transfers between devices: none -> 29.6 us  [the longest x12 15.1 us: send_xy(): return lax.ppermute(x, ('x', 'y'), [(i, i ^ 2 * dx + dy) for i in range(4)])]
    ppermute x0 -> x21, waiting for transfers between devices: none -> 28.1 us  [the longest x12 19.2 us: send_xy(): return lax.ppermute(x, ('x', 'y'), [(i, i ^ 2 * dx + dy) for i in range(4)])]
    all_to_all x2 -> x0, waiting for transfers between devices: 14.9 us -> none  [the longest x1 8.06 us: local(): total = lax.all_to_all(total, 'z', 0, 0, tiled=True)]
    all_to_all x2 -> x0, starting transfers between devices: 7.38 us -> none  [the longest x1 3.98 us: local(): gates = lax.all_to_all(gates, ('x', 'core', 'z', 'y'), 0, 0, tiled=True)]
    ppermute x2 -> x4, waiting for transfers between devices: 4.54 us -> 0.01 us  [send_core(): return lax.ppermute(x, 'core', [(0, 1), (1, 0)])]
    pallas_call x1 -> x2, Pallas kernels: 10.9 us -> 12.8 us  [attend(): pl.pallas_call(functools.partial(attend_kernel, mine, cols, folded, first...]
  transfers between devices with their start and end apart: 4 -> 25, of which waited for: 4 -> 12; matrix products, arithmetic and copies ran while one was open for 2% -> 1% of each run, Pallas kernels for 0% -> 16%
where the time goes in v3:
time: 79.3 us; the launch traced here: 79.1 us
  starting transfers between devices  30.5 us (38%)
  waiting for transfers between devices  28.1 us (35%)
  Pallas kernels  12.8 us (16%)
  between operations  3.47 us (4%)
  other arithmetic  2.51 us (3%)
  local copies, waits for them, and re-layouts  1.72 us (2%)
    ppermute x12, waiting for transfers between devices, send_xy(): return lax.ppermute(x, ('x', 'y'), [(i, i ^ 2 * dx + dy) for i in range(4)])  19.2 us
    ppermute x12, starting transfers between devices, send_xy(): return lax.ppermute(x, ('x', 'y'), [(i, i ^ 2 * dx + dy) for i in range(4)])  15.1 us
    ppermute x9, starting transfers between devices, send_z(): return lax.ppermute(x, 'z', [(i, i ^ k) for i in range(cols)])  14.6 us
    pallas_call x2, Pallas kernels, attend(): pl.pallas_call(functools.partial(attend_kernel, mine, cols, folded, first...  12.8 us
    ppermute x9, waiting for transfers between devices, send_z(): return lax.ppermute(x, 'z', [(i, i ^ k) for i in range(cols)])  8.93 us
  transfers between devices with their start and end apart: 25, of which 12 were waited for; matrix products, arithmetic and copies ran while one was open for 1% of the time, Pallas kernels for 16%

profile of v3, /device:TPU:0, one launch (start us, length us, event | category | flops | bytes accessed | tf_op | source)
XLA Modules:
  0.0 79.1 jit_solution(8630046200751700420)
XLA Ops:
  0.6 0.7 fusion.13
  1.4 0.7 fusion.14
  2.1 3.1 %collective-permute-start = (bf16[2,32,512]{2,1,0:T(8,128)(2,1)S(1)}, bf16[2,32,512]{2,1,0:T(8,128)(2,1)S(1)}, u32[]{:S(2)}, u32[]{:S(2)}) collective-permute-start(bf16[2,32,512]{2,1,0:T(8,128)(2,1)S(1)} %pad_maximum_fusion.10), channel_id=1, source_target_pairs={{0,2},{2,0},{4,6},{6,4},{1,3},{3,1},{5,7},{7,5},{8,10},{10,8},{12,... | collective-permute-start | bytes 196616 | tf_op jit(solution)/shard_map/ppermute | solution.py:264
  5.2 2.6 %collective-permute-start.1 = (bf16[2,32,512]{2,1,0:T(8,128)(2,1)S(1)}, bf16[2,32,512]{2,1,0:T(8,128)(2,1)S(1)}, u32[]{:S(2)}, u32[]{:S(2)}) collective-permute-start(bf16[2,32,512]{2,1,0:T(8,128)(2,1)S(1)} %pad_maximum_fusion.10), channel_id=1, source_target_pairs={{0,4},{2,6},{4,0},{6,2},{1,5},{3,7},{5,1},{7,3},{8,12},{10,14},{12... | collective-permute-start | bytes 196616 | tf_op jit(solution)/shard_map/ppermute | solution.py:264
  7.8 4.7 %collective-permute-done.1 = bf16[2,32,512]{2,1,0:T(8,128)(2,1)S(1)} collective-permute-done((bf16[2,32,512]{2,1,0:T(8,128)(2,1)S(1)}, bf16[2,32,512]{2,1,0:T(8,128)(2,1)S(1)}, u32[]{:S(2)}, u32[]{:S(2)}) %collective-permute-start.1) | collective-permute-done | bytes 65568 | tf_op jit(solution)/shard_map/ppermute | solution.py:264
  12.5 1.4 %collective-permute-done.2 = bf16[2,32,512]{2,1,0:T(8,128)(2,1)S(1)} collective-permute-done((bf16[2,32,512]{2,1,0:T(8,128)(2,1)S(1)}, bf16[2,32,512]{2,1,0:T(8,128)(2,1)S(1)}, u32[]{:S(2)}, u32[]{:S(2)}) %collective-permute-start.2) | collective-permute-done | bytes 65568 | tf_op jit(solution)/shard_map/ppermute | solution.py:264
  13.9 1.6 %collective-permute-start.7 = (bf16[128,512]{1,0:T(8,128)(2,1)S(1)}, bf16[128,512]{1,0:T(8,128)(2,1)S(1)}, u32[]{:S(2)}, u32[]{:S(2)}) collective-permute-start(bf16[128,512]{1,0:T(8,128)(2,1)S(1)} %pad_maximum_fusion.1), channel_id=1, source_target_pairs={{0,1},{1,0},{16,17},{17,16},{2,3},{3,2},{18,19},{19,18},{4,5},{5,4... | collective-permute-start | bytes 393224 | tf_op jit(solution)/shard_map/ppermute | solution.py:267
  15.5 1.5 %collective-permute-start.8 = (bf16[128,512]{1,0:T(8,128)(2,1)S(1)}, bf16[128,512]{1,0:T(8,128)(2,1)S(1)}, u32[]{:S(2)}, u32[]{:S(2)}) collective-permute-start(bf16[128,512]{1,0:T(8,128)(2,1)S(1)} %pad_maximum_fusion.1), channel_id=1, source_target_pairs={{0,16},{1,17},{16,0},{17,1},{2,18},{3,19},{18,2},{19,3},{4,20},{5,... | collective-permute-start | bytes 393224 | tf_op jit(solution)/shard_map/ppermute | solution.py:267
  17.0 0.5 collective-permute-start.9
  17.5 0.0 copy-start
  17.5 1.6 %collective-permute-start.3 = (bf16[128,512]{1,0:T(8,128)(2,1)S(1)}, bf16[128,512]{1,0:T(8,128)(2,1)S(1)}, u32[]{:S(2)}, u32[]{:S(2)}) collective-permute-start(bf16[128,512]{1,0:T(8,128)(2,1)S(1)} %pad_maximum_fusion), channel_id=1, source_target_pairs={{0,1},{1,0},{16,17},{17,16},{2,3},{3,2},{18,19},{19,18},{4,5},{5,4... | collective-permute-start | bytes 393224 | tf_op jit(solution)/shard_map/ppermute | solution.py:267
  19.1 4.0 %collective-permute-done.7 = bf16[128,512]{1,0:T(8,128)(2,1)S(1)} collective-permute-done((bf16[128,512]{1,0:T(8,128)(2,1)S(1)}, bf16[128,512]{1,0:T(8,128)(2,1)S(1)}, u32[]{:S(2)}, u32[]{:S(2)}) %collective-permute-start.7) | collective-permute-done | bytes 131104 | tf_op jit(solution)/shard_map/ppermute | solution.py:267
  23.2 0.1 collective-permute-start.10
  23.3 1.4 %collective-permute-start.4 = (bf16[128,512]{1,0:T(8,128)(2,1)S(1)}, bf16[128,512]{1,0:T(8,128)(2,1)S(1)}, u32[]{:S(2)}, u32[]{:S(2)}) collective-permute-start(bf16[128,512]{1,0:T(8,128)(2,1)S(1)} %pad_maximum_fusion), channel_id=1, source_target_pairs={{0,16},{1,17},{16,0},{17,1},{2,18},{3,19},{18,2},{19,3},{4,20},{5,... | collective-permute-start | bytes 393224 | tf_op jit(solution)/shard_map/ppermute | solution.py:267
  24.7 1.5 %collective-permute-start.5 = (bf16[128,512]{1,0:T(8,128)(2,1)S(1)}, bf16[128,512]{1,0:T(8,128)(2,1)S(1)}, u32[]{:S(2)}, u32[]{:S(2)}) collective-permute-start(bf16[128,512]{1,0:T(8,128)(2,1)S(1)} %pad_maximum_fusion), channel_id=1, source_target_pairs={{0,17},{1,16},{16,1},{17,0},{2,19},{3,18},{18,3},{19,2},{4,21},{5,... | collective-permute-start | bytes 393224 | tf_op jit(solution)/shard_map/ppermute | solution.py:267
  26.2 3.5 %collective-permute-done.4 = bf16[128,512]{1,0:T(8,128)(2,1)S(1)} collective-permute-done((bf16[128,512]{1,0:T(8,128)(2,1)S(1)}, bf16[128,512]{1,0:T(8,128)(2,1)S(1)}, u32[]{:S(2)}, u32[]{:S(2)}) %collective-permute-start.4) | collective-permute-done | bytes 131104 | tf_op jit(solution)/shard_map/ppermute | solution.py:267
  29.7 3.1 %collective-permute-done.5 = bf16[128,512]{1,0:T(8,128)(2,1)S(1)} collective-permute-done((bf16[128,512]{1,0:T(8,128)(2,1)S(1)}, bf16[128,512]{1,0:T(8,128)(2,1)S(1)}, u32[]{:S(2)}, u32[]{:S(2)}) %collective-permute-start.5) | collective-permute-done | bytes 131104 | tf_op jit(solution)/shard_map/ppermute | solution.py:267
  32.8 0.1 collective-permute-start.6
  33.6 6.4 %shard_map.110 = (bf16[128,4096]{1,0:T(8,128)(2,1)}, bf16[128,4096]{1,0:T(8,128)(2,1)}, bf16[2,2,528,128]{3,2,1,0:T(8,128)(2,1)S(1)}, bf16[2,2,528,128]{3,2,1,0:T(8,128)(2,1)S(1)}, f32[8,128]{1,0:T(8,128)S(1)}) custom-call(s32[128]{0:T(128)S(1)} %copy-done.2, s32[4]{0:T(128)S(1)} %copy-done.3, f32[1]{0:T(128)S(6)} %copy.28.gate_s, s32[1,128]{1,0:T(1,128)S(1)} %bitcast.69, ...), custom_call_target="tpu_custom_call" | custom-call | flops 1610612736 | bytes 4194304 | tf_op jit(solution)/shard_map/pallas_call | solution.py:206
  40.0 0.6 collective-permute-start.11
  40.6 6.4 %shard_map.111 = (bf16[128,4096]{1,0:T(8,128)(2,1)}, bf16[128,4096]{1,0:T(8,128)(2,1)}, bf16[2,2,528,128]{3,2,1,0:T(8,128)(2,1)S(1)}, bf16[2,2,528,128]{3,2,1,0:T(8,128)(2,1)S(1)}, f32[8,128]{1,0:T(8,128)}) custom-call(s32[128]{0:T(128)S(1)} %copy-done.2, s32[4]{0:T(128)S(1)} %copy-done.3, ...), custom_call_target="tpu_custom_call", output_to_operand_aliasing={{0}: (9, {}), {1}: (10, {})} | custom-call | flops 1610612736 | bytes 4194304 | tf_op jit(solution)/shard_map/pallas_call | solution.py:206
  47.0 0.1 collective-permute-start.18
  47.2 0.1 add_convert_fusion.1
  47.4 0.7 collective-permute-start.12
  48.1 1.3 %collective-permute-start.13 = (bf16[528,128]{1,0:T(8,128)(2,1)S(1)}, bf16[528,128]{1,0:T(8,128)(2,1)S(1)}, u32[]{:S(2)}, u32[]{:S(2)}) collective-permute-start(bf16[528,128]{1,0:T(8,128)(2,1)S(1)} %get-tuple-element.25), channel_id=1, source_target_pairs={{0,16},{1,17},{16,0},{17,1},{2,18},{3,19},{18,2},{19,3},{4,20},{5,... | collective-permute-start | bytes 405512 | tf_op jit(solution)/shard_map/ppermute | solution.py:267
  49.4 1.5 %collective-permute-start.14 = (bf16[528,128]{1,0:T(8,128)(2,1)S(1)}, bf16[528,128]{1,0:T(8,128)(2,1)S(1)}, u32[]{:S(2)}, u32[]{:S(2)}) collective-permute-start(bf16[528,128]{1,0:T(8,128)(2,1)S(1)} %get-tuple-element.24), channel_id=1, source_target_pairs={{0,17},{1,16},{16,1},{17,0},{2,19},{3,18},{18,3},{19,2},{4,21},{5,... | collective-permute-start | bytes 405512 | tf_op jit(solution)/shard_map/ppermute | solution.py:267
  50.9 0.2 add_convert_fusion
  51.1 0.7 collective-permute-start.19
  51.8 1.3 %collective-permute-start.20 = (bf16[528,128]{1,0:T(8,128)(2,1)S(1)}, bf16[528,128]{1,0:T(8,128)(2,1)S(1)}, u32[]{:S(2)}, u32[]{:S(2)}) collective-permute-start(bf16[528,128]{1,0:T(8,128)(2,1)S(1)} %get-tuple-element.28), channel_id=1, source_target_pairs={{0,16},{1,17},{16,0},{17,1},{2,18},{3,19},{18,2},{19,3},{4,20},{5,... | collective-permute-start | bytes 405512 | tf_op jit(solution)/shard_map/ppermute | solution.py:267
  53.2 0.2 collective-permute-done.12
  53.4 1.4 %collective-permute-start.21 = (bf16[528,128]{1,0:T(8,128)(2,1)S(1)}, bf16[528,128]{1,0:T(8,128)(2,1)S(1)}, u32[]{:S(2)}, u32[]{:S(2)}) collective-permute-start(bf16[528,128]{1,0:T(8,128)(2,1)S(1)} %get-tuple-element.27), channel_id=1, source_target_pairs={{0,17},{1,16},{16,1},{17,0},{2,19},{3,18},{18,3},{19,2},{4,21},{5,... | collective-permute-start | bytes 405512 | tf_op jit(solution)/shard_map/ppermute | solution.py:267
  54.8 3.4 %collective-permute-done.14 = bf16[528,128]{1,0:T(8,128)(2,1)S(1)} collective-permute-done((bf16[528,128]{1,0:T(8,128)(2,1)S(1)}, bf16[528,128]{1,0:T(8,128)(2,1)S(1)}, u32[]{:S(2)}, u32[]{:S(2)}) %collective-permute-start.14) | collective-permute-done | bytes 135200 | tf_op jit(solution)/shard_map/ppermute | solution.py:267
  58.2 0.1 fusion.5
  58.4 0.8 %collective-permute-done.19 = bf16[528,128]{1,0:T(8,128)(2,1)S(1)} collective-permute-done((bf16[528,128]{1,0:T(8,128)(2,1)S(1)}, bf16[528,128]{1,0:T(8,128)(2,1)S(1)}, u32[]{:S(2)}, u32[]{:S(2)}) %collective-permute-start.19) | collective-permute-done | bytes 135200 | tf_op jit(solution)/shard_map/ppermute | solution.py:267
  59.2 1.2 %collective-permute-done.20 = bf16[528,128]{1,0:T(8,128)(2,1)S(1)} collective-permute-done((bf16[528,128]{1,0:T(8,128)(2,1)S(1)}, bf16[528,128]{1,0:T(8,128)(2,1)S(1)}, u32[]{:S(2)}, u32[]{:S(2)}) %collective-permute-start.20) | collective-permute-done | bytes 135200 | tf_op jit(solution)/shard_map/ppermute | solution.py:267
  60.4 2.9 %collective-permute-done.21 = bf16[528,128]{1,0:T(8,128)(2,1)S(1)} collective-permute-done((bf16[528,128]{1,0:T(8,128)(2,1)S(1)}, bf16[528,128]{1,0:T(8,128)(2,1)S(1)}, u32[]{:S(2)}, u32[]{:S(2)}) %collective-permute-start.21) | collective-permute-done | bytes 135200 | tf_op jit(solution)/shard_map/ppermute | solution.py:267
  63.3 0.1 fusion.2
  63.4 0.1 collective-permute-start.15
  63.5 1.5 %collective-permute-start.16 = (bf16[144,128]{1,0:T(8,128)(2,1)S(1)}, bf16[144,128]{1,0:T(8,128)(2,1)S(1)}, u32[]{:S(2)}, u32[]{:S(2)}) collective-permute-start(bf16[144,128]{1,0:T(8,128)(2,1)S(1)} %get-tuple-element.66), channel_id=1, source_target_pairs={{0,4},{2,6},{4,0},{6,2},{1,5},{3,7},{5,1},{7,3},{8,12},{10,14},{12... | collective-permute-start | bytes 110600 | tf_op jit(solution)/shard_map/ppermute | solution.py:264
  65.0 2.8 %collective-permute-start.17 = (bf16[144,128]{1,0:T(8,128)(2,1)S(1)}, bf16[144,128]{1,0:T(8,128)(2,1)S(1)}, u32[]{:S(2)}, u32[]{:S(2)}) collective-permute-start(bf16[144,128]{1,0:T(8,128)(2,1)S(1)} %get-tuple-element.67), channel_id=1, source_target_pairs={{0,6},{2,4},{4,2},{6,0},{1,7},{3,5},{5,3},{7,1},{8,14},{10,12},{12... | collective-permute-start | bytes 110600 | tf_op jit(solution)/shard_map/ppermute | solution.py:264
  67.9 0.1 collective-permute-start.22
  68.0 1.5 %collective-permute-start.23 = (bf16[144,128]{1,0:T(8,128)(2,1)S(1)}, bf16[144,128]{1,0:T(8,128)(2,1)S(1)}, u32[]{:S(2)}, u32[]{:S(2)}) collective-permute-start(bf16[144,128]{1,0:T(8,128)(2,1)S(1)} %get-tuple-element.69), channel_id=1, source_target_pairs={{0,4},{2,6},{4,0},{6,2},{1,5},{3,7},{5,1},{7,3},{8,12},{10,14},{12... | collective-permute-start | bytes 110600 | tf_op jit(solution)/shard_map/ppermute | solution.py:264
  69.5 2.8 %collective-permute-start.24 = (bf16[144,128]{1,0:T(8,128)(2,1)S(1)}, bf16[144,128]{1,0:T(8,128)(2,1)S(1)}, u32[]{:S(2)}, u32[]{:S(2)}) collective-permute-start(bf16[144,128]{1,0:T(8,128)(2,1)S(1)} %get-tuple-element.70), channel_id=1, source_target_pairs={{0,6},{2,4},{4,2},{6,0},{1,7},{3,5},{5,3},{7,1},{8,14},{10,12},{12... | collective-permute-start | bytes 110600 | tf_op jit(solution)/shard_map/ppermute | solution.py:264
  72.4 0.5 collective-permute-done.23
  72.9 2.3 %collective-permute-done.24 = bf16[144,128]{1,0:T(8,128)(2,1)S(1)} collective-permute-done((bf16[144,128]{1,0:T(8,128)(2,1)S(1)}, bf16[144,128]{1,0:T(8,128)(2,1)S(1)}, u32[]{:S(2)}, u32[]{:S(2)}) %collective-permute-start.24) | collective-permute-done | bytes 36896 | tf_op jit(solution)/shard_map/ppermute | solution.py:264
  75.3 0.7 fusion.8
  76.7 0.6 pad_maximum_fusion.12
  77.3 0.6 pad_maximum_fusion.11
  (53 shorter events, 0.4 us)
Async XLA Ops:
  2.1 5.7 %collective-permute-start = (bf16[2,32,512]{2,1,0:T(8,128)(2,1)S(1)}, bf16[2,32,512]{2,1,0:T(8,128)(2,1)S(1)}, u32[]{:S(2)}, u32[]{:S(2)}) collective-permute-start(bf16[2,32,512]{2,1,0:T(8,128)(2,1)S(1)} %pad_maximum_fusion.10), channel_id=1, source_target_pairs={{0,2},{2,0},{4,6},{6,4},{1,3},{3,1},{5,7},{7,5},{8,10},{10,8},{12,... | collective-permute-start | bytes 196616 | tf_op jit(solution)/shard_map/ppermute | solution.py:264
  5.2 7.3 %collective-permute-start.1 = (bf16[2,32,512]{2,1,0:T(8,128)(2,1)S(1)}, bf16[2,32,512]{2,1,0:T(8,128)(2,1)S(1)}, u32[]{:S(2)}, u32[]{:S(2)}) collective-permute-start(bf16[2,32,512]{2,1,0:T(8,128)(2,1)S(1)} %pad_maximum_fusion.10), channel_id=1, source_target_pairs={{0,4},{2,6},{4,0},{6,2},{1,5},{3,7},{5,1},{7,3},{8,12},{10,14},{12... | collective-permute-start | bytes 196616 | tf_op jit(solution)/shard_map/ppermute | solution.py:264
  7.8 6.1 %collective-permute-start.2 = (bf16[2,32,512]{2,1,0:T(8,128)(2,1)S(1)}, bf16[2,32,512]{2,1,0:T(8,128)(2,1)S(1)}, u32[]{:S(2)}, u32[]{:S(2)}) collective-permute-start(bf16[2,32,512]{2,1,0:T(8,128)(2,1)S(1)} %pad_maximum_fusion.10), channel_id=1, source_target_pairs={{0,6},{2,4},{4,2},{6,0},{1,7},{3,5},{5,3},{7,1},{8,14},{10,12},{12... | collective-permute-start | bytes 196616 | tf_op jit(solution)/shard_map/ppermute | solution.py:264
  13.9 9.2 %collective-permute-start.7 = (bf16[128,512]{1,0:T(8,128)(2,1)S(1)}, bf16[128,512]{1,0:T(8,128)(2,1)S(1)}, u32[]{:S(2)}, u32[]{:S(2)}) collective-permute-start(bf16[128,512]{1,0:T(8,128)(2,1)S(1)} %pad_maximum_fusion.1), channel_id=1, source_target_pairs={{0,1},{1,0},{16,17},{17,16},{2,3},{3,2},{18,19},{19,18},{4,5},{5,4... | collective-permute-start | bytes 393224 | tf_op jit(solution)/shard_map/ppermute | solution.py:267
  15.5 7.7 %collective-permute-start.8 = (bf16[128,512]{1,0:T(8,128)(2,1)S(1)}, bf16[128,512]{1,0:T(8,128)(2,1)S(1)}, u32[]{:S(2)}, u32[]{:S(2)}) collective-permute-start(bf16[128,512]{1,0:T(8,128)(2,1)S(1)} %pad_maximum_fusion.1), channel_id=1, source_target_pairs={{0,16},{1,17},{16,0},{17,1},{2,18},{3,19},{18,2},{19,3},{4,20},{5,... | collective-permute-start | bytes 393224 | tf_op jit(solution)/shard_map/ppermute | solution.py:267
  17.0 6.2 %collective-permute-start.9 = (bf16[128,512]{1,0:T(8,128)(2,1)S(1)}, bf16[128,512]{1,0:T(8,128)(2,1)S(1)}, u32[]{:S(2)}, u32[]{:S(2)}) collective-permute-start(bf16[128,512]{1,0:T(8,128)(2,1)S(1)} %pad_maximum_fusion.1), channel_id=1, source_target_pairs={{0,17},{1,16},{16,1},{17,0},{2,19},{3,18},{18,3},{19,2},{4,21},{5,... | collective-permute-start | bytes 393224 | tf_op jit(solution)/shard_map/ppermute | solution.py:267
  17.5 16.1 %copy-start.1 = (bf16[128,4096]{1,0:T(8,128)(2,1)S(1)}, bf16[128,4096]{1,0:T(8,128)(2,1)}, u32[]{:S(2)}) copy-start(bf16[128,4096]{1,0:T(8,128)(2,1)} %dy_ref.3) | copy-start | bytes 3145732
  17.5 16.1 %copy-start = (bf16[128,4096]{1,0:T(8,128)(2,1)S(1)}, bf16[128,4096]{1,0:T(8,128)(2,1)}, u32[]{:S(2)}) copy-start(bf16[128,4096]{1,0:T(8,128)(2,1)} %q_ref.3) | copy-start | bytes 3145732
  17.5 16.1 %copy-start.2 = (s32[128]{0:T(128)S(1)}, s32[128]{0:T(128)}, u32[]{:S(2)}) copy-start(s32[128]{0:T(128)} %seg_s.3) | copy-start | bytes 1540
  17.5 16.1 %copy-start.3 = (s32[4]{0:T(128)S(1)}, s32[4]{0:T(128)}, u32[]{:S(2)}) copy-start(s32[4]{0:T(128)} %cnt_s.3) | copy-start | bytes 52
  17.5 8.7 %collective-permute-start.3 = (bf16[128,512]{1,0:T(8,128)(2,1)S(1)}, bf16[128,512]{1,0:T(8,128)(2,1)S(1)}, u32[]{:S(2)}, u32[]{:S(2)}) collective-permute-start(bf16[128,512]{1,0:T(8,128)(2,1)S(1)} %pad_maximum_fusion), channel_id=1, source_target_pairs={{0,1},{1,0},{16,17},{17,16},{2,3},{3,2},{18,19},{19,18},{4,5},{5,4... | collective-permute-start | bytes 393224 | tf_op jit(solution)/shard_map/ppermute | solution.py:267
  23.2 10.3 %collective-permute-start.10 = (bf16[2,256,512]{2,1,0:T(8,128)(2,1)S(1)}, bf16[2,256,512]{2,1,0:T(8,128)(2,1)S(1)}, u32[]{:S(2)}, u32[]{:S(2)}) collective-permute-start(bf16[2,256,512]{2,1,0:T(8,128)(2,1)S(1)} %bitcast.65), channel_id=1, source_target_pairs={{0,8},{8,0},{1,9},{9,1},{2,10},{10,2},{3,11},{11,3},{4,12},{12,4},... | collective-permute-start | bytes 1572872 | tf_op jit(solution)/shard_map/ppermute | solution.py:270
  23.3 6.4 %collective-permute-start.4 = (bf16[128,512]{1,0:T(8,128)(2,1)S(1)}, bf16[128,512]{1,0:T(8,128)(2,1)S(1)}, u32[]{:S(2)}, u32[]{:S(2)}) collective-permute-start(bf16[128,512]{1,0:T(8,128)(2,1)S(1)} %pad_maximum_fusion), channel_id=1, source_target_pairs={{0,16},{1,17},{16,0},{17,1},{2,18},{3,19},{18,2},{19,3},{4,20},{5,... | collective-permute-start | bytes 393224 | tf_op jit(solution)/shard_map/ppermute | solution.py:267
  24.7 8.1 %collective-permute-start.5 = (bf16[128,512]{1,0:T(8,128)(2,1)S(1)}, bf16[128,512]{1,0:T(8,128)(2,1)S(1)}, u32[]{:S(2)}, u32[]{:S(2)}) collective-permute-start(bf16[128,512]{1,0:T(8,128)(2,1)S(1)} %pad_maximum_fusion), channel_id=1, source_target_pairs={{0,17},{1,16},{16,1},{17,0},{2,19},{3,18},{18,3},{19,2},{4,21},{5,... | collective-permute-start | bytes 393224 | tf_op jit(solution)/shard_map/ppermute | solution.py:267
  32.8 7.8 %collective-permute-start.6 = (bf16[2,256,512]{2,1,0:T(8,128)(2,1)S(1)}, bf16[2,256,512]{2,1,0:T(8,128)(2,1)S(1)}, u32[]{:S(2)}, u32[]{:S(2)}) collective-permute-start(bf16[2,256,512]{2,1,0:T(8,128)(2,1)S(1)} %bitcast.67), channel_id=1, source_target_pairs={{0,8},{8,0},{1,9},{9,1},{2,10},{10,2},{3,11},{11,3},{4,12},{12,4},... | collective-permute-start | bytes 1572872 | tf_op jit(solution)/shard_map/ppermute | solution.py:270
  40.0 7.1 %collective-permute-start.11 = (bf16[2,2,528,128]{3,2,1,0:T(8,128)(2,1)S(1)}, bf16[2,2,528,128]{3,2,1,0:T(8,128)(2,1)S(1)}, u32[]{:S(2)}, u32[]{:S(2)}) collective-permute-start(bf16[2,2,528,128]{3,2,1,0:T(8,128)(2,1)S(1)} %get-tuple-element.20), channel_id=1, source_target_pairs={{0,8},{8,0},{1,9},{9,1},{2,10},{10,2},{3,11},{11,3},{4,12},{12,4},... | collective-permute-start | bytes 1622024 | tf_op jit(solution)/shard_map/ppermute | solution.py:270
  47.0 3.9 %collective-permute-start.18 = (bf16[2,2,528,128]{3,2,1,0:T(8,128)(2,1)S(1)}, bf16[2,2,528,128]{3,2,1,0:T(8,128)(2,1)S(1)}, u32[]{:S(2)}, u32[]{:S(2)}) collective-permute-start(bf16[2,2,528,128]{3,2,1,0:T(8,128)(2,1)S(1)} %get-tuple-element.22), channel_id=1, source_target_pairs={{0,8},{8,0},{1,9},{9,1},{2,10},{10,2},{3,11},{11,3},{4,12},{12,4},... | collective-permute-start | bytes 1622024 | tf_op jit(solution)/shard_map/ppermute | solution.py:270
  47.4 6.0 %collective-permute-start.12 = (bf16[528,128]{1,0:T(8,128)(2,1)S(1)}, bf16[528,128]{1,0:T(8,128)(2,1)S(1)}, u32[]{:S(2)}, u32[]{:S(2)}) collective-permute-start(bf16[528,128]{1,0:T(8,128)(2,1)S(1)} %get-tuple-element.23), channel_id=1, source_target_pairs={{0,1},{1,0},{16,17},{17,16},{2,3},{3,2},{18,19},{19,18},{4,5},{5,4... | collective-permute-start | bytes 405512 | tf_op jit(solution)/shard_map/ppermute | solution.py:267
  48.1 6.7 %collective-permute-start.13 = (bf16[528,128]{1,0:T(8,128)(2,1)S(1)}, bf16[528,128]{1,0:T(8,128)(2,1)S(1)}, u32[]{:S(2)}, u32[]{:S(2)}) collective-permute-start(bf16[528,128]{1,0:T(8,128)(2,1)S(1)} %get-tuple-element.25), channel_id=1, source_target_pairs={{0,16},{1,17},{16,0},{17,1},{2,18},{3,19},{18,2},{19,3},{4,20},{5,... | collective-permute-start | bytes 405512 | tf_op jit(solution)/shard_map/ppermute | solution.py:267
  49.4 8.8 %collective-permute-start.14 = (bf16[528,128]{1,0:T(8,128)(2,1)S(1)}, bf16[528,128]{1,0:T(8,128)(2,1)S(1)}, u32[]{:S(2)}, u32[]{:S(2)}) collective-permute-start(bf16[528,128]{1,0:T(8,128)(2,1)S(1)} %get-tuple-element.24), channel_id=1, source_target_pairs={{0,17},{1,16},{16,1},{17,0},{2,19},{3,18},{18,3},{19,2},{4,21},{5,... | collective-permute-start | bytes 405512 | tf_op jit(solution)/shard_map/ppermute | solution.py:267
  51.1 8.1 %collective-permute-start.19 = (bf16[528,128]{1,0:T(8,128)(2,1)S(1)}, bf16[528,128]{1,0:T(8,128)(2,1)S(1)}, u32[]{:S(2)}, u32[]{:S(2)}) collective-permute-start(bf16[528,128]{1,0:T(8,128)(2,1)S(1)} %get-tuple-element.26), channel_id=1, source_target_pairs={{0,1},{1,0},{16,17},{17,16},{2,3},{3,2},{18,19},{19,18},{4,5},{5,4... | collective-permute-start | bytes 405512 | tf_op jit(solution)/shard_map/ppermute | solution.py:267
  51.8 8.5 %collective-permute-start.20 = (bf16[528,128]{1,0:T(8,128)(2,1)S(1)}, bf16[528,128]{1,0:T(8,128)(2,1)S(1)}, u32[]{:S(2)}, u32[]{:S(2)}) collective-permute-start(bf16[528,128]{1,0:T(8,128)(2,1)S(1)} %get-tuple-element.28), channel_id=1, source_target_pairs={{0,16},{1,17},{16,0},{17,1},{2,18},{3,19},{18,2},{19,3},{4,20},{5,... | collective-permute-start | bytes 405512 | tf_op jit(solution)/shard_map/ppermute | solution.py:267
  53.4 9.9 %collective-permute-start.21 = (bf16[528,128]{1,0:T(8,128)(2,1)S(1)}, bf16[528,128]{1,0:T(8,128)(2,1)S(1)}, u32[]{:S(2)}, u32[]{:S(2)}) collective-permute-start(bf16[528,128]{1,0:T(8,128)(2,1)S(1)} %get-tuple-element.27), channel_id=1, source_target_pairs={{0,17},{1,16},{16,1},{17,0},{2,19},{3,18},{18,3},{19,2},{4,21},{5,... | collective-permute-start | bytes 405512 | tf_op jit(solution)/shard_map/ppermute | solution.py:267
  63.4 6.1 %collective-permute-start.15 = (bf16[144,128]{1,0:T(8,128)(2,1)S(1)}, bf16[144,128]{1,0:T(8,128)(2,1)S(1)}, u32[]{:S(2)}, u32[]{:S(2)}) collective-permute-start(bf16[144,128]{1,0:T(8,128)(2,1)S(1)} %get-tuple-element.65), channel_id=1, source_target_pairs={{0,2},{2,0},{4,6},{6,4},{1,3},{3,1},{5,7},{7,5},{8,10},{10,8},{12,... | collective-permute-start | bytes 110600 | tf_op jit(solution)/shard_map/ppermute | solution.py:264
  63.5 8.9 %collective-permute-start.16 = (bf16[144,128]{1,0:T(8,128)(2,1)S(1)}, bf16[144,128]{1,0:T(8,128)(2,1)S(1)}, u32[]{:S(2)}, u32[]{:S(2)}) collective-permute-start(bf16[144,128]{1,0:T(8,128)(2,1)S(1)} %get-tuple-element.66), channel_id=1, source_target_pairs={{0,4},{2,6},{4,0},{6,2},{1,5},{3,7},{5,1},{7,3},{8,12},{10,14},{12... | collective-permute-start | bytes 110600 | tf_op jit(solution)/shard_map/ppermute | solution.py:264
  65.0 7.3 %collective-permute-start.17 = (bf16[144,128]{1,0:T(8,128)(2,1)S(1)}, bf16[144,128]{1,0:T(8,128)(2,1)S(1)}, u32[]{:S(2)}, u32[]{:S(2)}) collective-permute-start(bf16[144,128]{1,0:T(8,128)(2,1)S(1)} %get-tuple-element.67), channel_id=1, source_target_pairs={{0,6},{2,4},{4,2},{6,0},{1,7},{3,5},{5,3},{7,1},{8,14},{10,12},{12... | collective-permute-start | bytes 110600 | tf_op jit(solution)/shard_map/ppermute | solution.py:264
  67.9 4.5 %collective-permute-start.22 = (bf16[144,128]{1,0:T(8,128)(2,1)S(1)}, bf16[144,128]{1,0:T(8,128)(2,1)S(1)}, u32[]{:S(2)}, u32[]{:S(2)}) collective-permute-start(bf16[144,128]{1,0:T(8,128)(2,1)S(1)} %get-tuple-element.68), channel_id=1, source_target_pairs={{0,2},{2,0},{4,6},{6,4},{1,3},{3,1},{5,7},{7,5},{8,10},{10,8},{12,... | collective-permute-start | bytes 110600 | tf_op jit(solution)/shard_map/ppermute | solution.py:264
  68.0 4.9 %collective-permute-start.23 = (bf16[144,128]{1,0:T(8,128)(2,1)S(1)}, bf16[144,128]{1,0:T(8,128)(2,1)S(1)}, u32[]{:S(2)}, u32[]{:S(2)}) collective-permute-start(bf16[144,128]{1,0:T(8,128)(2,1)S(1)} %get-tuple-element.69), channel_id=1, source_target_pairs={{0,4},{2,6},{4,0},{6,2},{1,5},{3,7},{5,1},{7,3},{8,12},{10,14},{12... | collective-permute-start | bytes 110600 | tf_op jit(solution)/shard_map/ppermute | solution.py:264
  69.5 5.8 %collective-permute-start.24 = (bf16[144,128]{1,0:T(8,128)(2,1)S(1)}, bf16[144,128]{1,0:T(8,128)(2,1)S(1)}, u32[]{:S(2)}, u32[]{:S(2)}) collective-permute-start(bf16[144,128]{1,0:T(8,128)(2,1)S(1)} %get-tuple-element.70), channel_id=1, source_target_pairs={{0,6},{2,4},{4,2},{6,0},{1,7},{3,5},{5,3},{7,1},{8,14},{10,12},{12... | collective-permute-start | bytes 110600 | tf_op jit(solution)/shard_map/ppermute | solution.py:264

commit v4 on v3

--- a/solution.py
+++ b/solution.py
@@ -103,32 +103,31 @@
         tile = (zi * (2 * mine) + yi * mine + n % mine) // TILE_TOK
         limit = jnp.where(in_a, cnt_s[img_a], cnt_s[img_b])
         bias[...] = jnp.where(tile < limit, 0.0, NEG)
-        rowsel[...] = jnp.broadcast_to(in_a.astype(jnp.float32), (hd, tokens)).T
+        side_a = jnp.broadcast_to(in_a.astype(jnp.float32), (hd, tokens)).T
+        rowsel[0] = side_a.astype(jnp.bfloat16)
+        rowsel[1] = (1.0 - side_a).astype(jnp.bfloat16)
         fetch(0, img_a, False)
         fetch(1, img_b, False)
 
-    rows_a = rowsel[...] > 0.5
     kcols = pl.ds(pl.multiple_of(step * hd, hd), hd)
     vcols = pl.ds(pl.multiple_of(width + step * hd, hd), hd)
     kcat = jnp.concatenate([kv[0, :, kcols], kv[1, :, kcols]], axis=1)
     vcat = jnp.concatenate([kv[0, :, vcols], kv[1, :, vcols]], axis=1)
-    kcat_t = kcat.astype(jnp.float32).T.astype(jnp.bfloat16)
-    vcat_t = vcat.astype(jnp.float32).T.astype(jnp.bfloat16)
-    zero = jnp.zeros((tokens, hd), jnp.bfloat16)
+    kcat_t = kcat.T
+    vcat_t = vcat.T
     for g in range(group):
         feats = slice(g * hd, (g + 1) * hd)
         rows = slice(g * tokens, (g + 1) * tokens)
         q = q_ref[:, feats]
-        dy = dy_ref[:, feats].astype(jnp.float32)
-        do = (tg * dy).astype(jnp.bfloat16)
-        qc[rows, :hd] = jnp.where(rows_a, q, zero)
-        qc[rows, hd:] = jnp.where(rows_a, zero, q)
-        dc[rows, :hd] = jnp.where(rows_a, do, zero)
-        dc[rows, hd:] = jnp.where(rows_a, zero, do)
+        dy = dy_ref[:, feats]
+        for i in range(2):
+            side = slice(i * hd, (i + 1) * hd)
+            qc[rows, side] = q * rowsel[i]
+            dc[rows, side] = dy * rowsel[i]
 
     pair = 2
-    gsum = jnp.zeros((tokens, hd), jnp.float32)
     in_a2 = jnp.concatenate([in_a] * pair, axis=1)
+    tg2 = jnp.concatenate([tg] * pair, axis=1)
     for h in range(0, group, pair):
         rows = slice(h * tokens, (h + pair) * tokens)
         s = mm(kcat, qc[rows, :], NT)
@@ -140,22 +139,23 @@
         p16[:, rows] = ph
         dp = mm(vcat, dc[rows, :], NT)
         delta = jnp.sum(ph.astype(jnp.float32) * dp, axis=0, keepdims=True)
-        dsh = (scale * p * (dp - delta)).astype(jnp.bfloat16)
+        dsh = ((scale * tg2) * p * (dp - delta)).astype(jnp.bfloat16)
         ds16[:, rows] = dsh
         o = mm(vcat_t, ph, NN)
-        o = jnp.where(in_a2, o[:hd], o[hd:])
+        o = (tg2 * jnp.where(in_a2, o[:hd], o[hd:])).astype(jnp.bfloat16)
         dq = mm(kcat_t, dsh, NN)
-        dq = jnp.where(in_a2, dq[:hd], dq[hd:])
+        dq = jnp.where(in_a2, dq[:hd], dq[hd:]).astype(jnp.bfloat16)
         for j in range(pair):
             feats = slice((h + j) * hd, (h + j + 1) * hd)
             toks = slice(j * tokens, (j + 1) * tokens)
-            ot = o[:, toks].T
-            y_ref[:, feats] = (tg * ot).astype(jnp.bfloat16)
-            gsum = gsum + dy_ref[:, feats].astype(jnp.float32) * ot
-            dq_ref[:, feats] = dq[:, toks].T.astype(jnp.bfloat16)
-    g_ref[...] += jnp.sum(gsum.reshape(tokens // 8, 8, hd), axis=0)
+            y_ref[:, feats] = o[:, toks].T
+            dq_ref[:, feats] = dq[:, toks].T
     dk = mm(ds16[...], qc[...], NN).astype(jnp.bfloat16)
-    dv = mm(p16[...], dc[...], NN).astype(jnp.bfloat16)
+    dv = mm(p16[...], dc[...], NN)
+    gsum = dv * vcat.astype(jnp.float32)
+    gsum = jnp.sum(gsum.reshape(slots // 8, 8, 2 * hd), axis=0)
+    g_ref[...] += gsum[:, :hd] + gsum[:, hd:]
+    dv = (jnp.concatenate([tg, tg], axis=1) * dv).astype(jnp.bfloat16)
     par_a, dx_a = place(img_a)
     par_b, dx_b = place(img_b)
     krows = pl.ds(pl.multiple_of(step * half, half), half)
@@ -198,7 +198,7 @@
     hbm = pl.BlockSpec(memory_space=pl.ANY)
     cut = pl.BlockSpec((tokens, block), lambda i: (0, i + chunk * heads))
     gspec = pl.BlockSpec((8, hd), lambda i: (0, 0))
-    flops = 12 * heads * rows * slots * hd * 2
+    flops = 5 * 12 * heads * rows * slots * hd * 2
     first = prev is None
     if first:
         prev = (jnp.zeros((8, hd), jnp.float32), q, q)
@@ -236,7 +236,7 @@
             pltpu.VMEM((slots, rows), jnp.bfloat16),
             pltpu.VMEM((slots, rows), jnp.bfloat16),
             pltpu.VMEM((slots, tokens), jnp.float32),
-            pltpu.VMEM((tokens, hd), jnp.float32),
+            pltpu.VMEM((2, tokens, hd), jnp.bfloat16),
             pltpu.SemaphoreType.DMA((4,)),
         ],
         compiler_params=pltpu.CompilerParams(
@@ -250,6 +250,42 @@
     )(seg, counts, gate, seg.reshape(1, tokens), q, dy, own, other, *prev)
 
 
+def finish_kernel(heads, mine, gate_s, *refs):
+    ins, (dk_ref, dv_ref, g_ref) = refs[:-3], refs[-3:]
+    hd = ins[0].shape[1]
+    each = len(ins) // CHUNKS
+    for c in range(CHUNKS):
+        total = ins[c * each][...].astype(jnp.float32)
+        for r in ins[c * each + 1 : (c + 1) * each]:
+            total = total + r[...].astype(jnp.float32)
+        for h in range(heads):
+            lanes = slice((c * heads + h) * hd, (c * heads + h + 1) * hd)
+            dk_ref[:, lanes] = total[h * mine : (h + 1) * mine]
+            dv_ref[:, lanes] = total[(heads + h) * mine : (heads + h + 1) * mine]
+    digits = total[2 * heads * mine :]
+    line = lax.broadcasted_iota(jnp.int32, digits.shape, 0)
+    units = jnp.zeros(digits.shape, jnp.float32)
+    for i in range(GROWS):
+        units = jnp.where(line == i, 4.0 ** (GTOP - i), units)
+    tg = jnp.tanh(jnp.full((1, hd), gate_s[0], jnp.float32))
+    terms = jnp.sum(digits * units, axis=0, keepdims=True) * (1.0 - tg * tg)
+    g_ref[0] = jnp.sum(terms)
+
+
+def finish(mine, gate, cuts):
+    heads = KV_HEADS // CHUNKS
+    hd = cuts[0].shape[1]
+    smem = pl.BlockSpec(memory_space=pltpu.SMEM)
+    vmem = pl.BlockSpec(memory_space=pltpu.VMEM)
+    full = jax.ShapeDtypeStruct((mine, KV_HEADS * hd), jnp.float32)
+    return pl.pallas_call(
+        functools.partial(finish_kernel, heads, mine),
+        in_specs=[smem] + [vmem] * len(cuts),
+        out_specs=[vmem, vmem, smem],
+        out_shape=[full, full, jax.ShapeDtypeStruct((1,), jnp.float32)],
+    )(gate, *cuts)
+
+
 def local(queries, keys, values, seg_image, tile_counts, gate, cotangent):
     f32, bf16 = jnp.float32, jnp.bfloat16
     mine, width = keys.shape
@@ -269,58 +305,59 @@
     def send_core(x):
         return lax.ppermute(x, "core", [(0, 1), (1, 0)])
 
-    kv = jnp.stack(
-        [
-            jnp.concatenate([keys[:, c * wide : (c + 1) * wide], values[:, c * wide : (c + 1) * wide]], axis=1)
-            for c in range(CHUNKS)
-        ]
-    )
+    kv = jnp.stack([keys, values])
     if folded:
         col = [kv] + [send_z(kv, k) for k in (1, 2, 3)]
     else:
         col = [lax.all_gather(kv, "z", axis=1, tiled=True)]
 
-    prev = None
-    reduced = []
-    for c in range(CHUNKS):
-        block = jnp.concatenate([p[c] for p in col], axis=0)
+    def gather(c):
+        lanes = slice(c * wide, (c + 1) * wide)
+        block = jnp.concatenate([jnp.concatenate([p[0, :, lanes], p[1, :, lanes]], axis=1) for p in col], axis=0)
         own = jnp.concatenate([block] + [send_xy(block, *p) for p in PEERS], axis=0)
         own = own.reshape(2, 2 * half, 2 * wide)
-        other = send_core(own)
+        return own, send_core(own)
+
+    def reduce_core(part_own, part_other):
+        got = send_core(part_other)
+        return (part_own.astype(f32) + got.astype(f32)).astype(bf16)
+
+    def reduce_xy(both):
+        total = both[0, 0].astype(f32)
+        for dx, dy in PEERS:
+            total = total + send_xy(both[dx, dy], dx, dy).astype(f32)
+        return total
+
+    pieces = [gather(c) for c in range(CHUNKS)]
+    prev = None
+    both = None
+    totals = []
+    for c in range(CHUNKS):
+        own, other = pieces[c]
+        if c:
+            own, other, both = lax.optimization_barrier((own, other, both))
         y, dq, part_own, part_other, g = attend(
             c, mine, cols, folded, seg_image, tile_counts, gate, queries, cotangent, own, other, prev
         )
         prev = (g, y, dq)
-        got = send_core(part_other)
-        both = (part_own.astype(f32) + got.astype(f32)).astype(bf16)
-        total = both[0, 0].astype(f32)
-        for dx, dy in PEERS:
-            total = total + send_xy(both[dx, dy], dx, dy).astype(f32)
+        if c:
+            totals.append(reduce_xy(both))
+            part_other, totals[-1] = lax.optimization_barrier((part_other, totals[-1]))
+        both = reduce_core(part_own, part_other)
+    totals.append(reduce_xy(both))
+
+    cuts = []
+    for total in totals:
         grads, gates = total[: 2 * heads * half], total[2 * heads * half :]
         grads = grads.reshape(2 * heads, cols, mine, hd)
         if folded:
             grads, gates = grads.astype(bf16), gates.astype(bf16)
-            cut = [
-                jnp.concatenate([grads[:, k].reshape(2 * heads * mine, hd), gates], axis=0) for k in range(cols)
-            ]
-            total = cut[0].astype(f32)
-            for k in (1, 2, 3):
-                total = total + send_z(cut[k], k).astype(f32)
-            grads, gates = total[: 2 * heads * mine], total[2 * heads * mine :]
+            cut = [jnp.concatenate([grads[:, k].reshape(-1, hd), gates], axis=0) for k in range(cols)]
+            cuts += [cut[0]] + [send_z(cut[k], k) for k in (1, 2, 3)]
         else:
             grads = lax.psum_scatter(grads, "z", scatter_dimension=1, tiled=True)
-            gates = lax.psum(gates, "z")
-        reduced.append(grads.reshape(2 * heads, mine, hd))
-
-    def lay(blocks):
-        return jnp.concatenate(blocks, axis=1)
-
-    dk = lay([r[i] for r in reduced for i in range(heads)])
-    dv = lay([r[heads + i] for r in reduced for i in range(heads)])
-    units = 4.0 ** (GTOP - jnp.arange(GROWS, dtype=f32))
-    tg = jnp.tanh(gate[0])
-    grad_gate = ((1.0 - tg * tg) * jnp.sum(gates * units[:, None])).reshape(1)
-    return (y, dq, dk, dv, grad_gate)
+            cuts.append(jnp.concatenate([grads.reshape(-1, hd), lax.psum(gates, "z")], axis=0))
+    return (y, dq, *finish(mine, gate, cuts))
 
 
 def solution(mesh):

time: 79.3 us -> 69.2 us (0.87)
  waiting for transfers between devices: 28.1 us -> 18.5 us
  between operations: 3.47 us -> 1.66 us
  Pallas kernels: 12.8 us -> 14.4 us
  starting transfers between devices: 30.5 us -> 29.4 us
    ppermute x12, waiting for transfers between devices: 19.2 us -> 6.54 us  [send_xy(): return lax.ppermute(x, ('x', 'y'), [(i, i ^ 2 * dx + dy) for i in range(4)])]
    ppermute x4, waiting for transfers between devices: 0.01 us -> 3.78 us  [send_core(): return lax.ppermute(x, 'core', [(0, 1), (1, 0)])]
    pallas_call x0 -> x1, Pallas kernels: none -> 1.58 us  [finish(): pl.pallas_call(functools.partial(finish_kernel, heads, mine), in_specs=[s...]
    slice x6 -> x2, local copies, waits for them, and re-layouts: 1.51 us -> 0.02 us  [local(): grads[:, k].reshape(-1, hd)]
    squeeze x5 -> x7, local copies, waits for them, and re-layouts: 0.07 us -> 1.55 us  [the longest x4 0.76 us: gather(): p[0, :, lanes]]
    ppermute x12, starting transfers between devices: 15.1 us -> 14.2 us  [send_xy(): return lax.ppermute(x, ('x', 'y'), [(i, i ^ 2 * dx + dy) for i in range(4)])]
  transfers between devices with their start and end apart: 25 -> 25, of which waited for: 12 -> 11; matrix products, arithmetic and copies ran while one was open for 1% -> 4% of each run, Pallas kernels for 16% -> 19%
where the time goes in v4:
time: 69.2 us; the launch traced here: 68.8 us
  starting transfers between devices  29.4 us (42%)
  waiting for transfers between devices  18.5 us (27%)
  Pallas kernels  14.4 us (21%)
  other arithmetic  2.52 us (4%)
  local copies, waits for them, and re-layouts  2.29 us (3%)
  between operations  1.66 us (2%)
    ppermute x9, starting transfers between devices, send_z(): return lax.ppermute(x, 'z', [(i, i ^ k) for i in range(cols)])  14.4 us
    ppermute x12, starting transfers between devices, send_xy(): return lax.ppermute(x, ('x', 'y'), [(i, i ^ 2 * dx + dy) for i in range(4)])  14.2 us
    pallas_call x2, Pallas kernels, attend(): pl.pallas_call(functools.partial(attend_kernel, mine, cols, folded, first...  12.8 us
    ppermute x9, waiting for transfers between devices, send_z(): return lax.ppermute(x, 'z', [(i, i ^ k) for i in range(cols)])  8.22 us
    ppermute x12, waiting for transfers between devices, send_xy(): return lax.ppermute(x, ('x', 'y'), [(i, i ^ 2 * dx + dy) for i in range(4)])  6.54 us
    ppermute x4, waiting for transfers between devices, send_core(): return lax.ppermute(x, 'core', [(0, 1), (1, 0)])  3.78 us
    pallas_call x1, Pallas kernels, finish(): pl.pallas_call(functools.partial(finish_kernel, heads, mine), in_specs=[s...  1.58 us
  transfers between devices with their start and end apart: 25, of which 11 were waited for; matrix products, arithmetic and copies ran while one was open for 4% of the time, Pallas kernels for 19%

profile of v4, /device:TPU:0, one launch (start us, length us, event | category | flops | bytes accessed | tf_op | source)
XLA Modules:
  0.0 68.8 jit_solution(15988719230665843387)
XLA Ops:
  0.6 0.8 %pad_maximum_fusion.8 = bf16[2,32,512]{2,1,0:T(8,128)(2,1)S(1)} fusion(bf16[1,32,512]{2,1,0:T(8,128)(2,1)} %bitcast.77, bf16[1,32,512]{2,1,0:T(8,128)(2,1)} %bitcast.75), kind=kLoop, calls=%fused_computation.26 | loop fusion | flops 32768 | bytes 131072 | tf_op jit(solution)/shard_map/stack | solution.py:308
  1.4 3.1 %collective-permute-start = (bf16[2,32,512]{2,1,0:T(8,128)(2,1)S(1)}, bf16[2,32,512]{2,1,0:T(8,128)(2,1)S(1)}, u32[]{:S(2)}, u32[]{:S(2)}) collective-permute-start(bf16[2,32,512]{2,1,0:T(8,128)(2,1)S(1)} %pad_maximum_fusion.8), channel_id=1, source_target_pairs={{0,2},{2,0},{4,6},{6,4},{1,3},{3,1},{5,7},{7,5},{8,10},{10,8},{12,... | collective-permute-start | bytes 196616 | tf_op jit(solution)/shard_map/ppermute | solution.py:300
  4.5 2.6 %collective-permute-start.1 = (bf16[2,32,512]{2,1,0:T(8,128)(2,1)S(1)}, bf16[2,32,512]{2,1,0:T(8,128)(2,1)S(1)}, u32[]{:S(2)}, u32[]{:S(2)}) collective-permute-start(bf16[2,32,512]{2,1,0:T(8,128)(2,1)S(1)} %pad_maximum_fusion.8), channel_id=1, source_target_pairs={{0,4},{2,6},{4,0},{6,2},{1,5},{3,7},{5,1},{7,3},{8,12},{10,14},{12... | collective-permute-start | bytes 196616 | tf_op jit(solution)/shard_map/ppermute | solution.py:300
  7.1 0.7 %slice_bitcast_fusion.14 = (bf16[32,256]{1,0:T(8,128)(2,1)S(1)}, bf16[32,256]{1,0:T(8,128)(2,1)S(1)}) fusion(bf16[1,32,512]{2,1,0:T(8,128)(2,1)} %bitcast.76), kind=kLoop, calls=%fused_computation.48 | loop fusion | bytes 65536 | tf_op jit(solution)/shard_map/squeeze | solution.py:316
  7.8 0.7 %slice_bitcast_fusion.13 = (bf16[32,256]{1,0:T(8,128)(2,1)S(1)}, bf16[32,256]{1,0:T(8,128)(2,1)S(1)}) fusion(bf16[1,32,512]{2,1,0:T(8,128)(2,1)} %bitcast.78), kind=kLoop, calls=%fused_computation.47 | loop fusion | bytes 65536 | tf_op jit(solution)/shard_map/squeeze | solution.py:316
  8.6 3.1 %collective-permute-done.1 = bf16[2,32,512]{2,1,0:T(8,128)(2,1)S(1)} collective-permute-done((bf16[2,32,512]{2,1,0:T(8,128)(2,1)S(1)}, bf16[2,32,512]{2,1,0:T(8,128)(2,1)S(1)}, u32[]{:S(2)}, u32[]{:S(2)}) %collective-permute-start.1) | collective-permute-done | bytes 65568 | tf_op jit(solution)/shard_map/ppermute | solution.py:300
  11.8 1.4 %collective-permute-done.2 = bf16[2,32,512]{2,1,0:T(8,128)(2,1)S(1)} collective-permute-done((bf16[2,32,512]{2,1,0:T(8,128)(2,1)S(1)}, bf16[2,32,512]{2,1,0:T(8,128)(2,1)S(1)}, u32[]{:S(2)}, u32[]{:S(2)}) %collective-permute-start.2) | collective-permute-done | bytes 65568 | tf_op jit(solution)/shard_map/ppermute | solution.py:300
  13.2 1.6 %collective-permute-start.7 = (bf16[128,512]{1,0:T(8,128)(2,1)S(1)}, bf16[128,512]{1,0:T(8,128)(2,1)S(1)}, u32[]{:S(2)}, u32[]{:S(2)}) collective-permute-start(bf16[128,512]{1,0:T(8,128)(2,1)S(1)} %maximum_maximum_fusion.1), channel_id=1, source_target_pairs={{0,1},{1,0},{16,17},{17,16},{2,3},{3,2},{18,19},{19,18},{4,5},{5,4... | collective-permute-start | bytes 393224 | tf_op jit(solution)/shard_map/ppermute | solution.py:303
  14.8 1.5 %collective-permute-start.8 = (bf16[128,512]{1,0:T(8,128)(2,1)S(1)}, bf16[128,512]{1,0:T(8,128)(2,1)S(1)}, u32[]{:S(2)}, u32[]{:S(2)}) collective-permute-start(bf16[128,512]{1,0:T(8,128)(2,1)S(1)} %maximum_maximum_fusion.1), channel_id=1, source_target_pairs={{0,16},{1,17},{16,0},{17,1},{2,18},{3,19},{18,2},{19,3},{4,20},{5,... | collective-permute-start | bytes 393224 | tf_op jit(solution)/shard_map/ppermute | solution.py:303
  16.3 0.5 collective-permute-start.9
  16.7 2.9 %collective-permute-done.7 = bf16[128,512]{1,0:T(8,128)(2,1)S(1)} collective-permute-done((bf16[128,512]{1,0:T(8,128)(2,1)S(1)}, bf16[128,512]{1,0:T(8,128)(2,1)S(1)}, u32[]{:S(2)}, u32[]{:S(2)}) %collective-permute-start.7) | collective-permute-done | bytes 131104 | tf_op jit(solution)/shard_map/ppermute | solution.py:303
  19.6 0.1 collective-permute-done.8
  19.7 2.4 %collective-permute-done.9 = bf16[128,512]{1,0:T(8,128)(2,1)S(1)} collective-permute-done((bf16[128,512]{1,0:T(8,128)(2,1)S(1)}, bf16[128,512]{1,0:T(8,128)(2,1)S(1)}, u32[]{:S(2)}, u32[]{:S(2)}) %collective-permute-start.9) | collective-permute-done | bytes 131104 | tf_op jit(solution)/shard_map/ppermute | solution.py:303
  22.1 0.1 collective-permute-start.10
  22.9 0.6 collective-permute-start.3
  23.5 1.5 %collective-permute-start.4 = (bf16[128,512]{1,0:T(8,128)(2,1)S(1)}, bf16[128,512]{1,0:T(8,128)(2,1)S(1)}, u32[]{:S(2)}, u32[]{:S(2)}) collective-permute-start(bf16[128,512]{1,0:T(8,128)(2,1)S(1)} %maximum_maximum_fusion), channel_id=1, source_target_pairs={{0,16},{1,17},{16,0},{17,1},{2,18},{3,19},{18,2},{19,3},{4,20},{5,... | collective-permute-start | bytes 393224 | tf_op jit(solution)/shard_map/ppermute | solution.py:303
  24.9 1.5 %collective-permute-start.5 = (bf16[128,512]{1,0:T(8,128)(2,1)S(1)}, bf16[128,512]{1,0:T(8,128)(2,1)S(1)}, u32[]{:S(2)}, u32[]{:S(2)}) collective-permute-start(bf16[128,512]{1,0:T(8,128)(2,1)S(1)} %maximum_maximum_fusion), channel_id=1, source_target_pairs={{0,17},{1,16},{16,1},{17,0},{2,19},{3,18},{18,3},{19,2},{4,21},{5,... | collective-permute-start | bytes 393224 | tf_op jit(solution)/shard_map/ppermute | solution.py:303
  26.5 6.4 %shard_map.110 = (bf16[128,4096]{1,0:T(8,128)(2,1)}, bf16[128,4096]{1,0:T(8,128)(2,1)}, bf16[2,2,528,128]{3,2,1,0:T(8,128)(2,1)S(1)}, bf16[2,2,528,128]{3,2,1,0:T(8,128)(2,1)S(1)}, f32[8,128]{1,0:T(8,128)S(1)}) custom-call(s32[128]{0:T(128)S(1)} %copy-done.2, s32[4]{0:T(128)S(1)} %copy-done.3, f32[1]{0:T(128)S(6)} %copy.28.gate_s, s32[1,128]{1,0:T(1,128)S(1)} %bitcast.71, ...), custom_call_target="tpu_custom_call" | custom-call | flops 8053063680 | bytes 4194304 | tf_op jit(solution)/shard_map/pallas_call | solution.py:206
  32.9 0.1 collective-permute-start.11
  33.1 0.5 collective-permute-start.6
  33.6 1.3 %collective-permute-done.11 = bf16[2,2,528,128]{3,2,1,0:T(8,128)(2,1)S(1)} collective-permute-done((bf16[2,2,528,128]{3,2,1,0:T(8,128)(2,1)S(1)}, bf16[2,2,528,128]{3,2,1,0:T(8,128)(2,1)S(1)}, u32[]{:S(2)}, u32[]{:S(2)}) %collective-permute-start.11) | collective-permute-done | bytes 540704 | tf_op jit(solution)/shard_map/ppermute | solution.py:306
  34.9 0.1 add_convert_fusion.1
  35.1 0.6 collective-permute-done.6.other
  35.7 0.6 collective-permute-start.12
  36.3 1.5 %collective-permute-start.13 = (bf16[528,128]{1,0:T(8,128)(2,1)S(1)}, bf16[528,128]{1,0:T(8,128)(2,1)S(1)}, u32[]{:S(2)}, u32[]{:S(2)}) collective-permute-start(bf16[528,128]{1,0:T(8,128)(2,1)S(1)} %get-tuple-element.44), channel_id=1, source_target_pairs={{0,16},{1,17},{16,0},{17,1},{2,18},{3,19},{18,2},{19,3},{4,20},{5,... | collective-permute-start | bytes 405512 | tf_op jit(solution)/shard_map/ppermute | solution.py:303
  37.7 1.5 %collective-permute-start.14 = (bf16[528,128]{1,0:T(8,128)(2,1)S(1)}, bf16[528,128]{1,0:T(8,128)(2,1)S(1)}, u32[]{:S(2)}, u32[]{:S(2)}) collective-permute-start(bf16[528,128]{1,0:T(8,128)(2,1)S(1)} %get-tuple-element.43), channel_id=1, source_target_pairs={{0,17},{1,16},{16,1},{17,0},{2,19},{3,18},{18,3},{19,2},{4,21},{5,... | collective-permute-start | bytes 405512 | tf_op jit(solution)/shard_map/ppermute | solution.py:303
  39.3 6.4 %shard_map.111 = (bf16[128,4096]{1,0:T(8,128)(2,1)}, bf16[128,4096]{1,0:T(8,128)(2,1)}, bf16[2,2,528,128]{3,2,1,0:T(8,128)(2,1)S(1)}, bf16[2,2,528,128]{3,2,1,0:T(8,128)(2,1)S(1)}, f32[8,128]{1,0:T(8,128)}) custom-call(s32[128]{0:T(128)S(1)} %copy-done.2, s32[4]{0:T(128)S(1)} %copy-done.3, ...), custom_call_target="tpu_custom_call", output_to_operand_aliasing={{0}: (9, {}), {1}: (10, {})} | custom-call | flops 8053063680 | bytes 4194304 | tf_op jit(solution)/shard_map/pallas_call | solution.py:206
  45.7 0.1 fusion.4
  45.8 0.1 collective-permute-start.18
  45.9 1.9 %collective-permute-done.18 = bf16[2,2,528,128]{3,2,1,0:T(8,128)(2,1)S(1)} collective-permute-done((bf16[2,2,528,128]{3,2,1,0:T(8,128)(2,1)S(1)}, bf16[2,2,528,128]{3,2,1,0:T(8,128)(2,1)S(1)}, u32[]{:S(2)}, u32[]{:S(2)}) %collective-permute-start.18) | collective-permute-done | bytes 540704 | tf_op jit(solution)/shard_map/ppermute | solution.py:306
  47.8 0.1 add_convert_fusion
  47.9 0.6 collective-permute-start.19
  48.5 1.5 %collective-permute-start.20 = (bf16[528,128]{1,0:T(8,128)(2,1)S(1)}, bf16[528,128]{1,0:T(8,128)(2,1)S(1)}, u32[]{:S(2)}, u32[]{:S(2)}) collective-permute-start(bf16[528,128]{1,0:T(8,128)(2,1)S(1)} %get-tuple-element.41), channel_id=1, source_target_pairs={{0,16},{1,17},{16,0},{17,1},{2,18},{3,19},{18,2},{19,3},{4,20},{5,... | collective-permute-start | bytes 405512 | tf_op jit(solution)/shard_map/ppermute | solution.py:303
  50.0 1.5 %collective-permute-start.21 = (bf16[528,128]{1,0:T(8,128)(2,1)S(1)}, bf16[528,128]{1,0:T(8,128)(2,1)S(1)}, u32[]{:S(2)}, u32[]{:S(2)}) collective-permute-start(bf16[528,128]{1,0:T(8,128)(2,1)S(1)} %get-tuple-element.40), channel_id=1, source_target_pairs={{0,17},{1,16},{16,1},{17,0},{2,19},{3,18},{18,3},{19,2},{4,21},{5,... | collective-permute-start | bytes 405512 | tf_op jit(solution)/shard_map/ppermute | solution.py:303
  51.5 0.6 pad_maximum_fusion
  52.1 0.2 collective-permute-start.15
  52.3 2.2 %collective-permute-start.16 = (bf16[144,128]{1,0:T(8,128)(2,1)S(1)}, bf16[144,128]{1,0:T(8,128)(2,1)S(1)}, u32[]{:S(2)}, u32[]{:S(2)}) collective-permute-start(bf16[144,128]{1,0:T(8,128)(2,1)S(1)} %get-tuple-element.75), channel_id=1, source_target_pairs={{0,4},{2,6},{4,0},{6,2},{1,5},{3,7},{5,1},{7,3},{8,12},{10,14},{12... | collective-permute-start | bytes 110600 | tf_op jit(solution)/shard_map/ppermute | solution.py:300
  54.5 2.0 %collective-permute-start.17 = (bf16[144,128]{1,0:T(8,128)(2,1)S(1)}, bf16[144,128]{1,0:T(8,128)(2,1)S(1)}, u32[]{:S(2)}, u32[]{:S(2)}) collective-permute-start(bf16[144,128]{1,0:T(8,128)(2,1)S(1)} %get-tuple-element.73), channel_id=1, source_target_pairs={{0,6},{2,4},{4,2},{6,0},{1,7},{3,5},{5,3},{7,1},{8,14},{10,12},{12... | collective-permute-start | bytes 110600 | tf_op jit(solution)/shard_map/ppermute | solution.py:300
  56.5 1.2 %collective-permute-done.21 = bf16[528,128]{1,0:T(8,128)(2,1)S(1)} collective-permute-done((bf16[528,128]{1,0:T(8,128)(2,1)S(1)}, bf16[528,128]{1,0:T(8,128)(2,1)S(1)}, u32[]{:S(2)}, u32[]{:S(2)}) %collective-permute-start.21) | collective-permute-done | bytes 135200 | tf_op jit(solution)/shard_map/ppermute | solution.py:303
  57.7 0.1 fusion.2
  57.8 0.6 pad_maximum_fusion.4
  58.5 0.2 collective-permute-start.22
  58.6 2.2 %collective-permute-start.23 = (bf16[144,128]{1,0:T(8,128)(2,1)S(1)}, bf16[144,128]{1,0:T(8,128)(2,1)S(1)}, u32[]{:S(2)}, u32[]{:S(2)}) collective-permute-start(bf16[144,128]{1,0:T(8,128)(2,1)S(1)} %get-tuple-element.71), channel_id=1, source_target_pairs={{0,4},{2,6},{4,0},{6,2},{1,5},{3,7},{5,1},{7,3},{8,12},{10,14},{12... | collective-permute-start | bytes 110600 | tf_op jit(solution)/shard_map/ppermute | solution.py:300
  60.8 2.0 %collective-permute-start.24 = (bf16[144,128]{1,0:T(8,128)(2,1)S(1)}, bf16[144,128]{1,0:T(8,128)(2,1)S(1)}, u32[]{:S(2)}, u32[]{:S(2)}) collective-permute-start(bf16[144,128]{1,0:T(8,128)(2,1)S(1)} %get-tuple-element.69), channel_id=1, source_target_pairs={{0,6},{2,4},{4,2},{6,0},{1,7},{3,5},{5,3},{7,1},{8,14},{10,12},{12... | collective-permute-start | bytes 110600 | tf_op jit(solution)/shard_map/ppermute | solution.py:300
  62.9 0.6 collective-permute-done.23.refs_6_
  63.5 3.1 %collective-permute-done.24.refs_7_ = bf16[144,128]{1,0:T(8,128)(2,1)S(1)} collective-permute-done((bf16[144,128]{1,0:T(8,128)(2,1)S(1)}, bf16[144,128]{1,0:T(8,128)(2,1)S(1)}, u32[]{:S(2)}, u32[]{:S(2)}) %collective-permute-start.24) | collective-permute-done | bytes 36896 | tf_op jit(solution)/shard_map/ppermute | solution.py:300
  66.6 0.6 copy-done.9
  67.2 1.6 %shard_map.112 = (f32[32,512]{1,0:T(8,128)}, f32[32,512]{1,0:T(8,128)}, f32[1]{0:T(128)}) custom-call(f32[1]{0:T(128)S(6)} %copy.28.gate_s, bf16[144,128]{1,0:T(8,128)(2,1)} %get-tuple-element.76.refs_0_, bf16[144,128]{1,0:T(8,128)(2,1)} %copy-done.4, bf16[144,128]{1,0:T(8,128)(2,1)} %copy-done.5, bf16[144,128]{1,0:T(8,128)(2,1)} %copy-done.6, ...), custom_call_target="tpu_custom_call" | custom-call | tf_op jit(solution)/shard_map/pallas_call | solution.py:281
  (61 shorter events, 0.3 us)
Async XLA Ops:
  1.4 7.2 %collective-permute-start = (bf16[2,32,512]{2,1,0:T(8,128)(2,1)S(1)}, bf16[2,32,512]{2,1,0:T(8,128)(2,1)S(1)}, u32[]{:S(2)}, u32[]{:S(2)}) collective-permute-start(bf16[2,32,512]{2,1,0:T(8,128)(2,1)S(1)} %pad_maximum_fusion.8), channel_id=1, source_target_pairs={{0,2},{2,0},{4,6},{6,4},{1,3},{3,1},{5,7},{7,5},{8,10},{10,8},{12,... | collective-permute-start | bytes 196616 | tf_op jit(solution)/shard_map/ppermute | solution.py:300
  4.5 7.3 %collective-permute-start.1 = (bf16[2,32,512]{2,1,0:T(8,128)(2,1)S(1)}, bf16[2,32,512]{2,1,0:T(8,128)(2,1)S(1)}, u32[]{:S(2)}, u32[]{:S(2)}) collective-permute-start(bf16[2,32,512]{2,1,0:T(8,128)(2,1)S(1)} %pad_maximum_fusion.8), channel_id=1, source_target_pairs={{0,4},{2,6},{4,0},{6,2},{1,5},{3,7},{5,1},{7,3},{8,12},{10,14},{12... | collective-permute-start | bytes 196616 | tf_op jit(solution)/shard_map/ppermute | solution.py:300
  7.1 6.1 %collective-permute-start.2 = (bf16[2,32,512]{2,1,0:T(8,128)(2,1)S(1)}, bf16[2,32,512]{2,1,0:T(8,128)(2,1)S(1)}, u32[]{:S(2)}, u32[]{:S(2)}) collective-permute-start(bf16[2,32,512]{2,1,0:T(8,128)(2,1)S(1)} %pad_maximum_fusion.8), channel_id=1, source_target_pairs={{0,6},{2,4},{4,2},{6,0},{1,7},{3,5},{5,3},{7,1},{8,14},{10,12},{12... | collective-permute-start | bytes 196616 | tf_op jit(solution)/shard_map/ppermute | solution.py:300
  8.6 17.9 %copy-start = (bf16[128,4096]{1,0:T(8,128)(2,1)S(1)}, bf16[128,4096]{1,0:T(8,128)(2,1)}, u32[]{:S(2)}) copy-start(bf16[128,4096]{1,0:T(8,128)(2,1)} %q_ref.3) | copy-start | bytes 3145732
  8.6 17.9 %copy-start.1 = (bf16[128,4096]{1,0:T(8,128)(2,1)S(1)}, bf16[128,4096]{1,0:T(8,128)(2,1)}, u32[]{:S(2)}) copy-start(bf16[128,4096]{1,0:T(8,128)(2,1)} %dy_ref.3) | copy-start | bytes 3145732
  8.6 17.9 %copy-start.2 = (s32[128]{0:T(128)S(1)}, s32[128]{0:T(128)}, u32[]{:S(2)}) copy-start(s32[128]{0:T(128)} %seg_s.3) | copy-start | bytes 1540
  8.6 17.9 %copy-start.3 = (s32[4]{0:T(128)S(1)}, s32[4]{0:T(128)}, u32[]{:S(2)}) copy-start(s32[4]{0:T(128)} %cnt_s.3) | copy-start | bytes 52
  13.2 6.4 %collective-permute-start.7 = (bf16[128,512]{1,0:T(8,128)(2,1)S(1)}, bf16[128,512]{1,0:T(8,128)(2,1)S(1)}, u32[]{:S(2)}, u32[]{:S(2)}) collective-permute-start(bf16[128,512]{1,0:T(8,128)(2,1)S(1)} %maximum_maximum_fusion.1), channel_id=1, source_target_pairs={{0,1},{1,0},{16,17},{17,16},{2,3},{3,2},{18,19},{19,18},{4,5},{5,4... | collective-permute-start | bytes 393224 | tf_op jit(solution)/shard_map/ppermute | solution.py:303
  14.8 5.0 %collective-permute-start.8 = (bf16[128,512]{1,0:T(8,128)(2,1)S(1)}, bf16[128,512]{1,0:T(8,128)(2,1)S(1)}, u32[]{:S(2)}, u32[]{:S(2)}) collective-permute-start(bf16[128,512]{1,0:T(8,128)(2,1)S(1)} %maximum_maximum_fusion.1), channel_id=1, source_target_pairs={{0,16},{1,17},{16,0},{17,1},{2,18},{3,19},{18,2},{19,3},{4,20},{5,... | collective-permute-start | bytes 393224 | tf_op jit(solution)/shard_map/ppermute | solution.py:303
  16.3 5.9 %collective-permute-start.9 = (bf16[128,512]{1,0:T(8,128)(2,1)S(1)}, bf16[128,512]{1,0:T(8,128)(2,1)S(1)}, u32[]{:S(2)}, u32[]{:S(2)}) collective-permute-start(bf16[128,512]{1,0:T(8,128)(2,1)S(1)} %maximum_maximum_fusion.1), channel_id=1, source_target_pairs={{0,17},{1,16},{16,1},{17,0},{2,19},{3,18},{18,3},{19,2},{4,21},{5,... | collective-permute-start | bytes 393224 | tf_op jit(solution)/shard_map/ppermute | solution.py:303
  22.1 4.3 %collective-permute-start.10 = (bf16[2,256,512]{2,1,0:T(8,128)(2,1)S(1)}, bf16[2,256,512]{2,1,0:T(8,128)(2,1)S(1)}, u32[]{:S(2)}, u32[]{:S(2)}) collective-permute-start(bf16[2,256,512]{2,1,0:T(8,128)(2,1)S(1)} %bitcast.69), channel_id=1, source_target_pairs={{0,8},{8,0},{1,9},{9,1},{2,10},{10,2},{3,11},{11,3},{4,12},{12,4},... | collective-permute-start | bytes 1572872 | tf_op jit(solution)/shard_map/ppermute | solution.py:306
  22.9 10.1 %collective-permute-start.3 = (bf16[128,512]{1,0:T(8,128)(2,1)S(1)}, bf16[128,512]{1,0:T(8,128)(2,1)S(1)}, u32[]{:S(2)}, u32[]{:S(2)}) collective-permute-start(bf16[128,512]{1,0:T(8,128)(2,1)S(1)} %maximum_maximum_fusion), channel_id=1, source_target_pairs={{0,1},{1,0},{16,17},{17,16},{2,3},{3,2},{18,19},{19,18},{4,5},{5,4... | collective-permute-start | bytes 393224 | tf_op jit(solution)/shard_map/ppermute | solution.py:303
  23.5 9.6 %collective-permute-start.4 = (bf16[128,512]{1,0:T(8,128)(2,1)S(1)}, bf16[128,512]{1,0:T(8,128)(2,1)S(1)}, u32[]{:S(2)}, u32[]{:S(2)}) collective-permute-start(bf16[128,512]{1,0:T(8,128)(2,1)S(1)} %maximum_maximum_fusion), channel_id=1, source_target_pairs={{0,16},{1,17},{16,0},{17,1},{2,18},{3,19},{18,2},{19,3},{4,20},{5,... | collective-permute-start | bytes 393224 | tf_op jit(solution)/shard_map/ppermute | solution.py:303
  24.9 8.1 %collective-permute-start.5 = (bf16[128,512]{1,0:T(8,128)(2,1)S(1)}, bf16[128,512]{1,0:T(8,128)(2,1)S(1)}, u32[]{:S(2)}, u32[]{:S(2)}) collective-permute-start(bf16[128,512]{1,0:T(8,128)(2,1)S(1)} %maximum_maximum_fusion), channel_id=1, source_target_pairs={{0,17},{1,16},{16,1},{17,0},{2,19},{3,18},{18,3},{19,2},{4,21},{5,... | collective-permute-start | bytes 393224 | tf_op jit(solution)/shard_map/ppermute | solution.py:303
  32.9 2.0 %collective-permute-start.11 = (bf16[2,2,528,128]{3,2,1,0:T(8,128)(2,1)S(1)}, bf16[2,2,528,128]{3,2,1,0:T(8,128)(2,1)S(1)}, u32[]{:S(2)}, u32[]{:S(2)}) collective-permute-start(bf16[2,2,528,128]{3,2,1,0:T(8,128)(2,1)S(1)} %get-tuple-element.23), channel_id=1, source_target_pairs={{0,8},{8,0},{1,9},{9,1},{2,10},{10,2},{3,11},{11,3},{4,12},{12,4},... | collective-permute-start | bytes 1622024 | tf_op jit(solution)/shard_map/ppermute | solution.py:306
  33.1 2.6 %collective-permute-start.6 = (bf16[2,256,512]{2,1,0:T(8,128)(2,1)S(1)}, bf16[2,256,512]{2,1,0:T(8,128)(2,1)S(1)}, u32[]{:S(2)}, u32[]{:S(2)}) collective-permute-start(bf16[2,256,512]{2,1,0:T(8,128)(2,1)S(1)} %bitcast.67), channel_id=1, source_target_pairs={{0,8},{8,0},{1,9},{9,1},{2,10},{10,2},{3,11},{11,3},{4,12},{12,4},... | collective-permute-start | bytes 1572872 | tf_op jit(solution)/shard_map/ppermute | solution.py:306
  35.7 9.9 %collective-permute-start.12 = (bf16[528,128]{1,0:T(8,128)(2,1)S(1)}, bf16[528,128]{1,0:T(8,128)(2,1)S(1)}, u32[]{:S(2)}, u32[]{:S(2)}) collective-permute-start(bf16[528,128]{1,0:T(8,128)(2,1)S(1)} %get-tuple-element.42), channel_id=1, source_target_pairs={{0,1},{1,0},{16,17},{17,16},{2,3},{3,2},{18,19},{19,18},{4,5},{5,4... | collective-permute-start | bytes 405512 | tf_op jit(solution)/shard_map/ppermute | solution.py:303
  36.3 9.4 %collective-permute-start.13 = (bf16[528,128]{1,0:T(8,128)(2,1)S(1)}, bf16[528,128]{1,0:T(8,128)(2,1)S(1)}, u32[]{:S(2)}, u32[]{:S(2)}) collective-permute-start(bf16[528,128]{1,0:T(8,128)(2,1)S(1)} %get-tuple-element.44), channel_id=1, source_target_pairs={{0,16},{1,17},{16,0},{17,1},{2,18},{3,19},{18,2},{19,3},{4,20},{5,... | collective-permute-start | bytes 405512 | tf_op jit(solution)/shard_map/ppermute | solution.py:303
  37.7 7.9 %collective-permute-start.14 = (bf16[528,128]{1,0:T(8,128)(2,1)S(1)}, bf16[528,128]{1,0:T(8,128)(2,1)S(1)}, u32[]{:S(2)}, u32[]{:S(2)}) collective-permute-start(bf16[528,128]{1,0:T(8,128)(2,1)S(1)} %get-tuple-element.43), channel_id=1, source_target_pairs={{0,17},{1,16},{16,1},{17,0},{2,19},{3,18},{18,3},{19,2},{4,21},{5,... | collective-permute-start | bytes 405512 | tf_op jit(solution)/shard_map/ppermute | solution.py:303
  45.8 2.0 %collective-permute-start.18 = (bf16[2,2,528,128]{3,2,1,0:T(8,128)(2,1)S(1)}, bf16[2,2,528,128]{3,2,1,0:T(8,128)(2,1)S(1)}, u32[]{:S(2)}, u32[]{:S(2)}) collective-permute-start(bf16[2,2,528,128]{3,2,1,0:T(8,128)(2,1)S(1)} %get-tuple-element.35), channel_id=1, source_target_pairs={{0,8},{8,0},{1,9},{9,1},{2,10},{10,2},{3,11},{11,3},{4,12},{12,4},... | collective-permute-start | bytes 1622024 | tf_op jit(solution)/shard_map/ppermute | solution.py:306
  47.9 6.6 %collective-permute-start.19 = (bf16[528,128]{1,0:T(8,128)(2,1)S(1)}, bf16[528,128]{1,0:T(8,128)(2,1)S(1)}, u32[]{:S(2)}, u32[]{:S(2)}) collective-permute-start(bf16[528,128]{1,0:T(8,128)(2,1)S(1)} %get-tuple-element.39), channel_id=1, source_target_pairs={{0,1},{1,0},{16,17},{17,16},{2,3},{3,2},{18,19},{19,18},{4,5},{5,4... | collective-permute-start | bytes 405512 | tf_op jit(solution)/shard_map/ppermute | solution.py:303
  48.5 8.0 %collective-permute-start.20 = (bf16[528,128]{1,0:T(8,128)(2,1)S(1)}, bf16[528,128]{1,0:T(8,128)(2,1)S(1)}, u32[]{:S(2)}, u32[]{:S(2)}) collective-permute-start(bf16[528,128]{1,0:T(8,128)(2,1)S(1)} %get-tuple-element.41), channel_id=1, source_target_pairs={{0,16},{1,17},{16,0},{17,1},{2,18},{3,19},{18,2},{19,3},{4,20},{5,... | collective-permute-start | bytes 405512 | tf_op jit(solution)/shard_map/ppermute | solution.py:303
  50.0 7.7 %collective-permute-start.21 = (bf16[528,128]{1,0:T(8,128)(2,1)S(1)}, bf16[528,128]{1,0:T(8,128)(2,1)S(1)}, u32[]{:S(2)}, u32[]{:S(2)}) collective-permute-start(bf16[528,128]{1,0:T(8,128)(2,1)S(1)} %get-tuple-element.40), channel_id=1, source_target_pairs={{0,17},{1,16},{16,1},{17,0},{2,19},{3,18},{18,3},{19,2},{4,21},{5,... | collective-permute-start | bytes 405512 | tf_op jit(solution)/shard_map/ppermute | solution.py:303
  52.1 8.7 %collective-permute-start.15 = (bf16[144,128]{1,0:T(8,128)(2,1)S(1)}, bf16[144,128]{1,0:T(8,128)(2,1)S(1)}, u32[]{:S(2)}, u32[]{:S(2)}) collective-permute-start(bf16[144,128]{1,0:T(8,128)(2,1)S(1)} %get-tuple-element.74), channel_id=1, source_target_pairs={{0,2},{2,0},{4,6},{6,4},{1,3},{3,1},{5,7},{7,5},{8,10},{10,8},{12,... | collective-permute-start | bytes 110600 | tf_op jit(solution)/shard_map/ppermute | solution.py:300
  52.3 10.6 %collective-permute-start.16 = (bf16[144,128]{1,0:T(8,128)(2,1)S(1)}, bf16[144,128]{1,0:T(8,128)(2,1)S(1)}, u32[]{:S(2)}, u32[]{:S(2)}) collective-permute-start(bf16[144,128]{1,0:T(8,128)(2,1)S(1)} %get-tuple-element.75), channel_id=1, source_target_pairs={{0,4},{2,6},{4,0},{6,2},{1,5},{3,7},{5,1},{7,3},{8,12},{10,14},{12... | collective-permute-start | bytes 110600 | tf_op jit(solution)/shard_map/ppermute | solution.py:300
  54.5 8.3 %collective-permute-start.17 = (bf16[144,128]{1,0:T(8,128)(2,1)S(1)}, bf16[144,128]{1,0:T(8,128)(2,1)S(1)}, u32[]{:S(2)}, u32[]{:S(2)}) collective-permute-start(bf16[144,128]{1,0:T(8,128)(2,1)S(1)} %get-tuple-element.73), channel_id=1, source_target_pairs={{0,6},{2,4},{4,2},{6,0},{1,7},{3,5},{5,3},{7,1},{8,14},{10,12},{12... | collective-permute-start | bytes 110600 | tf_op jit(solution)/shard_map/ppermute | solution.py:300
  58.5 4.4 %collective-permute-start.22 = (bf16[144,128]{1,0:T(8,128)(2,1)S(1)}, bf16[144,128]{1,0:T(8,128)(2,1)S(1)}, u32[]{:S(2)}, u32[]{:S(2)}) collective-permute-start(bf16[144,128]{1,0:T(8,128)(2,1)S(1)} %get-tuple-element.70), channel_id=1, source_target_pairs={{0,2},{2,0},{4,6},{6,4},{1,3},{3,1},{5,7},{7,5},{8,10},{10,8},{12,... | collective-permute-start | bytes 110600 | tf_op jit(solution)/shard_map/ppermute | solution.py:300
  58.6 4.9 %collective-permute-start.23 = (bf16[144,128]{1,0:T(8,128)(2,1)S(1)}, bf16[144,128]{1,0:T(8,128)(2,1)S(1)}, u32[]{:S(2)}, u32[]{:S(2)}) collective-permute-start(bf16[144,128]{1,0:T(8,128)(2,1)S(1)} %get-tuple-element.71), channel_id=1, source_target_pairs={{0,4},{2,6},{4,0},{6,2},{1,5},{3,7},{5,1},{7,3},{8,12},{10,14},{12... | collective-permute-start | bytes 110600 | tf_op jit(solution)/shard_map/ppermute | solution.py:300
  60.8 5.8 %copy-start.4 = (bf16[144,128]{1,0:T(8,128)(2,1)}, bf16[144,128]{1,0:T(8,128)(2,1)S(1)}, u32[]{:S(2)}) copy-start(bf16[144,128]{1,0:T(8,128)(2,1)S(1)} %collective-permute-done.15.refs_1_) | copy-start | bytes 110596
  60.8 5.8 %collective-permute-start.24 = (bf16[144,128]{1,0:T(8,128)(2,1)S(1)}, bf16[144,128]{1,0:T(8,128)(2,1)S(1)}, u32[]{:S(2)}, u32[]{:S(2)}) collective-permute-start(bf16[144,128]{1,0:T(8,128)(2,1)S(1)} %get-tuple-element.69), channel_id=1, source_target_pairs={{0,6},{2,4},{4,2},{6,0},{1,7},{3,5},{5,3},{7,1},{8,14},{10,12},{12... | collective-permute-start | bytes 110600 | tf_op jit(solution)/shard_map/ppermute | solution.py:300
  62.9 3.7 %copy-start.5 = (bf16[144,128]{1,0:T(8,128)(2,1)}, bf16[144,128]{1,0:T(8,128)(2,1)S(1)}, u32[]{:S(2)}) copy-start(bf16[144,128]{1,0:T(8,128)(2,1)S(1)} %collective-permute-done.16.refs_2_) | copy-start | bytes 110596
  62.9 3.7 %copy-start.6 = (bf16[144,128]{1,0:T(8,128)(2,1)}, bf16[144,128]{1,0:T(8,128)(2,1)S(1)}, u32[]{:S(2)}) copy-start(bf16[144,128]{1,0:T(8,128)(2,1)S(1)} %collective-permute-done.17.refs_3_) | copy-start | bytes 110596
  62.9 3.7 %copy-start.7 = (bf16[144,128]{1,0:T(8,128)(2,1)}, bf16[144,128]{1,0:T(8,128)(2,1)S(1)}, u32[]{:S(2)}) copy-start(bf16[144,128]{1,0:T(8,128)(2,1)S(1)} %collective-permute-done.22.refs_5_) | copy-start | bytes 110596
  63.5 3.2 %copy-start.8 = (bf16[144,128]{1,0:T(8,128)(2,1)}, bf16[144,128]{1,0:T(8,128)(2,1)S(1)}, u32[]{:S(2)}) copy-start(bf16[144,128]{1,0:T(8,128)(2,1)S(1)} %collective-permute-done.23.refs_6_) | copy-start | bytes 110596
  66.6 0.6 copy-start.9

commit v5 on v4

--- a/solution.py
+++ b/solution.py
@@ -17,7 +17,9 @@
 CHUNKS = 2
 GROWS = 16
 GTOP = 8
-PEERS = ((0, 1), (1, 0), (1, 1))
+STRIP = 32
+PEERS = ((1, 1), (1, 0), (0, 1))
+LINE = (3, 2, 1)
 
 NT = (((1,), (1,)), ((), ()))
 NN = (((1,), (0,)), ((), ()))
@@ -54,6 +56,8 @@
     dc,
     p16,
     ds16,
+    sbuf,
+    dbuf,
     bias,
     rowsel,
     sems,
@@ -125,36 +129,72 @@
             qc[rows, side] = q * rowsel[i]
             dc[rows, side] = dy * rowsel[i]
 
-    pair = 2
-    in_a2 = jnp.concatenate([in_a] * pair, axis=1)
-    tg2 = jnp.concatenate([tg] * pair, axis=1)
-    for h in range(0, group, pair):
-        rows = slice(h * tokens, (h + pair) * tokens)
-        s = mm(kcat, qc[rows, :], NT)
-        s = s + jnp.concatenate([bias[...]] * pair, axis=1)
-        top = jnp.max(s, axis=0, keepdims=True)
-        e = jnp.exp2((s - top) * (scale * LOG2E))
-        p = e * (1.0 / jnp.sum(e, axis=0, keepdims=True))
-        ph = p.astype(jnp.bfloat16)
-        p16[:, rows] = ph
-        dp = mm(vcat, dc[rows, :], NT)
-        delta = jnp.sum(ph.astype(jnp.float32) * dp, axis=0, keepdims=True)
-        dsh = ((scale * tg2) * p * (dp - delta)).astype(jnp.bfloat16)
-        ds16[:, rows] = dsh
-        o = mm(vcat_t, ph, NN)
+    span = 2 * tokens
+    blocks = group // 2
+    strips = [slice(i, i + STRIP) for i in range(0, slots, STRIP)]
+    in_a2 = jnp.concatenate([in_a, in_a], axis=1)
+    tg2 = jnp.concatenate([tg, tg], axis=1)
+    slope = scale * tg2
+
+    def fold8(x):
+        return jnp.sum(x.reshape(x.shape[0] // 8, 8, x.shape[1]), axis=0)
+
+    def products(h):
+        rows = slice(h * span, (h + 1) * span)
+        sbuf[h % 2] = mm(kcat, qc[rows, :], NT)
+        dbuf[h % 2] = mm(vcat, dc[rows, :], NT)
+
+    def softmax(h):
+        i = h % 2
+        rows = slice(h * span, (h + 1) * span)
+        top = jnp.full((8, span), NEG, jnp.float32)
+        for strip in strips:
+            x = sbuf[i, strip] + jnp.concatenate([bias[strip], bias[strip]], axis=1)
+            sbuf[i, strip] = x
+            top = jnp.maximum(top, jnp.max(x.reshape(STRIP // 8, 8, span), axis=0))
+        top = jnp.max(top, axis=0, keepdims=True) * (scale * LOG2E)
+        norm = jnp.zeros((8, span), jnp.float32)
+        dots = jnp.zeros((8, span), jnp.float32)
+        for strip in strips:
+            e = jnp.exp2(sbuf[i, strip] * (scale * LOG2E) - top)
+            sbuf[i, strip] = e
+            norm = norm + fold8(e)
+            dots = dots + fold8(e * dbuf[i, strip])
+        inv = 1.0 / jnp.sum(norm, axis=0, keepdims=True)
+        delta = slope * (inv * jnp.sum(dots, axis=0, keepdims=True))
+        for strip in strips:
+            p = sbuf[i, strip] * inv
+            p16[strip, rows] = p.astype(jnp.bfloat16)
+            ds16[strip, rows] = (p * (slope * dbuf[i, strip] - delta)).astype(jnp.bfloat16)
+
+    def outputs(h):
+        rows = slice(h * span, (h + 1) * span)
+        o = mm(vcat_t, p16[:, rows], NN)
         o = (tg2 * jnp.where(in_a2, o[:hd], o[hd:])).astype(jnp.bfloat16)
-        dq = mm(kcat_t, dsh, NN)
+        dq = mm(kcat_t, ds16[:, rows], NN)
         dq = jnp.where(in_a2, dq[:hd], dq[hd:]).astype(jnp.bfloat16)
-        for j in range(pair):
-            feats = slice((h + j) * hd, (h + j + 1) * hd)
+        for j in range(2):
+            feats = slice((2 * h + j) * hd, (2 * h + j + 1) * hd)
             toks = slice(j * tokens, (j + 1) * tokens)
             y_ref[:, feats] = o[:, toks].T
             dq_ref[:, feats] = dq[:, toks].T
-    dk = mm(ds16[...], qc[...], NN).astype(jnp.bfloat16)
-    dv = mm(p16[...], dc[...], NN)
-    gsum = dv * vcat.astype(jnp.float32)
-    gsum = jnp.sum(gsum.reshape(slots // 8, 8, 2 * hd), axis=0)
-    g_ref[...] += gsum[:, :hd] + gsum[:, hd:]
+
+    def slot_grads(lo, hi):
+        rows = slice(lo * span, hi * span)
+        return mm(ds16[:, rows], qc[rows, :], NN), mm(p16[:, rows], dc[rows, :], NN)
+
+    products(0)
+    dk = dv = 0.0
+    for h in range(blocks):
+        if h + 1 < blocks:
+            products(h + 1)
+        softmax(h)
+        outputs(h)
+        if h % 2:
+            more = slot_grads(h - 1, h + 1)
+            dk, dv = dk + more[0], dv + more[1]
+    dk = dk.astype(jnp.bfloat16)
+    g_ref[...] += fold8((dv * vcat.astype(jnp.float32))[:, :hd] + (dv * vcat.astype(jnp.float32))[:, hd:])
     dv = (jnp.concatenate([tg, tg], axis=1) * dv).astype(jnp.bfloat16)
     par_a, dx_a = place(img_a)
     par_b, dx_b = place(img_b)
@@ -176,6 +216,8 @@
             d = jnp.round(left * (1.0 / unit))
             left = left - d * unit
             digits = jnp.where(line == i, d, digits)
+        if not first:
+            g_ref[...] = jnp.broadcast_to(1.0 - tg * tg, g_ref.shape)
         for i in range(4):
             for j in range(2):
                 acc[i, j, 2 * heads * half :] = digits.astype(jnp.bfloat16)
@@ -235,6 +277,8 @@
             pltpu.VMEM((rows, 2 * hd), jnp.bfloat16),
             pltpu.VMEM((slots, rows), jnp.bfloat16),
             pltpu.VMEM((slots, rows), jnp.bfloat16),
+            pltpu.VMEM((2, slots, 2 * tokens), jnp.float32),
+            pltpu.VMEM((2, slots, 2 * tokens), jnp.float32),
             pltpu.VMEM((slots, tokens), jnp.float32),
             pltpu.VMEM((2, tokens, hd), jnp.bfloat16),
             pltpu.SemaphoreType.DMA((4,)),
@@ -250,26 +294,52 @@
     )(seg, counts, gate, seg.reshape(1, tokens), q, dy, own, other, *prev)
 
 
-def finish_kernel(heads, mine, gate_s, *refs):
+def add_up(refs, at):
+    total = refs[0][at].astype(jnp.float32)
+    for r in refs[1:]:
+        total = total + r[at].astype(jnp.float32)
+    return total
+
+
+def fold_kernel(cols, mine, both, *refs):
+    outs = refs[len(PEERS) :]
+    parts = (both.at[0, 0],) + refs[: len(PEERS)]
+    groups = (outs[0].shape[0] - GROWS) // mine
+    gates = add_up(parts, slice(groups * cols * mine, None)).astype(jnp.bfloat16)
+    for k in range(cols):
+        for b in range(groups):
+            at = (b * cols + k) * mine
+            outs[k][b * mine : (b + 1) * mine] = add_up(parts, slice(at, at + mine)).astype(jnp.bfloat16)
+        outs[k][groups * mine :] = gates
+
+
+def fold(cols, mine, both, recv):
+    rows = (both.shape[2] - GROWS) // cols + GROWS
+    vmem = pl.BlockSpec(memory_space=pltpu.VMEM)
+    return pl.pallas_call(
+        functools.partial(fold_kernel, cols, mine),
+        in_specs=[vmem] * (1 + len(recv)),
+        out_specs=[vmem] * cols,
+        out_shape=[jax.ShapeDtypeStruct((rows, both.shape[3]), jnp.bfloat16)] * cols,
+    )(both, *recv)
+
+
+def finish_kernel(heads, mine, gate, *refs):
     ins, (dk_ref, dv_ref, g_ref) = refs[:-3], refs[-3:]
     hd = ins[0].shape[1]
     each = len(ins) // CHUNKS
     for c in range(CHUNKS):
-        total = ins[c * each][...].astype(jnp.float32)
-        for r in ins[c * each + 1 : (c + 1) * each]:
-            total = total + r[...].astype(jnp.float32)
-        for h in range(heads):
-            lanes = slice((c * heads + h) * hd, (c * heads + h + 1) * hd)
-            dk_ref[:, lanes] = total[h * mine : (h + 1) * mine]
-            dv_ref[:, lanes] = total[(heads + h) * mine : (heads + h + 1) * mine]
-    digits = total[2 * heads * mine :]
+        parts = ins[c * each : (c + 1) * each]
+        for h in range(2 * heads):
+            out = (dk_ref, dv_ref)[h // heads]
+            lanes = slice((c * heads + h % heads) * hd, (c * heads + h % heads + 1) * hd)
+            out[:, lanes] = add_up(parts, slice(h * mine, (h + 1) * mine))
+    digits = add_up(parts, slice(2 * heads * mine, None))
     line = lax.broadcasted_iota(jnp.int32, digits.shape, 0)
     units = jnp.zeros(digits.shape, jnp.float32)
     for i in range(GROWS):
         units = jnp.where(line == i, 4.0 ** (GTOP - i), units)
-    tg = jnp.tanh(jnp.full((1, hd), gate_s[0], jnp.float32))
-    terms = jnp.sum(digits * units, axis=0, keepdims=True) * (1.0 - tg * tg)
-    g_ref[0] = jnp.sum(terms)
+    g_ref[0] = jnp.sum(jnp.sum(digits * units, axis=0, keepdims=True) * gate[0:1, :])
 
 
 def finish(mine, gate, cuts):
@@ -280,7 +350,7 @@
     full = jax.ShapeDtypeStruct((mine, KV_HEADS * hd), jnp.float32)
     return pl.pallas_call(
         functools.partial(finish_kernel, heads, mine),
-        in_specs=[smem] + [vmem] * len(cuts),
+        in_specs=[vmem] + [vmem] * len(cuts),
         out_specs=[vmem, vmem, smem],
         out_shape=[full, full, jax.ShapeDtypeStruct((1,), jnp.float32)],
     )(gate, *cuts)
@@ -305,16 +375,18 @@
     def send_core(x):
         return lax.ppermute(x, "core", [(0, 1), (1, 0)])
 
-    kv = jnp.stack([keys, values])
+    kv = lax.optimization_barrier(jnp.stack([keys, values]))
     if folded:
-        col = [kv] + [send_z(kv, k) for k in (1, 2, 3)]
+        col = {k: send_z(kv, k) for k in LINE}
+        col = [kv] + [col[k] for k in sorted(col)]
     else:
         col = [lax.all_gather(kv, "z", axis=1, tiled=True)]
 
     def gather(c):
         lanes = slice(c * wide, (c + 1) * wide)
         block = jnp.concatenate([jnp.concatenate([p[0, :, lanes], p[1, :, lanes]], axis=1) for p in col], axis=0)
-        own = jnp.concatenate([block] + [send_xy(block, *p) for p in PEERS], axis=0)
+        recv = {p: send_xy(block, *p) for p in PEERS}
+        own = jnp.concatenate([block] + [recv[p] for p in sorted(recv)], axis=0)
         own = own.reshape(2, 2 * half, 2 * wide)
         return own, send_core(own)
 
@@ -323,15 +395,15 @@
         return (part_own.astype(f32) + got.astype(f32)).astype(bf16)
 
     def reduce_xy(both):
-        total = both[0, 0].astype(f32)
-        for dx, dy in PEERS:
-            total = total + send_xy(both[dx, dy], dx, dy).astype(f32)
-        return total
+        recv = [send_xy(both[p], *p) for p in PEERS]
+        if folded:
+            return fold(cols, mine, both, recv)
+        return [sum(r.astype(f32) for r in [both[0, 0]] + recv)]
 
     pieces = [gather(c) for c in range(CHUNKS)]
     prev = None
     both = None
-    totals = []
+    sums = []
     for c in range(CHUNKS):
         own, other = pieces[c]
         if c:
@@ -341,23 +413,21 @@
         )
         prev = (g, y, dq)
         if c:
-            totals.append(reduce_xy(both))
-            part_other, totals[-1] = lax.optimization_barrier((part_other, totals[-1]))
+            sums.append(reduce_xy(both))
+            part_other, sums[-1] = lax.optimization_barrier((part_other, sums[-1]))
         both = reduce_core(part_own, part_other)
-    totals.append(reduce_xy(both))
+    sums.append(reduce_xy(both))
 
     cuts = []
-    for total in totals:
-        grads, gates = total[: 2 * heads * half], total[2 * heads * half :]
-        grads = grads.reshape(2 * heads, cols, mine, hd)
+    for cut in sums:
         if folded:
-            grads, gates = grads.astype(bf16), gates.astype(bf16)
-            cut = [jnp.concatenate([grads[:, k].reshape(-1, hd), gates], axis=0) for k in range(cols)]
-            cuts += [cut[0]] + [send_z(cut[k], k) for k in (1, 2, 3)]
+            cuts += [cut[0]] + [send_z(cut[k], k) for k in LINE]
         else:
+            grads, gates = cut[0][: 2 * heads * half], cut[0][2 * heads * half :]
+            grads = grads.reshape(2 * heads, cols, mine, hd)
             grads = lax.psum_scatter(grads, "z", scatter_dimension=1, tiled=True)
             cuts.append(jnp.concatenate([grads.reshape(-1, hd), lax.psum(gates, "z")], axis=0))
-    return (y, dq, *finish(mine, gate, cuts))
+    return (y, dq, *finish(mine, g, cuts))
 
 
 def solution(mesh):

time: 69.2 us -> 71.3 us (1.030)
  waiting for transfers between devices: 18.5 us -> 21.9 us
  starting transfers between devices: 29.4 us -> 26.9 us
  Pallas kernels: 14.4 us -> 16.1 us
  other arithmetic: 2.52 us -> 1.13 us
  local copies, waits for them, and re-layouts: 2.29 us -> 3.34 us
    pallas_call x1 -> x3, Pallas kernels: 1.58 us -> 5.31 us  [the longest x2 3.73 us: fold(): pl.pallas_call(functools.partial(fold_kernel, cols, mine), in_specs=[vmem...]
    ppermute x12, waiting for transfers between devices: 6.54 us -> 9.65 us  [send_xy(): return lax.ppermute(x, ('x', 'y'), [(i, i ^ 2 * dx + dy) for i in range(4)])]
    unnamed x24 -> x48, local copies, waits for them, and re-layouts: 0.67 us -> 3.24 us
    pallas_call x2, Pallas kernels: 12.8 us -> 10.8 us  [attend(): pl.pallas_call(functools.partial(attend_kernel, mine, cols, folded, first...]
    ppermute x9, starting transfers between devices: 14.4 us -> 12.5 us  [send_z(): return lax.ppermute(x, 'z', [(i, i ^ k) for i in range(cols)])]
    concatenate x2 -> x0, other arithmetic: 1.25 us -> none  [local(): jnp.concatenate([grads[:, k].reshape(-1, hd), gates], axis=0)]
    squeeze x3 -> x2, local copies, waits for them, and re-layouts: 0.79 us -> 0.06 us  [reduce_xy(): recv = [send_xy(both[p], *p) for p in PEERS]]
    squeeze x4, local copies, waits for them, and re-layouts: 0.76 us -> 0.02 us  [gather(): p[0, :, lanes]]
  transfers between devices with their start and end apart: 25 -> 25, of which waited for: 11 -> 14; matrix products, arithmetic and copies ran while one was open for 4% -> 0% of each run, Pallas kernels for 19% -> 18%
where the time goes in v5:
time: 71.3 us; the launch traced here: 71 us
  starting transfers between devices  26.9 us (38%)
  waiting for transfers between devices  21.9 us (31%)
  Pallas kernels  16.1 us (23%)
  local copies, waits for them, and re-layouts  3.34 us (5%)
  between operations  1.65 us (2%)
  other arithmetic  1.13 us (2%)
    ppermute x12, starting transfers between devices, send_xy(): return lax.ppermute(x, ('x', 'y'), [(i, i ^ 2 * dx + dy) for i in range(4)])  14.2 us
    ppermute x9, starting transfers between devices, send_z(): return lax.ppermute(x, 'z', [(i, i ^ k) for i in range(cols)])  12.5 us
    pallas_call x2, Pallas kernels, attend(): pl.pallas_call(functools.partial(attend_kernel, mine, cols, folded, first...  10.8 us
    ppermute x12, waiting for transfers between devices, send_xy(): return lax.ppermute(x, ('x', 'y'), [(i, i ^ 2 * dx + dy) for i in range(4)])  9.65 us
    ppermute x9, waiting for transfers between devices, send_z(): return lax.ppermute(x, 'z', [(i, i ^ k) for i in range(cols)])  8.63 us
    pallas_call x2, Pallas kernels, fold(): pl.pallas_call(functools.partial(fold_kernel, cols, mine), in_specs=[vmem...  3.73 us
    ppermute x4, waiting for transfers between devices, send_core(): return lax.ppermute(x, 'core', [(0, 1), (1, 0)])  3.66 us
    unnamed x48, local copies, waits for them, and re-layouts  3.24 us
  transfers between devices with their start and end apart: 25, of which 14 were waited for; matrix products, arithmetic and copies ran while one was open for 0% of the time, Pallas kernels for 18%

profile of v5, /device:TPU:0, one launch (start us, length us, event | category | flops | bytes accessed | tf_op | source)
XLA Modules:
  0.0 71.0 jit_solution(13443333595184083047)
XLA Ops:
  0.6 0.8 %pad_maximum_fusion = bf16[2,32,512]{2,1,0:T(8,128)(2,1)S(1)} fusion(bf16[1,32,512]{2,1,0:T(8,128)(2,1)} %bitcast.55, bf16[1,32,512]{2,1,0:T(8,128)(2,1)} %bitcast.56), kind=kLoop, calls=%fused_computation.10 | loop fusion | flops 32768 | bytes 131072 | tf_op jit(solution)/shard_map/stack | solution.py:378
  1.4 3.1 %collective-permute-start = (bf16[2,32,512]{2,1,0:T(8,128)(2,1)S(1)}, bf16[2,32,512]{2,1,0:T(8,128)(2,1)S(1)}, u32[]{:S(2)}, u32[]{:S(2)}) collective-permute-start(bf16[2,32,512]{2,1,0:T(8,128)(2,1)S(1)} %pad_maximum_fusion), channel_id=1, source_target_pairs={{0,2},{2,0},{4,6},{6,4},{1,3},{3,1},{5,7},{7,5},{8,10},{10,8},{12,... | collective-permute-start | bytes 196616 | tf_op jit(solution)/shard_map/ppermute | solution.py:370
  4.5 2.6 %collective-permute-start.1 = (bf16[2,32,512]{2,1,0:T(8,128)(2,1)S(1)}, bf16[2,32,512]{2,1,0:T(8,128)(2,1)S(1)}, u32[]{:S(2)}, u32[]{:S(2)}) collective-permute-start(bf16[2,32,512]{2,1,0:T(8,128)(2,1)S(1)} %pad_maximum_fusion), channel_id=1, source_target_pairs={{0,4},{2,6},{4,0},{6,2},{1,5},{3,7},{5,1},{7,3},{8,12},{10,14},{12... | collective-permute-start | bytes 196616 | tf_op jit(solution)/shard_map/ppermute | solution.py:370
  7.2 4.6 %collective-permute-done.1 = bf16[2,32,512]{2,1,0:T(8,128)(2,1)S(1)} collective-permute-done((bf16[2,32,512]{2,1,0:T(8,128)(2,1)S(1)}, bf16[2,32,512]{2,1,0:T(8,128)(2,1)S(1)}, u32[]{:S(2)}, u32[]{:S(2)}) %collective-permute-start.1) | collective-permute-done | bytes 65568 | tf_op jit(solution)/shard_map/ppermute | solution.py:370
  11.8 1.4 %collective-permute-done.2 = bf16[2,32,512]{2,1,0:T(8,128)(2,1)S(1)} collective-permute-done((bf16[2,32,512]{2,1,0:T(8,128)(2,1)S(1)}, bf16[2,32,512]{2,1,0:T(8,128)(2,1)S(1)}, u32[]{:S(2)}, u32[]{:S(2)}) %collective-permute-start.2) | collective-permute-done | bytes 65568 | tf_op jit(solution)/shard_map/ppermute | solution.py:370
  13.2 1.6 %collective-permute-start.7 = (bf16[128,512]{1,0:T(8,128)(2,1)S(1)}, bf16[128,512]{1,0:T(8,128)(2,1)S(1)}, u32[]{:S(2)}, u32[]{:S(2)}) collective-permute-start(bf16[128,512]{1,0:T(8,128)(2,1)S(1)} %maximum_maximum_fusion.1), channel_id=1, source_target_pairs={{0,1},{1,0},{16,17},{17,16},{2,3},{3,2},{18,19},{19,18},{4,5},{5,4... | collective-permute-start | bytes 393224 | tf_op jit(solution)/shard_map/ppermute | solution.py:373
  14.8 1.5 %collective-permute-start.8 = (bf16[128,512]{1,0:T(8,128)(2,1)S(1)}, bf16[128,512]{1,0:T(8,128)(2,1)S(1)}, u32[]{:S(2)}, u32[]{:S(2)}) collective-permute-start(bf16[128,512]{1,0:T(8,128)(2,1)S(1)} %maximum_maximum_fusion.1), channel_id=1, source_target_pairs={{0,16},{1,17},{16,0},{17,1},{2,18},{3,19},{18,2},{19,3},{4,20},{5,... | collective-permute-start | bytes 393224 | tf_op jit(solution)/shard_map/ppermute | solution.py:373
  16.3 0.5 collective-permute-start.9
  16.7 2.9 %collective-permute-done.7 = bf16[128,512]{1,0:T(8,128)(2,1)S(1)} collective-permute-done((bf16[128,512]{1,0:T(8,128)(2,1)S(1)}, bf16[128,512]{1,0:T(8,128)(2,1)S(1)}, u32[]{:S(2)}, u32[]{:S(2)}) %collective-permute-start.7) | collective-permute-done | bytes 131104 | tf_op jit(solution)/shard_map/ppermute | solution.py:373
  19.6 0.1 collective-permute-done.8
  19.7 2.4 %collective-permute-done.9 = bf16[128,512]{1,0:T(8,128)(2,1)S(1)} collective-permute-done((bf16[128,512]{1,0:T(8,128)(2,1)S(1)}, bf16[128,512]{1,0:T(8,128)(2,1)S(1)}, u32[]{:S(2)}, u32[]{:S(2)}) %collective-permute-start.9) | collective-permute-done | bytes 131104 | tf_op jit(solution)/shard_map/ppermute | solution.py:373
  22.1 0.1 collective-permute-start.10
  22.9 0.6 collective-permute-start.3
  23.5 1.5 %collective-permute-start.4 = (bf16[128,512]{1,0:T(8,128)(2,1)S(1)}, bf16[128,512]{1,0:T(8,128)(2,1)S(1)}, u32[]{:S(2)}, u32[]{:S(2)}) collective-permute-start(bf16[128,512]{1,0:T(8,128)(2,1)S(1)} %maximum_maximum_fusion), channel_id=1, source_target_pairs={{0,16},{1,17},{16,0},{17,1},{2,18},{3,19},{18,2},{19,3},{4,20},{5,... | collective-permute-start | bytes 393224 | tf_op jit(solution)/shard_map/ppermute | solution.py:373
  24.9 1.5 %collective-permute-start.5 = (bf16[128,512]{1,0:T(8,128)(2,1)S(1)}, bf16[128,512]{1,0:T(8,128)(2,1)S(1)}, u32[]{:S(2)}, u32[]{:S(2)}) collective-permute-start(bf16[128,512]{1,0:T(8,128)(2,1)S(1)} %maximum_maximum_fusion), channel_id=1, source_target_pairs={{0,17},{1,16},{16,1},{17,0},{2,19},{3,18},{18,3},{19,2},{4,21},{5,... | collective-permute-start | bytes 393224 | tf_op jit(solution)/shard_map/ppermute | solution.py:373
  26.5 5.4 %shard_map.110 = (bf16[128,4096]{1,0:T(8,128)(2,1)}, bf16[128,4096]{1,0:T(8,128)(2,1)}, bf16[2,2,528,128]{3,2,1,0:T(8,128)(2,1)S(1)}, bf16[2,2,528,128]{3,2,1,0:T(8,128)(2,1)S(1)}, f32[8,128]{1,0:T(8,128)S(1)}) custom-call(s32[128]{0:T(128)S(1)} %copy-done.3, s32[4]{0:T(128)S(1)} %copy-done.4, f32[1]{0:T(128)S(6)} %copy.28.gate_s, s32[1,128]{1,0:T(1,128)S(1)} %bitcast.53, ...), custom_call_target="tpu_custom_call" | custom-call | flops 8053063680 | bytes 4194304 | tf_op jit(solution)/shard_map/pallas_call | solution.py:248
  31.9 0.1 collective-permute-start.11
  32.1 0.8 %collective-permute-done.5 = bf16[128,512]{1,0:T(8,128)(2,1)S(1)} collective-permute-done((bf16[128,512]{1,0:T(8,128)(2,1)S(1)}, bf16[128,512]{1,0:T(8,128)(2,1)S(1)}, u32[]{:S(2)}, u32[]{:S(2)}) %collective-permute-start.5) | collective-permute-done | bytes 131104 | tf_op jit(solution)/shard_map/ppermute | solution.py:373
  32.9 1.0 %collective-permute-done.11 = bf16[2,2,528,128]{3,2,1,0:T(8,128)(2,1)S(1)} collective-permute-done((bf16[2,2,528,128]{3,2,1,0:T(8,128)(2,1)S(1)}, bf16[2,2,528,128]{3,2,1,0:T(8,128)(2,1)S(1)}, u32[]{:S(2)}, u32[]{:S(2)}) %collective-permute-start.11) | collective-permute-done | bytes 540704 | tf_op jit(solution)/shard_map/ppermute | solution.py:376
  33.9 0.2 add_convert_fusion.1.both
  34.1 0.7 %collective-permute-done.6.other = bf16[2,256,512]{2,1,0:T(8,128)(2,1)S(1)} collective-permute-done((bf16[2,256,512]{2,1,0:T(8,128)(2,1)S(1)}, bf16[2,256,512]{2,1,0:T(8,128)(2,1)S(1)}, u32[]{:S(2)}, u32[]{:S(2)}) %collective-permute-start.6) | collective-permute-done | bytes 524320 | tf_op jit(solution)/shard_map/ppermute | solution.py:376
  34.9 1.5 %collective-permute-start.12 = (bf16[528,128]{1,0:T(8,128)(2,1)S(1)}, bf16[528,128]{1,0:T(8,128)(2,1)S(1)}, u32[]{:S(2)}, u32[]{:S(2)}) collective-permute-start(bf16[528,128]{1,0:T(8,128)(2,1)S(1)} %get-tuple-element.68), channel_id=1, source_target_pairs={{0,17},{1,16},{16,1},{17,0},{2,19},{3,18},{18,3},{19,2},{4,21},{5,... | collective-permute-start | bytes 405512 | tf_op jit(solution)/shard_map/ppermute | solution.py:373
  36.3 0.6 collective-permute-start.13
  36.9 1.5 %collective-permute-start.14 = (bf16[528,128]{1,0:T(8,128)(2,1)S(1)}, bf16[528,128]{1,0:T(8,128)(2,1)S(1)}, u32[]{:S(2)}, u32[]{:S(2)}) collective-permute-start(bf16[528,128]{1,0:T(8,128)(2,1)S(1)} %get-tuple-element.66), channel_id=1, source_target_pairs={{0,1},{1,0},{16,17},{17,16},{2,3},{3,2},{18,19},{19,18},{4,5},{5,4... | collective-permute-start | bytes 405512 | tf_op jit(solution)/shard_map/ppermute | solution.py:373
  38.4 5.4 %shard_map.111 = (bf16[128,4096]{1,0:T(8,128)(2,1)}, bf16[128,4096]{1,0:T(8,128)(2,1)}, bf16[2,2,528,128]{3,2,1,0:T(8,128)(2,1)S(1)}, bf16[2,2,528,128]{3,2,1,0:T(8,128)(2,1)S(1)}, f32[8,128]{1,0:T(8,128)S(1)}) custom-call(s32[128]{0:T(128)S(1)} %copy-done.3, s32[4]{0:T(128)S(1)} %copy-done.4, ...), custom_call_target="tpu_custom_call", output_to_operand_aliasing={{0}: (9, {}), {1}: (10, {})} | custom-call | flops 8053063680 | bytes 4194304 | tf_op jit(solution)/shard_map/pallas_call | solution.py:248
  43.8 0.6 copy-done
  44.4 0.6 copy-done.7
  45.1 0.6 copy-done.11
  45.7 1.9 %shard_map.112 = (bf16[144,128]{1,0:T(8,128)(2,1)}, bf16[144,128]{1,0:T(8,128)(2,1)}, bf16[144,128]{1,0:T(8,128)(2,1)}, bf16[144,128]{1,0:T(8,128)(2,1)}) custom-call(bf16[2,2,528,128]{3,2,1,0:T(8,128)(2,1)} %copy-done.5, bf16[528,128]{1,0:T(8,128)(2,1)} %copy-done.7, bf16[528,128]{1,0:T(8,128)(2,1)} %copy-done.9, bf16[528,128]{1,0:T(8,128)(2,1)} %copy-done.11), custom_call_target="tpu_custom_call" | custom-call | tf_op jit(solution)/shard_map/pallas_call | solution.py:319
  47.6 1.9 %collective-permute-done.18 = bf16[2,2,528,128]{3,2,1,0:T(8,128)(2,1)S(1)} collective-permute-done((bf16[2,2,528,128]{3,2,1,0:T(8,128)(2,1)S(1)}, bf16[2,2,528,128]{3,2,1,0:T(8,128)(2,1)S(1)}, u32[]{:S(2)}, u32[]{:S(2)}) %collective-permute-start.18) | collective-permute-done | bytes 540704 | tf_op jit(solution)/shard_map/ppermute | solution.py:376
  49.5 0.1 add_convert_fusion.both
  49.7 1.5 %collective-permute-start.19 = (bf16[528,128]{1,0:T(8,128)(2,1)S(1)}, bf16[528,128]{1,0:T(8,128)(2,1)S(1)}, u32[]{:S(2)}, u32[]{:S(2)}) collective-permute-start(bf16[528,128]{1,0:T(8,128)(2,1)S(1)} %get-tuple-element.65), channel_id=1, source_target_pairs={{0,17},{1,16},{16,1},{17,0},{2,19},{3,18},{18,3},{19,2},{4,21},{5,... | collective-permute-start | bytes 405512 | tf_op jit(solution)/shard_map/ppermute | solution.py:373
  51.2 0.6 collective-permute-start.20
  51.8 1.5 %collective-permute-start.21 = (bf16[528,128]{1,0:T(8,128)(2,1)S(1)}, bf16[528,128]{1,0:T(8,128)(2,1)S(1)}, u32[]{:S(2)}, u32[]{:S(2)}) collective-permute-start(bf16[528,128]{1,0:T(8,128)(2,1)S(1)} %get-tuple-element.63), channel_id=1, source_target_pairs={{0,1},{1,0},{16,17},{17,16},{2,3},{3,2},{18,19},{19,18},{4,5},{5,4... | collective-permute-start | bytes 405512 | tf_op jit(solution)/shard_map/ppermute | solution.py:373
  53.3 1.8 %collective-permute-start.15 = (bf16[144,128]{1,0:T(8,128)(2,1)S(1)}, bf16[144,128]{1,0:T(8,128)(2,1)S(1)}, u32[]{:S(2)}, u32[]{:S(2)}) collective-permute-start(bf16[144,128]{1,0:T(8,128)(2,1)S(1)} %copy-done.21), channel_id=1, source_target_pairs={{0,6},{2,4},{4,2},{6,0},{1,7},{3,5},{5,3},{7,1},{8,14},{10,12},{12... | collective-permute-start | bytes 110600 | tf_op jit(solution)/shard_map/ppermute | solution.py:370
  55.1 2.0 %collective-permute-done.19.refs_0_ = bf16[528,128]{1,0:T(8,128)(2,1)S(1)} collective-permute-done((bf16[528,128]{1,0:T(8,128)(2,1)S(1)}, bf16[528,128]{1,0:T(8,128)(2,1)S(1)}, u32[]{:S(2)}, u32[]{:S(2)}) %collective-permute-start.19) | collective-permute-done | bytes 135200 | tf_op jit(solution)/shard_map/ppermute | solution.py:373
  57.1 0.6 collective-permute-start.17
  57.8 0.5 collective-permute-done.20.refs_1_
  58.3 1.0 %collective-permute-done.21.refs_2_ = bf16[528,128]{1,0:T(8,128)(2,1)S(1)} collective-permute-done((bf16[528,128]{1,0:T(8,128)(2,1)S(1)}, bf16[528,128]{1,0:T(8,128)(2,1)S(1)}, u32[]{:S(2)}, u32[]{:S(2)}) %collective-permute-start.21) | collective-permute-done | bytes 135200 | tf_op jit(solution)/shard_map/ppermute | solution.py:373
  59.2 0.6 copy-done.12
  59.9 1.9 %shard_map.113 = (bf16[144,128]{1,0:T(8,128)(2,1)}, bf16[144,128]{1,0:T(8,128)(2,1)}, bf16[144,128]{1,0:T(8,128)(2,1)}, bf16[144,128]{1,0:T(8,128)(2,1)}) custom-call(bf16[2,2,528,128]{3,2,1,0:T(8,128)(2,1)} %copy-done.6, bf16[528,128]{1,0:T(8,128)(2,1)} %copy-done.8, bf16[528,128]{1,0:T(8,128)(2,1)} %copy-done.10, bf16[528,128]{1,0:T(8,128)(2,1)} %copy-done.12), custom_call_target="tpu_custom_call" | custom-call | tf_op jit(solution)/shard_map/pallas_call | solution.py:319
  61.8 1.8 %collective-permute-start.22 = (bf16[144,128]{1,0:T(8,128)(2,1)}, bf16[144,128]{1,0:T(8,128)(2,1)S(1)}, u32[]{:S(2)}, u32[]{:S(2)}) collective-permute-start(bf16[144,128]{1,0:T(8,128)(2,1)} %get-tuple-element.57), channel_id=1, source_target_pairs={{0,6},{2,4},{4,2},{6,0},{1,7},{3,5},{5,3},{7,1},{8,14},{10,12},{12... | collective-permute-start | bytes 110600 | tf_op jit(solution)/shard_map/ppermute | solution.py:370
  63.6 0.3 collective-permute-start.23
  63.8 2.3 %collective-permute-start.24 = (bf16[144,128]{1,0:T(8,128)(2,1)}, bf16[144,128]{1,0:T(8,128)(2,1)S(1)}, u32[]{:S(2)}, u32[]{:S(2)}) collective-permute-start(bf16[144,128]{1,0:T(8,128)(2,1)} %get-tuple-element.59), channel_id=1, source_target_pairs={{0,2},{2,0},{4,6},{6,4},{1,3},{3,1},{5,7},{7,5},{8,10},{10,8},{12,... | collective-permute-start | bytes 110600 | tf_op jit(solution)/shard_map/ppermute | solution.py:370
  66.2 1.6 %collective-permute-done.22.refs_5_ = bf16[144,128]{1,0:T(8,128)(2,1)S(1)} collective-permute-done((bf16[144,128]{1,0:T(8,128)(2,1)}, bf16[144,128]{1,0:T(8,128)(2,1)S(1)}, u32[]{:S(2)}, u32[]{:S(2)}) %collective-permute-start.22) | collective-permute-done | bytes 36896 | tf_op jit(solution)/shard_map/ppermute | solution.py:370
  67.7 1.1 %collective-permute-done.23.refs_6_ = bf16[144,128]{1,0:T(8,128)(2,1)S(1)} collective-permute-done((bf16[144,128]{1,0:T(8,128)(2,1)}, bf16[144,128]{1,0:T(8,128)(2,1)S(1)}, u32[]{:S(2)}, u32[]{:S(2)}) %collective-permute-start.23) | collective-permute-done | bytes 36896 | tf_op jit(solution)/shard_map/ppermute | solution.py:370
  68.9 0.6 copy-done.17
  69.5 1.6 %shard_map.114 = (f32[32,512]{1,0:T(8,128)}, f32[32,512]{1,0:T(8,128)}, f32[1]{0:T(128)}) custom-call(f32[8,128]{1,0:T(8,128)} %copy-done, bf16[144,128]{1,0:T(8,128)(2,1)} %get-tuple-element.50.refs_0_, bf16[144,128]{1,0:T(8,128)(2,1)} %copy-done.13, bf16[144,128]{1,0:T(8,128)(2,1)} %copy-done.14, bf16[144,128]{1,0:T(8,128)(2,1)} %copy-done.15, ...), custom_call_target="tpu_custom_call" | custom-call | tf_op jit(solution)/shard_map/pallas_call | solution.py:351
  (76 shorter events, 0.4 us)
Async XLA Ops:
  1.4 5.7 %collective-permute-start = (bf16[2,32,512]{2,1,0:T(8,128)(2,1)S(1)}, bf16[2,32,512]{2,1,0:T(8,128)(2,1)S(1)}, u32[]{:S(2)}, u32[]{:S(2)}) collective-permute-start(bf16[2,32,512]{2,1,0:T(8,128)(2,1)S(1)} %pad_maximum_fusion), channel_id=1, source_target_pairs={{0,2},{2,0},{4,6},{6,4},{1,3},{3,1},{5,7},{7,5},{8,10},{10,8},{12,... | collective-permute-start | bytes 196616 | tf_op jit(solution)/shard_map/ppermute | solution.py:370
  4.5 7.3 %collective-permute-start.1 = (bf16[2,32,512]{2,1,0:T(8,128)(2,1)S(1)}, bf16[2,32,512]{2,1,0:T(8,128)(2,1)S(1)}, u32[]{:S(2)}, u32[]{:S(2)}) collective-permute-start(bf16[2,32,512]{2,1,0:T(8,128)(2,1)S(1)} %pad_maximum_fusion), channel_id=1, source_target_pairs={{0,4},{2,6},{4,0},{6,2},{1,5},{3,7},{5,1},{7,3},{8,12},{10,14},{12... | collective-permute-start | bytes 196616 | tf_op jit(solution)/shard_map/ppermute | solution.py:370
  7.1 6.1 %collective-permute-start.2 = (bf16[2,32,512]{2,1,0:T(8,128)(2,1)S(1)}, bf16[2,32,512]{2,1,0:T(8,128)(2,1)S(1)}, u32[]{:S(2)}, u32[]{:S(2)}) collective-permute-start(bf16[2,32,512]{2,1,0:T(8,128)(2,1)S(1)} %pad_maximum_fusion), channel_id=1, source_target_pairs={{0,6},{2,4},{4,2},{6,0},{1,7},{3,5},{5,3},{7,1},{8,14},{10,12},{12... | collective-permute-start | bytes 196616 | tf_op jit(solution)/shard_map/ppermute | solution.py:370
  7.1 19.4 %copy-start.1 = (bf16[128,4096]{1,0:T(8,128)(2,1)S(1)}, bf16[128,4096]{1,0:T(8,128)(2,1)}, u32[]{:S(2)}) copy-start(bf16[128,4096]{1,0:T(8,128)(2,1)} %q_ref.3) | copy-start | bytes 3145732
  7.1 19.4 %copy-start.2 = (bf16[128,4096]{1,0:T(8,128)(2,1)S(1)}, bf16[128,4096]{1,0:T(8,128)(2,1)}, u32[]{:S(2)}) copy-start(bf16[128,4096]{1,0:T(8,128)(2,1)} %dy_ref.3) | copy-start | bytes 3145732
  7.1 19.4 %copy-start.3 = (s32[128]{0:T(128)S(1)}, s32[128]{0:T(128)}, u32[]{:S(2)}) copy-start(s32[128]{0:T(128)} %seg_s.3) | copy-start | bytes 1540
  7.1 19.4 %copy-start.4 = (s32[4]{0:T(128)S(1)}, s32[4]{0:T(128)}, u32[]{:S(2)}) copy-start(s32[4]{0:T(128)} %cnt_s.3) | copy-start | bytes 52
  13.2 6.4 %collective-permute-start.7 = (bf16[128,512]{1,0:T(8,128)(2,1)S(1)}, bf16[128,512]{1,0:T(8,128)(2,1)S(1)}, u32[]{:S(2)}, u32[]{:S(2)}) collective-permute-start(bf16[128,512]{1,0:T(8,128)(2,1)S(1)} %maximum_maximum_fusion.1), channel_id=1, source_target_pairs={{0,1},{1,0},{16,17},{17,16},{2,3},{3,2},{18,19},{19,18},{4,5},{5,4... | collective-permute-start | bytes 393224 | tf_op jit(solution)/shard_map/ppermute | solution.py:373
  14.8 5.0 %collective-permute-start.8 = (bf16[128,512]{1,0:T(8,128)(2,1)S(1)}, bf16[128,512]{1,0:T(8,128)(2,1)S(1)}, u32[]{:S(2)}, u32[]{:S(2)}) collective-permute-start(bf16[128,512]{1,0:T(8,128)(2,1)S(1)} %maximum_maximum_fusion.1), channel_id=1, source_target_pairs={{0,16},{1,17},{16,0},{17,1},{2,18},{3,19},{18,2},{19,3},{4,20},{5,... | collective-permute-start | bytes 393224 | tf_op jit(solution)/shard_map/ppermute | solution.py:373
  16.3 5.9 %collective-permute-start.9 = (bf16[128,512]{1,0:T(8,128)(2,1)S(1)}, bf16[128,512]{1,0:T(8,128)(2,1)S(1)}, u32[]{:S(2)}, u32[]{:S(2)}) collective-permute-start(bf16[128,512]{1,0:T(8,128)(2,1)S(1)} %maximum_maximum_fusion.1), channel_id=1, source_target_pairs={{0,17},{1,16},{16,1},{17,0},{2,19},{3,18},{18,3},{19,2},{4,21},{5,... | collective-permute-start | bytes 393224 | tf_op jit(solution)/shard_map/ppermute | solution.py:373
  22.1 4.3 %collective-permute-start.10 = (bf16[2,256,512]{2,1,0:T(8,128)(2,1)S(1)}, bf16[2,256,512]{2,1,0:T(8,128)(2,1)S(1)}, u32[]{:S(2)}, u32[]{:S(2)}) collective-permute-start(bf16[2,256,512]{2,1,0:T(8,128)(2,1)S(1)} %bitcast.51), channel_id=1, source_target_pairs={{0,8},{8,0},{1,9},{9,1},{2,10},{10,2},{3,11},{11,3},{4,12},{12,4},... | collective-permute-start | bytes 1572872 | tf_op jit(solution)/shard_map/ppermute | solution.py:376
  22.9 9.1 %collective-permute-start.3 = (bf16[128,512]{1,0:T(8,128)(2,1)S(1)}, bf16[128,512]{1,0:T(8,128)(2,1)S(1)}, u32[]{:S(2)}, u32[]{:S(2)}) collective-permute-start(bf16[128,512]{1,0:T(8,128)(2,1)S(1)} %maximum_maximum_fusion), channel_id=1, source_target_pairs={{0,1},{1,0},{16,17},{17,16},{2,3},{3,2},{18,19},{19,18},{4,5},{5,4... | collective-permute-start | bytes 393224 | tf_op jit(solution)/shard_map/ppermute | solution.py:373
  23.5 8.6 %collective-permute-start.4 = (bf16[128,512]{1,0:T(8,128)(2,1)S(1)}, bf16[128,512]{1,0:T(8,128)(2,1)S(1)}, u32[]{:S(2)}, u32[]{:S(2)}) collective-permute-start(bf16[128,512]{1,0:T(8,128)(2,1)S(1)} %maximum_maximum_fusion), channel_id=1, source_target_pairs={{0,16},{1,17},{16,0},{17,1},{2,18},{3,19},{18,2},{19,3},{4,20},{5,... | collective-permute-start | bytes 393224 | tf_op jit(solution)/shard_map/ppermute | solution.py:373
  24.9 7.9 %collective-permute-start.5 = (bf16[128,512]{1,0:T(8,128)(2,1)S(1)}, bf16[128,512]{1,0:T(8,128)(2,1)S(1)}, u32[]{:S(2)}, u32[]{:S(2)}) collective-permute-start(bf16[128,512]{1,0:T(8,128)(2,1)S(1)} %maximum_maximum_fusion), channel_id=1, source_target_pairs={{0,17},{1,16},{16,1},{17,0},{2,19},{3,18},{18,3},{19,2},{4,21},{5,... | collective-permute-start | bytes 393224 | tf_op jit(solution)/shard_map/ppermute | solution.py:373
  31.9 2.0 %collective-permute-start.11 = (bf16[2,2,528,128]{3,2,1,0:T(8,128)(2,1)S(1)}, bf16[2,2,528,128]{3,2,1,0:T(8,128)(2,1)S(1)}, u32[]{:S(2)}, u32[]{:S(2)}) collective-permute-start(bf16[2,2,528,128]{3,2,1,0:T(8,128)(2,1)S(1)} %get-tuple-element.35), channel_id=1, source_target_pairs={{0,8},{8,0},{1,9},{9,1},{2,10},{10,2},{3,11},{11,3},{4,12},{12,4},... | collective-permute-start | bytes 1622024 | tf_op jit(solution)/shard_map/ppermute | solution.py:376
  32.9 2.0 %collective-permute-start.6 = (bf16[2,256,512]{2,1,0:T(8,128)(2,1)S(1)}, bf16[2,256,512]{2,1,0:T(8,128)(2,1)S(1)}, u32[]{:S(2)}, u32[]{:S(2)}) collective-permute-start(bf16[2,256,512]{2,1,0:T(8,128)(2,1)S(1)} %bitcast.49), channel_id=1, source_target_pairs={{0,8},{8,0},{1,9},{9,1},{2,10},{10,2},{3,11},{11,3},{4,12},{12,4},... | collective-permute-start | bytes 1572872 | tf_op jit(solution)/shard_map/ppermute | solution.py:376
  34.1 9.7 %copy-start.5 = (bf16[2,2,528,128]{3,2,1,0:T(8,128)(2,1)}, bf16[2,2,528,128]{3,2,1,0:T(8,128)(2,1)S(1)}, u32[]{:S(2)}) copy-start(bf16[2,2,528,128]{3,2,1,0:T(8,128)(2,1)S(1)} %add_convert_fusion.1.both) | copy-start | bytes 1622020
  34.9 9.5 %collective-permute-start.12 = (bf16[528,128]{1,0:T(8,128)(2,1)S(1)}, bf16[528,128]{1,0:T(8,128)(2,1)S(1)}, u32[]{:S(2)}, u32[]{:S(2)}) collective-permute-start(bf16[528,128]{1,0:T(8,128)(2,1)S(1)} %get-tuple-element.68), channel_id=1, source_target_pairs={{0,17},{1,16},{16,1},{17,0},{2,19},{3,18},{18,3},{19,2},{4,21},{5,... | collective-permute-start | bytes 405512 | tf_op jit(solution)/shard_map/ppermute | solution.py:373
  36.3 8.1 %collective-permute-start.13 = (bf16[528,128]{1,0:T(8,128)(2,1)S(1)}, bf16[528,128]{1,0:T(8,128)(2,1)S(1)}, u32[]{:S(2)}, u32[]{:S(2)}) collective-permute-start(bf16[528,128]{1,0:T(8,128)(2,1)S(1)} %get-tuple-element.67), channel_id=1, source_target_pairs={{0,16},{1,17},{16,0},{17,1},{2,18},{3,19},{18,2},{19,3},{4,20},{5,... | collective-permute-start | bytes 405512 | tf_op jit(solution)/shard_map/ppermute | solution.py:373
  36.9 7.5 %collective-permute-start.14 = (bf16[528,128]{1,0:T(8,128)(2,1)S(1)}, bf16[528,128]{1,0:T(8,128)(2,1)S(1)}, u32[]{:S(2)}, u32[]{:S(2)}) collective-permute-start(bf16[528,128]{1,0:T(8,128)(2,1)S(1)} %get-tuple-element.66), channel_id=1, source_target_pairs={{0,1},{1,0},{16,17},{17,16},{2,3},{3,2},{18,19},{19,18},{4,5},{5,4... | collective-permute-start | bytes 405512 | tf_op jit(solution)/shard_map/ppermute | solution.py:373
  43.8 0.6 copy-start
  44.4 0.6 copy-start.7
  44.4 0.7 copy-start.9
  45.1 0.6 copy-start.11
  47.6 1.9 %collective-permute-start.18 = (bf16[2,2,528,128]{3,2,1,0:T(8,128)(2,1)S(1)}, bf16[2,2,528,128]{3,2,1,0:T(8,128)(2,1)S(1)}, u32[]{:S(2)}, u32[]{:S(2)}) collective-permute-start(bf16[2,2,528,128]{3,2,1,0:T(8,128)(2,1)S(1)} %get-tuple-element.55), channel_id=1, source_target_pairs={{0,8},{8,0},{1,9},{9,1},{2,10},{10,2},{3,11},{11,3},{4,12},{12,4},... | collective-permute-start | bytes 1622024 | tf_op jit(solution)/shard_map/ppermute | solution.py:376
  49.5 3.8 %copy-start.21 = (bf16[144,128]{1,0:T(8,128)(2,1)S(1)}, bf16[144,128]{1,0:T(8,128)(2,1)}, u32[]{:S(2)}) copy-start(bf16[144,128]{1,0:T(8,128)(2,1)} %get-tuple-element.51) | copy-start | bytes 110596
  49.5 5.6 %copy-start.20 = (bf16[144,128]{1,0:T(8,128)(2,1)S(1)}, bf16[144,128]{1,0:T(8,128)(2,1)}, u32[]{:S(2)}) copy-start(bf16[144,128]{1,0:T(8,128)(2,1)} %get-tuple-element.52) | copy-start | bytes 110596
  49.5 7.6 %copy-start.19 = (bf16[144,128]{1,0:T(8,128)(2,1)S(1)}, bf16[144,128]{1,0:T(8,128)(2,1)}, u32[]{:S(2)}) copy-start(bf16[144,128]{1,0:T(8,128)(2,1)} %get-tuple-element.53) | copy-start | bytes 110596
  49.7 9.5 %copy-start.6 = (bf16[2,2,528,128]{3,2,1,0:T(8,128)(2,1)}, bf16[2,2,528,128]{3,2,1,0:T(8,128)(2,1)S(1)}, u32[]{:S(2)}) copy-start(bf16[2,2,528,128]{3,2,1,0:T(8,128)(2,1)S(1)} %add_convert_fusion.both) | copy-start | bytes 1622020
  49.7 7.4 %collective-permute-start.19 = (bf16[528,128]{1,0:T(8,128)(2,1)S(1)}, bf16[528,128]{1,0:T(8,128)(2,1)S(1)}, u32[]{:S(2)}, u32[]{:S(2)}) collective-permute-start(bf16[528,128]{1,0:T(8,128)(2,1)S(1)} %get-tuple-element.65), channel_id=1, source_target_pairs={{0,17},{1,16},{16,1},{17,0},{2,19},{3,18},{18,3},{19,2},{4,21},{5,... | collective-permute-start | bytes 405512 | tf_op jit(solution)/shard_map/ppermute | solution.py:373
  51.2 7.1 %collective-permute-start.20 = (bf16[528,128]{1,0:T(8,128)(2,1)S(1)}, bf16[528,128]{1,0:T(8,128)(2,1)S(1)}, u32[]{:S(2)}, u32[]{:S(2)}) collective-permute-start(bf16[528,128]{1,0:T(8,128)(2,1)S(1)} %get-tuple-element.64), channel_id=1, source_target_pairs={{0,16},{1,17},{16,0},{17,1},{2,18},{3,19},{18,2},{19,3},{4,20},{5,... | collective-permute-start | bytes 405512 | tf_op jit(solution)/shard_map/ppermute | solution.py:373
  51.8 7.5 %collective-permute-start.21 = (bf16[528,128]{1,0:T(8,128)(2,1)S(1)}, bf16[528,128]{1,0:T(8,128)(2,1)S(1)}, u32[]{:S(2)}, u32[]{:S(2)}) collective-permute-start(bf16[528,128]{1,0:T(8,128)(2,1)S(1)} %get-tuple-element.63), channel_id=1, source_target_pairs={{0,1},{1,0},{16,17},{17,16},{2,3},{3,2},{18,19},{19,18},{4,5},{5,4... | collective-permute-start | bytes 405512 | tf_op jit(solution)/shard_map/ppermute | solution.py:373
  53.3 10.5 %collective-permute-start.15 = (bf16[144,128]{1,0:T(8,128)(2,1)S(1)}, bf16[144,128]{1,0:T(8,128)(2,1)S(1)}, u32[]{:S(2)}, u32[]{:S(2)}) collective-permute-start(bf16[144,128]{1,0:T(8,128)(2,1)S(1)} %copy-done.21), channel_id=1, source_target_pairs={{0,6},{2,4},{4,2},{6,0},{1,7},{3,5},{5,3},{7,1},{8,14},{10,12},{12... | collective-permute-start | bytes 110600 | tf_op jit(solution)/shard_map/ppermute | solution.py:370
  55.1 11.0 %collective-permute-start.16 = (bf16[144,128]{1,0:T(8,128)(2,1)S(1)}, bf16[144,128]{1,0:T(8,128)(2,1)S(1)}, u32[]{:S(2)}, u32[]{:S(2)}) collective-permute-start(bf16[144,128]{1,0:T(8,128)(2,1)S(1)} %copy-done.20), channel_id=1, source_target_pairs={{0,4},{2,6},{4,0},{6,2},{1,5},{3,7},{5,1},{7,3},{8,12},{10,14},{12... | collective-permute-start | bytes 110600 | tf_op jit(solution)/shard_map/ppermute | solution.py:370
  57.1 2.1 %copy-start.8 = (bf16[528,128]{1,0:T(8,128)(2,1)}, bf16[528,128]{1,0:T(8,128)(2,1)S(1)}, u32[]{:S(2)}) copy-start(bf16[528,128]{1,0:T(8,128)(2,1)S(1)} %collective-permute-done.19.refs_0_) | copy-start | bytes 405508
  57.1 9.0 %collective-permute-start.17 = (bf16[144,128]{1,0:T(8,128)(2,1)S(1)}, bf16[144,128]{1,0:T(8,128)(2,1)S(1)}, u32[]{:S(2)}, u32[]{:S(2)}) collective-permute-start(bf16[144,128]{1,0:T(8,128)(2,1)S(1)} %copy-done.19), channel_id=1, source_target_pairs={{0,2},{2,0},{4,6},{6,4},{1,3},{3,1},{5,7},{7,5},{8,10},{10,8},{12,... | collective-permute-start | bytes 110600 | tf_op jit(solution)/shard_map/ppermute | solution.py:370
  58.3 1.0 %copy-start.10 = (bf16[528,128]{1,0:T(8,128)(2,1)}, bf16[528,128]{1,0:T(8,128)(2,1)S(1)}, u32[]{:S(2)}) copy-start(bf16[528,128]{1,0:T(8,128)(2,1)S(1)} %collective-permute-done.20.refs_1_) | copy-start | bytes 405508
  59.2 0.6 copy-start.12
  61.8 6.0 %collective-permute-start.22 = (bf16[144,128]{1,0:T(8,128)(2,1)}, bf16[144,128]{1,0:T(8,128)(2,1)S(1)}, u32[]{:S(2)}, u32[]{:S(2)}) collective-permute-start(bf16[144,128]{1,0:T(8,128)(2,1)} %get-tuple-element.57), channel_id=1, source_target_pairs={{0,6},{2,4},{4,2},{6,0},{1,7},{3,5},{5,3},{7,1},{8,14},{10,12},{12... | collective-permute-start | bytes 110600 | tf_op jit(solution)/shard_map/ppermute | solution.py:370
  63.6 5.3 %collective-permute-start.23 = (bf16[144,128]{1,0:T(8,128)(2,1)}, bf16[144,128]{1,0:T(8,128)(2,1)S(1)}, u32[]{:S(2)}, u32[]{:S(2)}) collective-permute-start(bf16[144,128]{1,0:T(8,128)(2,1)} %get-tuple-element.58), channel_id=1, source_target_pairs={{0,4},{2,6},{4,0},{6,2},{1,5},{3,7},{5,1},{7,3},{8,12},{10,14},{12... | collective-permute-start | bytes 110600 | tf_op jit(solution)/shard_map/ppermute | solution.py:370
  63.8 5.0 %copy-start.13 = (bf16[144,128]{1,0:T(8,128)(2,1)}, bf16[144,128]{1,0:T(8,128)(2,1)S(1)}, u32[]{:S(2)}) copy-start(bf16[144,128]{1,0:T(8,128)(2,1)S(1)} %collective-permute-done.15.refs_1_) | copy-start | bytes 110596
  63.8 5.0 %collective-permute-start.24 = (bf16[144,128]{1,0:T(8,128)(2,1)}, bf16[144,128]{1,0:T(8,128)(2,1)S(1)}, u32[]{:S(2)}, u32[]{:S(2)}) collective-permute-start(bf16[144,128]{1,0:T(8,128)(2,1)} %get-tuple-element.59), channel_id=1, source_target_pairs={{0,2},{2,0},{4,6},{6,4},{1,3},{3,1},{5,7},{7,5},{8,10},{10,8},{12,... | collective-permute-start | bytes 110600 | tf_op jit(solution)/shard_map/ppermute | solution.py:370
  66.2 2.7 %copy-start.14 = (bf16[144,128]{1,0:T(8,128)(2,1)}, bf16[144,128]{1,0:T(8,128)(2,1)S(1)}, u32[]{:S(2)}) copy-start(bf16[144,128]{1,0:T(8,128)(2,1)S(1)} %collective-permute-done.16.refs_2_) | copy-start | bytes 110596
  66.2 2.7 %copy-start.15 = (bf16[144,128]{1,0:T(8,128)(2,1)}, bf16[144,128]{1,0:T(8,128)(2,1)S(1)}, u32[]{:S(2)}) copy-start(bf16[144,128]{1,0:T(8,128)(2,1)S(1)} %collective-permute-done.17.refs_3_) | copy-start | bytes 110596
  67.7 1.1 %copy-start.16 = (bf16[144,128]{1,0:T(8,128)(2,1)}, bf16[144,128]{1,0:T(8,128)(2,1)S(1)}, u32[]{:S(2)}) copy-start(bf16[144,128]{1,0:T(8,128)(2,1)S(1)} %collective-permute-done.22.refs_5_) | copy-start | bytes 110596
  68.8 0.6 copy-start.17
  68.8 0.6 copy-start.18

commit v6 on v5

v6 whole, which is shorter than its diff:
```python
import functools

import jax
import jax.numpy as jnp
from jax import lax
from jax.experimental import pallas as pl
from jax.experimental.pallas import tpu as pltpu
from jax.sharding import Mesh
from jax.sharding import PartitionSpec as P

KV_HEADS = 4
TILE_TOK = 64
IMG_TOK = 256
AXES = ("x", "core", "z", "y")
NEG = -1e30
LOG2E = 1.4426950408889634
GROWS = 16
GTOP = 8
STRIP = 32

NT = (((1,), (1,)), ((), ()))
NN = (((1,), (0,)), ((), ()))


def mm(a, b, dims):
    return lax.dot_general(a, b, dims, preferred_element_type=jnp.float32)


def attend_kernel(
    mine,
    cols,
    folded,
    seg_s,
    cnt_s,
    gate_s,
    seg_v,
    q_ref,
    dy_ref,
    own,
    other,
    y_ref,
    dq_ref,
    part_own,
    part_other,
    g_ref,
    kv,
    acc,
    qc,
    dc,
    p16,
    ds16,
    sbuf,
    dbuf,
    bias,
    rowsel,
    sems,
):
    step = pl.program_id(0)
    heads = pl.num_programs(0)
    tokens = q_ref.shape[0]
    slots, width = kv.shape[1], kv.shape[2] // 2
    half = slots // 2
    hd = width // heads
    group = q_ref.shape[1] // hd
    scale = 1.0 / hd**0.5
    core, xpos = lax.axis_index("core"), lax.axis_index("x")
    ypos, zpos = lax.axis_index("y"), lax.axis_index("z")
    img_a, img_b = seg_s[0], seg_s[tokens - 1]

    def place(img, h):
        par, dx = img % 2, (img // 2) ^ xpos
        return par, jnp.where(par == 0, h, dx), jnp.where(par == 0, dx, h)

    def fetch(i, img, start):
        for h in range(2):
            par, j0, j1 = place(img, h)
            for src, mask in ((own, par == core), (other, par != core)):

                @pl.when(mask)
                def _():
                    c = pltpu.make_async_copy(src.at[j0, j1], kv.at[i, pl.ds(h * half, half)], sems.at[i])
                    c.start() if start else c.wait()

    def tile_of(n, img):
        side, rest = n // half, n % half
        outer, inner = rest // mine, rest % mine
        if folded:
            z0 = (2 * (outer % 2) + outer // 2) ^ zpos
            y0 = side ^ ypos
            z1 = ((outer // 2) * 2 + side) ^ zpos
            y1 = (outer % 2) ^ ypos
        else:
            z0 = z1 = outer
            y0 = y1 = side ^ ypos
        even = img % 2 == 0
        z, y = jnp.where(even, z0, z1), jnp.where(even, y0, y1)
        return (z * (2 * mine) + y * mine + inner) // TILE_TOK

    in_a = seg_v[...] == img_a
    tg = jnp.tanh(jnp.full((1, hd), gate_s[0], jnp.float32))

    @pl.when(step == 0)
    def _():
        fetch(0, img_a, True)
        fetch(1, img_b, True)
        acc[...] = jnp.zeros_like(acc)
        g_ref[...] = jnp.zeros_like(g_ref)
        n = lax.broadcasted_iota(jnp.int32, (slots, tokens), 0)
        seen_a = tile_of(n, img_a) < cnt_s[img_a]
        seen_b = tile_of(n, img_b) < cnt_s[img_b]
        seen = jnp.where(in_a, seen_a.astype(jnp.float32), seen_b.astype(jnp.float32))
        bias[...] = jnp.where(seen > 0.5, 0.0, NEG)
        side_a = jnp.broadcast_to(in_a.astype(jnp.float32), (hd, tokens)).T
        rowsel[0] = side_a.astype(jnp.bfloat16)
        rowsel[1] = (1.0 - side_a).astype(jnp.bfloat16)
        fetch(0, img_a, False)
        fetch(1, img_b, False)

    kcols = pl.ds(pl.multiple_of(step * hd, hd), hd)
    vcols = pl.ds(pl.multiple_of(width + step * hd, hd), hd)
    kcat = jnp.concatenate([kv[0, :, kcols], kv[1, :, kcols]], axis=1)
    vcat = jnp.concatenate([kv[0, :, vcols], kv[1, :, vcols]], axis=1)
    kcat_t = kcat.T
    vcat_t = vcat.T
    for g in range(group):
        feats = slice(g * hd, (g + 1) * hd)
        rows = slice(g * tokens, (g + 1) * tokens)
        q = q_ref[:, feats]
        dy = dy_ref[:, feats]
        for i in range(2):
            side = slice(i * hd, (i + 1) * hd)
            qc[rows, side] = q * rowsel[i]
            dc[rows, side] = dy * rowsel[i]

    span = 2 * tokens
    blocks = group // 2
    strips = [slice(i, i + STRIP) for i in range(0, slots, STRIP)]
    in_a2 = jnp.concatenate([in_a, in_a], axis=1)
    tg2 = jnp.concatenate([tg, tg], axis=1)
    slope = scale * tg2

    def fold8(x):
        return jnp.sum(x.reshape(x.shape[0] // 8, 8, x.shape[1]), axis=0)

    def products(h):
        rows = slice(h * span, (h + 1) * span)
        sbuf[h % 2] = mm(kcat, qc[rows, :], NT)
        dbuf[h % 2] = mm(vcat, dc[rows, :], NT)

    def softmax(h):
        i = h % 2
        rows = slice(h * span, (h + 1) * span)
        top = jnp.full((8, span), NEG, jnp.float32)
        for strip in strips:
            x = sbuf[i, strip] + jnp.concatenate([bias[strip], bias[strip]], axis=1)
            sbuf[i, strip] = x
            top = jnp.maximum(top, jnp.max(x.reshape(STRIP // 8, 8, span), axis=0))
        top = jnp.max(top, axis=0, keepdims=True) * (scale * LOG2E)
        norm = jnp.zeros((8, span), jnp.float32)
        dots = jnp.zeros((8, span), jnp.float32)
        for strip in strips:
            e = jnp.exp2(sbuf[i, strip] * (scale * LOG2E) - top)
            sbuf[i, strip] = e
            norm = norm + fold8(e)
            dots = dots + fold8(e * dbuf[i, strip])
        inv = 1.0 / jnp.sum(norm, axis=0, keepdims=True)
        delta = slope * (inv * jnp.sum(dots, axis=0, keepdims=True))
        for strip in strips:
            p = sbuf[i, strip] * inv
            p16[strip, rows] = p.astype(jnp.bfloat16)
            ds16[strip, rows] = (p * (slope * dbuf[i, strip] - delta)).astype(jnp.bfloat16)

    def outputs(h):
        rows = slice(h * span, (h + 1) * span)
        o = mm(vcat_t, p16[:, rows], NN)
        o = (tg2 * jnp.where(in_a2, o[:hd], o[hd:])).astype(jnp.bfloat16)
        dq = mm(kcat_t, ds16[:, rows], NN)
        dq = jnp.where(in_a2, dq[:hd], dq[hd:]).astype(jnp.bfloat16)
        for j in range(2):
            feats = slice((2 * h + j) * hd, (2 * h + j + 1) * hd)
            toks = slice(j * tokens, (j + 1) * tokens)
            y_ref[:, feats] = o[:, toks].T
            dq_ref[:, feats] = dq[:, toks].T

    def slot_grads(lo, hi):
        rows = slice(lo * span, hi * span)
        return mm(ds16[:, rows], qc[rows, :], NN), mm(p16[:, rows], dc[rows, :], NN)

    products(0)
    dk = dv = 0.0
    for h in range(blocks):
        if h + 1 < blocks:
            products(h + 1)
        softmax(h)
        outputs(h)
        if h % 2:
            more = slot_grads(h - 1, h + 1)
            dk, dv = dk + more[0], dv + more[1]
    dk = dk.astype(jnp.bfloat16)
    g_ref[...] += fold8((dv * vcat.astype(jnp.float32))[:, :hd] + (dv * vcat.astype(jnp.float32))[:, hd:])
    dv = (jnp.concatenate([tg, tg], axis=1) * dv).astype(jnp.bfloat16)
    pieces = 2 * acc.shape[3]
    per = slots // pieces
    krows = pl.ds(pl.multiple_of(step * per, per), per)
    vrows = pl.ds(pl.multiple_of((heads + step) * per, per), per)
    for img, lanes in ((img_b, slice(hd, 2 * hd)), (img_a, slice(0, hd))):
        for h in range(2):
            par, j0, j1 = place(img, h)
            for j in range(pieces // 2):
                at = slice(h * half + j * per, h * half + (j + 1) * per)
                acc[par, j0, j1, j, krows] = dk[at, lanes]
                acc[par, j0, j1, j, vrows] = dv[at, lanes]

    @pl.when(step == heads - 1)
    def _():
        left = jnp.broadcast_to(jnp.sum(g_ref[...], axis=0, keepdims=True), (GROWS, hd))
        line = lax.broadcasted_iota(jnp.int32, (GROWS, hd), 0)
        digits = jnp.zeros((GROWS, hd), jnp.float32)
        for i in range(GROWS):
            unit = 4.0 ** (GTOP - i)
            d = jnp.round(left * (1.0 / unit))
            left = left - d * unit
            digits = jnp.where(line == i, d, digits)
        digits = digits.astype(jnp.bfloat16)
        g_ref[...] = jnp.broadcast_to(1.0 - tg * tg, g_ref.shape)
        for i in range(8):
            for j in range(pieces // 2):
                acc[i // 4, i // 2 % 2, i % 2, j, 2 * heads * per :] = digits
        c1 = pltpu.make_async_copy(acc.at[1 - core], part_other, sems.at[2])
        c0 = pltpu.make_async_copy(acc.at[core], part_own, sems.at[3])
        c1.start()
        c0.start()
        c1.wait()
        c0.wait()


def attend(mine, cols, folded, seg, counts, gate, q, dy, own, other):
    tokens, feats = q.shape
    slots, width2 = 2 * own.shape[2], own.shape[3]
    hd = width2 // 2 // KV_HEADS
    block = feats // KV_HEADS
    rows = block // hd * tokens
    smem = pl.BlockSpec(memory_space=pltpu.SMEM)
    hbm = pl.BlockSpec(memory_space=pl.ANY)
    cut = pl.BlockSpec((tokens, block), lambda i: (0, i))
    gspec = pl.BlockSpec((8, hd), lambda i: (0, 0))
    flops = 12 * KV_HEADS * rows * slots * hd * 2
    pieces = 8 if folded else 2
    part = (2, 2, pieces // 2, 2 * KV_HEADS * (slots // pieces) + GROWS, hd)
    return pl.pallas_call(
        functools.partial(attend_kernel, mine, cols, folded),
        grid=(KV_HEADS,),
        in_specs=[
            smem,
            smem,
            smem,
            pl.BlockSpec((1, tokens), lambda i: (0, 0)),
            cut,
            cut,
            hbm,
            hbm,
        ],
        out_specs=[cut, cut, hbm, hbm, gspec],
        out_shape=[
            jax.ShapeDtypeStruct(q.shape, jnp.bfloat16),
            jax.ShapeDtypeStruct(q.shape, jnp.bfloat16),
            jax.ShapeDtypeStruct(part, jnp.bfloat16),
            jax.ShapeDtypeStruct(part, jnp.bfloat16),
            jax.ShapeDtypeStruct((8, hd), jnp.float32),
        ],
        scratch_shapes=[
            pltpu.VMEM((2, slots, width2), jnp.bfloat16),
            pltpu.VMEM((2,) + part, jnp.bfloat16),
            pltpu.VMEM((rows, 2 * hd), jnp.bfloat16),
            pltpu.VMEM((rows, 2 * hd), jnp.bfloat16),
            pltpu.VMEM((slots, rows), jnp.bfloat16),
            pltpu.VMEM((slots, rows), jnp.bfloat16),
            pltpu.VMEM((2, slots, 2 * tokens), jnp.float32),
            pltpu.VMEM((2, slots, 2 * tokens), jnp.float32),
            pltpu.VMEM((slots, tokens), jnp.float32),
            pltpu.VMEM((2, tokens, hd), jnp.bfloat16),
            pltpu.SemaphoreType.DMA((4,)),
        ],
        compiler_params=pltpu.CompilerParams(
            dimension_semantics=("arbitrary",), vmem_limit_bytes=32 * 1024 * 1024
        ),
        cost_estimate=pl.CostEstimate(
            flops=flops,
            bytes_accessed=8 * q.size + 8 * own.size,
            transcendentals=KV_HEADS * rows * slots,
        ),
    )(seg, counts, gate, seg.reshape(1, tokens), q, dy, own, other)


def add_up(refs, at):
    total = refs[0][at].astype(jnp.float32)
    for r in refs[1:]:
        total = total + r[at].astype(jnp.float32)
    return total


def finish_kernel(mine, gate, *refs):
    ins, (dk_ref, dv_ref, g_ref) = refs[:-3], refs[-3:]
    hd = ins[0].shape[1]
    for h in range(2 * KV_HEADS):
        out = (dk_ref, dv_ref)[h // KV_HEADS]
        lanes = slice(h % KV_HEADS * hd, (h % KV_HEADS + 1) * hd)
        out[:, lanes] = add_up(ins, slice(h * mine, (h + 1) * mine))
    digits = add_up(ins, slice(2 * KV_HEADS * mine, None))
    line = lax.broadcasted_iota(jnp.int32, digits.shape, 0)
    units = jnp.zeros(digits.shape, jnp.float32)
    for i in range(GROWS):
        units = jnp.where(line == i, 4.0 ** (GTOP - i), units)
    g_ref[0] = jnp.sum(jnp.sum(digits * units, axis=0, keepdims=True) * gate[0:1, :])


def finish(mine, gate, parts):
    hd = parts[0].shape[1]
    smem = pl.BlockSpec(memory_space=pltpu.SMEM)
    vmem = pl.BlockSpec(memory_space=pltpu.VMEM)
    full = jax.ShapeDtypeStruct((mine, KV_HEADS * hd), jnp.float32)
    return pl.pallas_call(
        functools.partial(finish_kernel, mine),
        in_specs=[vmem] + [vmem] * len(parts),
        out_specs=[vmem, vmem, smem],
        out_shape=[full, full, jax.ShapeDtypeStruct((1,), jnp.float32)],
        compiler_params=pltpu.CompilerParams(vmem_limit_bytes=4 * 1024 * 1024),
    )(gate, *parts)


def local(queries, keys, values, seg_image, tile_counts, gate, cotangent):
    f32, bf16 = jnp.float32, jnp.bfloat16
    mine, width = keys.shape
    hd = width // KV_HEADS
    cols = lax.axis_size("z")
    folded = cols == 4
    half = cols * mine

    def swap(x, even, odd):
        perm = []
        for i in range(8 * cols):
            place = [i // (4 * cols), i // (2 * cols) % 2, i // 2 % cols, i % 2]
            dim, bit = odd if place[1] else even
            place[dim] ^= bit
            perm.append((i, ((place[0] * 2 + place[1]) * cols + place[2]) * 2 + place[3]))
        return lax.ppermute(x, AXES, perm)

    x1, y1, z1, z2 = (0, 1), (3, 1), (2, 1), (2, 2)
    near = ((z2, y1), (z1, z2))
    far = ((x1, z1), (y1, x1)) if folded else ((x1, y1), (y1, x1))
    steps = near + far if folded else far

    buf = jnp.concatenate([keys, values], axis=1)
    if not folded:
        buf = lax.all_gather(buf, "z", axis=0, tiled=True)
    for even, odd in steps:
        buf = jnp.concatenate([buf, swap(buf, even, odd)], axis=0)
    own = buf.reshape(2, 2, half, 2 * width)
    core = ((1, 1), (1, 1))
    other = swap(own, *core)

    y, dq, part_own, part_other, g = attend(
        mine, cols, folded, seg_image, tile_counts, gate, queries, cotangent, own, other
    )

    part = (part_own.astype(f32) + swap(part_other, *core).astype(f32)).astype(bf16)
    part = part.reshape((-1,) + part.shape[3:])
    for even, odd in steps[::-1]:
        keep, away = jnp.split(part, 2)
        parts = [keep, swap(away, even, odd)]
        part = (parts[0].astype(f32) + parts[1].astype(f32)).astype(bf16)
    if folded:
        parts = [p[0] for p in parts]
    else:
        part = parts[0][0].astype(f32) + parts[1][0].astype(f32)
        grads, gates = part[:-GROWS].reshape(2 * KV_HEADS, cols, mine, hd), part[-GROWS:]
        grads = lax.psum_scatter(grads, "z", scatter_dimension=1, tiled=True)
        parts = [jnp.concatenate([grads.reshape(-1, hd), lax.psum(gates, "z")], axis=0)]
    return (y, dq, *finish(mine, g, parts))


def solution(mesh):
    section, mp = mesh.shape["section"], mesh.shape["mp"]
    fine = Mesh(mesh.devices.reshape(section // 2, 2, mp // 2, 2), AXES)
    rows = P(AXES, None)
    return jax.shard_map(
        local,
        mesh=fine,
        in_specs=(rows, rows, rows, P(AXES), P(), P(), rows),
        out_specs=(rows, rows, rows, rows, P()),
        check_vma=False,
    )
```

time: 71.3 us -> 73.6 us (1.032)
  waiting for transfers between devices: 21.9 us -> 40 us
  starting transfers between devices: 26.9 us -> 19.2 us
  Pallas kernels: 16.1 us -> 10.3 us
  local copies, waits for them, and re-layouts: 3.34 us -> 1.73 us
    ppermute x25 -> x10, waiting for transfers between devices: 21.9 us -> 40 us  [swap(): return lax.ppermute(x, AXES, perm)]
    ppermute x25 -> x10, starting transfers between devices: 26.9 us -> 19.2 us  [swap(): return lax.ppermute(x, AXES, perm)]
    pallas_call x5 -> x2, Pallas kernels: 16.1 us -> 10.3 us  [the longest x1 9.61 us: attend(): pl.pallas_call(functools.partial(attend_kernel, mine, cols, folded), grid...]
    unnamed x48 -> x12, local copies, waits for them, and re-layouts: 3.24 us -> 0.82 us
    another operation x1 -> x0, other arithmetic: 0.78 us -> none  [local(): kv = lax.optimization_barrier(jnp.stack([keys, values]))]
    concatenate x2, local copies, waits for them, and re-layouts: 0.02 us -> 0.8 us  [the longest x1 0.76 us: local(): buf = jnp.concatenate([keys, values], axis=1)]
  transfers between devices with their start and end apart: 25 -> 10, of which waited for: 14 -> 10; matrix products, arithmetic and copies ran while one was open for 0% -> 0% of each run, Pallas kernels for 18% -> 0%
where the time goes in v6:
time: 73.6 us; the launch traced here: 73.3 us
  waiting for transfers between devices  40 us (54%)
  starting transfers between devices  19.2 us (26%)
  Pallas kernels  10.3 us (14%)
  local copies, waits for them, and re-layouts  1.73 us (2%)
  between operations  1.41 us (2%)
    ppermute x10, waiting for transfers between devices, swap(): return lax.ppermute(x, AXES, perm)  40 us
    ppermute x10, starting transfers between devices, swap(): return lax.ppermute(x, AXES, perm)  19.2 us
    pallas_call x1, Pallas kernels, attend(): pl.pallas_call(functools.partial(attend_kernel, mine, cols, folded), grid...  9.61 us
  transfers between devices with their start and end apart: 10, of which 10 were waited for; matrix products, arithmetic and copies ran while one was open for 0% of the time, Pallas kernels for 0%

profile of v6, /device:TPU:0, one launch (start us, length us, event | category | flops | bytes accessed | tf_op | source)
XLA Modules:
  0.0 73.3 jit_solution(6917788167739437066)
XLA Ops:
  0.6 0.8 %constant_dynamic-update-slice_fusion.1 = (bf16[32,1024]{1,0:T(8,128)(2,1)S(1)}, bf16[512,1024]{1,0:T(8,128)(2,1)S(1)}) fusion(bf16[32,512]{1,0:T(8,128)(2,1)} %param.8), kind=kLoop, calls=%fused_computation.10 | loop fusion | bytes 98304
  1.4 0.8 %constant_dynamic-update-slice_fusion = (bf16[32,1024]{1,0:T(8,128)(2,1)S(1)}, bf16[512,1024]{1,0:T(8,128)(2,1)S(1)}) fusion(bf16[32,1024]{1,0:T(8,128)(2,1)S(1)} %get-tuple-element.27, bf16[32,512]{1,0:T(8,128)(2,1)} %param.9, bf16[512,1024]{1,0:T(8,128)(2,1)S(1)} %get-tuple-element.28), kind=kLoop, calls=%fused_computation.9 | loop fusion | bytes 98304 | tf_op jit(solution)/shard_map/concatenate | solution.py:353
  2.2 4.0 %collective-permute-start = (bf16[32,1024]{1,0:T(8,128)(2,1)S(1)}, bf16[32,1024]{1,0:T(8,128)(2,1)S(1)}, u32[]{:S(2)}, u32[]{:S(2)}) collective-permute-start(bf16[32,1024]{1,0:T(8,128)(2,1)S(1)} %get-tuple-element.25), channel_id=1, source_target_pairs={{0,4},{1,5},{2,6},{3,7},{4,0},{5,1},{6,2},{7,3},{8,9},{9,8},{10,11... | collective-permute-start | bytes 196616 | tf_op jit(solution)/shard_map/ppermute | solution.py:346
  6.2 2.2 %collective-permute-done = bf16[32,1024]{1,0:T(8,128)(2,1)S(1)} collective-permute-done((bf16[32,1024]{1,0:T(8,128)(2,1)S(1)}, bf16[32,1024]{1,0:T(8,128)(2,1)S(1)}, u32[]{:S(2)}, u32[]{:S(2)}) %collective-permute-start) | collective-permute-done | bytes 65568 | tf_op jit(solution)/shard_map/ppermute | solution.py:346
  8.4 2.0 %collective-permute-start.1 = (bf16[64,1024]{1,0:T(8,128)(2,1)S(1)}, bf16[64,1024]{1,0:T(8,128)(2,1)S(1)}, u32[]{:S(2)}, u32[]{:S(2)}) collective-permute-start(bf16[64,1024]{1,0:T(8,128)(2,1)S(1)} %pad_maximum_fusion.2), channel_id=1, source_target_pairs={{0,2},{1,3},{2,0},{3,1},{4,6},{5,7},{6,4},{7,5},{8,12},{9,13},{10,... | collective-permute-start | bytes 393224 | tf_op jit(solution)/shard_map/ppermute | solution.py:346
  10.4 3.3 %collective-permute-done.1 = bf16[64,1024]{1,0:T(8,128)(2,1)S(1)} collective-permute-done((bf16[64,1024]{1,0:T(8,128)(2,1)S(1)}, bf16[64,1024]{1,0:T(8,128)(2,1)S(1)}, u32[]{:S(2)}, u32[]{:S(2)}) %collective-permute-start.1) | collective-permute-done | bytes 131104 | tf_op jit(solution)/shard_map/ppermute | solution.py:346
  13.7 1.9 %collective-permute-start.2 = (bf16[128,1024]{1,0:T(8,128)(2,1)S(1)}, bf16[128,1024]{1,0:T(8,128)(2,1)S(1)}, u32[]{:S(2)}, u32[]{:S(2)}) collective-permute-start(bf16[128,1024]{1,0:T(8,128)(2,1)S(1)} %pad_maximum_fusion.1), channel_id=1, source_target_pairs={{0,16},{1,17},{2,18},{3,19},{4,20},{5,21},{6,22},{7,23},{8,10},{9,... | collective-permute-start | bytes 786440 | tf_op jit(solution)/shard_map/ppermute | solution.py:346
  15.7 4.5 %collective-permute-done.2 = bf16[128,1024]{1,0:T(8,128)(2,1)S(1)} collective-permute-done((bf16[128,1024]{1,0:T(8,128)(2,1)S(1)}, bf16[128,1024]{1,0:T(8,128)(2,1)S(1)}, u32[]{:S(2)}, u32[]{:S(2)}) %collective-permute-start.2) | collective-permute-done | bytes 262176 | tf_op jit(solution)/shard_map/ppermute | solution.py:346
  20.2 0.0 copy-start.1
  20.2 0.0 copy-start
  20.2 0.0 copy-start.2
  20.2 0.0 copy-start.3
  20.3 2.0 %collective-permute-start.3 = (bf16[256,1024]{1,0:T(8,128)(2,1)S(1)}, bf16[256,1024]{1,0:T(8,128)(2,1)S(1)}, u32[]{:S(2)}, u32[]{:S(2)}) collective-permute-start(bf16[256,1024]{1,0:T(8,128)(2,1)S(1)} %pad_maximum_fusion), channel_id=1, source_target_pairs={{0,1},{1,0},{2,3},{3,2},{4,5},{5,4},{6,7},{7,6},{8,24},{9,25},{10,... | collective-permute-start | bytes 1572872 | tf_op jit(solution)/shard_map/ppermute | solution.py:346
  22.3 7.2 %collective-permute-done.3 = bf16[256,1024]{1,0:T(8,128)(2,1)S(1)} collective-permute-done((bf16[256,1024]{1,0:T(8,128)(2,1)S(1)}, bf16[256,1024]{1,0:T(8,128)(2,1)S(1)}, u32[]{:S(2)}, u32[]{:S(2)}) %collective-permute-start.3) | collective-permute-done | bytes 524320 | tf_op jit(solution)/shard_map/ppermute | solution.py:346
  29.5 0.1 collective-permute-start.4
  30.3 2.0 %collective-permute-done.4.other = bf16[2,2,128,1024]{3,2,1,0:T(8,128)(2,1)S(1)} collective-permute-done((bf16[2,2,128,1024]{3,2,1,0:T(8,128)(2,1)S(1)}, bf16[2,2,128,1024]{3,2,1,0:T(8,128)(2,1)S(1)}, u32[]{:S(2)}, u32[]{:S(2)}) %collective-permute-start.4) | collective-permute-done | bytes 1048608 | tf_op jit(solution)/shard_map/ppermute | solution.py:346
  32.3 0.0 copy-done.1
  32.3 0.0 copy-done
  32.3 0.0 copy-done.2
  32.3 0.0 copy-done.3
  32.3 9.6 %shard_map.110 = (bf16[128,4096]{1,0:T(8,128)(2,1)}, bf16[128,4096]{1,0:T(8,128)(2,1)}, bf16[2,2,4,272,128]{4,3,2,1,0:T(8,128)(2,1)S(1)}, bf16[2,2,4,272,128]{4,3,2,1,0:T(8,128)(2,1)S(1)}, f32[8,128]{1,0:T(8,128)S(1)}) custom-call(s32[128]{0:T(128)S(1)} %copy-done.2, s32[4]{0:T(128)S(1)} %copy-done.3, f32[1]{0:T(128)S(6)} %copy.18.gate_s, ...), custom_call_target="tpu_custom_call" | custom-call | flops 3221225472 | bytes 8388608 | tf_op jit(solution)/shard_map/pallas_call | solution.py:250
  41.9 0.2 collective-permute-start.5
  42.1 2.6 %collective-permute-done.5 = bf16[2,2,4,272,128]{4,3,2,1,0:T(8,128)(2,1)S(1)} collective-permute-done((bf16[2,2,4,272,128]{4,3,2,1,0:T(8,128)(2,1)S(1)}, bf16[2,2,4,272,128]{4,3,2,1,0:T(8,128)(2,1)S(1)}, u32[]{:S(2)}, u32[]{:S(2)}) %collective-permute-start.5) | collective-permute-done | bytes 1114144 | tf_op jit(solution)/shard_map/ppermute | solution.py:346
  44.7 0.3 add_convert_fusion
  45.0 0.1 fusion.1
  45.1 2.0 %collective-permute-start.6 = (bf16[8,272,128]{2,1,0:T(8,128)(2,1)S(1)}, bf16[8,272,128]{2,1,0:T(8,128)(2,1)S(1)}, u32[]{:S(2)}, u32[]{:S(2)}) collective-permute-start(bf16[8,272,128]{2,1,0:T(8,128)(2,1)S(1)} %bitcast.13), channel_id=1, source_target_pairs={{0,1},{1,0},{2,3},{3,2},{4,5},{5,4},{6,7},{7,6},{8,24},{9,25},{10,... | collective-permute-start | bytes 1671176 | tf_op jit(solution)/shard_map/ppermute | solution.py:346
  47.1 7.6 %collective-permute-done.6 = bf16[8,272,128]{2,1,0:T(8,128)(2,1)S(1)} collective-permute-done((bf16[8,272,128]{2,1,0:T(8,128)(2,1)S(1)}, bf16[8,272,128]{2,1,0:T(8,128)(2,1)S(1)}, u32[]{:S(2)}, u32[]{:S(2)}) %collective-permute-start.6) | collective-permute-done | bytes 557088 | tf_op jit(solution)/shard_map/ppermute | solution.py:346
  54.7 0.2 fusion
  54.9 1.9 %collective-permute-start.7 = (bf16[4,272,128]{2,1,0:T(8,128)(2,1)S(1)}, bf16[4,272,128]{2,1,0:T(8,128)(2,1)S(1)}, u32[]{:S(2)}, u32[]{:S(2)}) collective-permute-start(bf16[4,272,128]{2,1,0:T(8,128)(2,1)S(1)} %split.38), channel_id=1, source_target_pairs={{0,16},{1,17},{2,18},{3,19},{4,20},{5,21},{6,22},{7,23},{8,10},{9,... | collective-permute-start | bytes 835592 | tf_op jit(solution)/shard_map/ppermute | solution.py:346
  56.9 4.7 %collective-permute-done.7 = bf16[4,272,128]{2,1,0:T(8,128)(2,1)S(1)} collective-permute-done((bf16[4,272,128]{2,1,0:T(8,128)(2,1)S(1)}, bf16[4,272,128]{2,1,0:T(8,128)(2,1)S(1)}, u32[]{:S(2)}, u32[]{:S(2)}) %collective-permute-start.7) | collective-permute-done | bytes 278560 | tf_op jit(solution)/shard_map/ppermute | solution.py:346
  61.6 0.1 add_convert_fusion.1
  61.7 1.7 %collective-permute-start.8 = (bf16[2,272,128]{2,1,0:T(8,128)(2,1)S(1)}, bf16[2,272,128]{2,1,0:T(8,128)(2,1)S(1)}, u32[]{:S(2)}, u32[]{:S(2)}) collective-permute-start(bf16[2,272,128]{2,1,0:T(8,128)(2,1)S(1)} %split.40), channel_id=1, source_target_pairs={{0,2},{1,3},{2,0},{3,1},{4,6},{5,7},{6,4},{7,5},{8,12},{9,13},{10,... | collective-permute-start | bytes 417800 | tf_op jit(solution)/shard_map/ppermute | solution.py:346
  63.4 3.5 %collective-permute-done.8 = bf16[2,272,128]{2,1,0:T(8,128)(2,1)S(1)} collective-permute-done((bf16[2,272,128]{2,1,0:T(8,128)(2,1)S(1)}, bf16[2,272,128]{2,1,0:T(8,128)(2,1)S(1)}, u32[]{:S(2)}, u32[]{:S(2)}) %collective-permute-start.8) | collective-permute-done | bytes 139296 | tf_op jit(solution)/shard_map/ppermute | solution.py:346
  66.9 3.4 %collective-permute-start.9 = (bf16[1,272,128]{2,1,0:T(8,128)(2,1)S(1)}, bf16[1,272,128]{2,1,0:T(8,128)(2,1)S(1)}, u32[]{:S(2)}, u32[]{:S(2)}) collective-permute-start(bf16[1,272,128]{2,1,0:T(8,128)(2,1)S(1)} %get-tuple-element.23), channel_id=1, source_target_pairs={{0,4},{1,5},{2,6},{3,7},{4,0},{5,1},{6,2},{7,3},{8,9},{9,8},{10,11... | collective-permute-start | bytes 208904 | tf_op jit(solution)/shard_map/ppermute | solution.py:346
  70.3 2.3 %collective-permute-done.9 = bf16[1,272,128]{2,1,0:T(8,128)(2,1)S(1)} collective-permute-done((bf16[1,272,128]{2,1,0:T(8,128)(2,1)S(1)}, bf16[1,272,128]{2,1,0:T(8,128)(2,1)S(1)}, u32[]{:S(2)}, u32[]{:S(2)}) %collective-permute-start.9) | collective-permute-done | bytes 69664 | tf_op jit(solution)/shard_map/ppermute | solution.py:346
  72.6 0.7 shard_map.111
  (11 shorter events, 0.2 us)
Async XLA Ops:
  2.2 6.3 %collective-permute-start = (bf16[32,1024]{1,0:T(8,128)(2,1)S(1)}, bf16[32,1024]{1,0:T(8,128)(2,1)S(1)}, u32[]{:S(2)}, u32[]{:S(2)}) collective-permute-start(bf16[32,1024]{1,0:T(8,128)(2,1)S(1)} %get-tuple-element.25), channel_id=1, source_target_pairs={{0,4},{1,5},{2,6},{3,7},{4,0},{5,1},{6,2},{7,3},{8,9},{9,8},{10,11... | collective-permute-start | bytes 196616 | tf_op jit(solution)/shard_map/ppermute | solution.py:346
  8.4 5.3 %collective-permute-start.1 = (bf16[64,1024]{1,0:T(8,128)(2,1)S(1)}, bf16[64,1024]{1,0:T(8,128)(2,1)S(1)}, u32[]{:S(2)}, u32[]{:S(2)}) collective-permute-start(bf16[64,1024]{1,0:T(8,128)(2,1)S(1)} %pad_maximum_fusion.2), channel_id=1, source_target_pairs={{0,2},{1,3},{2,0},{3,1},{4,6},{5,7},{6,4},{7,5},{8,12},{9,13},{10,... | collective-permute-start | bytes 393224 | tf_op jit(solution)/shard_map/ppermute | solution.py:346
  13.7 6.4 %collective-permute-start.2 = (bf16[128,1024]{1,0:T(8,128)(2,1)S(1)}, bf16[128,1024]{1,0:T(8,128)(2,1)S(1)}, u32[]{:S(2)}, u32[]{:S(2)}) collective-permute-start(bf16[128,1024]{1,0:T(8,128)(2,1)S(1)} %pad_maximum_fusion.1), channel_id=1, source_target_pairs={{0,16},{1,17},{2,18},{3,19},{4,20},{5,21},{6,22},{7,23},{8,10},{9,... | collective-permute-start | bytes 786440 | tf_op jit(solution)/shard_map/ppermute | solution.py:346
  20.2 12.1 %copy-start.1 = (bf16[128,4096]{1,0:T(8,128)(2,1)S(1)}, bf16[128,4096]{1,0:T(8,128)(2,1)}, u32[]{:S(2)}) copy-start(bf16[128,4096]{1,0:T(8,128)(2,1)} %dy_ref.1) | copy-start | bytes 3145732
  20.2 12.1 %copy-start = (bf16[128,4096]{1,0:T(8,128)(2,1)S(1)}, bf16[128,4096]{1,0:T(8,128)(2,1)}, u32[]{:S(2)}) copy-start(bf16[128,4096]{1,0:T(8,128)(2,1)} %q_ref.1) | copy-start | bytes 3145732
  20.2 12.0 %copy-start.2 = (s32[128]{0:T(128)S(1)}, s32[128]{0:T(128)}, u32[]{:S(2)}) copy-start(s32[128]{0:T(128)} %seg_s.1) | copy-start | bytes 1540
  20.2 12.0 %copy-start.3 = (s32[4]{0:T(128)S(1)}, s32[4]{0:T(128)}, u32[]{:S(2)}) copy-start(s32[4]{0:T(128)} %cnt_s.1) | copy-start | bytes 52
  20.3 9.2 %collective-permute-start.3 = (bf16[256,1024]{1,0:T(8,128)(2,1)S(1)}, bf16[256,1024]{1,0:T(8,128)(2,1)S(1)}, u32[]{:S(2)}, u32[]{:S(2)}) collective-permute-start(bf16[256,1024]{1,0:T(8,128)(2,1)S(1)} %pad_maximum_fusion), channel_id=1, source_target_pairs={{0,1},{1,0},{2,3},{3,2},{4,5},{5,4},{6,7},{7,6},{8,24},{9,25},{10,... | collective-permute-start | bytes 1572872 | tf_op jit(solution)/shard_map/ppermute | solution.py:346
  29.5 2.7 %collective-permute-start.4 = (bf16[2,2,128,1024]{3,2,1,0:T(8,128)(2,1)S(1)}, bf16[2,2,128,1024]{3,2,1,0:T(8,128)(2,1)S(1)}, u32[]{:S(2)}, u32[]{:S(2)}) collective-permute-start(bf16[2,2,128,1024]{3,2,1,0:T(8,128)(2,1)S(1)} %bitcast.10), channel_id=1, source_target_pairs={{0,8},{1,9},{2,10},{3,11},{4,12},{5,13},{6,14},{7,15},{8,0},{9,1},... | collective-permute-start | bytes 3145736 | tf_op jit(solution)/shard_map/ppermute | solution.py:346
  41.9 2.8 %collective-permute-start.5 = (bf16[2,2,4,272,128]{4,3,2,1,0:T(8,128)(2,1)S(1)}, bf16[2,2,4,272,128]{4,3,2,1,0:T(8,128)(2,1)S(1)}, u32[]{:S(2)}, u32[]{:S(2)}) collective-permute-start(bf16[2,2,4,272,128]{4,3,2,1,0:T(8,128)(2,1)S(1)} %get-tuple-element.17), channel_id=1, source_target_pairs={{0,8},{1,9},{2,10},{3,11},{4,12},{5,13},{6,14},{7,15},{8,0},{9,1},... | collective-permute-start | bytes 3342344 | tf_op jit(solution)/shard_map/ppermute | solution.py:346
  45.1 9.6 %collective-permute-start.6 = (bf16[8,272,128]{2,1,0:T(8,128)(2,1)S(1)}, bf16[8,272,128]{2,1,0:T(8,128)(2,1)S(1)}, u32[]{:S(2)}, u32[]{:S(2)}) collective-permute-start(bf16[8,272,128]{2,1,0:T(8,128)(2,1)S(1)} %bitcast.13), channel_id=1, source_target_pairs={{0,1},{1,0},{2,3},{3,2},{4,5},{5,4},{6,7},{7,6},{8,24},{9,25},{10,... | collective-permute-start | bytes 1671176 | tf_op jit(solution)/shard_map/ppermute | solution.py:346
  54.9 6.6 %collective-permute-start.7 = (bf16[4,272,128]{2,1,0:T(8,128)(2,1)S(1)}, bf16[4,272,128]{2,1,0:T(8,128)(2,1)S(1)}, u32[]{:S(2)}, u32[]{:S(2)}) collective-permute-start(bf16[4,272,128]{2,1,0:T(8,128)(2,1)S(1)} %split.38), channel_id=1, source_target_pairs={{0,16},{1,17},{2,18},{3,19},{4,20},{5,21},{6,22},{7,23},{8,10},{9,... | collective-permute-start | bytes 835592 | tf_op jit(solution)/shard_map/ppermute | solution.py:346
  61.7 5.2 %collective-permute-start.8 = (bf16[2,272,128]{2,1,0:T(8,128)(2,1)S(1)}, bf16[2,272,128]{2,1,0:T(8,128)(2,1)S(1)}, u32[]{:S(2)}, u32[]{:S(2)}) collective-permute-start(bf16[2,272,128]{2,1,0:T(8,128)(2,1)S(1)} %split.40), channel_id=1, source_target_pairs={{0,2},{1,3},{2,0},{3,1},{4,6},{5,7},{6,4},{7,5},{8,12},{9,13},{10,... | collective-permute-start | bytes 417800 | tf_op jit(solution)/shard_map/ppermute | solution.py:346
  66.9 5.7 %collective-permute-start.9 = (bf16[1,272,128]{2,1,0:T(8,128)(2,1)S(1)}, bf16[1,272,128]{2,1,0:T(8,128)(2,1)S(1)}, u32[]{:S(2)}, u32[]{:S(2)}) collective-permute-start(bf16[1,272,128]{2,1,0:T(8,128)(2,1)S(1)} %get-tuple-element.23), channel_id=1, source_target_pairs={{0,4},{1,5},{2,6},{3,7},{4,0},{5,1},{6,2},{7,3},{8,9},{9,8},{10,11... | collective-permute-start | bytes 208904 | tf_op jit(solution)/shard_map/ppermute | solution.py:346

commit v7 on v6

--- a/solution.py
+++ b/solution.py
@@ -17,6 +17,7 @@
 GROWS = 16
 GTOP = 8
 STRIP = 32
+LINE = PEERS = (1, 2, 3)
 
 NT = (((1,), (1,)), ((), ()))
 NN = (((1,), (0,)), ((), ()))
@@ -67,34 +68,18 @@
     ypos, zpos = lax.axis_index("y"), lax.axis_index("z")
     img_a, img_b = seg_s[0], seg_s[tokens - 1]
 
-    def place(img, h):
-        par, dx = img % 2, (img // 2) ^ xpos
-        return par, jnp.where(par == 0, h, dx), jnp.where(par == 0, dx, h)
+    def place(img):
+        return img % 2, (img // 2) ^ xpos
 
     def fetch(i, img, start):
-        for h in range(2):
-            par, j0, j1 = place(img, h)
-            for src, mask in ((own, par == core), (other, par != core)):
-
-                @pl.when(mask)
-                def _():
-                    c = pltpu.make_async_copy(src.at[j0, j1], kv.at[i, pl.ds(h * half, half)], sems.at[i])
+        par, dx = place(img)
+        for src, mask in ((own, par == core), (other, par != core)):
+
+            @pl.when(mask)
+            def _():
+                for h in range(2):
+                    c = pltpu.make_async_copy(src.at[dx, h], kv.at[i, pl.ds(h * half, half)], sems.at[i])
                     c.start() if start else c.wait()
-
-    def tile_of(n, img):
-        side, rest = n // half, n % half
-        outer, inner = rest // mine, rest % mine
-        if folded:
-            z0 = (2 * (outer % 2) + outer // 2) ^ zpos
-            y0 = side ^ ypos
-            z1 = ((outer // 2) * 2 + side) ^ zpos
-            y1 = (outer % 2) ^ ypos
-        else:
-            z0 = z1 = outer
-            y0 = y1 = side ^ ypos
-        even = img % 2 == 0
-        z, y = jnp.where(even, z0, z1), jnp.where(even, y0, y1)
-        return (z * (2 * mine) + y * mine + inner) // TILE_TOK
 
     in_a = seg_v[...] == img_a
     tg = jnp.tanh(jnp.full((1, hd), gate_s[0], jnp.float32))
@@ -106,10 +91,11 @@
         acc[...] = jnp.zeros_like(acc)
         g_ref[...] = jnp.zeros_like(g_ref)
         n = lax.broadcasted_iota(jnp.int32, (slots, tokens), 0)
-        seen_a = tile_of(n, img_a) < cnt_s[img_a]
-        seen_b = tile_of(n, img_b) < cnt_s[img_b]
-        seen = jnp.where(in_a, seen_a.astype(jnp.float32), seen_b.astype(jnp.float32))
-        bias[...] = jnp.where(seen > 0.5, 0.0, NEG)
+        z, y = n // mine % cols, (n // half) ^ ypos
+        if folded:
+            z = z ^ zpos
+        tile = (z * (2 * mine) + y * mine + n % mine) // TILE_TOK
+        bias[...] = jnp.where(tile < jnp.where(in_a, cnt_s[img_a], cnt_s[img_b]), 0.0, NEG)
         side_a = jnp.broadcast_to(in_a.astype(jnp.float32), (hd, tokens)).T
         rowsel[0] = side_a.astype(jnp.bfloat16)
         rowsel[1] = (1.0 - side_a).astype(jnp.bfloat16)
@@ -143,18 +129,20 @@
         return jnp.sum(x.reshape(x.shape[0] // 8, 8, x.shape[1]), axis=0)
 
     def products(h):
-        rows = slice(h * span, (h + 1) * span)
-        sbuf[h % 2] = mm(kcat, qc[rows, :], NT)
-        dbuf[h % 2] = mm(vcat, dc[rows, :], NT)
-
-    def softmax(h):
         i = h % 2
         rows = slice(h * span, (h + 1) * span)
+        s = mm(kcat, qc[rows, :], NT)
         top = jnp.full((8, span), NEG, jnp.float32)
         for strip in strips:
-            x = sbuf[i, strip] + jnp.concatenate([bias[strip], bias[strip]], axis=1)
+            x = s[strip] + jnp.concatenate([bias[strip], bias[strip]], axis=1)
             sbuf[i, strip] = x
             top = jnp.maximum(top, jnp.max(x.reshape(STRIP // 8, 8, span), axis=0))
+        dbuf[i] = mm(vcat, dc[rows, :], NT)
+        return top
+
+    def softmax(h, top):
+        i = h % 2
+        rows = slice(h * span, (h + 1) * span)
         top = jnp.max(top, axis=0, keepdims=True) * (scale * LOG2E)
         norm = jnp.zeros((8, span), jnp.float32)
         dots = jnp.zeros((8, span), jnp.float32)
@@ -186,12 +174,12 @@
         rows = slice(lo * span, hi * span)
         return mm(ds16[:, rows], qc[rows, :], NN), mm(p16[:, rows], dc[rows, :], NN)
 
-    products(0)
+    top = products(0)
     dk = dv = 0.0
     for h in range(blocks):
-        if h + 1 < blocks:
-            products(h + 1)
-        softmax(h)
+        ahead = products(h + 1) if h + 1 < blocks else None
+        softmax(h, top)
+        top = ahead
         outputs(h)
         if h % 2:
             more = slot_grads(h - 1, h + 1)
@@ -204,12 +192,29 @@
     krows = pl.ds(pl.multiple_of(step * per, per), per)
     vrows = pl.ds(pl.multiple_of((heads + step) * per, per), per)
     for img, lanes in ((img_b, slice(hd, 2 * hd)), (img_a, slice(0, hd))):
-        for h in range(2):
-            par, j0, j1 = place(img, h)
-            for j in range(pieces // 2):
-                at = slice(h * half + j * per, h * half + (j + 1) * per)
-                acc[par, j0, j1, j, krows] = dk[at, lanes]
-                acc[par, j0, j1, j, vrows] = dv[at, lanes]
+        par, dx = place(img)
+        for j in range(pieces):
+            at = slice(j * per, (j + 1) * per)
+            acc[par, dx, j // (pieces // 2), j % (pieces // 2), krows] = dk[at, lanes]
+            acc[par, dx, j // (pieces // 2), j % (pieces // 2), vrows] = dv[at, lanes]
+
+    def leave(rows, i):
+        lay = slice(None), slice(None), slice(None), rows
+        return (
+            pltpu.make_async_copy(acc.at[(1 - core,) + lay], part_other.at[lay], sems.at[2 + 2 * i]),
+            pltpu.make_async_copy(acc.at[(core,) + lay], part_own.at[lay], sems.at[3 + 2 * i]),
+        )
+
+    def head_rows(h):
+        return pl.ds(h * per, per), pl.ds((heads + h) * per, per)
+
+    for h in range(KV_HEADS):
+
+        @pl.when(step == h)
+        def _():
+            for i, rows in enumerate(head_rows(h)):
+                for c in leave(rows, 2 * h + i):
+                    c.start()
 
     @pl.when(step == heads - 1)
     def _():
@@ -226,12 +231,15 @@
         for i in range(8):
             for j in range(pieces // 2):
                 acc[i // 4, i // 2 % 2, i % 2, j, 2 * heads * per :] = digits
-        c1 = pltpu.make_async_copy(acc.at[1 - core], part_other, sems.at[2])
-        c0 = pltpu.make_async_copy(acc.at[core], part_own, sems.at[3])
-        c1.start()
-        c0.start()
-        c1.wait()
-        c0.wait()
+        tail = leave(pl.ds(2 * KV_HEADS * per, GROWS), 2 * KV_HEADS)
+        for c in tail:
+            c.start()
+        for h in range(KV_HEADS):
+            for i, rows in enumerate(head_rows(h)):
+                for c in leave(rows, 2 * h + i):
+                    c.wait()
+        for c in tail:
+            c.wait()
 
 
 def attend(mine, cols, folded, seg, counts, gate, q, dy, own, other):
@@ -279,7 +287,7 @@
             pltpu.VMEM((2, slots, 2 * tokens), jnp.float32),
             pltpu.VMEM((slots, tokens), jnp.float32),
             pltpu.VMEM((2, tokens, hd), jnp.bfloat16),
-            pltpu.SemaphoreType.DMA((4,)),
+            pltpu.SemaphoreType.DMA((4 + 4 * KV_HEADS,)),
         ],
         compiler_params=pltpu.CompilerParams(
             dimension_semantics=("arbitrary",), vmem_limit_bytes=32 * 1024 * 1024
@@ -336,44 +344,47 @@
     folded = cols == 4
     half = cols * mine
 
-    def swap(x, even, odd):
-        perm = []
-        for i in range(8 * cols):
-            place = [i // (4 * cols), i // (2 * cols) % 2, i // 2 % cols, i % 2]
-            dim, bit = odd if place[1] else even
-            place[dim] ^= bit
-            perm.append((i, ((place[0] * 2 + place[1]) * cols + place[2]) * 2 + place[3]))
-        return lax.ppermute(x, AXES, perm)
-
-    x1, y1, z1, z2 = (0, 1), (3, 1), (2, 1), (2, 2)
-    near = ((z2, y1), (z1, z2))
-    far = ((x1, z1), (y1, x1)) if folded else ((x1, y1), (y1, x1))
-    steps = near + far if folded else far
-
-    buf = jnp.concatenate([keys, values], axis=1)
-    if not folded:
-        buf = lax.all_gather(buf, "z", axis=0, tiled=True)
-    for even, odd in steps:
-        buf = jnp.concatenate([buf, swap(buf, even, odd)], axis=0)
-    own = buf.reshape(2, 2, half, 2 * width)
-    core = ((1, 1), (1, 1))
-    other = swap(own, *core)
+    def send_z(x, k):
+        return lax.ppermute(x, "z", [(i, i ^ k) for i in range(cols)])
+
+    def send_xy(x, p):
+        return lax.ppermute(x, ("x", "y"), [(i, i ^ p) for i in range(4)])
+
+    def send_core(x):
+        return lax.ppermute(x, "core", [(0, 1), (1, 0)])
+
+    kv = jnp.concatenate([keys, values], axis=1)
+    if folded:
+        line = [send_z(kv, k) for k in LINE]
+        near = [send_xy(kv, p) for p in (1, 2)]
+        line, near = lax.optimization_barrier((jnp.concatenate(line, axis=0), near))
+        block = jnp.concatenate([kv, line], axis=0)
+        diag = send_xy(block, 3)
+        own = [block, near[0], send_xy(line, 1), near[1], send_xy(line, 2), diag]
+    else:
+        line = lax.all_gather(kv, "z", axis=0, tiled=True)
+        own = [line] + [send_xy(line, p) for p in PEERS]
+    own = jnp.concatenate(own, axis=0).reshape(2, 2, half, 2 * width)
+    other = send_core(own)
 
     y, dq, part_own, part_other, g = attend(
         mine, cols, folded, seg_image, tile_counts, gate, queries, cotangent, own, other
     )
 
-    part = (part_own.astype(f32) + swap(part_other, *core).astype(f32)).astype(bf16)
-    part = part.reshape((-1,) + part.shape[3:])
-    for even, odd in steps[::-1]:
-        keep, away = jnp.split(part, 2)
-        parts = [keep, swap(away, even, odd)]
-        part = (parts[0].astype(f32) + parts[1].astype(f32)).astype(bf16)
+    part = (part_own.astype(f32) + send_core(part_other).astype(f32)).astype(bf16)
+    part = part.reshape((4,) + part.shape[2:])
     if folded:
-        parts = [p[0] for p in parts]
+        line = part[0, 1:].astype(f32)
+        for p in PEERS:
+            line = line + send_xy(part[p, 1:], p).astype(f32)
+        line = line.astype(bf16)
+        parts = [part[0, 0]] + [send_xy(part[p, 0], p) for p in PEERS]
+        parts += [send_z(line[k - 1], k) for k in LINE]
     else:
-        part = parts[0][0].astype(f32) + parts[1][0].astype(f32)
-        grads, gates = part[:-GROWS].reshape(2 * KV_HEADS, cols, mine, hd), part[-GROWS:]
+        line = part[0, 0].astype(f32)
+        for p in PEERS:
+            line = line + send_xy(part[p, 0], p).astype(f32)
+        grads, gates = line[:-GROWS].reshape(2 * KV_HEADS, cols, mine, hd), line[-GROWS:]
         grads = lax.psum_scatter(grads, "z", scatter_dimension=1, tiled=True)
         parts = [jnp.concatenate([grads.reshape(-1, hd), lax.psum(gates, "z")], axis=0)]
     return (y, dq, *finish(mine, g, parts))

time: 73.6 us -> 65 us (0.88)
  waiting for transfers between devices: 40 us -> 25.8 us
  starting transfers between devices: 19.2 us -> 25.3 us
    ppermute x10 -> x19, waiting for transfers between devices: 40 us -> 25.8 us  [the longest x11 15.9 us: send_xy(): return lax.ppermute(x, ('x', 'y'), [(i, i ^ p) for i in range(4)])]
    ppermute x10 -> x19, starting transfers between devices: 19.2 us -> 25.3 us  [the longest x11 14.9 us: send_xy(): return lax.ppermute(x, ('x', 'y'), [(i, i ^ p) for i in range(4)])]
  transfers between devices with their start and end apart: 10 -> 19, of which waited for: 10 -> 9; matrix products, arithmetic and copies ran while one was open for 0% -> 0% of each run, Pallas kernels for 0% -> 0%
where the time goes in v7:
time: 65 us; the launch traced here: 64.8 us
  waiting for transfers between devices  25.8 us (40%)
  starting transfers between devices  25.3 us (39%)
  Pallas kernels  10.1 us (16%)
  local copies, waits for them, and re-layouts  1.7 us (3%)
  between operations  1.44 us (2%)
    ppermute x11, waiting for transfers between devices, send_xy(): return lax.ppermute(x, ('x', 'y'), [(i, i ^ p) for i in range(4)])  15.9 us
    ppermute x11, starting transfers between devices, send_xy(): return lax.ppermute(x, ('x', 'y'), [(i, i ^ p) for i in range(4)])  14.9 us
    ppermute x6, starting transfers between devices, send_z(): return lax.ppermute(x, 'z', [(i, i ^ k) for i in range(cols)])  10.1 us
    pallas_call x1, Pallas kernels, attend(): pl.pallas_call(functools.partial(attend_kernel, mine, cols, folded), grid...  9.39 us
    ppermute x6, waiting for transfers between devices, send_z(): return lax.ppermute(x, 'z', [(i, i ^ k) for i in range(cols)])  5.29 us
    ppermute x2, waiting for transfers between devices, send_core(): return lax.ppermute(x, 'core', [(0, 1), (1, 0)])  4.62 us
  transfers between devices with their start and end apart: 19, of which 9 were waited for; matrix products, arithmetic and copies ran while one was open for 0% of the time, Pallas kernels for 0%

profile of v7, /device:TPU:0, one launch (start us, length us, event | category | flops | bytes accessed | tf_op | source)
XLA Modules:
  0.0 64.8 jit_solution(13076273706039229117)
XLA Ops:
  0.6 0.8 %constant_dynamic-update-slice_fusion.1 = (bf16[32,1024]{1,0:T(8,128)(2,1)S(1)}, bf16[512,1024]{1,0:T(8,128)(2,1)S(1)}) fusion(bf16[32,512]{1,0:T(8,128)(2,1)} %param.8), kind=kLoop, calls=%fused_computation.19 | loop fusion | bytes 98304
  1.4 0.8 %constant_dynamic-update-slice_fusion = (bf16[32,1024]{1,0:T(8,128)(2,1)S(1)}, bf16[512,1024]{1,0:T(8,128)(2,1)S(1)}) fusion(bf16[32,1024]{1,0:T(8,128)(2,1)S(1)} %get-tuple-element.39, bf16[32,512]{1,0:T(8,128)(2,1)} %param.9, bf16[512,1024]{1,0:T(8,128)(2,1)S(1)} %get-tuple-element.40), kind=kLoop, calls=%fused_computation.18 | loop fusion | bytes 98304 | tf_op jit(solution)/shard_map/concatenate | solution.py:356
  2.2 5.0 %collective-permute-start.2 = (bf16[32,1024]{1,0:T(8,128)(2,1)S(1)}, bf16[32,1024]{1,0:T(8,128)(2,1)S(1)}, u32[]{:S(2)}, u32[]{:S(2)}) collective-permute-start(bf16[32,1024]{1,0:T(8,128)(2,1)S(1)} %get-tuple-element.37), channel_id=1, source_target_pairs={{0,6},{2,4},{4,2},{6,0},{1,7},{3,5},{5,3},{7,1},{8,14},{10,12},{12... | collective-permute-start | bytes 196616 | tf_op jit(solution)/shard_map/ppermute | solution.py:348
  7.2 0.0 collective-permute-start.1
  7.2 0.6 collective-permute-start
  7.8 1.7 %collective-permute-start.4 = (bf16[32,1024]{1,0:T(8,128)(2,1)S(1)}, bf16[32,1024]{1,0:T(8,128)(2,1)S(1)}, u32[]{:S(2)}, u32[]{:S(2)}) collective-permute-start(bf16[32,1024]{1,0:T(8,128)(2,1)S(1)} %get-tuple-element.37), channel_id=1, source_target_pairs={{0,16},{1,17},{16,0},{17,1},{2,18},{3,19},{18,2},{19,3},{4,20},{5,... | collective-permute-start | bytes 196616 | tf_op jit(solution)/shard_map/ppermute | solution.py:351
  9.5 1.5 %collective-permute-start.3 = (bf16[32,1024]{1,0:T(8,128)(2,1)S(1)}, bf16[32,1024]{1,0:T(8,128)(2,1)S(1)}, u32[]{:S(2)}, u32[]{:S(2)}) collective-permute-start(bf16[32,1024]{1,0:T(8,128)(2,1)S(1)} %get-tuple-element.37), channel_id=1, source_target_pairs={{0,1},{1,0},{16,17},{17,16},{2,3},{3,2},{18,19},{19,18},{4,5},{5,4... | collective-permute-start | bytes 196616 | tf_op jit(solution)/shard_map/ppermute | solution.py:351
  11.0 0.0 collective-permute-done.2
  11.0 1.8 %collective-permute-done.1 = bf16[32,1024]{1,0:T(8,128)(2,1)S(1)} collective-permute-done((bf16[32,1024]{1,0:T(8,128)(2,1)S(1)}, bf16[32,1024]{1,0:T(8,128)(2,1)S(1)}, u32[]{:S(2)}, u32[]{:S(2)}) %collective-permute-start.1) | collective-permute-done | bytes 65568 | tf_op jit(solution)/shard_map/ppermute | solution.py:348
  12.8 0.0 collective-permute-done
  12.8 0.0 collective-permute-done.4
  12.8 0.9 %collective-permute-done.3 = bf16[32,1024]{1,0:T(8,128)(2,1)S(1)} collective-permute-done((bf16[32,1024]{1,0:T(8,128)(2,1)S(1)}, bf16[32,1024]{1,0:T(8,128)(2,1)S(1)}, u32[]{:S(2)}, u32[]{:S(2)}) %collective-permute-start.3) | collective-permute-done | bytes 65568 | tf_op jit(solution)/shard_map/ppermute | solution.py:351
  13.8 0.0 copy-start
  13.8 0.0 copy-start.2
  13.8 0.0 copy-start.3
  13.8 0.7 %collective-permute-start.6 = (bf16[96,1024]{1,0:T(8,128)(2,1)S(1)}, bf16[96,1024]{1,0:T(8,128)(2,1)S(1)}, u32[]{:S(2)}, u32[]{:S(2)}) collective-permute-start(bf16[96,1024]{1,0:T(8,128)(2,1)S(1)} %pad_maximum_fusion.1), channel_id=1, source_target_pairs={{0,16},{1,17},{16,0},{17,1},{2,18},{3,19},{18,2},{19,3},{4,20},{5,... | collective-permute-start | bytes 589832 | tf_op jit(solution)/shard_map/ppermute | solution.py:351
  14.5 1.5 %collective-permute-start.5 = (bf16[96,1024]{1,0:T(8,128)(2,1)S(1)}, bf16[96,1024]{1,0:T(8,128)(2,1)S(1)}, u32[]{:S(2)}, u32[]{:S(2)}) collective-permute-start(bf16[96,1024]{1,0:T(8,128)(2,1)S(1)} %pad_maximum_fusion.1), channel_id=1, source_target_pairs={{0,1},{1,0},{16,17},{17,16},{2,3},{3,2},{18,19},{19,18},{4,5},{5,4... | collective-permute-start | bytes 589832 | tf_op jit(solution)/shard_map/ppermute | solution.py:351
  16.0 1.4 %collective-permute-start.7 = (bf16[128,1024]{1,0:T(8,128)(2,1)S(1)}, bf16[128,1024]{1,0:T(8,128)(2,1)S(1)}, u32[]{:S(2)}, u32[]{:S(2)}) collective-permute-start(bf16[128,1024]{1,0:T(8,128)(2,1)S(1)} %pad_maximum_fusion), channel_id=1, source_target_pairs={{0,17},{1,16},{16,1},{17,0},{2,19},{3,18},{18,3},{19,2},{4,21},{5,... | collective-permute-start | bytes 786440 | tf_op jit(solution)/shard_map/ppermute | solution.py:351
  17.4 9.1 %collective-permute-done.5 = bf16[96,1024]{1,0:T(8,128)(2,1)S(1)} collective-permute-done((bf16[96,1024]{1,0:T(8,128)(2,1)S(1)}, bf16[96,1024]{1,0:T(8,128)(2,1)S(1)}, u32[]{:S(2)}, u32[]{:S(2)}) %collective-permute-start.5) | collective-permute-done | bytes 196640 | tf_op jit(solution)/shard_map/ppermute | solution.py:351
  26.5 0.0 collective-permute-done.6
  26.5 0.0 collective-permute-done.7
  26.6 0.1 collective-permute-start.8
  27.3 2.0 %collective-permute-done.8.other = bf16[2,2,128,1024]{3,2,1,0:T(8,128)(2,1)S(1)} collective-permute-done((bf16[2,2,128,1024]{3,2,1,0:T(8,128)(2,1)S(1)}, bf16[2,2,128,1024]{3,2,1,0:T(8,128)(2,1)S(1)}, u32[]{:S(2)}, u32[]{:S(2)}) %collective-permute-start.8) | collective-permute-done | bytes 1048608 | tf_op jit(solution)/shard_map/ppermute | solution.py:354
  29.3 0.0 copy-done.3
  29.3 9.4 %shard_map.110 = (bf16[128,4096]{1,0:T(8,128)(2,1)}, bf16[128,4096]{1,0:T(8,128)(2,1)}, bf16[2,2,4,272,128]{4,3,2,1,0:T(8,128)(2,1)S(1)}, bf16[2,2,4,272,128]{4,3,2,1,0:T(8,128)(2,1)S(1)}, f32[8,128]{1,0:T(8,128)S(1)}) custom-call(s32[128]{0:T(128)S(1)} %copy-done.2, s32[4]{0:T(128)S(1)} %copy-done.3, f32[1]{0:T(128)S(6)} %copy.20.gate_s, ...), custom_call_target="tpu_custom_call" | custom-call | flops 3221225472 | bytes 8388608 | tf_op jit(solution)/shard_map/pallas_call | solution.py:258
  38.7 0.2 collective-permute-start.9
  38.9 2.6 %collective-permute-done.9 = bf16[2,2,4,272,128]{4,3,2,1,0:T(8,128)(2,1)S(1)} collective-permute-done((bf16[2,2,4,272,128]{4,3,2,1,0:T(8,128)(2,1)S(1)}, bf16[2,2,4,272,128]{4,3,2,1,0:T(8,128)(2,1)S(1)}, u32[]{:S(2)}, u32[]{:S(2)}) %collective-permute-start.9) | collective-permute-done | bytes 1114144 | tf_op jit(solution)/shard_map/ppermute | solution.py:354
  41.5 0.3 add_convert_fusion
  41.9 1.6 %collective-permute-start.13 = (bf16[3,272,128]{2,1,0:T(8,128)(2,1)S(1)}, bf16[3,272,128]{2,1,0:T(8,128)(2,1)S(1)}, u32[]{:S(2)}, u32[]{:S(2)}) collective-permute-start(bf16[3,272,128]{2,1,0:T(8,128)(2,1)S(1)} %get-tuple-element.27), channel_id=1, source_target_pairs={{0,1},{1,0},{16,17},{17,16},{2,3},{3,2},{18,19},{19,18},{4,5},{5,4... | collective-permute-start | bytes 626696 | tf_op jit(solution)/shard_map/ppermute | solution.py:351
  43.5 1.1 %collective-permute-start.15 = (bf16[3,272,128]{2,1,0:T(8,128)(2,1)S(1)}, bf16[3,272,128]{2,1,0:T(8,128)(2,1)S(1)}, u32[]{:S(2)}, u32[]{:S(2)}) collective-permute-start(bf16[3,272,128]{2,1,0:T(8,128)(2,1)S(1)} %get-tuple-element.28), channel_id=1, source_target_pairs={{0,17},{1,16},{16,1},{17,0},{2,19},{3,18},{18,3},{19,2},{4,21},{5,... | collective-permute-start | bytes 626696 | tf_op jit(solution)/shard_map/ppermute | solution.py:351
  44.6 0.9 %collective-permute-start.14 = (bf16[3,272,128]{2,1,0:T(8,128)(2,1)S(1)}, bf16[3,272,128]{2,1,0:T(8,128)(2,1)S(1)}, u32[]{:S(2)}, u32[]{:S(2)}) collective-permute-start(bf16[3,272,128]{2,1,0:T(8,128)(2,1)S(1)} %get-tuple-element.29), channel_id=1, source_target_pairs={{0,16},{1,17},{16,0},{17,1},{2,18},{3,19},{18,2},{19,3},{4,20},{5,... | collective-permute-start | bytes 626696 | tf_op jit(solution)/shard_map/ppermute | solution.py:351
  45.5 1.7 %collective-permute-start.12 = (bf16[272,128]{1,0:T(8,128)(2,1)S(1)}, bf16[272,128]{1,0:T(8,128)(2,1)S(1)}, u32[]{:S(2)}, u32[]{:S(2)}) collective-permute-start(bf16[272,128]{1,0:T(8,128)(2,1)S(1)} %get-tuple-element.30), channel_id=1, source_target_pairs={{0,17},{1,16},{16,1},{17,0},{2,19},{3,18},{18,3},{19,2},{4,21},{5,... | collective-permute-start | bytes 208904 | tf_op jit(solution)/shard_map/ppermute | solution.py:351
  47.2 1.3 %collective-permute-start.11 = (bf16[272,128]{1,0:T(8,128)(2,1)S(1)}, bf16[272,128]{1,0:T(8,128)(2,1)S(1)}, u32[]{:S(2)}, u32[]{:S(2)}) collective-permute-start(bf16[272,128]{1,0:T(8,128)(2,1)S(1)} %get-tuple-element.31), channel_id=1, source_target_pairs={{0,16},{1,17},{16,0},{17,1},{2,18},{3,19},{18,2},{19,3},{4,20},{5,... | collective-permute-start | bytes 208904 | tf_op jit(solution)/shard_map/ppermute | solution.py:351
  48.5 5.1 %collective-permute-done.13 = bf16[3,272,128]{2,1,0:T(8,128)(2,1)S(1)} collective-permute-done((bf16[3,272,128]{2,1,0:T(8,128)(2,1)S(1)}, bf16[3,272,128]{2,1,0:T(8,128)(2,1)S(1)}, u32[]{:S(2)}, u32[]{:S(2)}) %collective-permute-start.13) | collective-permute-done | bytes 208928 | tf_op jit(solution)/shard_map/ppermute | solution.py:351
  53.7 1.5 %collective-permute-start.10 = (bf16[272,128]{1,0:T(8,128)(2,1)S(1)}, bf16[272,128]{1,0:T(8,128)(2,1)S(1)}, u32[]{:S(2)}, u32[]{:S(2)}) collective-permute-start(bf16[272,128]{1,0:T(8,128)(2,1)S(1)} %get-tuple-element.32), channel_id=1, source_target_pairs={{0,1},{1,0},{16,17},{17,16},{2,3},{3,2},{18,19},{19,18},{4,5},{5,4... | collective-permute-start | bytes 208904 | tf_op jit(solution)/shard_map/ppermute | solution.py:351
  55.2 0.0 collective-permute-done.15
  55.2 0.8 %collective-permute-done.14 = bf16[3,272,128]{2,1,0:T(8,128)(2,1)S(1)} collective-permute-done((bf16[3,272,128]{2,1,0:T(8,128)(2,1)S(1)}, bf16[3,272,128]{2,1,0:T(8,128)(2,1)S(1)}, u32[]{:S(2)}, u32[]{:S(2)}) %collective-permute-start.14) | collective-permute-done | bytes 208928 | tf_op jit(solution)/shard_map/ppermute | solution.py:351
  56.0 0.1 fusion.2
  56.1 2.2 %collective-permute-start.18 = (bf16[272,128]{1,0:T(8,128)(2,1)S(1)}, bf16[272,128]{1,0:T(8,128)(2,1)S(1)}, u32[]{:S(2)}, u32[]{:S(2)}) collective-permute-start(bf16[272,128]{1,0:T(8,128)(2,1)S(1)} %get-tuple-element.34), channel_id=1, source_target_pairs={{0,6},{2,4},{4,2},{6,0},{1,7},{3,5},{5,3},{7,1},{8,14},{10,12},{12... | collective-permute-start | bytes 208904 | tf_op jit(solution)/shard_map/ppermute | solution.py:348
  58.4 0.0 collective-permute-start.17
  58.4 0.0 collective-permute-done.12.refs_3_
  58.4 2.2 %collective-permute-start.16 = (bf16[272,128]{1,0:T(8,128)(2,1)S(1)}, bf16[272,128]{1,0:T(8,128)(2,1)S(1)}, u32[]{:S(2)}, u32[]{:S(2)}) collective-permute-start(bf16[272,128]{1,0:T(8,128)(2,1)S(1)} %get-tuple-element.36), channel_id=1, source_target_pairs={{0,2},{2,0},{4,6},{6,4},{1,3},{3,1},{5,7},{7,5},{8,10},{10,8},{12,... | collective-permute-start | bytes 208904 | tf_op jit(solution)/shard_map/ppermute | solution.py:348
  60.6 0.0 collective-permute-done.11.refs_2_
  60.6 0.0 collective-permute-done.10.refs_1_
  60.6 1.8 %collective-permute-done.18.refs_6_ = bf16[272,128]{1,0:T(8,128)(2,1)S(1)} collective-permute-done((bf16[272,128]{1,0:T(8,128)(2,1)S(1)}, bf16[272,128]{1,0:T(8,128)(2,1)S(1)}, u32[]{:S(2)}, u32[]{:S(2)}) %collective-permute-start.18) | collective-permute-done | bytes 69664 | tf_op jit(solution)/shard_map/ppermute | solution.py:348
  62.4 1.6 %collective-permute-done.17.refs_5_ = bf16[272,128]{1,0:T(8,128)(2,1)S(1)} collective-permute-done((bf16[272,128]{1,0:T(8,128)(2,1)S(1)}, bf16[272,128]{1,0:T(8,128)(2,1)S(1)}, u32[]{:S(2)}, u32[]{:S(2)}) %collective-permute-start.17) | collective-permute-done | bytes 69664 | tf_op jit(solution)/shard_map/ppermute | solution.py:348
  64.1 0.0 collective-permute-done.16.refs_4_
  64.1 0.7 %shard_map.111 = (f32[32,512]{1,0:T(8,128)}, f32[32,512]{1,0:T(8,128)}, f32[1]{0:T(128)}) custom-call(f32[8,128]{1,0:T(8,128)S(1)} %get-tuple-element.21.gate, bf16[272,128]{1,0:T(8,128)(2,1)S(1)} %get-tuple-element.33.refs_0_, bf16[272,128]{1,0:T(8,128)(2,1)S(1)} %collective-permute-done.10.refs_1_, bf16[272,128]{1,0:T(8,128)(2,1)S(1)} %collective-permute-done.11.refs_2_, ...), custom_call_target="tpu_custom_call" | custom-call | tf_op jit(solution)/shard_map/pallas_call | solution.py:330
  (15 shorter events, 0.2 us)
Async XLA Ops:
  2.2 8.9 %collective-permute-start.2 = (bf16[32,1024]{1,0:T(8,128)(2,1)S(1)}, bf16[32,1024]{1,0:T(8,128)(2,1)S(1)}, u32[]{:S(2)}, u32[]{:S(2)}) collective-permute-start(bf16[32,1024]{1,0:T(8,128)(2,1)S(1)} %get-tuple-element.37), channel_id=1, source_target_pairs={{0,6},{2,4},{4,2},{6,0},{1,7},{3,5},{5,3},{7,1},{8,14},{10,12},{12... | collective-permute-start | bytes 196616 | tf_op jit(solution)/shard_map/ppermute | solution.py:348
  7.2 5.6 %collective-permute-start.1 = (bf16[32,1024]{1,0:T(8,128)(2,1)S(1)}, bf16[32,1024]{1,0:T(8,128)(2,1)S(1)}, u32[]{:S(2)}, u32[]{:S(2)}) collective-permute-start(bf16[32,1024]{1,0:T(8,128)(2,1)S(1)} %get-tuple-element.37), channel_id=1, source_target_pairs={{0,4},{2,6},{4,0},{6,2},{1,5},{3,7},{5,1},{7,3},{8,12},{10,14},{12... | collective-permute-start | bytes 196616 | tf_op jit(solution)/shard_map/ppermute | solution.py:348
  7.2 5.6 %collective-permute-start = (bf16[32,1024]{1,0:T(8,128)(2,1)S(1)}, bf16[32,1024]{1,0:T(8,128)(2,1)S(1)}, u32[]{:S(2)}, u32[]{:S(2)}) collective-permute-start(bf16[32,1024]{1,0:T(8,128)(2,1)S(1)} %get-tuple-element.37), channel_id=1, source_target_pairs={{0,2},{2,0},{4,6},{6,4},{1,3},{3,1},{5,7},{7,5},{8,10},{10,8},{12,... | collective-permute-start | bytes 196616 | tf_op jit(solution)/shard_map/ppermute | solution.py:348
  7.8 5.1 %collective-permute-start.4 = (bf16[32,1024]{1,0:T(8,128)(2,1)S(1)}, bf16[32,1024]{1,0:T(8,128)(2,1)S(1)}, u32[]{:S(2)}, u32[]{:S(2)}) collective-permute-start(bf16[32,1024]{1,0:T(8,128)(2,1)S(1)} %get-tuple-element.37), channel_id=1, source_target_pairs={{0,16},{1,17},{16,0},{17,1},{2,18},{3,19},{18,2},{19,3},{4,20},{5,... | collective-permute-start | bytes 196616 | tf_op jit(solution)/shard_map/ppermute | solution.py:351
  9.5 4.3 %collective-permute-start.3 = (bf16[32,1024]{1,0:T(8,128)(2,1)S(1)}, bf16[32,1024]{1,0:T(8,128)(2,1)S(1)}, u32[]{:S(2)}, u32[]{:S(2)}) collective-permute-start(bf16[32,1024]{1,0:T(8,128)(2,1)S(1)} %get-tuple-element.37), channel_id=1, source_target_pairs={{0,1},{1,0},{16,17},{17,16},{2,3},{3,2},{18,19},{19,18},{4,5},{5,4... | collective-permute-start | bytes 196616 | tf_op jit(solution)/shard_map/ppermute | solution.py:351
  13.8 15.6 %copy-start.1 = (bf16[128,4096]{1,0:T(8,128)(2,1)S(1)}, bf16[128,4096]{1,0:T(8,128)(2,1)}, u32[]{:S(2)}) copy-start(bf16[128,4096]{1,0:T(8,128)(2,1)} %dy_ref.1) | copy-start | bytes 3145732
  13.8 15.5 %copy-start = (bf16[128,4096]{1,0:T(8,128)(2,1)S(1)}, bf16[128,4096]{1,0:T(8,128)(2,1)}, u32[]{:S(2)}) copy-start(bf16[128,4096]{1,0:T(8,128)(2,1)} %q_ref.1) | copy-start | bytes 3145732
  13.8 15.5 %copy-start.2 = (s32[128]{0:T(128)S(1)}, s32[128]{0:T(128)}, u32[]{:S(2)}) copy-start(s32[128]{0:T(128)} %seg_s.1) | copy-start | bytes 1540
  13.8 15.5 %copy-start.3 = (s32[4]{0:T(128)S(1)}, s32[4]{0:T(128)}, u32[]{:S(2)}) copy-start(s32[4]{0:T(128)} %cnt_s.1) | copy-start | bytes 52
  13.8 12.7 %collective-permute-start.6 = (bf16[96,1024]{1,0:T(8,128)(2,1)S(1)}, bf16[96,1024]{1,0:T(8,128)(2,1)S(1)}, u32[]{:S(2)}, u32[]{:S(2)}) collective-permute-start(bf16[96,1024]{1,0:T(8,128)(2,1)S(1)} %pad_maximum_fusion.1), channel_id=1, source_target_pairs={{0,16},{1,17},{16,0},{17,1},{2,18},{3,19},{18,2},{19,3},{4,20},{5,... | collective-permute-start | bytes 589832 | tf_op jit(solution)/shard_map/ppermute | solution.py:351
  14.5 12.0 %collective-permute-start.5 = (bf16[96,1024]{1,0:T(8,128)(2,1)S(1)}, bf16[96,1024]{1,0:T(8,128)(2,1)S(1)}, u32[]{:S(2)}, u32[]{:S(2)}) collective-permute-start(bf16[96,1024]{1,0:T(8,128)(2,1)S(1)} %pad_maximum_fusion.1), channel_id=1, source_target_pairs={{0,1},{1,0},{16,17},{17,16},{2,3},{3,2},{18,19},{19,18},{4,5},{5,4... | collective-permute-start | bytes 589832 | tf_op jit(solution)/shard_map/ppermute | solution.py:351
  16.0 10.5 %collective-permute-start.7 = (bf16[128,1024]{1,0:T(8,128)(2,1)S(1)}, bf16[128,1024]{1,0:T(8,128)(2,1)S(1)}, u32[]{:S(2)}, u32[]{:S(2)}) collective-permute-start(bf16[128,1024]{1,0:T(8,128)(2,1)S(1)} %pad_maximum_fusion), channel_id=1, source_target_pairs={{0,17},{1,16},{16,1},{17,0},{2,19},{3,18},{18,3},{19,2},{4,21},{5,... | collective-permute-start | bytes 786440 | tf_op jit(solution)/shard_map/ppermute | solution.py:351
  26.6 2.7 %collective-permute-start.8 = (bf16[2,2,128,1024]{3,2,1,0:T(8,128)(2,1)S(1)}, bf16[2,2,128,1024]{3,2,1,0:T(8,128)(2,1)S(1)}, u32[]{:S(2)}, u32[]{:S(2)}) collective-permute-start(bf16[2,2,128,1024]{3,2,1,0:T(8,128)(2,1)S(1)} %bitcast.28), channel_id=1, source_target_pairs={{0,8},{8,0},{1,9},{9,1},{2,10},{10,2},{3,11},{11,3},{4,12},{12,4},... | collective-permute-start | bytes 3145736 | tf_op jit(solution)/shard_map/ppermute | solution.py:354
  38.7 2.8 %collective-permute-start.9 = (bf16[2,2,4,272,128]{4,3,2,1,0:T(8,128)(2,1)S(1)}, bf16[2,2,4,272,128]{4,3,2,1,0:T(8,128)(2,1)S(1)}, u32[]{:S(2)}, u32[]{:S(2)}) collective-permute-start(bf16[2,2,4,272,128]{4,3,2,1,0:T(8,128)(2,1)S(1)} %get-tuple-element.23), channel_id=1, source_target_pairs={{0,8},{8,0},{1,9},{9,1},{2,10},{10,2},{3,11},{11,3},{4,12},{12,4},... | collective-permute-start | bytes 3342344 | tf_op jit(solution)/shard_map/ppermute | solution.py:354
  41.9 11.7 %collective-permute-start.13 = (bf16[3,272,128]{2,1,0:T(8,128)(2,1)S(1)}, bf16[3,272,128]{2,1,0:T(8,128)(2,1)S(1)}, u32[]{:S(2)}, u32[]{:S(2)}) collective-permute-start(bf16[3,272,128]{2,1,0:T(8,128)(2,1)S(1)} %get-tuple-element.27), channel_id=1, source_target_pairs={{0,1},{1,0},{16,17},{17,16},{2,3},{3,2},{18,19},{19,18},{4,5},{5,4... | collective-permute-start | bytes 626696 | tf_op jit(solution)/shard_map/ppermute | solution.py:351
  43.5 11.7 %collective-permute-start.15 = (bf16[3,272,128]{2,1,0:T(8,128)(2,1)S(1)}, bf16[3,272,128]{2,1,0:T(8,128)(2,1)S(1)}, u32[]{:S(2)}, u32[]{:S(2)}) collective-permute-start(bf16[3,272,128]{2,1,0:T(8,128)(2,1)S(1)} %get-tuple-element.28), channel_id=1, source_target_pairs={{0,17},{1,16},{16,1},{17,0},{2,19},{3,18},{18,3},{19,2},{4,21},{5,... | collective-permute-start | bytes 626696 | tf_op jit(solution)/shard_map/ppermute | solution.py:351
  44.6 11.4 %collective-permute-start.14 = (bf16[3,272,128]{2,1,0:T(8,128)(2,1)S(1)}, bf16[3,272,128]{2,1,0:T(8,128)(2,1)S(1)}, u32[]{:S(2)}, u32[]{:S(2)}) collective-permute-start(bf16[3,272,128]{2,1,0:T(8,128)(2,1)S(1)} %get-tuple-element.29), channel_id=1, source_target_pairs={{0,16},{1,17},{16,0},{17,1},{2,18},{3,19},{18,2},{19,3},{4,20},{5,... | collective-permute-start | bytes 626696 | tf_op jit(solution)/shard_map/ppermute | solution.py:351
  45.5 12.9 %collective-permute-start.12 = (bf16[272,128]{1,0:T(8,128)(2,1)S(1)}, bf16[272,128]{1,0:T(8,128)(2,1)S(1)}, u32[]{:S(2)}, u32[]{:S(2)}) collective-permute-start(bf16[272,128]{1,0:T(8,128)(2,1)S(1)} %get-tuple-element.30), channel_id=1, source_target_pairs={{0,17},{1,16},{16,1},{17,0},{2,19},{3,18},{18,3},{19,2},{4,21},{5,... | collective-permute-start | bytes 208904 | tf_op jit(solution)/shard_map/ppermute | solution.py:351
  47.2 13.3 %collective-permute-start.11 = (bf16[272,128]{1,0:T(8,128)(2,1)S(1)}, bf16[272,128]{1,0:T(8,128)(2,1)S(1)}, u32[]{:S(2)}, u32[]{:S(2)}) collective-permute-start(bf16[272,128]{1,0:T(8,128)(2,1)S(1)} %get-tuple-element.31), channel_id=1, source_target_pairs={{0,16},{1,17},{16,0},{17,1},{2,18},{3,19},{18,2},{19,3},{4,20},{5,... | collective-permute-start | bytes 208904 | tf_op jit(solution)/shard_map/ppermute | solution.py:351
  53.7 6.9 %collective-permute-start.10 = (bf16[272,128]{1,0:T(8,128)(2,1)S(1)}, bf16[272,128]{1,0:T(8,128)(2,1)S(1)}, u32[]{:S(2)}, u32[]{:S(2)}) collective-permute-start(bf16[272,128]{1,0:T(8,128)(2,1)S(1)} %get-tuple-element.32), channel_id=1, source_target_pairs={{0,1},{1,0},{16,17},{17,16},{2,3},{3,2},{18,19},{19,18},{4,5},{5,4... | collective-permute-start | bytes 208904 | tf_op jit(solution)/shard_map/ppermute | solution.py:351
  56.1 6.3 %collective-permute-start.18 = (bf16[272,128]{1,0:T(8,128)(2,1)S(1)}, bf16[272,128]{1,0:T(8,128)(2,1)S(1)}, u32[]{:S(2)}, u32[]{:S(2)}) collective-permute-start(bf16[272,128]{1,0:T(8,128)(2,1)S(1)} %get-tuple-element.34), channel_id=1, source_target_pairs={{0,6},{2,4},{4,2},{6,0},{1,7},{3,5},{5,3},{7,1},{8,14},{10,12},{12... | collective-permute-start | bytes 208904 | tf_op jit(solution)/shard_map/ppermute | solution.py:348
  58.4 5.7 %collective-permute-start.17 = (bf16[272,128]{1,0:T(8,128)(2,1)S(1)}, bf16[272,128]{1,0:T(8,128)(2,1)S(1)}, u32[]{:S(2)}, u32[]{:S(2)}) collective-permute-start(bf16[272,128]{1,0:T(8,128)(2,1)S(1)} %get-tuple-element.35), channel_id=1, source_target_pairs={{0,4},{2,6},{4,0},{6,2},{1,5},{3,7},{5,1},{7,3},{8,12},{10,14},{12... | collective-permute-start | bytes 208904 | tf_op jit(solution)/shard_map/ppermute | solution.py:348
  58.4 5.7 %collective-permute-start.16 = (bf16[272,128]{1,0:T(8,128)(2,1)S(1)}, bf16[272,128]{1,0:T(8,128)(2,1)S(1)}, u32[]{:S(2)}, u32[]{:S(2)}) collective-permute-start(bf16[272,128]{1,0:T(8,128)(2,1)S(1)} %get-tuple-element.36), channel_id=1, source_target_pairs={{0,2},{2,0},{4,6},{6,4},{1,3},{3,1},{5,7},{7,5},{8,10},{10,8},{12,... | collective-permute-start | bytes 208904 | tf_op jit(solution)/shard_map/ppermute | solution.py:348

commit v8 on v7

--- a/solution.py
+++ b/solution.py
@@ -27,7 +27,104 @@
     return lax.dot_general(a, b, dims, preferred_element_type=jnp.float32)
 
 
-def attend_kernel(
+def prepare_kernel(seg_s, seg_v, q_ref, dy_ref, qc, dc, qt, dt, rowsel):
+    tokens = q_ref.shape[0]
+    hd = rowsel.shape[2]
+    in_a = (seg_v[...] == seg_s[0]).astype(jnp.float32)
+
+    @pl.when(pl.program_id(0) == 0)
+    def _():
+        side_a = jnp.broadcast_to(in_a, (hd, tokens)).T
+        rowsel[0] = side_a.astype(jnp.bfloat16)
+        rowsel[1] = (1.0 - side_a).astype(jnp.bfloat16)
+
+    lanesel = [jnp.broadcast_to(m, (hd, tokens)).astype(jnp.bfloat16) for m in (in_a, 1.0 - in_a)]
+    for g in range(q_ref.shape[1] // hd):
+        feats = slice(g * hd, (g + 1) * hd)
+        rows = slice(g * tokens, (g + 1) * tokens)
+        for src, plain, turned in ((q_ref, qc, qt), (dy_ref, dc, dt)):
+            x = src[:, feats]
+            xt = x.T
+            for i in range(2):
+                side = slice(i * hd, (i + 1) * hd)
+                plain[0, rows, side] = x * rowsel[i]
+                turned[0, side, rows] = xt * lanesel[i]
+
+
+def prepare(hd, seg, q, dy):
+    tokens, feats = q.shape
+    block = feats // KV_HEADS
+    rows = block // hd * tokens
+    cut = pl.BlockSpec((tokens, block), lambda i: (0, i))
+    shapes = [(rows, 2 * hd)] * 2 + [(2 * hd, rows)] * 2
+    return pl.pallas_call(
+        prepare_kernel,
+        grid=(KV_HEADS,),
+        in_specs=[
+            pl.BlockSpec(memory_space=pltpu.SMEM),
+            pl.BlockSpec((1, tokens), lambda i: (0, 0)),
+            cut,
+            cut,
+        ],
+        out_specs=[pl.BlockSpec((1,) + s, lambda i: (i, 0, 0)) for s in shapes],
+        out_shape=[jax.ShapeDtypeStruct((KV_HEADS,) + s, jnp.bfloat16) for s in shapes],
+        scratch_shapes=[pltpu.VMEM((2, tokens, hd), jnp.bfloat16)],
+        compiler_params=pltpu.CompilerParams(vmem_limit_bytes=16 * 1024 * 1024),
+        cost_estimate=pl.CostEstimate(flops=4 * 10**9, bytes_accessed=20 * q.size, transcendentals=0),
+    )(seg, seg.reshape(1, tokens), q, dy)
+
+
+def outputs_kernel(seg_s, gate_s, seg_v, p16, ds16, k_ref, v_ref, y_ref, dq_ref):
+    tokens = y_ref.shape[0]
+    hd = k_ref.shape[2]
+    span = 2 * tokens
+    in_a = seg_v[...] == seg_s[0]
+    in_a2 = jnp.concatenate([in_a, in_a], axis=1)
+    tg2 = jnp.tanh(jnp.full((1, span), gate_s[0], jnp.float32))
+    kcat_t = jnp.concatenate([k_ref[0], k_ref[1]], axis=1).T
+    vcat_t = jnp.concatenate([v_ref[0], v_ref[1]], axis=1).T
+    for h in range(y_ref.shape[1] // hd // 2):
+        rows = slice(h * span, (h + 1) * span)
+        o = mm(vcat_t, p16[0, :, rows], NN)
+        o = (tg2 * jnp.where(in_a2, o[:hd], o[hd:])).astype(jnp.bfloat16)
+        dq = mm(kcat_t, ds16[0, :, rows], NN)
+        dq = jnp.where(in_a2, dq[:hd], dq[hd:]).astype(jnp.bfloat16)
+        for j in range(2):
+            feats = slice((2 * h + j) * hd, (2 * h + j + 1) * hd)
+            toks = slice(j * tokens, (j + 1) * tokens)
+            y_ref[:, feats] = o[:, toks].T
+            dq_ref[:, feats] = dq[:, toks].T
+
+
+def outputs(seg, gate, p16, ds16, kv):
+    tokens = seg.shape[0]
+    slots, rows = p16.shape[1:]
+    hd = kv.shape[2] // 2 // KV_HEADS
+    block = rows // tokens * hd
+    smem = pl.BlockSpec(memory_space=pltpu.SMEM)
+    full = pl.BlockSpec((1, slots, rows), lambda i: (i, 0, 0))
+    cut = pl.BlockSpec((tokens, block), lambda i: (0, i))
+    shape = jax.ShapeDtypeStruct((tokens, KV_HEADS * block), jnp.bfloat16)
+    return pl.pallas_call(
+        outputs_kernel,
+        grid=(KV_HEADS,),
+        in_specs=[
+            smem,
+            smem,
+            pl.BlockSpec((1, tokens), lambda i: (0, 0)),
+            full,
+            full,
+            pl.BlockSpec((2, slots, hd), lambda i: (0, 0, i)),
+            pl.BlockSpec((2, slots, hd), lambda i: (0, 0, KV_HEADS + i)),
+        ],
+        out_specs=[cut, cut],
+        out_shape=[shape, shape],
+        compiler_params=pltpu.CompilerParams(vmem_limit_bytes=16 * 1024 * 1024),
+        cost_estimate=pl.CostEstimate(flops=5 * 10**9, bytes_accessed=12 * p16.size, transcendentals=0),
+    )(seg, gate, seg.reshape(1, tokens), p16, ds16, kv, kv)
+
+
+def scores_kernel(
     mine,
     cols,
     folded,
@@ -35,34 +132,32 @@
     cnt_s,
     gate_s,
     seg_v,
-    q_ref,
-    dy_ref,
+    qc,
+    dc,
+    qt,
+    dt,
     own,
     other,
-    y_ref,
-    dq_ref,
+    p16,
+    ds16,
+    kv_out,
     part_own,
     part_other,
     g_ref,
     kv,
     acc,
-    qc,
-    dc,
-    p16,
-    ds16,
     sbuf,
     dbuf,
     bias,
-    rowsel,
     sems,
 ):
     step = pl.program_id(0)
     heads = pl.num_programs(0)
-    tokens = q_ref.shape[0]
+    tokens = seg_v.shape[1]
     slots, width = kv.shape[1], kv.shape[2] // 2
     half = slots // 2
     hd = width // heads
-    group = q_ref.shape[1] // hd
+    group = qc.shape[1] // tokens
     scale = 1.0 / hd**0.5
     core, xpos = lax.axis_index("core"), lax.axis_index("x")
     ypos, zpos = lax.axis_index("y"), lax.axis_index("z")
@@ -96,34 +191,18 @@
             z = z ^ zpos
         tile = (z * (2 * mine) + y * mine + n % mine) // TILE_TOK
         bias[...] = jnp.where(tile < jnp.where(in_a, cnt_s[img_a], cnt_s[img_b]), 0.0, NEG)
-        side_a = jnp.broadcast_to(in_a.astype(jnp.float32), (hd, tokens)).T
-        rowsel[0] = side_a.astype(jnp.bfloat16)
-        rowsel[1] = (1.0 - side_a).astype(jnp.bfloat16)
         fetch(0, img_a, False)
         fetch(1, img_b, False)
+        pltpu.make_async_copy(kv, kv_out, sems.at[2]).start()
 
     kcols = pl.ds(pl.multiple_of(step * hd, hd), hd)
     vcols = pl.ds(pl.multiple_of(width + step * hd, hd), hd)
     kcat = jnp.concatenate([kv[0, :, kcols], kv[1, :, kcols]], axis=1)
     vcat = jnp.concatenate([kv[0, :, vcols], kv[1, :, vcols]], axis=1)
-    kcat_t = kcat.T
-    vcat_t = vcat.T
-    for g in range(group):
-        feats = slice(g * hd, (g + 1) * hd)
-        rows = slice(g * tokens, (g + 1) * tokens)
-        q = q_ref[:, feats]
-        dy = dy_ref[:, feats]
-        for i in range(2):
-            side = slice(i * hd, (i + 1) * hd)
-            qc[rows, side] = q * rowsel[i]
-            dc[rows, side] = dy * rowsel[i]
-
     span = 2 * tokens
     blocks = group // 2
     strips = [slice(i, i + STRIP) for i in range(0, slots, STRIP)]
-    in_a2 = jnp.concatenate([in_a, in_a], axis=1)
-    tg2 = jnp.concatenate([tg, tg], axis=1)
-    slope = scale * tg2
+    slope = scale * jnp.concatenate([tg, tg], axis=1)
 
     def fold8(x):
         return jnp.sum(x.reshape(x.shape[0] // 8, 8, x.shape[1]), axis=0)
@@ -131,13 +210,13 @@
     def products(h):
         i = h % 2
         rows = slice(h * span, (h + 1) * span)
-        s = mm(kcat, qc[rows, :], NT)
+        s = mm(kcat, qt[0, :, rows], NN)
         top = jnp.full((8, span), NEG, jnp.float32)
         for strip in strips:
             x = s[strip] + jnp.concatenate([bias[strip], bias[strip]], axis=1)
             sbuf[i, strip] = x
             top = jnp.maximum(top, jnp.max(x.reshape(STRIP // 8, 8, span), axis=0))
-        dbuf[i] = mm(vcat, dc[rows, :], NT)
+        dbuf[i] = mm(vcat, dt[0, :, rows], NN)
         return top
 
     def softmax(h, top):
@@ -155,24 +234,12 @@
         delta = slope * (inv * jnp.sum(dots, axis=0, keepdims=True))
         for strip in strips:
             p = sbuf[i, strip] * inv
-            p16[strip, rows] = p.astype(jnp.bfloat16)
-            ds16[strip, rows] = (p * (slope * dbuf[i, strip] - delta)).astype(jnp.bfloat16)
-
-    def outputs(h):
-        rows = slice(h * span, (h + 1) * span)
-        o = mm(vcat_t, p16[:, rows], NN)
-        o = (tg2 * jnp.where(in_a2, o[:hd], o[hd:])).astype(jnp.bfloat16)
-        dq = mm(kcat_t, ds16[:, rows], NN)
-        dq = jnp.where(in_a2, dq[:hd], dq[hd:]).astype(jnp.bfloat16)
-        for j in range(2):
-            feats = slice((2 * h + j) * hd, (2 * h + j + 1) * hd)
-            toks = slice(j * tokens, (j + 1) * tokens)
-            y_ref[:, feats] = o[:, toks].T
-            dq_ref[:, feats] = dq[:, toks].T
+            p16[0, strip, rows] = p.astype(jnp.bfloat16)
+            ds16[0, strip, rows] = (p * (slope * dbuf[i, strip] - delta)).astype(jnp.bfloat16)
 
     def slot_grads(lo, hi):
         rows = slice(lo * span, hi * span)
-        return mm(ds16[:, rows], qc[rows, :], NN), mm(p16[:, rows], dc[rows, :], NN)
+        return mm(ds16[0, :, rows], qc[0, rows, :], NN), mm(p16[0, :, rows], dc[0, rows, :], NN)
 
     top = products(0)
     dk = dv = 0.0
@@ -180,7 +247,6 @@
         ahead = products(h + 1) if h + 1 < blocks else None
         softmax(h, top)
         top = ahead
-        outputs(h)
         if h % 2:
             more = slot_grads(h - 1, h + 1)
             dk, dv = dk + more[0], dv + more[1]
@@ -201,8 +267,8 @@
     def leave(rows, i):
         lay = slice(None), slice(None), slice(None), rows
         return (
-            pltpu.make_async_copy(acc.at[(1 - core,) + lay], part_other.at[lay], sems.at[2 + 2 * i]),
-            pltpu.make_async_copy(acc.at[(core,) + lay], part_own.at[lay], sems.at[3 + 2 * i]),
+            pltpu.make_async_copy(acc.at[(1 - core,) + lay], part_other.at[lay], sems.at[3 + 2 * i]),
+            pltpu.make_async_copy(acc.at[(core,) + lay], part_own.at[lay], sems.at[4 + 2 * i]),
         )
 
     def head_rows(h):
@@ -240,38 +306,36 @@
                     c.wait()
         for c in tail:
             c.wait()
-
-
-def attend(mine, cols, folded, seg, counts, gate, q, dy, own, other):
-    tokens, feats = q.shape
+        pltpu.make_async_copy(kv, kv_out, sems.at[2]).wait()
+
+
+def scores(mine, cols, folded, seg, counts, gate, prepared, own, other):
+    tokens = seg.shape[0]
     slots, width2 = 2 * own.shape[2], own.shape[3]
     hd = width2 // 2 // KV_HEADS
-    block = feats // KV_HEADS
-    rows = block // hd * tokens
+    rows = prepared[0].shape[1]
     smem = pl.BlockSpec(memory_space=pltpu.SMEM)
     hbm = pl.BlockSpec(memory_space=pl.ANY)
-    cut = pl.BlockSpec((tokens, block), lambda i: (0, i))
     gspec = pl.BlockSpec((8, hd), lambda i: (0, 0))
-    flops = 12 * KV_HEADS * rows * slots * hd * 2
+    full = pl.BlockSpec((1, slots, rows), lambda i: (i, 0, 0))
     pieces = 8 if folded else 2
     part = (2, 2, pieces // 2, 2 * KV_HEADS * (slots // pieces) + GROWS, hd)
     return pl.pallas_call(
-        functools.partial(attend_kernel, mine, cols, folded),
+        functools.partial(scores_kernel, mine, cols, folded),
         grid=(KV_HEADS,),
         in_specs=[
             smem,
             smem,
             smem,
             pl.BlockSpec((1, tokens), lambda i: (0, 0)),
-            cut,
-            cut,
-            hbm,
-            hbm,
-        ],
-        out_specs=[cut, cut, hbm, hbm, gspec],
+        ]
+        + [pl.BlockSpec((1,) + x.shape[1:], lambda i: (i, 0, 0)) for x in prepared]
+        + [hbm, hbm],
+        out_specs=[full, full, hbm, hbm, hbm, gspec],
         out_shape=[
-            jax.ShapeDtypeStruct(q.shape, jnp.bfloat16),
-            jax.ShapeDtypeStruct(q.shape, jnp.bfloat16),
+            jax.ShapeDtypeStruct((KV_HEADS, slots, rows), jnp.bfloat16),
+            jax.ShapeDtypeStruct((KV_HEADS, slots, rows), jnp.bfloat16),
+            jax.ShapeDtypeStruct((2, slots, width2), jnp.bfloat16),
             jax.ShapeDtypeStruct(part, jnp.bfloat16),
             jax.ShapeDtypeStruct(part, jnp.bfloat16),
             jax.ShapeDtypeStruct((8, hd), jnp.float32),
@@ -279,25 +343,18 @@
         scratch_shapes=[
             pltpu.VMEM((2, slots, width2), jnp.bfloat16),
             pltpu.VMEM((2,) + part, jnp.bfloat16),
-            pltpu.VMEM((rows, 2 * hd), jnp.bfloat16),
-            pltpu.VMEM((rows, 2 * hd), jnp.bfloat16),
-            pltpu.VMEM((slots, rows), jnp.bfloat16),
-            pltpu.VMEM((slots, rows), jnp.bfloat16),
             pltpu.VMEM((2, slots, 2 * tokens), jnp.float32),
             pltpu.VMEM((2, slots, 2 * tokens), jnp.float32),
             pltpu.VMEM((slots, tokens), jnp.float32),
-            pltpu.VMEM((2, tokens, hd), jnp.bfloat16),
-            pltpu.SemaphoreType.DMA((4 + 4 * KV_HEADS,)),
+            pltpu.SemaphoreType.DMA((5 + 4 * KV_HEADS,)),
         ],
-        compiler_params=pltpu.CompilerParams(
-            dimension_semantics=("arbitrary",), vmem_limit_bytes=32 * 1024 * 1024
-        ),
+        compiler_params=pltpu.CompilerParams(vmem_limit_bytes=28 * 1024 * 1024),
         cost_estimate=pl.CostEstimate(
-            flops=flops,
-            bytes_accessed=8 * q.size + 8 * own.size,
+            flops=8 * KV_HEADS * rows * slots * hd * 2,
+            bytes_accessed=12 * KV_HEADS * rows * slots,
             transcendentals=KV_HEADS * rows * slots,
         ),
-    )(seg, counts, gate, seg.reshape(1, tokens), q, dy, own, other)
+    )(seg, counts, gate, seg.reshape(1, tokens), *prepared, own, other)
 
 
 def add_up(refs, at):
@@ -353,32 +410,37 @@
     def send_core(x):
         return lax.ppermute(x, "core", [(0, 1), (1, 0)])
 
-    kv = jnp.concatenate([keys, values], axis=1)
+    kv = lax.optimization_barrier(jnp.concatenate([keys, values], axis=1))
     if folded:
         line = [send_z(kv, k) for k in LINE]
         near = [send_xy(kv, p) for p in (1, 2)]
-        line, near = lax.optimization_barrier((jnp.concatenate(line, axis=0), near))
+        line, near, seg_late = lax.optimization_barrier((jnp.concatenate(line, axis=0), near, seg_image))
         block = jnp.concatenate([kv, line], axis=0)
         diag = send_xy(block, 3)
         own = [block, near[0], send_xy(line, 1), near[1], send_xy(line, 2), diag]
     else:
         line = lax.all_gather(kv, "z", axis=0, tiled=True)
         own = [line] + [send_xy(line, p) for p in PEERS]
+        seg_late = seg_image
     own = jnp.concatenate(own, axis=0).reshape(2, 2, half, 2 * width)
+    prepared = list(prepare(hd, seg_late, queries, cotangent))
+    own, prepared[0] = lax.optimization_barrier((own, prepared[0]))
     other = send_core(own)
-
-    y, dq, part_own, part_other, g = attend(
-        mine, cols, folded, seg_image, tile_counts, gate, queries, cotangent, own, other
+    p16, ds16, kv_used, part_own, part_other, g = scores(
+        mine, cols, folded, seg_image, tile_counts, gate, prepared, own, other
     )
 
     part = (part_own.astype(f32) + send_core(part_other).astype(f32)).astype(bf16)
+    part, p16 = lax.optimization_barrier((part, p16))
+    y, dq = outputs(seg_image, gate, p16, ds16, kv_used)
     part = part.reshape((4,) + part.shape[2:])
     if folded:
         line = part[0, 1:].astype(f32)
         for p in PEERS:
             line = line + send_xy(part[p, 1:], p).astype(f32)
-        line = line.astype(bf16)
-        parts = [part[0, 0]] + [send_xy(part[p, 0], p) for p in PEERS]
+        late, y = lax.optimization_barrier((part, y))
+        line, y = lax.optimization_barrier((line.astype(bf16), y))
+        parts = [late[0, 0]] + [send_xy(late[p, 0], p) for p in PEERS]
         parts += [send_z(line[k - 1], k) for k in LINE]
     else:
         line = part[0, 0].astype(f32)

time: 65 us -> 66.3 us (1.020)
  Pallas kernels: 10.1 us -> 14.3 us
  waiting for transfers between devices: 25.8 us -> 23.2 us
  starting transfers between devices: 25.3 us -> 24.4 us
  other arithmetic: 0.47 us -> 1.33 us
    ppermute x11, waiting for transfers between devices: 15.9 us -> 11 us  [send_xy(): return lax.ppermute(x, ('x', 'y'), [(i, i ^ p) for i in range(4)])]
    pallas_call x1 -> x3, Pallas kernels: 9.39 us -> 13.6 us  [the longest x1 7.15 us: scores(): pl.pallas_call(functools.partial(scores_kernel, mine, cols, folded), grid...]
    ppermute x6, waiting for transfers between devices: 5.29 us -> 7.59 us  [send_z(): return lax.ppermute(x, 'z', [(i, i ^ k) for i in range(cols)])]
    ppermute x6, starting transfers between devices: 10.1 us -> 8.84 us  [send_z(): return lax.ppermute(x, 'z', [(i, i ^ k) for i in range(cols)])]
    concatenate x1 -> x2, other arithmetic: 0.01 us -> 0.88 us  [the longest x1 0.87 us: local(): kv = lax.optimization_barrier(jnp.concatenate([keys, values], axis=1))]
    concatenate x1 -> x0, local copies, waits for them, and re-layouts: 0.76 us -> none  [local(): kv = jnp.concatenate([keys, values], axis=1)]
  transfers between devices with their start and end apart: 19 -> 19, of which waited for: 9 -> 9; matrix products, arithmetic and copies ran while one was open for 0% -> 0% of each run, Pallas kernels for 0% -> 4%
where the time goes in v8:
time: 66.3 us; the launch traced here: 66.1 us
  starting transfers between devices  24.4 us (37%)
  waiting for transfers between devices  23.2 us (35%)
  Pallas kernels  14.3 us (22%)
  between operations  1.46 us (2%)
  local copies, waits for them, and re-layouts  1.4 us (2%)
  other arithmetic  1.33 us (2%)
    ppermute x11, starting transfers between devices, send_xy(): return lax.ppermute(x, ('x', 'y'), [(i, i ^ p) for i in range(4)])  15.3 us
    ppermute x11, waiting for transfers between devices, send_xy(): return lax.ppermute(x, ('x', 'y'), [(i, i ^ p) for i in range(4)])  11 us
    ppermute x6, starting transfers between devices, send_z(): return lax.ppermute(x, 'z', [(i, i ^ k) for i in range(cols)])  8.84 us
    ppermute x6, waiting for transfers between devices, send_z(): return lax.ppermute(x, 'z', [(i, i ^ k) for i in range(cols)])  7.59 us
    pallas_call x1, Pallas kernels, scores(): pl.pallas_call(functools.partial(scores_kernel, mine, cols, folded), grid...  7.15 us
    ppermute x2, waiting for transfers between devices, send_core(): return lax.ppermute(x, 'core', [(0, 1), (1, 0)])  4.63 us
    pallas_call x1, Pallas kernels, outputs(): pl.pallas_call(outputs_kernel, grid=(KV_HEADS,), in_specs=[smem, smem, pl...  4 us
    pallas_call x1, Pallas kernels, prepare(): pl.pallas_call(prepare_kernel, grid=(KV_HEADS,), in_specs=[pl.BlockSpec(m...  2.47 us
  transfers between devices with their start and end apart: 19, of which 9 were waited for; matrix products, arithmetic and copies ran while one was open for 0% of the time, Pallas kernels for 4%

profile of v8, /device:TPU:0, one launch (start us, length us, event | category | flops | bytes accessed | tf_op | source)
XLA Modules:
  0.0 66.1 jit_solution(11674407262082838873)
XLA Ops:
  0.7 0.9 %pad_maximum_fusion.2 = bf16[32,1024]{1,0:T(8,128)(2,1)S(1)} fusion(bf16[32,512]{1,0:T(8,128)(2,1)} %param.9, bf16[32,512]{1,0:T(8,128)(2,1)} %param.8), kind=kLoop, calls=%fused_computation.18 | loop fusion | flops 131072 | bytes 131072 | tf_op jit(solution)/shard_map/concatenate | solution.py:413
  1.5 2.9 %collective-permute-start.4 = (bf16[32,1024]{1,0:T(8,128)(2,1)S(1)}, bf16[32,1024]{1,0:T(8,128)(2,1)S(1)}, u32[]{:S(2)}, u32[]{:S(2)}) collective-permute-start(bf16[32,1024]{1,0:T(8,128)(2,1)S(1)} %pad_maximum_fusion.2), channel_id=1, source_target_pairs={{0,16},{1,17},{16,0},{17,1},{2,18},{3,19},{18,2},{19,3},{4,20},{5,... | collective-permute-start | bytes 196616 | tf_op jit(solution)/shard_map/ppermute | solution.py:408
  4.5 1.5 %collective-permute-start.3 = (bf16[32,1024]{1,0:T(8,128)(2,1)S(1)}, bf16[32,1024]{1,0:T(8,128)(2,1)S(1)}, u32[]{:S(2)}, u32[]{:S(2)}) collective-permute-start(bf16[32,1024]{1,0:T(8,128)(2,1)S(1)} %pad_maximum_fusion.2), channel_id=1, source_target_pairs={{0,1},{1,0},{16,17},{17,16},{2,3},{3,2},{18,19},{19,18},{4,5},{5,4... | collective-permute-start | bytes 196616 | tf_op jit(solution)/shard_map/ppermute | solution.py:408
  6.0 3.6 %collective-permute-start.2 = (bf16[32,1024]{1,0:T(8,128)(2,1)S(1)}, bf16[32,1024]{1,0:T(8,128)(2,1)S(1)}, u32[]{:S(2)}, u32[]{:S(2)}) collective-permute-start(bf16[32,1024]{1,0:T(8,128)(2,1)S(1)} %pad_maximum_fusion.2), channel_id=1, source_target_pairs={{0,6},{2,4},{4,2},{6,0},{1,7},{3,5},{5,3},{7,1},{8,14},{10,12},{12... | collective-permute-start | bytes 196616 | tf_op jit(solution)/shard_map/ppermute | solution.py:405
  9.6 0.0 collective-permute-start.1
  9.6 0.8 %collective-permute-start = (bf16[32,1024]{1,0:T(8,128)(2,1)S(1)}, bf16[32,1024]{1,0:T(8,128)(2,1)S(1)}, u32[]{:S(2)}, u32[]{:S(2)}) collective-permute-start(bf16[32,1024]{1,0:T(8,128)(2,1)S(1)} %pad_maximum_fusion.2), channel_id=1, source_target_pairs={{0,2},{2,0},{4,6},{6,4},{1,3},{3,1},{5,7},{7,5},{8,10},{10,8},{12,... | collective-permute-start | bytes 196616 | tf_op jit(solution)/shard_map/ppermute | solution.py:405
  10.4 2.2 %collective-permute-done.2 = bf16[32,1024]{1,0:T(8,128)(2,1)S(1)} collective-permute-done((bf16[32,1024]{1,0:T(8,128)(2,1)S(1)}, bf16[32,1024]{1,0:T(8,128)(2,1)S(1)}, u32[]{:S(2)}, u32[]{:S(2)}) %collective-permute-start.2) | collective-permute-done | bytes 65568 | tf_op jit(solution)/shard_map/ppermute | solution.py:405
  12.6 2.3 %collective-permute-done.1 = bf16[32,1024]{1,0:T(8,128)(2,1)S(1)} collective-permute-done((bf16[32,1024]{1,0:T(8,128)(2,1)S(1)}, bf16[32,1024]{1,0:T(8,128)(2,1)S(1)}, u32[]{:S(2)}, u32[]{:S(2)}) %collective-permute-start.1) | collective-permute-done | bytes 65568 | tf_op jit(solution)/shard_map/ppermute | solution.py:405
  14.8 0.0 collective-permute-done
  14.9 0.0 collective-permute-done.4
  14.9 0.0 collective-permute-done.3
  14.9 0.6 collective-permute-start.6
  15.5 0.5 collective-permute-start.5
  16.0 2.5 %collective-permute-start.7 = (bf16[128,1024]{1,0:T(8,128)(2,1)S(1)}, bf16[128,1024]{1,0:T(8,128)(2,1)S(1)}, u32[]{:S(2)}, u32[]{:S(2)}) collective-permute-start(bf16[128,1024]{1,0:T(8,128)(2,1)S(1)} %pad_maximum_fusion), channel_id=1, source_target_pairs={{0,17},{1,16},{16,1},{17,0},{2,19},{3,18},{18,3},{19,2},{4,21},{5,... | collective-permute-start | bytes 786440 | tf_op jit(solution)/shard_map/ppermute | solution.py:408
  18.5 0.0 copy-done
  18.5 1.2 %copy-done.3 = bf16[128,4096]{1,0:T(8,128)(2,1)S(1)} copy-done((bf16[128,4096]{1,0:T(8,128)(2,1)S(1)}, bf16[128,4096]{1,0:T(8,128)(2,1)}, u32[]{:S(2)}) %copy-start.3) | copy-done | bytes 1048600
  19.7 2.5 %shard_map.110 = (bf16[4,1024,256]{2,1,0:T(8,128)(2,1)S(1)}, bf16[4,1024,256]{2,1,0:T(8,128)(2,1)S(1)}, bf16[4,256,1024]{2,1,0:T(8,128)(2,1)S(1)}, bf16[4,256,1024]{2,1,0:T(8,128)(2,1)S(1)}) custom-call(s32[128]{0:T(128)S(1)} %copy-done, s32[1,128]{1,0:T(1,128)S(1)} %bitcast.31, bf16[128,4096]{1,0:T(8,128)(2,1)S(1)} %copy-done.2, bf16[128,4096]{1,0:T(8,128)(2,1)S(1)} %copy-done.3), custom_call_target="tpu_custom_call" | custom-call | flops 4000000000 | bytes 10485760 | tf_op jit(solution)/shard_map/pallas_call | solution.py:60
  22.2 0.0 copy-start.1
  22.3 4.2 %collective-permute-done.5 = bf16[96,1024]{1,0:T(8,128)(2,1)S(1)} collective-permute-done((bf16[96,1024]{1,0:T(8,128)(2,1)S(1)}, bf16[96,1024]{1,0:T(8,128)(2,1)S(1)}, u32[]{:S(2)}, u32[]{:S(2)}) %collective-permute-start.5) | collective-permute-done | bytes 196640 | tf_op jit(solution)/shard_map/ppermute | solution.py:408
  26.6 0.0 collective-permute-done.6
  26.6 0.0 collective-permute-done.7
  26.6 0.1 collective-permute-start.8
  27.4 2.0 %collective-permute-done.8.other = bf16[2,2,128,1024]{3,2,1,0:T(8,128)(2,1)S(1)} collective-permute-done((bf16[2,2,128,1024]{3,2,1,0:T(8,128)(2,1)S(1)}, bf16[2,2,128,1024]{3,2,1,0:T(8,128)(2,1)S(1)}, u32[]{:S(2)}, u32[]{:S(2)}) %collective-permute-start.8) | collective-permute-done | bytes 1048608 | tf_op jit(solution)/shard_map/ppermute | solution.py:411
  29.4 7.2 %shard_map.111 = (bf16[4,256,1024]{2,1,0:T(8,128)(2,1)S(1)}, bf16[4,256,1024]{2,1,0:T(8,128)(2,1)S(1)}, bf16[2,256,1024]{2,1,0:T(8,128)(2,1)S(1)}, bf16[2,2,4,27...) custom-call(s32[128]{0:T(128)S(1)} %copy-done, s32[4]{0:T(128)S(1)} %copy-done.1, ...), custom_call_target="tpu_custom_call" | custom-call | flops 2147483648 | bytes 12582912 | tf_op jit(solution)/shard_map/pallas_call | solution.py:323
  36.5 0.2 collective-permute-start.9
  36.7 2.6 %collective-permute-done.9 = bf16[2,2,4,272,128]{4,3,2,1,0:T(8,128)(2,1)S(1)} collective-permute-done((bf16[2,2,4,272,128]{4,3,2,1,0:T(8,128)(2,1)S(1)}, bf16[2,2,4,272,128]{4,3,2,1,0:T(8,128)(2,1)S(1)}, u32[]{:S(2)}, u32[]{:S(2)}) %collective-permute-start.9) | collective-permute-done | bytes 1114144 | tf_op jit(solution)/shard_map/ppermute | solution.py:411
  39.3 0.3 add_convert_fusion
  39.7 4.0 %shard_map.112 = (bf16[128,4096]{1,0:T(8,128)(2,1)}, bf16[128,4096]{1,0:T(8,128)(2,1)}) custom-call(s32[128]{0:T(128)S(1)} %copy-done, f32[1]{0:T(128)S(6)} %copy.18.gate_s, s32[1,128]{1,0:T(1,128)S(1)} %bitcast.33, bf16[4,256,1024]{2,1,0:T(8,128)(2,1)S(1)} %get-tuple-element.46.p16, bf16[4,256,1024]{2,1,0:T(8,128)(2,1)S(1)} %get-tuple-element.47.ds16, ...), custom_call_target="tpu_custom_call" | custom-call | flops 5000000000 | bytes 12582912 | tf_op jit(solution)/shard_map/pallas_call | solution.py:108
  43.7 1.1 %collective-permute-start.10 = (bf16[3,272,128]{2,1,0:T(8,128)(2,1)S(1)}, bf16[3,272,128]{2,1,0:T(8,128)(2,1)S(1)}, u32[]{:S(2)}, u32[]{:S(2)}) collective-permute-start(bf16[3,272,128]{2,1,0:T(8,128)(2,1)S(1)} %get-tuple-element.63), channel_id=1, source_target_pairs={{0,1},{1,0},{16,17},{17,16},{2,3},{3,2},{18,19},{19,18},{4,5},{5,4... | collective-permute-start | bytes 626696 | tf_op jit(solution)/shard_map/ppermute | solution.py:408
  44.8 1.8 %collective-permute-start.12 = (bf16[3,272,128]{2,1,0:T(8,128)(2,1)S(1)}, bf16[3,272,128]{2,1,0:T(8,128)(2,1)S(1)}, u32[]{:S(2)}, u32[]{:S(2)}) collective-permute-start(bf16[3,272,128]{2,1,0:T(8,128)(2,1)S(1)} %get-tuple-element.64), channel_id=1, source_target_pairs={{0,17},{1,16},{16,1},{17,0},{2,19},{3,18},{18,3},{19,2},{4,21},{5,... | collective-permute-start | bytes 626696 | tf_op jit(solution)/shard_map/ppermute | solution.py:408
  46.6 0.5 collective-permute-start.11
  47.2 1.6 %collective-permute-start.15 = (bf16[272,128]{1,0:T(8,128)(2,1)S(1)}, bf16[272,128]{1,0:T(8,128)(2,1)S(1)}, u32[]{:S(2)}, u32[]{:S(2)}) collective-permute-start(bf16[272,128]{1,0:T(8,128)(2,1)S(1)} %get-tuple-element.59), channel_id=1, source_target_pairs={{0,17},{1,16},{16,1},{17,0},{2,19},{3,18},{18,3},{19,2},{4,21},{5,... | collective-permute-start | bytes 208904 | tf_op jit(solution)/shard_map/ppermute | solution.py:408
  48.8 1.0 %collective-permute-start.14 = (bf16[272,128]{1,0:T(8,128)(2,1)S(1)}, bf16[272,128]{1,0:T(8,128)(2,1)S(1)}, u32[]{:S(2)}, u32[]{:S(2)}) collective-permute-start(bf16[272,128]{1,0:T(8,128)(2,1)S(1)} %get-tuple-element.60), channel_id=1, source_target_pairs={{0,16},{1,17},{16,0},{17,1},{2,18},{3,19},{18,2},{19,3},{4,20},{5,... | collective-permute-start | bytes 208904 | tf_op jit(solution)/shard_map/ppermute | solution.py:408
  49.9 5.5 %collective-permute-done.10 = bf16[3,272,128]{2,1,0:T(8,128)(2,1)S(1)} collective-permute-done((bf16[3,272,128]{2,1,0:T(8,128)(2,1)S(1)}, bf16[3,272,128]{2,1,0:T(8,128)(2,1)S(1)}, u32[]{:S(2)}, u32[]{:S(2)}) %collective-permute-start.10) | collective-permute-done | bytes 208928 | tf_op jit(solution)/shard_map/ppermute | solution.py:408
  55.4 1.1 %collective-permute-start.13 = (bf16[272,128]{1,0:T(8,128)(2,1)S(1)}, bf16[272,128]{1,0:T(8,128)(2,1)S(1)}, u32[]{:S(2)}, u32[]{:S(2)}) collective-permute-start(bf16[272,128]{1,0:T(8,128)(2,1)S(1)} %get-tuple-element.61), channel_id=1, source_target_pairs={{0,1},{1,0},{16,17},{17,16},{2,3},{3,2},{18,19},{19,18},{4,5},{5,4... | collective-permute-start | bytes 208904 | tf_op jit(solution)/shard_map/ppermute | solution.py:408
  56.5 0.0 collective-permute-done.12
  56.5 1.2 %collective-permute-done.11 = bf16[3,272,128]{2,1,0:T(8,128)(2,1)S(1)} collective-permute-done((bf16[3,272,128]{2,1,0:T(8,128)(2,1)S(1)}, bf16[3,272,128]{2,1,0:T(8,128)(2,1)S(1)}, u32[]{:S(2)}, u32[]{:S(2)}) %collective-permute-start.11) | collective-permute-done | bytes 208928 | tf_op jit(solution)/shard_map/ppermute | solution.py:408
  57.7 0.1 fusion.2
  57.8 0.9 %collective-permute-start.18 = (bf16[272,128]{1,0:T(8,128)(2,1)S(1)}, bf16[272,128]{1,0:T(8,128)(2,1)S(1)}, u32[]{:S(2)}, u32[]{:S(2)}) collective-permute-start(bf16[272,128]{1,0:T(8,128)(2,1)S(1)} %get-tuple-element.66), channel_id=1, source_target_pairs={{0,6},{2,4},{4,2},{6,0},{1,7},{3,5},{5,3},{7,1},{8,14},{10,12},{12... | collective-permute-start | bytes 208904 | tf_op jit(solution)/shard_map/ppermute | solution.py:405
  58.7 1.0 %collective-permute-start.17 = (bf16[272,128]{1,0:T(8,128)(2,1)S(1)}, bf16[272,128]{1,0:T(8,128)(2,1)S(1)}, u32[]{:S(2)}, u32[]{:S(2)}) collective-permute-start(bf16[272,128]{1,0:T(8,128)(2,1)S(1)} %get-tuple-element.67), channel_id=1, source_target_pairs={{0,4},{2,6},{4,0},{6,2},{1,5},{3,7},{5,1},{7,3},{8,12},{10,14},{12... | collective-permute-start | bytes 208904 | tf_op jit(solution)/shard_map/ppermute | solution.py:405
  59.7 0.0 collective-permute-done.15.refs_3_
  59.7 2.6 %collective-permute-start.16 = (bf16[272,128]{1,0:T(8,128)(2,1)S(1)}, bf16[272,128]{1,0:T(8,128)(2,1)S(1)}, u32[]{:S(2)}, u32[]{:S(2)}) collective-permute-start(bf16[272,128]{1,0:T(8,128)(2,1)S(1)} %get-tuple-element.68), channel_id=1, source_target_pairs={{0,2},{2,0},{4,6},{6,4},{1,3},{3,1},{5,7},{7,5},{8,10},{10,8},{12,... | collective-permute-start | bytes 208904 | tf_op jit(solution)/shard_map/ppermute | solution.py:405
  62.3 0.0 collective-permute-done.14.refs_2_
  62.3 0.0 collective-permute-done.13.refs_1_
  62.3 1.8 %collective-permute-done.18.refs_6_ = bf16[272,128]{1,0:T(8,128)(2,1)S(1)} collective-permute-done((bf16[272,128]{1,0:T(8,128)(2,1)S(1)}, bf16[272,128]{1,0:T(8,128)(2,1)S(1)}, u32[]{:S(2)}, u32[]{:S(2)}) %collective-permute-start.18) | collective-permute-done | bytes 69664 | tf_op jit(solution)/shard_map/ppermute | solution.py:405
  64.1 1.3 %collective-permute-done.17.refs_5_ = bf16[272,128]{1,0:T(8,128)(2,1)S(1)} collective-permute-done((bf16[272,128]{1,0:T(8,128)(2,1)S(1)}, bf16[272,128]{1,0:T(8,128)(2,1)S(1)}, u32[]{:S(2)}, u32[]{:S(2)}) %collective-permute-start.17) | collective-permute-done | bytes 69664 | tf_op jit(solution)/shard_map/ppermute | solution.py:405
  65.4 0.0 collective-permute-done.16.refs_4_
  65.4 0.7 %shard_map.113 = (f32[32,512]{1,0:T(8,128)}, f32[32,512]{1,0:T(8,128)}, f32[1]{0:T(128)}) custom-call(f32[8,128]{1,0:T(8,128)S(1)} %get-tuple-element.53.gate, bf16[272,128]{1,0:T(8,128)(2,1)S(1)} %get-tuple-element.62.refs_0_, bf16[272,128]{1,0:T(8,128)(2,1)S(1)} %collective-permute-done.13.refs_1_, bf16[272,128]{1,0:T(8,128)(2,1)S(1)} %collective-permute-done.14.refs_2_, ...), custom_call_target="tpu_custom_call" | custom-call | tf_op jit(solution)/shard_map/pallas_call | solution.py:387
  (17 shorter events, 0.2 us)
Async XLA Ops:
  0.6 17.9 %copy-start = (s32[128]{0:T(128)S(1)}, s32[128]{0:T(128)}, u32[]{:S(2)}) copy-start(s32[128]{0:T(128)} %seg_s.4) | copy-start | bytes 1540
  0.6 17.9 %copy-start.2 = (bf16[128,4096]{1,0:T(8,128)(2,1)S(1)}, bf16[128,4096]{1,0:T(8,128)(2,1)}, u32[]{:S(2)}) copy-start(bf16[128,4096]{1,0:T(8,128)(2,1)} %q_ref.1) | copy-start | bytes 3145732
  1.5 13.3 %collective-permute-start.4 = (bf16[32,1024]{1,0:T(8,128)(2,1)S(1)}, bf16[32,1024]{1,0:T(8,128)(2,1)S(1)}, u32[]{:S(2)}, u32[]{:S(2)}) collective-permute-start(bf16[32,1024]{1,0:T(8,128)(2,1)S(1)} %pad_maximum_fusion.2), channel_id=1, source_target_pairs={{0,16},{1,17},{16,0},{17,1},{2,18},{3,19},{18,2},{19,3},{4,20},{5,... | collective-permute-start | bytes 196616 | tf_op jit(solution)/shard_map/ppermute | solution.py:408
  4.5 10.4 %collective-permute-start.3 = (bf16[32,1024]{1,0:T(8,128)(2,1)S(1)}, bf16[32,1024]{1,0:T(8,128)(2,1)S(1)}, u32[]{:S(2)}, u32[]{:S(2)}) collective-permute-start(bf16[32,1024]{1,0:T(8,128)(2,1)S(1)} %pad_maximum_fusion.2), channel_id=1, source_target_pairs={{0,1},{1,0},{16,17},{17,16},{2,3},{3,2},{18,19},{19,18},{4,5},{5,4... | collective-permute-start | bytes 196616 | tf_op jit(solution)/shard_map/ppermute | solution.py:408
  6.0 6.6 %collective-permute-start.2 = (bf16[32,1024]{1,0:T(8,128)(2,1)S(1)}, bf16[32,1024]{1,0:T(8,128)(2,1)S(1)}, u32[]{:S(2)}, u32[]{:S(2)}) collective-permute-start(bf16[32,1024]{1,0:T(8,128)(2,1)S(1)} %pad_maximum_fusion.2), channel_id=1, source_target_pairs={{0,6},{2,4},{4,2},{6,0},{1,7},{3,5},{5,3},{7,1},{8,14},{10,12},{12... | collective-permute-start | bytes 196616 | tf_op jit(solution)/shard_map/ppermute | solution.py:405
  9.6 5.2 %collective-permute-start.1 = (bf16[32,1024]{1,0:T(8,128)(2,1)S(1)}, bf16[32,1024]{1,0:T(8,128)(2,1)S(1)}, u32[]{:S(2)}, u32[]{:S(2)}) collective-permute-start(bf16[32,1024]{1,0:T(8,128)(2,1)S(1)} %pad_maximum_fusion.2), channel_id=1, source_target_pairs={{0,4},{2,6},{4,0},{6,2},{1,5},{3,7},{5,1},{7,3},{8,12},{10,14},{12... | collective-permute-start | bytes 196616 | tf_op jit(solution)/shard_map/ppermute | solution.py:405
  9.6 5.2 %collective-permute-start = (bf16[32,1024]{1,0:T(8,128)(2,1)S(1)}, bf16[32,1024]{1,0:T(8,128)(2,1)S(1)}, u32[]{:S(2)}, u32[]{:S(2)}) collective-permute-start(bf16[32,1024]{1,0:T(8,128)(2,1)S(1)} %pad_maximum_fusion.2), channel_id=1, source_target_pairs={{0,2},{2,0},{4,6},{6,4},{1,3},{3,1},{5,7},{7,5},{8,10},{10,8},{12,... | collective-permute-start | bytes 196616 | tf_op jit(solution)/shard_map/ppermute | solution.py:405
  14.9 11.7 %collective-permute-start.6 = (bf16[96,1024]{1,0:T(8,128)(2,1)S(1)}, bf16[96,1024]{1,0:T(8,128)(2,1)S(1)}, u32[]{:S(2)}, u32[]{:S(2)}) collective-permute-start(bf16[96,1024]{1,0:T(8,128)(2,1)S(1)} %pad_maximum_fusion.1), channel_id=1, source_target_pairs={{0,16},{1,17},{16,0},{17,1},{2,18},{3,19},{18,2},{19,3},{4,20},{5,... | collective-permute-start | bytes 589832 | tf_op jit(solution)/shard_map/ppermute | solution.py:408
  15.5 11.1 %collective-permute-start.5 = (bf16[96,1024]{1,0:T(8,128)(2,1)S(1)}, bf16[96,1024]{1,0:T(8,128)(2,1)S(1)}, u32[]{:S(2)}, u32[]{:S(2)}) collective-permute-start(bf16[96,1024]{1,0:T(8,128)(2,1)S(1)} %pad_maximum_fusion.1), channel_id=1, source_target_pairs={{0,1},{1,0},{16,17},{17,16},{2,3},{3,2},{18,19},{19,18},{4,5},{5,4... | collective-permute-start | bytes 589832 | tf_op jit(solution)/shard_map/ppermute | solution.py:408
  16.0 10.6 %collective-permute-start.7 = (bf16[128,1024]{1,0:T(8,128)(2,1)S(1)}, bf16[128,1024]{1,0:T(8,128)(2,1)S(1)}, u32[]{:S(2)}, u32[]{:S(2)}) collective-permute-start(bf16[128,1024]{1,0:T(8,128)(2,1)S(1)} %pad_maximum_fusion), channel_id=1, source_target_pairs={{0,17},{1,16},{16,1},{17,0},{2,19},{3,18},{18,3},{19,2},{4,21},{5,... | collective-permute-start | bytes 786440 | tf_op jit(solution)/shard_map/ppermute | solution.py:408
  18.5 1.2 %copy-start.3 = (bf16[128,4096]{1,0:T(8,128)(2,1)S(1)}, bf16[128,4096]{1,0:T(8,128)(2,1)}, u32[]{:S(2)}) copy-start(bf16[128,4096]{1,0:T(8,128)(2,1)} %dy_ref.1) | copy-start | bytes 3145732
  22.2 7.1 %copy-start.1 = (s32[4]{0:T(128)S(1)}, s32[4]{0:T(128)}, u32[]{:S(2)}) copy-start(s32[4]{0:T(128)} %cnt_s.1) | copy-start | bytes 52
  26.6 2.7 %collective-permute-start.8 = (bf16[2,2,128,1024]{3,2,1,0:T(8,128)(2,1)S(1)}, bf16[2,2,128,1024]{3,2,1,0:T(8,128)(2,1)S(1)}, u32[]{:S(2)}, u32[]{:S(2)}) collective-permute-start(bf16[2,2,128,1024]{3,2,1,0:T(8,128)(2,1)S(1)} %bitcast.29), channel_id=1, source_target_pairs={{0,8},{8,0},{1,9},{9,1},{2,10},{10,2},{3,11},{11,3},{4,12},{12,4},... | collective-permute-start | bytes 3145736 | tf_op jit(solution)/shard_map/ppermute | solution.py:411
  36.5 2.8 %collective-permute-start.9 = (bf16[2,2,4,272,128]{4,3,2,1,0:T(8,128)(2,1)S(1)}, bf16[2,2,4,272,128]{4,3,2,1,0:T(8,128)(2,1)S(1)}, u32[]{:S(2)}, u32[]{:S(2)}) collective-permute-start(bf16[2,2,4,272,128]{4,3,2,1,0:T(8,128)(2,1)S(1)} %get-tuple-element.43), channel_id=1, source_target_pairs={{0,8},{8,0},{1,9},{9,1},{2,10},{10,2},{3,11},{11,3},{4,12},{12,4},... | collective-permute-start | bytes 3342344 | tf_op jit(solution)/shard_map/ppermute | solution.py:411
  43.7 11.7 %collective-permute-start.10 = (bf16[3,272,128]{2,1,0:T(8,128)(2,1)S(1)}, bf16[3,272,128]{2,1,0:T(8,128)(2,1)S(1)}, u32[]{:S(2)}, u32[]{:S(2)}) collective-permute-start(bf16[3,272,128]{2,1,0:T(8,128)(2,1)S(1)} %get-tuple-element.63), channel_id=1, source_target_pairs={{0,1},{1,0},{16,17},{17,16},{2,3},{3,2},{18,19},{19,18},{4,5},{5,4... | collective-permute-start | bytes 626696 | tf_op jit(solution)/shard_map/ppermute | solution.py:408
  44.8 11.7 %collective-permute-start.12 = (bf16[3,272,128]{2,1,0:T(8,128)(2,1)S(1)}, bf16[3,272,128]{2,1,0:T(8,128)(2,1)S(1)}, u32[]{:S(2)}, u32[]{:S(2)}) collective-permute-start(bf16[3,272,128]{2,1,0:T(8,128)(2,1)S(1)} %get-tuple-element.64), channel_id=1, source_target_pairs={{0,17},{1,16},{16,1},{17,0},{2,19},{3,18},{18,3},{19,2},{4,21},{5,... | collective-permute-start | bytes 626696 | tf_op jit(solution)/shard_map/ppermute | solution.py:408
  46.6 11.0 %collective-permute-start.11 = (bf16[3,272,128]{2,1,0:T(8,128)(2,1)S(1)}, bf16[3,272,128]{2,1,0:T(8,128)(2,1)S(1)}, u32[]{:S(2)}, u32[]{:S(2)}) collective-permute-start(bf16[3,272,128]{2,1,0:T(8,128)(2,1)S(1)} %get-tuple-element.65), channel_id=1, source_target_pairs={{0,16},{1,17},{16,0},{17,1},{2,18},{3,19},{18,2},{19,3},{4,20},{5,... | collective-permute-start | bytes 626696 | tf_op jit(solution)/shard_map/ppermute | solution.py:408
  47.2 12.5 %collective-permute-start.15 = (bf16[272,128]{1,0:T(8,128)(2,1)S(1)}, bf16[272,128]{1,0:T(8,128)(2,1)S(1)}, u32[]{:S(2)}, u32[]{:S(2)}) collective-permute-start(bf16[272,128]{1,0:T(8,128)(2,1)S(1)} %get-tuple-element.59), channel_id=1, source_target_pairs={{0,17},{1,16},{16,1},{17,0},{2,19},{3,18},{18,3},{19,2},{4,21},{5,... | collective-permute-start | bytes 208904 | tf_op jit(solution)/shard_map/ppermute | solution.py:408
  48.8 13.4 %collective-permute-start.14 = (bf16[272,128]{1,0:T(8,128)(2,1)S(1)}, bf16[272,128]{1,0:T(8,128)(2,1)S(1)}, u32[]{:S(2)}, u32[]{:S(2)}) collective-permute-start(bf16[272,128]{1,0:T(8,128)(2,1)S(1)} %get-tuple-element.60), channel_id=1, source_target_pairs={{0,16},{1,17},{16,0},{17,1},{2,18},{3,19},{18,2},{19,3},{4,20},{5,... | collective-permute-start | bytes 208904 | tf_op jit(solution)/shard_map/ppermute | solution.py:408
  55.4 6.9 %collective-permute-start.13 = (bf16[272,128]{1,0:T(8,128)(2,1)S(1)}, bf16[272,128]{1,0:T(8,128)(2,1)S(1)}, u32[]{:S(2)}, u32[]{:S(2)}) collective-permute-start(bf16[272,128]{1,0:T(8,128)(2,1)S(1)} %get-tuple-element.61), channel_id=1, source_target_pairs={{0,1},{1,0},{16,17},{17,16},{2,3},{3,2},{18,19},{19,18},{4,5},{5,4... | collective-permute-start | bytes 208904 | tf_op jit(solution)/shard_map/ppermute | solution.py:408
  57.8 6.3 %collective-permute-start.18 = (bf16[272,128]{1,0:T(8,128)(2,1)S(1)}, bf16[272,128]{1,0:T(8,128)(2,1)S(1)}, u32[]{:S(2)}, u32[]{:S(2)}) collective-permute-start(bf16[272,128]{1,0:T(8,128)(2,1)S(1)} %get-tuple-element.66), channel_id=1, source_target_pairs={{0,6},{2,4},{4,2},{6,0},{1,7},{3,5},{5,3},{7,1},{8,14},{10,12},{12... | collective-permute-start | bytes 208904 | tf_op jit(solution)/shard_map/ppermute | solution.py:405
  58.7 6.7 %collective-permute-start.17 = (bf16[272,128]{1,0:T(8,128)(2,1)S(1)}, bf16[272,128]{1,0:T(8,128)(2,1)S(1)}, u32[]{:S(2)}, u32[]{:S(2)}) collective-permute-start(bf16[272,128]{1,0:T(8,128)(2,1)S(1)} %get-tuple-element.67), channel_id=1, source_target_pairs={{0,4},{2,6},{4,0},{6,2},{1,5},{3,7},{5,1},{7,3},{8,12},{10,14},{12... | collective-permute-start | bytes 208904 | tf_op jit(solution)/shard_map/ppermute | solution.py:405
  59.7 5.7 %collective-permute-start.16 = (bf16[272,128]{1,0:T(8,128)(2,1)S(1)}, bf16[272,128]{1,0:T(8,128)(2,1)S(1)}, u32[]{:S(2)}, u32[]{:S(2)}) collective-permute-start(bf16[272,128]{1,0:T(8,128)(2,1)S(1)} %get-tuple-element.68), channel_id=1, source_target_pairs={{0,2},{2,0},{4,6},{6,4},{1,3},{3,1},{5,7},{7,5},{8,10},{10,8},{12,... | collective-permute-start | bytes 208904 | tf_op jit(solution)/shard_map/ppermute | solution.py:405

commit v9 on v8

--- a/solution.py
+++ b/solution.py
@@ -25,53 +25,6 @@
 
 def mm(a, b, dims):
     return lax.dot_general(a, b, dims, preferred_element_type=jnp.float32)
-
-
-def prepare_kernel(seg_s, seg_v, q_ref, dy_ref, qc, dc, qt, dt, rowsel):
-    tokens = q_ref.shape[0]
-    hd = rowsel.shape[2]
-    in_a = (seg_v[...] == seg_s[0]).astype(jnp.float32)
-
-    @pl.when(pl.program_id(0) == 0)
-    def _():
-        side_a = jnp.broadcast_to(in_a, (hd, tokens)).T
-        rowsel[0] = side_a.astype(jnp.bfloat16)
-        rowsel[1] = (1.0 - side_a).astype(jnp.bfloat16)
-
-    lanesel = [jnp.broadcast_to(m, (hd, tokens)).astype(jnp.bfloat16) for m in (in_a, 1.0 - in_a)]
-    for g in range(q_ref.shape[1] // hd):
-        feats = slice(g * hd, (g + 1) * hd)
-        rows = slice(g * tokens, (g + 1) * tokens)
-        for src, plain, turned in ((q_ref, qc, qt), (dy_ref, dc, dt)):
-            x = src[:, feats]
-            xt = x.T
-            for i in range(2):
-                side = slice(i * hd, (i + 1) * hd)
-                plain[0, rows, side] = x * rowsel[i]
-                turned[0, side, rows] = xt * lanesel[i]
-
-
-def prepare(hd, seg, q, dy):
-    tokens, feats = q.shape
-    block = feats // KV_HEADS
-    rows = block // hd * tokens
-    cut = pl.BlockSpec((tokens, block), lambda i: (0, i))
-    shapes = [(rows, 2 * hd)] * 2 + [(2 * hd, rows)] * 2
-    return pl.pallas_call(
-        prepare_kernel,
-        grid=(KV_HEADS,),
-        in_specs=[
-            pl.BlockSpec(memory_space=pltpu.SMEM),
-            pl.BlockSpec((1, tokens), lambda i: (0, 0)),
-            cut,
-            cut,
-        ],
-        out_specs=[pl.BlockSpec((1,) + s, lambda i: (i, 0, 0)) for s in shapes],
-        out_shape=[jax.ShapeDtypeStruct((KV_HEADS,) + s, jnp.bfloat16) for s in shapes],
-        scratch_shapes=[pltpu.VMEM((2, tokens, hd), jnp.bfloat16)],
-        compiler_params=pltpu.CompilerParams(vmem_limit_bytes=16 * 1024 * 1024),
-        cost_estimate=pl.CostEstimate(flops=4 * 10**9, bytes_accessed=20 * q.size, transcendentals=0),
-    )(seg, seg.reshape(1, tokens), q, dy)
 
 
 def outputs_kernel(seg_s, gate_s, seg_v, p16, ds16, k_ref, v_ref, y_ref, dq_ref):
@@ -132,10 +85,8 @@
     cnt_s,
     gate_s,
     seg_v,
-    qc,
-    dc,
-    qt,
-    dt,
+    q_ref,
+    dy_ref,
     own,
     other,
     p16,
@@ -146,6 +97,9 @@
     g_ref,
     kv,
     acc,
+    qc,
+    dc,
+    rowsel,
     sbuf,
     dbuf,
     bias,
@@ -157,7 +111,7 @@
     slots, width = kv.shape[1], kv.shape[2] // 2
     half = slots // 2
     hd = width // heads
-    group = qc.shape[1] // tokens
+    group = qc.shape[0] // tokens
     scale = 1.0 / hd**0.5
     core, xpos = lax.axis_index("core"), lax.axis_index("x")
     ypos, zpos = lax.axis_index("y"), lax.axis_index("z")
@@ -191,6 +145,9 @@
             z = z ^ zpos
         tile = (z * (2 * mine) + y * mine + n % mine) // TILE_TOK
         bias[...] = jnp.where(tile < jnp.where(in_a, cnt_s[img_a], cnt_s[img_b]), 0.0, NEG)
+        side_a = jnp.broadcast_to(in_a.astype(jnp.float32), (hd, tokens)).T
+        rowsel[0] = side_a.astype(jnp.bfloat16)
+        rowsel[1] = (1.0 - side_a).astype(jnp.bfloat16)
         fetch(0, img_a, False)
         fetch(1, img_b, False)
         pltpu.make_async_copy(kv, kv_out, sems.at[2]).start()
@@ -199,6 +156,15 @@
     vcols = pl.ds(pl.multiple_of(width + step * hd, hd), hd)
     kcat = jnp.concatenate([kv[0, :, kcols], kv[1, :, kcols]], axis=1)
     vcat = jnp.concatenate([kv[0, :, vcols], kv[1, :, vcols]], axis=1)
+    for g in range(group):
+        feats = slice(g * hd, (g + 1) * hd)
+        rows = slice(g * tokens, (g + 1) * tokens)
+        q, dy = q_ref[:, feats], dy_ref[:, feats]
+        for i in range(2):
+            side = slice(i * hd, (i + 1) * hd)
+            qc[rows, side] = q * rowsel[i]
+            dc[rows, side] = dy * rowsel[i]
+
     span = 2 * tokens
     blocks = group // 2
     strips = [slice(i, i + STRIP) for i in range(0, slots, STRIP)]
@@ -210,13 +176,13 @@
     def products(h):
         i = h % 2
         rows = slice(h * span, (h + 1) * span)
-        s = mm(kcat, qt[0, :, rows], NN)
+        s = mm(kcat, qc[rows, :], NT)
         top = jnp.full((8, span), NEG, jnp.float32)
         for strip in strips:
             x = s[strip] + jnp.concatenate([bias[strip], bias[strip]], axis=1)
             sbuf[i, strip] = x
             top = jnp.maximum(top, jnp.max(x.reshape(STRIP // 8, 8, span), axis=0))
-        dbuf[i] = mm(vcat, dt[0, :, rows], NN)
+        dbuf[i] = mm(vcat, dc[rows, :], NT)
         return top
 
     def softmax(h, top):
@@ -239,7 +205,7 @@
 
     def slot_grads(lo, hi):
         rows = slice(lo * span, hi * span)
-        return mm(ds16[0, :, rows], qc[0, rows, :], NN), mm(p16[0, :, rows], dc[0, rows, :], NN)
+        return mm(ds16[0, :, rows], qc[rows, :], NN), mm(p16[0, :, rows], dc[rows, :], NN)
 
     top = products(0)
     dk = dv = 0.0
@@ -309,11 +275,12 @@
         pltpu.make_async_copy(kv, kv_out, sems.at[2]).wait()
 
 
-def scores(mine, cols, folded, seg, counts, gate, prepared, own, other):
+def scores(mine, cols, folded, seg, counts, gate, q, dy, own, other):
     tokens = seg.shape[0]
     slots, width2 = 2 * own.shape[2], own.shape[3]
     hd = width2 // 2 // KV_HEADS
-    rows = prepared[0].shape[1]
+    block = q.shape[1] // KV_HEADS
+    rows = block // hd * tokens
     smem = pl.BlockSpec(memory_space=pltpu.SMEM)
     hbm = pl.BlockSpec(memory_space=pl.ANY)
     gspec = pl.BlockSpec((8, hd), lambda i: (0, 0))
@@ -329,7 +296,7 @@
             smem,
             pl.BlockSpec((1, tokens), lambda i: (0, 0)),
         ]
-        + [pl.BlockSpec((1,) + x.shape[1:], lambda i: (i, 0, 0)) for x in prepared]
+        + [pl.BlockSpec((tokens, block), lambda i: (0, i))] * 2
         + [hbm, hbm],
         out_specs=[full, full, hbm, hbm, hbm, gspec],
         out_shape=[
@@ -343,6 +310,9 @@
         scratch_shapes=[
             pltpu.VMEM((2, slots, width2), jnp.bfloat16),
             pltpu.VMEM((2,) + part, jnp.bfloat16),
+            pltpu.VMEM((rows, 2 * hd), jnp.bfloat16),
+            pltpu.VMEM((rows, 2 * hd), jnp.bfloat16),
+            pltpu.VMEM((2, tokens, hd), jnp.bfloat16),
             pltpu.VMEM((2, slots, 2 * tokens), jnp.float32),
             pltpu.VMEM((2, slots, 2 * tokens), jnp.float32),
             pltpu.VMEM((slots, tokens), jnp.float32),
@@ -354,7 +324,7 @@
             bytes_accessed=12 * KV_HEADS * rows * slots,
             transcendentals=KV_HEADS * rows * slots,
         ),
-    )(seg, counts, gate, seg.reshape(1, tokens), *prepared, own, other)
+    )(seg, counts, gate, seg.reshape(1, tokens), q, dy, own, other)
 
 
 def add_up(refs, at):
@@ -414,20 +384,17 @@
     if folded:
         line = [send_z(kv, k) for k in LINE]
         near = [send_xy(kv, p) for p in (1, 2)]
-        line, near, seg_late = lax.optimization_barrier((jnp.concatenate(line, axis=0), near, seg_image))
+        line, near = lax.optimization_barrier((jnp.concatenate(line, axis=0), near))
         block = jnp.concatenate([kv, line], axis=0)
         diag = send_xy(block, 3)
         own = [block, near[0], send_xy(line, 1), near[1], send_xy(line, 2), diag]
     else:
         line = lax.all_gather(kv, "z", axis=0, tiled=True)
         own = [line] + [send_xy(line, p) for p in PEERS]
-        seg_late = seg_image
     own = jnp.concatenate(own, axis=0).reshape(2, 2, half, 2 * width)
-    prepared = list(prepare(hd, seg_late, queries, cotangent))
-    own, prepared[0] = lax.optimization_barrier((own, prepared[0]))
     other = send_core(own)
     p16, ds16, kv_used, part_own, part_other, g = scores(
-        mine, cols, folded, seg_image, tile_counts, gate, prepared, own, other
+        mine, cols, folded, seg_image, tile_counts, gate, queries, cotangent, own, other
     )
 
     part = (part_own.astype(f32) + send_core(part_other).astype(f32)).astype(bf16)
@@ -435,13 +402,11 @@
     y, dq = outputs(seg_image, gate, p16, ds16, kv_used)
     part = part.reshape((4,) + part.shape[2:])
     if folded:
-        line = part[0, 1:].astype(f32)
+        line = part[0].astype(f32)
         for p in PEERS:
-            line = line + send_xy(part[p, 1:], p).astype(f32)
-        late, y = lax.optimization_barrier((part, y))
+            line = line + send_xy(part[p], p).astype(f32)
         line, y = lax.optimization_barrier((line.astype(bf16), y))
-        parts = [late[0, 0]] + [send_xy(late[p, 0], p) for p in PEERS]
-        parts += [send_z(line[k - 1], k) for k in LINE]
+        parts = [line[0]] + [send_z(line[k], k) for k in LINE]
     else:
         line = part[0, 0].astype(f32)
         for p in PEERS:

time: 66.3 us -> 65.6 us (0.989)
  waiting for transfers between devices: 23.2 us -> 29.4 us
  starting transfers between devices: 24.4 us -> 20.7 us
  Pallas kernels: 14.3 us -> 12.4 us
  local copies, waits for them, and re-layouts: 1.4 us -> 0.18 us
    ppermute x11 -> x8, waiting for transfers between devices: 11 us -> 16.4 us  [send_xy(): return lax.ppermute(x, ('x', 'y'), [(i, i ^ p) for i in range(4)])]
    ppermute x11 -> x8, starting transfers between devices: 15.3 us -> 11.6 us  [send_xy(): return lax.ppermute(x, ('x', 'y'), [(i, i ^ p) for i in range(4)])]
    pallas_call x1 -> x0, Pallas kernels: 2.47 us -> none  [prepare(): pl.pallas_call(prepare_kernel, grid=(KV_HEADS,), in_specs=[pl.BlockSpec(m...]
    unnamed x14, local copies, waits for them, and re-layouts: 1.3 us -> 0.08 us
    ppermute x6, waiting for transfers between devices: 7.59 us -> 8.38 us  [send_z(): return lax.ppermute(x, 'z', [(i, i ^ k) for i in range(cols)])]
  transfers between devices with their start and end apart: 19 -> 16, of which waited for: 9 -> 9; matrix products, arithmetic and copies ran while one was open for 0% -> 0% of each run, Pallas kernels for 4% -> 6%
where the time goes in v9:
time: 65.6 us; the launch traced here: 65.4 us
  waiting for transfers between devices  29.4 us (45%)
  starting transfers between devices  20.7 us (32%)
  Pallas kernels  12.4 us (19%)
  between operations  1.45 us (2%)
  other arithmetic  1.26 us (2%)
    ppermute x8, waiting for transfers between devices, send_xy(): return lax.ppermute(x, ('x', 'y'), [(i, i ^ p) for i in range(4)])  16.4 us
    ppermute x8, starting transfers between devices, send_xy(): return lax.ppermute(x, ('x', 'y'), [(i, i ^ p) for i in range(4)])  11.6 us
    ppermute x6, starting transfers between devices, send_z(): return lax.ppermute(x, 'z', [(i, i ^ k) for i in range(cols)])  8.84 us
    ppermute x6, waiting for transfers between devices, send_z(): return lax.ppermute(x, 'z', [(i, i ^ k) for i in range(cols)])  8.38 us
    pallas_call x1, Pallas kernels, scores(): pl.pallas_call(functools.partial(scores_kernel, mine, cols, folded), grid...  7.73 us
    ppermute x2, waiting for transfers between devices, send_core(): return lax.ppermute(x, 'core', [(0, 1), (1, 0)])  4.62 us
    pallas_call x1, Pallas kernels, outputs(): pl.pallas_call(outputs_kernel, grid=(KV_HEADS,), in_specs=[smem, smem, pl...  3.98 us
  transfers between devices with their start and end apart: 16, of which 9 were waited for; matrix products, arithmetic and copies ran while one was open for 0% of the time, Pallas kernels for 6%

profile of v9, /device:TPU:0, one launch (start us, length us, event | category | flops | bytes accessed | tf_op | source)
XLA Modules:
  0.0 65.4 jit_solution(17843716732786853202)
XLA Ops:
  0.6 0.8 %pad_maximum_fusion.2 = bf16[32,1024]{1,0:T(8,128)(2,1)S(1)} fusion(bf16[32,512]{1,0:T(8,128)(2,1)} %param.9, bf16[32,512]{1,0:T(8,128)(2,1)} %param.8), kind=kLoop, calls=%fused_computation.15 | loop fusion | flops 131072 | bytes 131072 | tf_op jit(solution)/shard_map/concatenate | solution.py:383
  1.4 2.9 %collective-permute-start.4 = (bf16[32,1024]{1,0:T(8,128)(2,1)S(1)}, bf16[32,1024]{1,0:T(8,128)(2,1)S(1)}, u32[]{:S(2)}, u32[]{:S(2)}) collective-permute-start(bf16[32,1024]{1,0:T(8,128)(2,1)S(1)} %pad_maximum_fusion.2), channel_id=1, source_target_pairs={{0,16},{1,17},{16,0},{17,1},{2,18},{3,19},{18,2},{19,3},{4,20},{5,... | collective-permute-start | bytes 196616 | tf_op jit(solution)/shard_map/ppermute | solution.py:378
  4.4 1.5 %collective-permute-start.3 = (bf16[32,1024]{1,0:T(8,128)(2,1)S(1)}, bf16[32,1024]{1,0:T(8,128)(2,1)S(1)}, u32[]{:S(2)}, u32[]{:S(2)}) collective-permute-start(bf16[32,1024]{1,0:T(8,128)(2,1)S(1)} %pad_maximum_fusion.2), channel_id=1, source_target_pairs={{0,1},{1,0},{16,17},{17,16},{2,3},{3,2},{18,19},{19,18},{4,5},{5,4... | collective-permute-start | bytes 196616 | tf_op jit(solution)/shard_map/ppermute | solution.py:378
  5.9 3.6 %collective-permute-start.2 = (bf16[32,1024]{1,0:T(8,128)(2,1)S(1)}, bf16[32,1024]{1,0:T(8,128)(2,1)S(1)}, u32[]{:S(2)}, u32[]{:S(2)}) collective-permute-start(bf16[32,1024]{1,0:T(8,128)(2,1)S(1)} %pad_maximum_fusion.2), channel_id=1, source_target_pairs={{0,6},{2,4},{4,2},{6,0},{1,7},{3,5},{5,3},{7,1},{8,14},{10,12},{12... | collective-permute-start | bytes 196616 | tf_op jit(solution)/shard_map/ppermute | solution.py:375
  9.5 0.0 collective-permute-start.1
  9.5 0.8 %collective-permute-start = (bf16[32,1024]{1,0:T(8,128)(2,1)S(1)}, bf16[32,1024]{1,0:T(8,128)(2,1)S(1)}, u32[]{:S(2)}, u32[]{:S(2)}) collective-permute-start(bf16[32,1024]{1,0:T(8,128)(2,1)S(1)} %pad_maximum_fusion.2), channel_id=1, source_target_pairs={{0,2},{2,0},{4,6},{6,4},{1,3},{3,1},{5,7},{7,5},{8,10},{10,8},{12,... | collective-permute-start | bytes 196616 | tf_op jit(solution)/shard_map/ppermute | solution.py:375
  10.3 2.2 %collective-permute-done.2 = bf16[32,1024]{1,0:T(8,128)(2,1)S(1)} collective-permute-done((bf16[32,1024]{1,0:T(8,128)(2,1)S(1)}, bf16[32,1024]{1,0:T(8,128)(2,1)S(1)}, u32[]{:S(2)}, u32[]{:S(2)}) %collective-permute-start.2) | collective-permute-done | bytes 65568 | tf_op jit(solution)/shard_map/ppermute | solution.py:375
  12.5 2.3 %collective-permute-done.1 = bf16[32,1024]{1,0:T(8,128)(2,1)S(1)} collective-permute-done((bf16[32,1024]{1,0:T(8,128)(2,1)S(1)}, bf16[32,1024]{1,0:T(8,128)(2,1)S(1)}, u32[]{:S(2)}, u32[]{:S(2)}) %collective-permute-start.1) | collective-permute-done | bytes 65568 | tf_op jit(solution)/shard_map/ppermute | solution.py:375
  14.7 0.0 collective-permute-done
  14.7 0.0 collective-permute-done.4
  14.8 0.0 collective-permute-done.3
  14.8 0.6 collective-permute-start.6
  15.4 0.5 collective-permute-start.5
  15.9 0.0 copy-start.1
  15.9 0.0 copy-start
  15.9 0.0 copy-start.2
  15.9 0.0 copy-start.3
  15.9 2.5 %collective-permute-start.7 = (bf16[128,1024]{1,0:T(8,128)(2,1)S(1)}, bf16[128,1024]{1,0:T(8,128)(2,1)S(1)}, u32[]{:S(2)}, u32[]{:S(2)}) collective-permute-start(bf16[128,1024]{1,0:T(8,128)(2,1)S(1)} %pad_maximum_fusion), channel_id=1, source_target_pairs={{0,17},{1,16},{16,1},{17,0},{2,19},{3,18},{18,3},{19,2},{4,21},{5,... | collective-permute-start | bytes 786440 | tf_op jit(solution)/shard_map/ppermute | solution.py:378
  18.5 7.9 %collective-permute-done.5 = bf16[96,1024]{1,0:T(8,128)(2,1)S(1)} collective-permute-done((bf16[96,1024]{1,0:T(8,128)(2,1)S(1)}, bf16[96,1024]{1,0:T(8,128)(2,1)S(1)}, u32[]{:S(2)}, u32[]{:S(2)}) %collective-permute-start.5) | collective-permute-done | bytes 196640 | tf_op jit(solution)/shard_map/ppermute | solution.py:378
  26.4 0.0 collective-permute-done.6
  26.5 0.0 collective-permute-done.7
  26.5 0.1 collective-permute-start.8
  27.2 2.0 %collective-permute-done.8.other = bf16[2,2,128,1024]{3,2,1,0:T(8,128)(2,1)S(1)} collective-permute-done((bf16[2,2,128,1024]{3,2,1,0:T(8,128)(2,1)S(1)}, bf16[2,2,128,1024]{3,2,1,0:T(8,128)(2,1)S(1)}, u32[]{:S(2)}, u32[]{:S(2)}) %collective-permute-start.8) | collective-permute-done | bytes 1048608 | tf_op jit(solution)/shard_map/ppermute | solution.py:381
  29.2 0.0 copy-done.1
  29.3 0.0 copy-done
  29.3 0.0 copy-done.2
  29.3 0.0 copy-done.3
  29.3 7.7 %shard_map.110 = (bf16[4,256,1024]{2,1,0:T(8,128)(2,1)S(1)}, bf16[4,256,1024]{2,1,0:T(8,128)(2,1)S(1)}, bf16[2,256,1024]{2,1,0:T(8,128)(2,1)S(1)}, bf16[2,2,4,27...) custom-call(s32[128]{0:T(128)S(1)} %copy-done.3, s32[4]{0:T(128)S(1)} %copy-done.2, ...), custom_call_target="tpu_custom_call" | custom-call | flops 2147483648 | bytes 12582912 | tf_op jit(solution)/shard_map/pallas_call | solution.py:290
  37.0 0.2 collective-permute-start.9
  37.2 2.6 %collective-permute-done.9 = bf16[2,2,4,272,128]{4,3,2,1,0:T(8,128)(2,1)S(1)} collective-permute-done((bf16[2,2,4,272,128]{4,3,2,1,0:T(8,128)(2,1)S(1)}, bf16[2,2,4,272,128]{4,3,2,1,0:T(8,128)(2,1)S(1)}, u32[]{:S(2)}, u32[]{:S(2)}) %collective-permute-start.9) | collective-permute-done | bytes 1114144 | tf_op jit(solution)/shard_map/ppermute | solution.py:381
  39.8 0.3 add_convert_fusion
  40.1 0.1 slice_bitcast_fusion.2
  40.2 1.2 %collective-permute-start.10 = (bf16[4,272,128]{2,1,0:T(8,128)(2,1)S(1)}, bf16[4,272,128]{2,1,0:T(8,128)(2,1)S(1)}, u32[]{:S(2)}, u32[]{:S(2)}) collective-permute-start(bf16[4,272,128]{2,1,0:T(8,128)(2,1)S(1)} %get-tuple-element.41), channel_id=1, source_target_pairs={{0,1},{1,0},{16,17},{17,16},{2,3},{3,2},{18,19},{19,18},{4,5},{5,4... | collective-permute-start | bytes 835592 | tf_op jit(solution)/shard_map/ppermute | solution.py:378
  41.4 1.8 %collective-permute-start.12 = (bf16[4,272,128]{2,1,0:T(8,128)(2,1)S(1)}, bf16[4,272,128]{2,1,0:T(8,128)(2,1)S(1)}, u32[]{:S(2)}, u32[]{:S(2)}) collective-permute-start(bf16[4,272,128]{2,1,0:T(8,128)(2,1)S(1)} %get-tuple-element.42), channel_id=1, source_target_pairs={{0,17},{1,16},{16,1},{17,0},{2,19},{3,18},{18,3},{19,2},{4,21},{5,... | collective-permute-start | bytes 835592 | tf_op jit(solution)/shard_map/ppermute | solution.py:378
  43.2 0.5 collective-permute-start.11
  43.7 4.0 %shard_map.111 = (bf16[128,4096]{1,0:T(8,128)(2,1)}, bf16[128,4096]{1,0:T(8,128)(2,1)}) custom-call(s32[128]{0:T(128)S(1)} %copy-done.3, f32[1]{0:T(128)S(6)} %copy.18.gate_s, s32[1,128]{1,0:T(1,128)S(1)} %bitcast.25, bf16[4,256,1024]{2,1,0:T(8,128)(2,1)S(1)} %get-tuple-element.30.p16, bf16[4,256,1024]{2,1,0:T(8,128)(2,1)S(1)} %get-tuple-element.31.ds16, ...), custom_call_target="tpu_custom_call" | custom-call | flops 5000000000 | bytes 12582912 | tf_op jit(solution)/shard_map/pallas_call | solution.py:61
  47.7 7.2 %collective-permute-done.10 = bf16[4,272,128]{2,1,0:T(8,128)(2,1)S(1)} collective-permute-done((bf16[4,272,128]{2,1,0:T(8,128)(2,1)S(1)}, bf16[4,272,128]{2,1,0:T(8,128)(2,1)S(1)}, u32[]{:S(2)}, u32[]{:S(2)}) %collective-permute-start.10) | collective-permute-done | bytes 278560 | tf_op jit(solution)/shard_map/ppermute | solution.py:378
  54.9 0.0 collective-permute-done.12
  54.9 1.2 %collective-permute-done.11 = bf16[4,272,128]{2,1,0:T(8,128)(2,1)S(1)} collective-permute-done((bf16[4,272,128]{2,1,0:T(8,128)(2,1)S(1)}, bf16[4,272,128]{2,1,0:T(8,128)(2,1)S(1)}, u32[]{:S(2)}, u32[]{:S(2)}) %collective-permute-start.11) | collective-permute-done | bytes 278560 | tf_op jit(solution)/shard_map/ppermute | solution.py:378
  56.1 0.1 fusion.2
  56.3 0.9 %collective-permute-start.15 = (bf16[272,128]{1,0:T(8,128)(2,1)S(1)}, bf16[272,128]{1,0:T(8,128)(2,1)S(1)}, u32[]{:S(2)}, u32[]{:S(2)}) collective-permute-start(bf16[272,128]{1,0:T(8,128)(2,1)S(1)} %get-tuple-element.44), channel_id=1, source_target_pairs={{0,6},{2,4},{4,2},{6,0},{1,7},{3,5},{5,3},{7,1},{8,14},{10,12},{12... | collective-permute-start | bytes 208904 | tf_op jit(solution)/shard_map/ppermute | solution.py:375
  57.2 1.0 %collective-permute-start.14 = (bf16[272,128]{1,0:T(8,128)(2,1)S(1)}, bf16[272,128]{1,0:T(8,128)(2,1)S(1)}, u32[]{:S(2)}, u32[]{:S(2)}) collective-permute-start(bf16[272,128]{1,0:T(8,128)(2,1)S(1)} %get-tuple-element.45), channel_id=1, source_target_pairs={{0,4},{2,6},{4,0},{6,2},{1,5},{3,7},{5,1},{7,3},{8,12},{10,14},{12... | collective-permute-start | bytes 208904 | tf_op jit(solution)/shard_map/ppermute | solution.py:375
  58.2 2.6 %collective-permute-start.13 = (bf16[272,128]{1,0:T(8,128)(2,1)S(1)}, bf16[272,128]{1,0:T(8,128)(2,1)S(1)}, u32[]{:S(2)}, u32[]{:S(2)}) collective-permute-start(bf16[272,128]{1,0:T(8,128)(2,1)S(1)} %get-tuple-element.46), channel_id=1, source_target_pairs={{0,2},{2,0},{4,6},{6,4},{1,3},{3,1},{5,7},{7,5},{8,10},{10,8},{12,... | collective-permute-start | bytes 208904 | tf_op jit(solution)/shard_map/ppermute | solution.py:375
  60.8 2.1 %collective-permute-done.15.refs_3_ = bf16[272,128]{1,0:T(8,128)(2,1)S(1)} collective-permute-done((bf16[272,128]{1,0:T(8,128)(2,1)S(1)}, bf16[272,128]{1,0:T(8,128)(2,1)S(1)}, u32[]{:S(2)}, u32[]{:S(2)}) %collective-permute-start.15) | collective-permute-done | bytes 69664 | tf_op jit(solution)/shard_map/ppermute | solution.py:375
  62.9 1.8 %collective-permute-done.14.refs_2_ = bf16[272,128]{1,0:T(8,128)(2,1)S(1)} collective-permute-done((bf16[272,128]{1,0:T(8,128)(2,1)S(1)}, bf16[272,128]{1,0:T(8,128)(2,1)S(1)}, u32[]{:S(2)}, u32[]{:S(2)}) %collective-permute-start.14) | collective-permute-done | bytes 69664 | tf_op jit(solution)/shard_map/ppermute | solution.py:375
  64.7 0.0 collective-permute-done.13.refs_1_
  64.7 0.7 %shard_map.112 = (f32[32,512]{1,0:T(8,128)}, f32[32,512]{1,0:T(8,128)}, f32[1]{0:T(128)}) custom-call(f32[8,128]{1,0:T(8,128)S(1)} %get-tuple-element.36.gate, bf16[272,128]{1,0:T(8,128)(2,1)S(1)} %get-tuple-element.47.refs_0_, bf16[272,128]{1,0:T(8,128)(2,1)S(1)} %collective-permute-done.13.refs_1_, bf16[272,128]{1,0:T(8,128)(2,1)S(1)} %collective-permute-done.14.refs_2_, ...), custom_call_target="tpu_custom_call" | custom-call | tf_op jit(solution)/shard_map/pallas_call | solution.py:357
  (10 shorter events, 0.1 us)
Async XLA Ops:
  1.4 13.3 %collective-permute-start.4 = (bf16[32,1024]{1,0:T(8,128)(2,1)S(1)}, bf16[32,1024]{1,0:T(8,128)(2,1)S(1)}, u32[]{:S(2)}, u32[]{:S(2)}) collective-permute-start(bf16[32,1024]{1,0:T(8,128)(2,1)S(1)} %pad_maximum_fusion.2), channel_id=1, source_target_pairs={{0,16},{1,17},{16,0},{17,1},{2,18},{3,19},{18,2},{19,3},{4,20},{5,... | collective-permute-start | bytes 196616 | tf_op jit(solution)/shard_map/ppermute | solution.py:378
  4.4 10.4 %collective-permute-start.3 = (bf16[32,1024]{1,0:T(8,128)(2,1)S(1)}, bf16[32,1024]{1,0:T(8,128)(2,1)S(1)}, u32[]{:S(2)}, u32[]{:S(2)}) collective-permute-start(bf16[32,1024]{1,0:T(8,128)(2,1)S(1)} %pad_maximum_fusion.2), channel_id=1, source_target_pairs={{0,1},{1,0},{16,17},{17,16},{2,3},{3,2},{18,19},{19,18},{4,5},{5,4... | collective-permute-start | bytes 196616 | tf_op jit(solution)/shard_map/ppermute | solution.py:378
  5.9 6.6 %collective-permute-start.2 = (bf16[32,1024]{1,0:T(8,128)(2,1)S(1)}, bf16[32,1024]{1,0:T(8,128)(2,1)S(1)}, u32[]{:S(2)}, u32[]{:S(2)}) collective-permute-start(bf16[32,1024]{1,0:T(8,128)(2,1)S(1)} %pad_maximum_fusion.2), channel_id=1, source_target_pairs={{0,6},{2,4},{4,2},{6,0},{1,7},{3,5},{5,3},{7,1},{8,14},{10,12},{12... | collective-permute-start | bytes 196616 | tf_op jit(solution)/shard_map/ppermute | solution.py:375
  9.5 5.2 %collective-permute-start.1 = (bf16[32,1024]{1,0:T(8,128)(2,1)S(1)}, bf16[32,1024]{1,0:T(8,128)(2,1)S(1)}, u32[]{:S(2)}, u32[]{:S(2)}) collective-permute-start(bf16[32,1024]{1,0:T(8,128)(2,1)S(1)} %pad_maximum_fusion.2), channel_id=1, source_target_pairs={{0,4},{2,6},{4,0},{6,2},{1,5},{3,7},{5,1},{7,3},{8,12},{10,14},{12... | collective-permute-start | bytes 196616 | tf_op jit(solution)/shard_map/ppermute | solution.py:375
  9.5 5.2 %collective-permute-start = (bf16[32,1024]{1,0:T(8,128)(2,1)S(1)}, bf16[32,1024]{1,0:T(8,128)(2,1)S(1)}, u32[]{:S(2)}, u32[]{:S(2)}) collective-permute-start(bf16[32,1024]{1,0:T(8,128)(2,1)S(1)} %pad_maximum_fusion.2), channel_id=1, source_target_pairs={{0,2},{2,0},{4,6},{6,4},{1,3},{3,1},{5,7},{7,5},{8,10},{10,8},{12,... | collective-permute-start | bytes 196616 | tf_op jit(solution)/shard_map/ppermute | solution.py:375
  14.8 11.7 %collective-permute-start.6 = (bf16[96,1024]{1,0:T(8,128)(2,1)S(1)}, bf16[96,1024]{1,0:T(8,128)(2,1)S(1)}, u32[]{:S(2)}, u32[]{:S(2)}) collective-permute-start(bf16[96,1024]{1,0:T(8,128)(2,1)S(1)} %pad_maximum_fusion.1), channel_id=1, source_target_pairs={{0,16},{1,17},{16,0},{17,1},{2,18},{3,19},{18,2},{19,3},{4,20},{5,... | collective-permute-start | bytes 589832 | tf_op jit(solution)/shard_map/ppermute | solution.py:378
  15.4 11.1 %collective-permute-start.5 = (bf16[96,1024]{1,0:T(8,128)(2,1)S(1)}, bf16[96,1024]{1,0:T(8,128)(2,1)S(1)}, u32[]{:S(2)}, u32[]{:S(2)}) collective-permute-start(bf16[96,1024]{1,0:T(8,128)(2,1)S(1)} %pad_maximum_fusion.1), channel_id=1, source_target_pairs={{0,1},{1,0},{16,17},{17,16},{2,3},{3,2},{18,19},{19,18},{4,5},{5,4... | collective-permute-start | bytes 589832 | tf_op jit(solution)/shard_map/ppermute | solution.py:378
  15.9 13.4 %copy-start.1 = (bf16[128,4096]{1,0:T(8,128)(2,1)S(1)}, bf16[128,4096]{1,0:T(8,128)(2,1)}, u32[]{:S(2)}) copy-start(bf16[128,4096]{1,0:T(8,128)(2,1)} %dy_ref.1) | copy-start | bytes 3145732
  15.9 13.4 %copy-start = (bf16[128,4096]{1,0:T(8,128)(2,1)S(1)}, bf16[128,4096]{1,0:T(8,128)(2,1)}, u32[]{:S(2)}) copy-start(bf16[128,4096]{1,0:T(8,128)(2,1)} %q_ref.1) | copy-start | bytes 3145732
  15.9 13.3 %copy-start.2 = (s32[4]{0:T(128)S(1)}, s32[4]{0:T(128)}, u32[]{:S(2)}) copy-start(s32[4]{0:T(128)} %cnt_s.1) | copy-start | bytes 52
  15.9 13.3 %copy-start.3 = (s32[128]{0:T(128)S(1)}, s32[128]{0:T(128)}, u32[]{:S(2)}) copy-start(s32[128]{0:T(128)} %seg_s.3) | copy-start | bytes 1540
  15.9 10.6 %collective-permute-start.7 = (bf16[128,1024]{1,0:T(8,128)(2,1)S(1)}, bf16[128,1024]{1,0:T(8,128)(2,1)S(1)}, u32[]{:S(2)}, u32[]{:S(2)}) collective-permute-start(bf16[128,1024]{1,0:T(8,128)(2,1)S(1)} %pad_maximum_fusion), channel_id=1, source_target_pairs={{0,17},{1,16},{16,1},{17,0},{2,19},{3,18},{18,3},{19,2},{4,21},{5,... | collective-permute-start | bytes 786440 | tf_op jit(solution)/shard_map/ppermute | solution.py:378
  26.5 2.7 %collective-permute-start.8 = (bf16[2,2,128,1024]{3,2,1,0:T(8,128)(2,1)S(1)}, bf16[2,2,128,1024]{3,2,1,0:T(8,128)(2,1)S(1)}, u32[]{:S(2)}, u32[]{:S(2)}) collective-permute-start(bf16[2,2,128,1024]{3,2,1,0:T(8,128)(2,1)S(1)} %bitcast.22), channel_id=1, source_target_pairs={{0,8},{8,0},{1,9},{9,1},{2,10},{10,2},{3,11},{11,3},{4,12},{12,4},... | collective-permute-start | bytes 3145736 | tf_op jit(solution)/shard_map/ppermute | solution.py:381
  37.0 2.8 %collective-permute-start.9 = (bf16[2,2,4,272,128]{4,3,2,1,0:T(8,128)(2,1)S(1)}, bf16[2,2,4,272,128]{4,3,2,1,0:T(8,128)(2,1)S(1)}, u32[]{:S(2)}, u32[]{:S(2)}) collective-permute-start(bf16[2,2,4,272,128]{4,3,2,1,0:T(8,128)(2,1)S(1)} %get-tuple-element.27), channel_id=1, source_target_pairs={{0,8},{8,0},{1,9},{9,1},{2,10},{10,2},{3,11},{11,3},{4,12},{12,4},... | collective-permute-start | bytes 3342344 | tf_op jit(solution)/shard_map/ppermute | solution.py:381
  40.2 14.7 %collective-permute-start.10 = (bf16[4,272,128]{2,1,0:T(8,128)(2,1)S(1)}, bf16[4,272,128]{2,1,0:T(8,128)(2,1)S(1)}, u32[]{:S(2)}, u32[]{:S(2)}) collective-permute-start(bf16[4,272,128]{2,1,0:T(8,128)(2,1)S(1)} %get-tuple-element.41), channel_id=1, source_target_pairs={{0,1},{1,0},{16,17},{17,16},{2,3},{3,2},{18,19},{19,18},{4,5},{5,4... | collective-permute-start | bytes 835592 | tf_op jit(solution)/shard_map/ppermute | solution.py:378
  41.4 13.5 %collective-permute-start.12 = (bf16[4,272,128]{2,1,0:T(8,128)(2,1)S(1)}, bf16[4,272,128]{2,1,0:T(8,128)(2,1)S(1)}, u32[]{:S(2)}, u32[]{:S(2)}) collective-permute-start(bf16[4,272,128]{2,1,0:T(8,128)(2,1)S(1)} %get-tuple-element.42), channel_id=1, source_target_pairs={{0,17},{1,16},{16,1},{17,0},{2,19},{3,18},{18,3},{19,2},{4,21},{5,... | collective-permute-start | bytes 835592 | tf_op jit(solution)/shard_map/ppermute | solution.py:378
  43.2 12.9 %collective-permute-start.11 = (bf16[4,272,128]{2,1,0:T(8,128)(2,1)S(1)}, bf16[4,272,128]{2,1,0:T(8,128)(2,1)S(1)}, u32[]{:S(2)}, u32[]{:S(2)}) collective-permute-start(bf16[4,272,128]{2,1,0:T(8,128)(2,1)S(1)} %get-tuple-element.43), channel_id=1, source_target_pairs={{0,16},{1,17},{16,0},{17,1},{2,18},{3,19},{18,2},{19,3},{4,20},{5,... | collective-permute-start | bytes 835592 | tf_op jit(solution)/shard_map/ppermute | solution.py:378
  56.3 6.6 %collective-permute-start.15 = (bf16[272,128]{1,0:T(8,128)(2,1)S(1)}, bf16[272,128]{1,0:T(8,128)(2,1)S(1)}, u32[]{:S(2)}, u32[]{:S(2)}) collective-permute-start(bf16[272,128]{1,0:T(8,128)(2,1)S(1)} %get-tuple-element.44), channel_id=1, source_target_pairs={{0,6},{2,4},{4,2},{6,0},{1,7},{3,5},{5,3},{7,1},{8,14},{10,12},{12... | collective-permute-start | bytes 208904 | tf_op jit(solution)/shard_map/ppermute | solution.py:375
  57.2 7.5 %collective-permute-start.14 = (bf16[272,128]{1,0:T(8,128)(2,1)S(1)}, bf16[272,128]{1,0:T(8,128)(2,1)S(1)}, u32[]{:S(2)}, u32[]{:S(2)}) collective-permute-start(bf16[272,128]{1,0:T(8,128)(2,1)S(1)} %get-tuple-element.45), channel_id=1, source_target_pairs={{0,4},{2,6},{4,0},{6,2},{1,5},{3,7},{5,1},{7,3},{8,12},{10,14},{12... | collective-permute-start | bytes 208904 | tf_op jit(solution)/shard_map/ppermute | solution.py:375
  58.2 6.5 %collective-permute-start.13 = (bf16[272,128]{1,0:T(8,128)(2,1)S(1)}, bf16[272,128]{1,0:T(8,128)(2,1)S(1)}, u32[]{:S(2)}, u32[]{:S(2)}) collective-permute-start(bf16[272,128]{1,0:T(8,128)(2,1)S(1)} %get-tuple-element.46), channel_id=1, source_target_pairs={{0,2},{2,0},{4,6},{6,4},{1,3},{3,1},{5,7},{7,5},{8,10},{10,8},{12,... | collective-permute-start | bytes 208904 | tf_op jit(solution)/shard_map/ppermute | solution.py:375

commit v10 on v9

--- a/solution.py
+++ b/solution.py
@@ -41,7 +41,7 @@
         o = mm(vcat_t, p16[0, :, rows], NN)
         o = (tg2 * jnp.where(in_a2, o[:hd], o[hd:])).astype(jnp.bfloat16)
         dq = mm(kcat_t, ds16[0, :, rows], NN)
-        dq = jnp.where(in_a2, dq[:hd], dq[hd:]).astype(jnp.bfloat16)
+        dq = (tg2 * (1.0 / hd**0.5) * jnp.where(in_a2, dq[:hd], dq[hd:])).astype(jnp.bfloat16)
         for j in range(2):
             feats = slice((2 * h + j) * hd, (2 * h + j + 1) * hd)
             toks = slice(j * tokens, (j + 1) * tokens)
@@ -104,6 +104,7 @@
     dbuf,
     bias,
     sems,
+    fetched,
 ):
     step = pl.program_id(0)
     heads = pl.num_programs(0)
@@ -120,23 +121,30 @@
     def place(img):
         return img % 2, (img // 2) ^ xpos
 
-    def fetch(i, img, start):
-        par, dx = place(img)
-        for src, mask in ((own, par == core), (other, par != core)):
-
-            @pl.when(mask)
-            def _():
-                for h in range(2):
-                    c = pltpu.make_async_copy(src.at[dx, h], kv.at[i, pl.ds(h * half, half)], sems.at[i])
-                    c.start() if start else c.wait()
+    def fetch(head, start):
+        for i, img in enumerate((img_a, img_b)):
+            par, dx = place(img)
+            for src, mask in ((own, par == core), (other, par != core)):
+
+                @pl.when(mask)
+                def _():
+                    for h in range(2):
+                        for lane in (head * hd, width + head * hd):
+                            lanes = pl.ds(lane, hd)
+                            c = pltpu.make_async_copy(
+                                src.at[dx, h, :, lanes],
+                                kv.at[i, pl.ds(h * half, half), lanes],
+                                fetched.at[head],
+                            )
+                            c.start() if start else c.wait()
 
     in_a = seg_v[...] == img_a
     tg = jnp.tanh(jnp.full((1, hd), gate_s[0], jnp.float32))
 
     @pl.when(step == 0)
     def _():
-        fetch(0, img_a, True)
-        fetch(1, img_b, True)
+        for h in range(KV_HEADS):
+            fetch(h, True)
         acc[...] = jnp.zeros_like(acc)
         g_ref[...] = jnp.zeros_like(g_ref)
         n = lax.broadcasted_iota(jnp.int32, (slots, tokens), 0)
@@ -148,8 +156,14 @@
         side_a = jnp.broadcast_to(in_a.astype(jnp.float32), (hd, tokens)).T
         rowsel[0] = side_a.astype(jnp.bfloat16)
         rowsel[1] = (1.0 - side_a).astype(jnp.bfloat16)
-        fetch(0, img_a, False)
-        fetch(1, img_b, False)
+    for h in range(KV_HEADS):
+
+        @pl.when(step == h)
+        def _():
+            fetch(h, False)
+
+    @pl.when(step == heads - 1)
+    def _():
         pltpu.make_async_copy(kv, kv_out, sems.at[2]).start()
 
     kcols = pl.ds(pl.multiple_of(step * hd, hd), hd)
@@ -168,7 +182,7 @@
     span = 2 * tokens
     blocks = group // 2
     strips = [slice(i, i + STRIP) for i in range(0, slots, STRIP)]
-    slope = scale * jnp.concatenate([tg, tg], axis=1)
+    tg2 = jnp.concatenate([tg, tg], axis=1)
 
     def fold8(x):
         return jnp.sum(x.reshape(x.shape[0] // 8, 8, x.shape[1]), axis=0)
@@ -197,11 +211,11 @@
             norm = norm + fold8(e)
             dots = dots + fold8(e * dbuf[i, strip])
         inv = 1.0 / jnp.sum(norm, axis=0, keepdims=True)
-        delta = slope * (inv * jnp.sum(dots, axis=0, keepdims=True))
+        delta = inv * jnp.sum(dots, axis=0, keepdims=True)
         for strip in strips:
             p = sbuf[i, strip] * inv
             p16[0, strip, rows] = p.astype(jnp.bfloat16)
-            ds16[0, strip, rows] = (p * (slope * dbuf[i, strip] - delta)).astype(jnp.bfloat16)
+            ds16[0, strip, rows] = (p * (dbuf[i, strip] - delta)).astype(jnp.bfloat16)
 
     def slot_grads(lo, hi):
         rows = slice(lo * span, hi * span)
@@ -216,9 +230,9 @@
         if h % 2:
             more = slot_grads(h - 1, h + 1)
             dk, dv = dk + more[0], dv + more[1]
-    dk = dk.astype(jnp.bfloat16)
+    dk = (scale * tg2 * dk).astype(jnp.bfloat16)
     g_ref[...] += fold8((dv * vcat.astype(jnp.float32))[:, :hd] + (dv * vcat.astype(jnp.float32))[:, hd:])
-    dv = (jnp.concatenate([tg, tg], axis=1) * dv).astype(jnp.bfloat16)
+    dv = (tg2 * dv).astype(jnp.bfloat16)
     pieces = 2 * acc.shape[3]
     per = slots // pieces
     krows = pl.ds(pl.multiple_of(step * per, per), per)
@@ -317,6 +331,7 @@
             pltpu.VMEM((2, slots, 2 * tokens), jnp.float32),
             pltpu.VMEM((slots, tokens), jnp.float32),
             pltpu.SemaphoreType.DMA((5 + 4 * KV_HEADS,)),
+            pltpu.SemaphoreType.DMA((KV_HEADS,)),
         ],
         compiler_params=pltpu.CompilerParams(vmem_limit_bytes=28 * 1024 * 1024),
         cost_estimate=pl.CostEstimate(
@@ -380,11 +395,12 @@
     def send_core(x):
         return lax.ppermute(x, "core", [(0, 1), (1, 0)])
 
-    kv = lax.optimization_barrier(jnp.concatenate([keys, values], axis=1))
+    kv = jnp.concatenate([keys, values], axis=1)
     if folded:
+        near = [send_xy(kv, p) for p in (1, 2)]
         line = [send_z(kv, k) for k in LINE]
-        near = [send_xy(kv, p) for p in (1, 2)]
         line, near = lax.optimization_barrier((jnp.concatenate(line, axis=0), near))
+        kv, line = lax.optimization_barrier((kv, line))
         block = jnp.concatenate([kv, line], axis=0)
         diag = send_xy(block, 3)
         own = [block, near[0], send_xy(line, 1), near[1], send_xy(line, 2), diag]
@@ -397,16 +413,17 @@
         mine, cols, folded, seg_image, tile_counts, gate, queries, cotangent, own, other
     )
 
-    part = (part_own.astype(f32) + send_core(part_other).astype(f32)).astype(bf16)
-    part, p16 = lax.optimization_barrier((part, p16))
+    got, p16 = lax.optimization_barrier((send_core(part_other), p16))
+    part = (part_own.astype(f32) + got.astype(f32)).astype(bf16)
     y, dq = outputs(seg_image, gate, p16, ds16, kv_used)
     part = part.reshape((4,) + part.shape[2:])
     if folded:
-        line = part[0].astype(f32)
+        parts = [part[0, 0]] + [send_xy(part[p, 0], p) for p in PEERS]
+        line = part[0, 1:].astype(f32)
         for p in PEERS:
-            line = line + send_xy(part[p], p).astype(f32)
+            line = line + send_xy(part[p, 1:], p).astype(f32)
         line, y = lax.optimization_barrier((line.astype(bf16), y))
-        parts = [line[0]] + [send_z(line[k], k) for k in LINE]
+        parts += [send_z(line[k - 1], k) for k in LINE]
     else:
         line = part[0, 0].astype(f32)
         for p in PEERS:

time: 65.6 us -> 63.3 us (0.965)
  waiting for transfers between devices: 29.4 us -> 22.5 us
  starting transfers between devices: 20.7 us -> 24.4 us
  local copies, waits for them, and re-layouts: 0.18 us -> 1.7 us
  other arithmetic: 1.26 us -> 0.45 us
    ppermute x8 -> x11, waiting for transfers between devices: 16.4 us -> 12.1 us  [send_xy(): return lax.ppermute(x, ('x', 'y'), [(i, i ^ p) for i in range(4)])]
    ppermute x6, waiting for transfers between devices: 8.38 us -> 5.84 us  [send_z(): return lax.ppermute(x, 'z', [(i, i ^ k) for i in range(cols)])]
    ppermute x8 -> x11, starting transfers between devices: 11.6 us -> 14.1 us  [send_xy(): return lax.ppermute(x, ('x', 'y'), [(i, i ^ p) for i in range(4)])]
    ppermute x6, starting transfers between devices: 8.84 us -> 10.1 us  [send_z(): return lax.ppermute(x, 'z', [(i, i ^ k) for i in range(cols)])]
    concatenate x1 -> x0, other arithmetic: 0.78 us -> none  [local(): kv = lax.optimization_barrier(jnp.concatenate([keys, values], axis=1))]
    concatenate x0 -> x1, local copies, waits for them, and re-layouts: none -> 0.76 us  [local(): kv = jnp.concatenate([keys, values], axis=1)]
    unnamed x14 -> x15, local copies, waits for them, and re-layouts: 0.08 us -> 0.84 us
  transfers between devices with their start and end apart: 16 -> 19, of which waited for: 9 -> 9; matrix products, arithmetic and copies ran while one was open for 0% -> 0% of each run, Pallas kernels for 6% -> 6%
where the time goes in v10:
time: 63.3 us; the launch traced here: 63.1 us
  starting transfers between devices  24.4 us (39%)
  waiting for transfers between devices  22.5 us (36%)
  Pallas kernels  12.5 us (20%)
  local copies, waits for them, and re-layouts  1.7 us (3%)
  between operations  1.44 us (2%)
    ppermute x11, starting transfers between devices, send_xy(): return lax.ppermute(x, ('x', 'y'), [(i, i ^ p) for i in range(4)])  14.1 us
    ppermute x11, waiting for transfers between devices, send_xy(): return lax.ppermute(x, ('x', 'y'), [(i, i ^ p) for i in range(4)])  12.1 us
    ppermute x6, starting transfers between devices, send_z(): return lax.ppermute(x, 'z', [(i, i ^ k) for i in range(cols)])  10.1 us
    pallas_call x1, Pallas kernels, scores(): pl.pallas_call(functools.partial(scores_kernel, mine, cols, folded), grid...  7.81 us
    ppermute x6, waiting for transfers between devices, send_z(): return lax.ppermute(x, 'z', [(i, i ^ k) for i in range(cols)])  5.84 us
    ppermute x2, waiting for transfers between devices, send_core(): return lax.ppermute(x, 'core', [(0, 1), (1, 0)])  4.62 us
    pallas_call x1, Pallas kernels, outputs(): pl.pallas_call(outputs_kernel, grid=(KV_HEADS,), in_specs=[smem, smem, pl...  4 us
  transfers between devices with their start and end apart: 19, of which 9 were waited for; matrix products, arithmetic and copies ran while one was open for 0% of the time, Pallas kernels for 6%

profile of v10, /device:TPU:0, one launch (start us, length us, event | category | flops | bytes accessed | tf_op | source)
XLA Modules:
  0.0 63.1 jit_solution(12845543968109905679)
XLA Ops:
  0.6 0.8 %constant_dynamic-update-slice_fusion.1 = bf16[32,1024]{1,0:T(8,128)(2,1)S(1)} fusion(bf16[32,512]{1,0:T(8,128)(2,1)} %param.8), kind=kLoop, calls=%fused_computation.19 | loop fusion | bytes 65536
  1.4 0.8 %constant_dynamic-update-slice_fusion = bf16[32,1024]{1,0:T(8,128)(2,1)S(1)} fusion(bf16[32,1024]{1,0:T(8,128)(2,1)S(1)} %constant_dynamic-update-slice_fusion.1, bf16[32,512]{1,0:T(8,128)(2,1)} %param.9), kind=kLoop, calls=%fused_computation.18 | loop fusion | bytes 65536 | tf_op jit(solution)/shard_map/concatenate | solution.py:398
  2.2 5.0 %collective-permute-start.2 = (bf16[32,1024]{1,0:T(8,128)(2,1)S(1)}, bf16[32,1024]{1,0:T(8,128)(2,1)S(1)}, u32[]{:S(2)}, u32[]{:S(2)}) collective-permute-start(bf16[32,1024]{1,0:T(8,128)(2,1)S(1)} %constant_dynamic-update-slice_fusion), channel_id=1, source_target_pairs={{0,6},{2,4},{4,2},{6,0},{1,7},{3,5},{5,3},{7,1},{8,14},{10,12},{12... | collective-permute-start | bytes 196616 | tf_op jit(solution)/shard_map/ppermute | solution.py:390
  7.2 0.0 collective-permute-start.1
  7.2 0.6 collective-permute-start
  7.8 1.7 %collective-permute-start.3 = (bf16[32,1024]{1,0:T(8,128)(2,1)S(1)}, bf16[32,1024]{1,0:T(8,128)(2,1)S(1)}, u32[]{:S(2)}, u32[]{:S(2)}) collective-permute-start(bf16[32,1024]{1,0:T(8,128)(2,1)S(1)} %constant_dynamic-update-slice_fusion), channel_id=1, source_target_pairs={{0,1},{1,0},{16,17},{17,16},{2,3},{3,2},{18,19},{19,18},{4,5},{5,4... | collective-permute-start | bytes 196616 | tf_op jit(solution)/shard_map/ppermute | solution.py:393
  9.5 1.5 %collective-permute-start.4 = (bf16[32,1024]{1,0:T(8,128)(2,1)S(1)}, bf16[32,1024]{1,0:T(8,128)(2,1)S(1)}, u32[]{:S(2)}, u32[]{:S(2)}) collective-permute-start(bf16[32,1024]{1,0:T(8,128)(2,1)S(1)} %constant_dynamic-update-slice_fusion), channel_id=1, source_target_pairs={{0,16},{1,17},{16,0},{17,1},{2,18},{3,19},{18,2},{19,3},{4,20},{5,... | collective-permute-start | bytes 196616 | tf_op jit(solution)/shard_map/ppermute | solution.py:393
  11.0 0.0 collective-permute-done.2
  11.0 1.8 %collective-permute-done.1 = bf16[32,1024]{1,0:T(8,128)(2,1)S(1)} collective-permute-done((bf16[32,1024]{1,0:T(8,128)(2,1)S(1)}, bf16[32,1024]{1,0:T(8,128)(2,1)S(1)}, u32[]{:S(2)}, u32[]{:S(2)}) %collective-permute-start.1) | collective-permute-done | bytes 65568 | tf_op jit(solution)/shard_map/ppermute | solution.py:390
  12.8 0.0 collective-permute-done
  12.8 0.0 collective-permute-done.3
  12.8 0.9 %collective-permute-done.4 = bf16[32,1024]{1,0:T(8,128)(2,1)S(1)} collective-permute-done((bf16[32,1024]{1,0:T(8,128)(2,1)S(1)}, bf16[32,1024]{1,0:T(8,128)(2,1)S(1)}, u32[]{:S(2)}, u32[]{:S(2)}) %collective-permute-start.4) | collective-permute-done | bytes 65568 | tf_op jit(solution)/shard_map/ppermute | solution.py:393
  13.8 0.7 %collective-permute-start.5 = (bf16[96,1024]{1,0:T(8,128)(2,1)S(1)}, bf16[96,1024]{1,0:T(8,128)(2,1)S(1)}, u32[]{:S(2)}, u32[]{:S(2)}) collective-permute-start(bf16[96,1024]{1,0:T(8,128)(2,1)S(1)} %pad_maximum_fusion.1), channel_id=1, source_target_pairs={{0,1},{1,0},{16,17},{17,16},{2,3},{3,2},{18,19},{19,18},{4,5},{5,4... | collective-permute-start | bytes 589832 | tf_op jit(solution)/shard_map/ppermute | solution.py:393
  14.4 1.5 %collective-permute-start.6 = (bf16[96,1024]{1,0:T(8,128)(2,1)S(1)}, bf16[96,1024]{1,0:T(8,128)(2,1)S(1)}, u32[]{:S(2)}, u32[]{:S(2)}) collective-permute-start(bf16[96,1024]{1,0:T(8,128)(2,1)S(1)} %pad_maximum_fusion.1), channel_id=1, source_target_pairs={{0,16},{1,17},{16,0},{17,1},{2,18},{3,19},{18,2},{19,3},{4,20},{5,... | collective-permute-start | bytes 589832 | tf_op jit(solution)/shard_map/ppermute | solution.py:393
  16.0 0.0 copy-start
  16.0 0.0 copy-start.2
  16.0 0.0 copy-start.3
  16.0 1.4 %collective-permute-start.7 = (bf16[128,1024]{1,0:T(8,128)(2,1)S(1)}, bf16[128,1024]{1,0:T(8,128)(2,1)S(1)}, u32[]{:S(2)}, u32[]{:S(2)}) collective-permute-start(bf16[128,1024]{1,0:T(8,128)(2,1)S(1)} %pad_maximum_fusion), channel_id=1, source_target_pairs={{0,17},{1,16},{16,1},{17,0},{2,19},{3,18},{18,3},{19,2},{4,21},{5,... | collective-permute-start | bytes 786440 | tf_op jit(solution)/shard_map/ppermute | solution.py:393
  17.4 2.6 %collective-permute-done.5 = bf16[96,1024]{1,0:T(8,128)(2,1)S(1)} collective-permute-done((bf16[96,1024]{1,0:T(8,128)(2,1)S(1)}, bf16[96,1024]{1,0:T(8,128)(2,1)S(1)}, u32[]{:S(2)}, u32[]{:S(2)}) %collective-permute-start.5) | collective-permute-done | bytes 196640 | tf_op jit(solution)/shard_map/ppermute | solution.py:393
  20.1 2.2 %collective-permute-done.6 = bf16[96,1024]{1,0:T(8,128)(2,1)S(1)} collective-permute-done((bf16[96,1024]{1,0:T(8,128)(2,1)S(1)}, bf16[96,1024]{1,0:T(8,128)(2,1)S(1)}, u32[]{:S(2)}, u32[]{:S(2)}) %collective-permute-start.6) | collective-permute-done | bytes 196640 | tf_op jit(solution)/shard_map/ppermute | solution.py:393
  22.3 4.3 %collective-permute-done.7 = bf16[128,1024]{1,0:T(8,128)(2,1)S(1)} collective-permute-done((bf16[128,1024]{1,0:T(8,128)(2,1)S(1)}, bf16[128,1024]{1,0:T(8,128)(2,1)S(1)}, u32[]{:S(2)}, u32[]{:S(2)}) %collective-permute-start.7) | collective-permute-done | bytes 262176 | tf_op jit(solution)/shard_map/ppermute | solution.py:393
  26.5 0.1 collective-permute-start.8
  27.3 2.0 %collective-permute-done.8.other = bf16[2,2,128,1024]{3,2,1,0:T(8,128)(2,1)S(1)} collective-permute-done((bf16[2,2,128,1024]{3,2,1,0:T(8,128)(2,1)S(1)}, bf16[2,2,128,1024]{3,2,1,0:T(8,128)(2,1)S(1)}, u32[]{:S(2)}, u32[]{:S(2)}) %collective-permute-start.8) | collective-permute-done | bytes 1048608 | tf_op jit(solution)/shard_map/ppermute | solution.py:396
  29.3 7.8 %shard_map.110 = (bf16[4,256,1024]{2,1,0:T(8,128)(2,1)S(1)}, bf16[4,256,1024]{2,1,0:T(8,128)(2,1)S(1)}, bf16[2,256,1024]{2,1,0:T(8,128)(2,1)S(1)}, bf16[2,2,4,27...) custom-call(s32[128]{0:T(128)S(1)} %copy-done.3, s32[4]{0:T(128)S(1)} %copy-done.2, ...), custom_call_target="tpu_custom_call" | custom-call | flops 2147483648 | bytes 12582912 | tf_op jit(solution)/shard_map/pallas_call | solution.py:304
  37.1 0.2 collective-permute-start.9
  37.3 2.6 %collective-permute-done.9 = bf16[2,2,4,272,128]{4,3,2,1,0:T(8,128)(2,1)S(1)} collective-permute-done((bf16[2,2,4,272,128]{4,3,2,1,0:T(8,128)(2,1)S(1)}, bf16[2,2,4,272,128]{4,3,2,1,0:T(8,128)(2,1)S(1)}, u32[]{:S(2)}, u32[]{:S(2)}) %collective-permute-start.9) | collective-permute-done | bytes 1114144 | tf_op jit(solution)/shard_map/ppermute | solution.py:396
  39.9 0.3 add_convert_fusion
  40.3 2.3 %collective-permute-start.12 = (bf16[3,272,128]{2,1,0:T(8,128)(2,1)S(1)}, bf16[3,272,128]{2,1,0:T(8,128)(2,1)S(1)}, u32[]{:S(2)}, u32[]{:S(2)}) collective-permute-start(bf16[3,272,128]{2,1,0:T(8,128)(2,1)S(1)} %get-tuple-element.50), channel_id=1, source_target_pairs={{0,17},{1,16},{16,1},{17,0},{2,19},{3,18},{18,3},{19,2},{4,21},{5,... | collective-permute-start | bytes 626696 | tf_op jit(solution)/shard_map/ppermute | solution.py:393
  42.7 0.5 collective-permute-start.11
  43.2 0.7 %collective-permute-start.10 = (bf16[3,272,128]{2,1,0:T(8,128)(2,1)S(1)}, bf16[3,272,128]{2,1,0:T(8,128)(2,1)S(1)}, u32[]{:S(2)}, u32[]{:S(2)}) collective-permute-start(bf16[3,272,128]{2,1,0:T(8,128)(2,1)S(1)} %get-tuple-element.49), channel_id=1, source_target_pairs={{0,1},{1,0},{16,17},{17,16},{2,3},{3,2},{18,19},{19,18},{4,5},{5,4... | collective-permute-start | bytes 626696 | tf_op jit(solution)/shard_map/ppermute | solution.py:393
  43.9 1.4 %collective-permute-start.13 = (bf16[272,128]{1,0:T(8,128)(2,1)S(1)}, bf16[272,128]{1,0:T(8,128)(2,1)S(1)}, u32[]{:S(2)}, u32[]{:S(2)}) collective-permute-start(bf16[272,128]{1,0:T(8,128)(2,1)S(1)} %get-tuple-element.47), channel_id=1, source_target_pairs={{0,1},{1,0},{16,17},{17,16},{2,3},{3,2},{18,19},{19,18},{4,5},{5,4... | collective-permute-start | bytes 208904 | tf_op jit(solution)/shard_map/ppermute | solution.py:393
  45.2 1.5 %collective-permute-start.14 = (bf16[272,128]{1,0:T(8,128)(2,1)S(1)}, bf16[272,128]{1,0:T(8,128)(2,1)S(1)}, u32[]{:S(2)}, u32[]{:S(2)}) collective-permute-start(bf16[272,128]{1,0:T(8,128)(2,1)S(1)} %get-tuple-element.46), channel_id=1, source_target_pairs={{0,16},{1,17},{16,0},{17,1},{2,18},{3,19},{18,2},{19,3},{4,20},{5,... | collective-permute-start | bytes 208904 | tf_op jit(solution)/shard_map/ppermute | solution.py:393
  46.7 4.0 %shard_map.111 = (bf16[128,4096]{1,0:T(8,128)(2,1)}, bf16[128,4096]{1,0:T(8,128)(2,1)}) custom-call(s32[128]{0:T(128)S(1)} %copy-done.3, f32[1]{0:T(128)S(6)} %copy.19.gate_s, s32[1,128]{1,0:T(1,128)S(1)} %bitcast.31, bf16[4,256,1024]{2,1,0:T(8,128)(2,1)S(1)} %get-tuple-element.34.p16, bf16[4,256,1024]{2,1,0:T(8,128)(2,1)S(1)} %get-tuple-element.35.ds16, ...), custom_call_target="tpu_custom_call" | custom-call | flops 5000000000 | bytes 12582912 | tf_op jit(solution)/shard_map/pallas_call | solution.py:61
  50.7 0.0 collective-permute-done.12
  50.7 0.9 %collective-permute-start.15 = (bf16[272,128]{1,0:T(8,128)(2,1)S(1)}, bf16[272,128]{1,0:T(8,128)(2,1)S(1)}, u32[]{:S(2)}, u32[]{:S(2)}) collective-permute-start(bf16[272,128]{1,0:T(8,128)(2,1)S(1)} %get-tuple-element.45), channel_id=1, source_target_pairs={{0,17},{1,16},{16,1},{17,0},{2,19},{3,18},{18,3},{19,2},{4,21},{5,... | collective-permute-start | bytes 208904 | tf_op jit(solution)/shard_map/ppermute | solution.py:393
  51.6 2.1 %collective-permute-done.11 = bf16[3,272,128]{2,1,0:T(8,128)(2,1)S(1)} collective-permute-done((bf16[3,272,128]{2,1,0:T(8,128)(2,1)S(1)}, bf16[3,272,128]{2,1,0:T(8,128)(2,1)S(1)}, u32[]{:S(2)}, u32[]{:S(2)}) %collective-permute-start.11) | collective-permute-done | bytes 208928 | tf_op jit(solution)/shard_map/ppermute | solution.py:393
  53.7 0.0 collective-permute-done.10
  53.7 0.1 fusion.2
  53.9 0.1 collective-permute-start.16
  53.9 2.3 %collective-permute-start.17 = (bf16[272,128]{1,0:T(8,128)(2,1)S(1)}, bf16[272,128]{1,0:T(8,128)(2,1)S(1)}, u32[]{:S(2)}, u32[]{:S(2)}) collective-permute-start(bf16[272,128]{1,0:T(8,128)(2,1)S(1)} %get-tuple-element.53), channel_id=1, source_target_pairs={{0,4},{2,6},{4,0},{6,2},{1,5},{3,7},{5,1},{7,3},{8,12},{10,14},{12... | collective-permute-start | bytes 208904 | tf_op jit(solution)/shard_map/ppermute | solution.py:390
  56.2 0.0 collective-permute-done.13.refs_1_
  56.2 2.1 %collective-permute-start.18 = (bf16[272,128]{1,0:T(8,128)(2,1)S(1)}, bf16[272,128]{1,0:T(8,128)(2,1)S(1)}, u32[]{:S(2)}, u32[]{:S(2)}) collective-permute-start(bf16[272,128]{1,0:T(8,128)(2,1)S(1)} %get-tuple-element.52), channel_id=1, source_target_pairs={{0,6},{2,4},{4,2},{6,0},{1,7},{3,5},{5,3},{7,1},{8,14},{10,12},{12... | collective-permute-start | bytes 208904 | tf_op jit(solution)/shard_map/ppermute | solution.py:390
  58.3 0.0 collective-permute-done.14.refs_2_
  58.3 0.0 collective-permute-done.15.refs_3_
  58.3 0.0 collective-permute-done.16.refs_4_
  58.3 4.0 %collective-permute-done.17.refs_5_ = bf16[272,128]{1,0:T(8,128)(2,1)S(1)} collective-permute-done((bf16[272,128]{1,0:T(8,128)(2,1)S(1)}, bf16[272,128]{1,0:T(8,128)(2,1)S(1)}, u32[]{:S(2)}, u32[]{:S(2)}) %collective-permute-start.17) | collective-permute-done | bytes 69664 | tf_op jit(solution)/shard_map/ppermute | solution.py:390
  62.4 0.0 collective-permute-done.18.refs_6_
  62.4 0.7 %shard_map.112 = (f32[32,512]{1,0:T(8,128)}, f32[32,512]{1,0:T(8,128)}, f32[1]{0:T(128)}) custom-call(f32[8,128]{1,0:T(8,128)S(1)} %get-tuple-element.40.gate, bf16[272,128]{1,0:T(8,128)(2,1)S(1)} %get-tuple-element.48.refs_0_, bf16[272,128]{1,0:T(8,128)(2,1)S(1)} %collective-permute-done.13.refs_1_, bf16[272,128]{1,0:T(8,128)(2,1)S(1)} %collective-permute-done.14.refs_2_, ...), custom_call_target="tpu_custom_call" | custom-call | tf_op jit(solution)/shard_map/pallas_call | solution.py:372
  (17 shorter events, 0.2 us)
Async XLA Ops:
  2.2 8.9 %collective-permute-start.2 = (bf16[32,1024]{1,0:T(8,128)(2,1)S(1)}, bf16[32,1024]{1,0:T(8,128)(2,1)S(1)}, u32[]{:S(2)}, u32[]{:S(2)}) collective-permute-start(bf16[32,1024]{1,0:T(8,128)(2,1)S(1)} %constant_dynamic-update-slice_fusion), channel_id=1, source_target_pairs={{0,6},{2,4},{4,2},{6,0},{1,7},{3,5},{5,3},{7,1},{8,14},{10,12},{12... | collective-permute-start | bytes 196616 | tf_op jit(solution)/shard_map/ppermute | solution.py:390
  7.2 5.6 %collective-permute-start.1 = (bf16[32,1024]{1,0:T(8,128)(2,1)S(1)}, bf16[32,1024]{1,0:T(8,128)(2,1)S(1)}, u32[]{:S(2)}, u32[]{:S(2)}) collective-permute-start(bf16[32,1024]{1,0:T(8,128)(2,1)S(1)} %constant_dynamic-update-slice_fusion), channel_id=1, source_target_pairs={{0,4},{2,6},{4,0},{6,2},{1,5},{3,7},{5,1},{7,3},{8,12},{10,14},{12... | collective-permute-start | bytes 196616 | tf_op jit(solution)/shard_map/ppermute | solution.py:390
  7.2 5.6 %collective-permute-start = (bf16[32,1024]{1,0:T(8,128)(2,1)S(1)}, bf16[32,1024]{1,0:T(8,128)(2,1)S(1)}, u32[]{:S(2)}, u32[]{:S(2)}) collective-permute-start(bf16[32,1024]{1,0:T(8,128)(2,1)S(1)} %constant_dynamic-update-slice_fusion), channel_id=1, source_target_pairs={{0,2},{2,0},{4,6},{6,4},{1,3},{3,1},{5,7},{7,5},{8,10},{10,8},{12,... | collective-permute-start | bytes 196616 | tf_op jit(solution)/shard_map/ppermute | solution.py:390
  7.8 5.1 %collective-permute-start.3 = (bf16[32,1024]{1,0:T(8,128)(2,1)S(1)}, bf16[32,1024]{1,0:T(8,128)(2,1)S(1)}, u32[]{:S(2)}, u32[]{:S(2)}) collective-permute-start(bf16[32,1024]{1,0:T(8,128)(2,1)S(1)} %constant_dynamic-update-slice_fusion), channel_id=1, source_target_pairs={{0,1},{1,0},{16,17},{17,16},{2,3},{3,2},{18,19},{19,18},{4,5},{5,4... | collective-permute-start | bytes 196616 | tf_op jit(solution)/shard_map/ppermute | solution.py:393
  9.5 4.3 %collective-permute-start.4 = (bf16[32,1024]{1,0:T(8,128)(2,1)S(1)}, bf16[32,1024]{1,0:T(8,128)(2,1)S(1)}, u32[]{:S(2)}, u32[]{:S(2)}) collective-permute-start(bf16[32,1024]{1,0:T(8,128)(2,1)S(1)} %constant_dynamic-update-slice_fusion), channel_id=1, source_target_pairs={{0,16},{1,17},{16,0},{17,1},{2,18},{3,19},{18,2},{19,3},{4,20},{5,... | collective-permute-start | bytes 196616 | tf_op jit(solution)/shard_map/ppermute | solution.py:393
  13.8 6.3 %collective-permute-start.5 = (bf16[96,1024]{1,0:T(8,128)(2,1)S(1)}, bf16[96,1024]{1,0:T(8,128)(2,1)S(1)}, u32[]{:S(2)}, u32[]{:S(2)}) collective-permute-start(bf16[96,1024]{1,0:T(8,128)(2,1)S(1)} %pad_maximum_fusion.1), channel_id=1, source_target_pairs={{0,1},{1,0},{16,17},{17,16},{2,3},{3,2},{18,19},{19,18},{4,5},{5,4... | collective-permute-start | bytes 589832 | tf_op jit(solution)/shard_map/ppermute | solution.py:393
  14.4 7.8 %collective-permute-start.6 = (bf16[96,1024]{1,0:T(8,128)(2,1)S(1)}, bf16[96,1024]{1,0:T(8,128)(2,1)S(1)}, u32[]{:S(2)}, u32[]{:S(2)}) collective-permute-start(bf16[96,1024]{1,0:T(8,128)(2,1)S(1)} %pad_maximum_fusion.1), channel_id=1, source_target_pairs={{0,16},{1,17},{16,0},{17,1},{2,18},{3,19},{18,2},{19,3},{4,20},{5,... | collective-permute-start | bytes 589832 | tf_op jit(solution)/shard_map/ppermute | solution.py:393
  15.9 13.3 %copy-start.1 = (bf16[128,4096]{1,0:T(8,128)(2,1)S(1)}, bf16[128,4096]{1,0:T(8,128)(2,1)}, u32[]{:S(2)}) copy-start(bf16[128,4096]{1,0:T(8,128)(2,1)} %dy_ref.1) | copy-start | bytes 3145732
  16.0 13.3 %copy-start = (bf16[128,4096]{1,0:T(8,128)(2,1)S(1)}, bf16[128,4096]{1,0:T(8,128)(2,1)}, u32[]{:S(2)}) copy-start(bf16[128,4096]{1,0:T(8,128)(2,1)} %q_ref.1) | copy-start | bytes 3145732
  16.0 13.3 %copy-start.2 = (s32[4]{0:T(128)S(1)}, s32[4]{0:T(128)}, u32[]{:S(2)}) copy-start(s32[4]{0:T(128)} %cnt_s.1) | copy-start | bytes 52
  16.0 13.3 %copy-start.3 = (s32[128]{0:T(128)S(1)}, s32[128]{0:T(128)}, u32[]{:S(2)}) copy-start(s32[128]{0:T(128)} %seg_s.3) | copy-start | bytes 1540
  16.0 10.5 %collective-permute-start.7 = (bf16[128,1024]{1,0:T(8,128)(2,1)S(1)}, bf16[128,1024]{1,0:T(8,128)(2,1)S(1)}, u32[]{:S(2)}, u32[]{:S(2)}) collective-permute-start(bf16[128,1024]{1,0:T(8,128)(2,1)S(1)} %pad_maximum_fusion), channel_id=1, source_target_pairs={{0,17},{1,16},{16,1},{17,0},{2,19},{3,18},{18,3},{19,2},{4,21},{5,... | collective-permute-start | bytes 786440 | tf_op jit(solution)/shard_map/ppermute | solution.py:393
  26.5 2.7 %collective-permute-start.8 = (bf16[2,2,128,1024]{3,2,1,0:T(8,128)(2,1)S(1)}, bf16[2,2,128,1024]{3,2,1,0:T(8,128)(2,1)S(1)}, u32[]{:S(2)}, u32[]{:S(2)}) collective-permute-start(bf16[2,2,128,1024]{3,2,1,0:T(8,128)(2,1)S(1)} %bitcast.28), channel_id=1, source_target_pairs={{0,8},{8,0},{1,9},{9,1},{2,10},{10,2},{3,11},{11,3},{4,12},{12,4},... | collective-permute-start | bytes 3145736 | tf_op jit(solution)/shard_map/ppermute | solution.py:396
  37.1 2.8 %collective-permute-start.9 = (bf16[2,2,4,272,128]{4,3,2,1,0:T(8,128)(2,1)S(1)}, bf16[2,2,4,272,128]{4,3,2,1,0:T(8,128)(2,1)S(1)}, u32[]{:S(2)}, u32[]{:S(2)}) collective-permute-start(bf16[2,2,4,272,128]{4,3,2,1,0:T(8,128)(2,1)S(1)} %get-tuple-element.31), channel_id=1, source_target_pairs={{0,8},{8,0},{1,9},{9,1},{2,10},{10,2},{3,11},{11,3},{4,12},{12,4},... | collective-permute-start | bytes 3342344 | tf_op jit(solution)/shard_map/ppermute | solution.py:396
  40.3 10.4 %collective-permute-start.12 = (bf16[3,272,128]{2,1,0:T(8,128)(2,1)S(1)}, bf16[3,272,128]{2,1,0:T(8,128)(2,1)S(1)}, u32[]{:S(2)}, u32[]{:S(2)}) collective-permute-start(bf16[3,272,128]{2,1,0:T(8,128)(2,1)S(1)} %get-tuple-element.50), channel_id=1, source_target_pairs={{0,17},{1,16},{16,1},{17,0},{2,19},{3,18},{18,3},{19,2},{4,21},{5,... | collective-permute-start | bytes 626696 | tf_op jit(solution)/shard_map/ppermute | solution.py:393
  42.7 11.0 %collective-permute-start.11 = (bf16[3,272,128]{2,1,0:T(8,128)(2,1)S(1)}, bf16[3,272,128]{2,1,0:T(8,128)(2,1)S(1)}, u32[]{:S(2)}, u32[]{:S(2)}) collective-permute-start(bf16[3,272,128]{2,1,0:T(8,128)(2,1)S(1)} %get-tuple-element.51), channel_id=1, source_target_pairs={{0,16},{1,17},{16,0},{17,1},{2,18},{3,19},{18,2},{19,3},{4,20},{5,... | collective-permute-start | bytes 626696 | tf_op jit(solution)/shard_map/ppermute | solution.py:393
  43.2 10.5 %collective-permute-start.10 = (bf16[3,272,128]{2,1,0:T(8,128)(2,1)S(1)}, bf16[3,272,128]{2,1,0:T(8,128)(2,1)S(1)}, u32[]{:S(2)}, u32[]{:S(2)}) collective-permute-start(bf16[3,272,128]{2,1,0:T(8,128)(2,1)S(1)} %get-tuple-element.49), channel_id=1, source_target_pairs={{0,1},{1,0},{16,17},{17,16},{2,3},{3,2},{18,19},{19,18},{4,5},{5,4... | collective-permute-start | bytes 626696 | tf_op jit(solution)/shard_map/ppermute | solution.py:393
  43.9 12.3 %collective-permute-start.13 = (bf16[272,128]{1,0:T(8,128)(2,1)S(1)}, bf16[272,128]{1,0:T(8,128)(2,1)S(1)}, u32[]{:S(2)}, u32[]{:S(2)}) collective-permute-start(bf16[272,128]{1,0:T(8,128)(2,1)S(1)} %get-tuple-element.47), channel_id=1, source_target_pairs={{0,1},{1,0},{16,17},{17,16},{2,3},{3,2},{18,19},{19,18},{4,5},{5,4... | collective-permute-start | bytes 208904 | tf_op jit(solution)/shard_map/ppermute | solution.py:393
  45.2 13.1 %collective-permute-start.14 = (bf16[272,128]{1,0:T(8,128)(2,1)S(1)}, bf16[272,128]{1,0:T(8,128)(2,1)S(1)}, u32[]{:S(2)}, u32[]{:S(2)}) collective-permute-start(bf16[272,128]{1,0:T(8,128)(2,1)S(1)} %get-tuple-element.46), channel_id=1, source_target_pairs={{0,16},{1,17},{16,0},{17,1},{2,18},{3,19},{18,2},{19,3},{4,20},{5,... | collective-permute-start | bytes 208904 | tf_op jit(solution)/shard_map/ppermute | solution.py:393
  50.7 7.6 %collective-permute-start.15 = (bf16[272,128]{1,0:T(8,128)(2,1)S(1)}, bf16[272,128]{1,0:T(8,128)(2,1)S(1)}, u32[]{:S(2)}, u32[]{:S(2)}) collective-permute-start(bf16[272,128]{1,0:T(8,128)(2,1)S(1)} %get-tuple-element.45), channel_id=1, source_target_pairs={{0,17},{1,16},{16,1},{17,0},{2,19},{3,18},{18,3},{19,2},{4,21},{5,... | collective-permute-start | bytes 208904 | tf_op jit(solution)/shard_map/ppermute | solution.py:393
  53.9 4.5 %collective-permute-start.16 = (bf16[272,128]{1,0:T(8,128)(2,1)S(1)}, bf16[272,128]{1,0:T(8,128)(2,1)S(1)}, u32[]{:S(2)}, u32[]{:S(2)}) collective-permute-start(bf16[272,128]{1,0:T(8,128)(2,1)S(1)} %get-tuple-element.54), channel_id=1, source_target_pairs={{0,2},{2,0},{4,6},{6,4},{1,3},{3,1},{5,7},{7,5},{8,10},{10,8},{12,... | collective-permute-start | bytes 208904 | tf_op jit(solution)/shard_map/ppermute | solution.py:390
  53.9 8.4 %collective-permute-start.17 = (bf16[272,128]{1,0:T(8,128)(2,1)S(1)}, bf16[272,128]{1,0:T(8,128)(2,1)S(1)}, u32[]{:S(2)}, u32[]{:S(2)}) collective-permute-start(bf16[272,128]{1,0:T(8,128)(2,1)S(1)} %get-tuple-element.53), channel_id=1, source_target_pairs={{0,4},{2,6},{4,0},{6,2},{1,5},{3,7},{5,1},{7,3},{8,12},{10,14},{12... | collective-permute-start | bytes 208904 | tf_op jit(solution)/shard_map/ppermute | solution.py:390
  56.2 6.1 %collective-permute-start.18 = (bf16[272,128]{1,0:T(8,128)(2,1)S(1)}, bf16[272,128]{1,0:T(8,128)(2,1)S(1)}, u32[]{:S(2)}, u32[]{:S(2)}) collective-permute-start(bf16[272,128]{1,0:T(8,128)(2,1)S(1)} %get-tuple-element.52), channel_id=1, source_target_pairs={{0,6},{2,4},{4,2},{6,0},{1,7},{3,5},{5,3},{7,1},{8,14},{10,12},{12... | collective-permute-start | bytes 208904 | tf_op jit(solution)/shard_map/ppermute | solution.py:390

commit v11 on v10

--- a/solution.py
+++ b/solution.py
@@ -16,7 +16,7 @@
 LOG2E = 1.4426950408889634
 GROWS = 16
 GTOP = 8
-STRIP = 32
+STRIP = 64
 LINE = PEERS = (1, 2, 3)
 
 NT = (((1,), (1,)), ((), ()))
@@ -179,8 +179,8 @@
             qc[rows, side] = q * rowsel[i]
             dc[rows, side] = dy * rowsel[i]
 
-    span = 2 * tokens
-    blocks = group // 2
+    span = tokens
+    blocks = group
     strips = [slice(i, i + STRIP) for i in range(0, slots, STRIP)]
     tg2 = jnp.concatenate([tg, tg], axis=1)
 
@@ -193,7 +193,7 @@
         s = mm(kcat, qc[rows, :], NT)
         top = jnp.full((8, span), NEG, jnp.float32)
         for strip in strips:
-            x = s[strip] + jnp.concatenate([bias[strip], bias[strip]], axis=1)
+            x = s[strip] + bias[strip]
             sbuf[i, strip] = x
             top = jnp.maximum(top, jnp.max(x.reshape(STRIP // 8, 8, span), axis=0))
         dbuf[i] = mm(vcat, dc[rows, :], NT)
@@ -227,8 +227,8 @@
         ahead = products(h + 1) if h + 1 < blocks else None
         softmax(h, top)
         top = ahead
-        if h % 2:
-            more = slot_grads(h - 1, h + 1)
+        if h % 4 == 3:
+            more = slot_grads(h - 3, h + 1)
             dk, dv = dk + more[0], dv + more[1]
     dk = (scale * tg2 * dk).astype(jnp.bfloat16)
     g_ref[...] += fold8((dv * vcat.astype(jnp.float32))[:, :hd] + (dv * vcat.astype(jnp.float32))[:, hd:])
@@ -327,8 +327,8 @@
             pltpu.VMEM((rows, 2 * hd), jnp.bfloat16),
             pltpu.VMEM((rows, 2 * hd), jnp.bfloat16),
             pltpu.VMEM((2, tokens, hd), jnp.bfloat16),
-            pltpu.VMEM((2, slots, 2 * tokens), jnp.float32),
-            pltpu.VMEM((2, slots, 2 * tokens), jnp.float32),
+            pltpu.VMEM((2, slots, tokens), jnp.float32),
+            pltpu.VMEM((2, slots, tokens), jnp.float32),
             pltpu.VMEM((slots, tokens), jnp.float32),
             pltpu.SemaphoreType.DMA((5 + 4 * KV_HEADS,)),
             pltpu.SemaphoreType.DMA((KV_HEADS,)),

time: 63.3 us -> 64.1 us (1.013)
  Pallas kernels: 12.5 us -> 13.3 us
    pallas_call x1, Pallas kernels: 7.81 us -> 8.62 us  [scores(): pl.pallas_call(functools.partial(scores_kernel, mine, cols, folded), grid...]
where the time goes in v11:
time: 64.1 us; the launch traced here: 63.9 us
  starting transfers between devices  24.4 us (38%)
  waiting for transfers between devices  22.5 us (35%)
  Pallas kernels  13.3 us (21%)
  local copies, waits for them, and re-layouts  1.7 us (3%)
  between operations  1.44 us (2%)
    ppermute x11, starting transfers between devices, send_xy(): return lax.ppermute(x, ('x', 'y'), [(i, i ^ p) for i in range(4)])  14.1 us
    ppermute x11, waiting for transfers between devices, send_xy(): return lax.ppermute(x, ('x', 'y'), [(i, i ^ p) for i in range(4)])  12.1 us
    ppermute x6, starting transfers between devices, send_z(): return lax.ppermute(x, 'z', [(i, i ^ k) for i in range(cols)])  10.1 us
    pallas_call x1, Pallas kernels, scores(): pl.pallas_call(functools.partial(scores_kernel, mine, cols, folded), grid...  8.62 us
    ppermute x6, waiting for transfers between devices, send_z(): return lax.ppermute(x, 'z', [(i, i ^ k) for i in range(cols)])  5.83 us
    ppermute x2, waiting for transfers between devices, send_core(): return lax.ppermute(x, 'core', [(0, 1), (1, 0)])  4.62 us
    pallas_call x1, Pallas kernels, outputs(): pl.pallas_call(outputs_kernel, grid=(KV_HEADS,), in_specs=[smem, smem, pl...  4 us
  transfers between devices with their start and end apart: 19, of which 9 were waited for; matrix products, arithmetic and copies ran while one was open for 0% of the time, Pallas kernels for 6%

profile of v11, /device:TPU:0, one launch (start us, length us, event | category | flops | bytes accessed | tf_op | source)
XLA Modules:
  0.0 63.9 jit_solution(8620873521524093660)
XLA Ops:
  0.6 0.8 %constant_dynamic-update-slice_fusion.1 = bf16[32,1024]{1,0:T(8,128)(2,1)S(1)} fusion(bf16[32,512]{1,0:T(8,128)(2,1)} %param.8), kind=kLoop, calls=%fused_computation.19 | loop fusion | bytes 65536
  1.4 0.8 %constant_dynamic-update-slice_fusion = bf16[32,1024]{1,0:T(8,128)(2,1)S(1)} fusion(bf16[32,1024]{1,0:T(8,128)(2,1)S(1)} %constant_dynamic-update-slice_fusion.1, bf16[32,512]{1,0:T(8,128)(2,1)} %param.9), kind=kLoop, calls=%fused_computation.18 | loop fusion | bytes 65536 | tf_op jit(solution)/shard_map/concatenate | solution.py:398
  2.2 5.0 %collective-permute-start.2 = (bf16[32,1024]{1,0:T(8,128)(2,1)S(1)}, bf16[32,1024]{1,0:T(8,128)(2,1)S(1)}, u32[]{:S(2)}, u32[]{:S(2)}) collective-permute-start(bf16[32,1024]{1,0:T(8,128)(2,1)S(1)} %constant_dynamic-update-slice_fusion), channel_id=1, source_target_pairs={{0,6},{2,4},{4,2},{6,0},{1,7},{3,5},{5,3},{7,1},{8,14},{10,12},{12... | collective-permute-start | bytes 196616 | tf_op jit(solution)/shard_map/ppermute | solution.py:390
  7.2 0.0 collective-permute-start.1
  7.2 0.6 collective-permute-start
  7.8 1.7 %collective-permute-start.3 = (bf16[32,1024]{1,0:T(8,128)(2,1)S(1)}, bf16[32,1024]{1,0:T(8,128)(2,1)S(1)}, u32[]{:S(2)}, u32[]{:S(2)}) collective-permute-start(bf16[32,1024]{1,0:T(8,128)(2,1)S(1)} %constant_dynamic-update-slice_fusion), channel_id=1, source_target_pairs={{0,1},{1,0},{16,17},{17,16},{2,3},{3,2},{18,19},{19,18},{4,5},{5,4... | collective-permute-start | bytes 196616 | tf_op jit(solution)/shard_map/ppermute | solution.py:393
  9.5 1.5 %collective-permute-start.4 = (bf16[32,1024]{1,0:T(8,128)(2,1)S(1)}, bf16[32,1024]{1,0:T(8,128)(2,1)S(1)}, u32[]{:S(2)}, u32[]{:S(2)}) collective-permute-start(bf16[32,1024]{1,0:T(8,128)(2,1)S(1)} %constant_dynamic-update-slice_fusion), channel_id=1, source_target_pairs={{0,16},{1,17},{16,0},{17,1},{2,18},{3,19},{18,2},{19,3},{4,20},{5,... | collective-permute-start | bytes 196616 | tf_op jit(solution)/shard_map/ppermute | solution.py:393
  11.0 0.0 collective-permute-done.2
  11.0 1.8 %collective-permute-done.1 = bf16[32,1024]{1,0:T(8,128)(2,1)S(1)} collective-permute-done((bf16[32,1024]{1,0:T(8,128)(2,1)S(1)}, bf16[32,1024]{1,0:T(8,128)(2,1)S(1)}, u32[]{:S(2)}, u32[]{:S(2)}) %collective-permute-start.1) | collective-permute-done | bytes 65568 | tf_op jit(solution)/shard_map/ppermute | solution.py:390
  12.8 0.0 collective-permute-done
  12.8 0.0 collective-permute-done.3
  12.8 0.9 %collective-permute-done.4 = bf16[32,1024]{1,0:T(8,128)(2,1)S(1)} collective-permute-done((bf16[32,1024]{1,0:T(8,128)(2,1)S(1)}, bf16[32,1024]{1,0:T(8,128)(2,1)S(1)}, u32[]{:S(2)}, u32[]{:S(2)}) %collective-permute-start.4) | collective-permute-done | bytes 65568 | tf_op jit(solution)/shard_map/ppermute | solution.py:393
  13.8 0.7 %collective-permute-start.5 = (bf16[96,1024]{1,0:T(8,128)(2,1)S(1)}, bf16[96,1024]{1,0:T(8,128)(2,1)S(1)}, u32[]{:S(2)}, u32[]{:S(2)}) collective-permute-start(bf16[96,1024]{1,0:T(8,128)(2,1)S(1)} %pad_maximum_fusion.1), channel_id=1, source_target_pairs={{0,1},{1,0},{16,17},{17,16},{2,3},{3,2},{18,19},{19,18},{4,5},{5,4... | collective-permute-start | bytes 589832 | tf_op jit(solution)/shard_map/ppermute | solution.py:393
  14.4 1.5 %collective-permute-start.6 = (bf16[96,1024]{1,0:T(8,128)(2,1)S(1)}, bf16[96,1024]{1,0:T(8,128)(2,1)S(1)}, u32[]{:S(2)}, u32[]{:S(2)}) collective-permute-start(bf16[96,1024]{1,0:T(8,128)(2,1)S(1)} %pad_maximum_fusion.1), channel_id=1, source_target_pairs={{0,16},{1,17},{16,0},{17,1},{2,18},{3,19},{18,2},{19,3},{4,20},{5,... | collective-permute-start | bytes 589832 | tf_op jit(solution)/shard_map/ppermute | solution.py:393
  16.0 0.0 copy-start
  16.0 0.0 copy-start.2
  16.0 0.0 copy-start.3
  16.0 1.4 %collective-permute-start.7 = (bf16[128,1024]{1,0:T(8,128)(2,1)S(1)}, bf16[128,1024]{1,0:T(8,128)(2,1)S(1)}, u32[]{:S(2)}, u32[]{:S(2)}) collective-permute-start(bf16[128,1024]{1,0:T(8,128)(2,1)S(1)} %pad_maximum_fusion), channel_id=1, source_target_pairs={{0,17},{1,16},{16,1},{17,0},{2,19},{3,18},{18,3},{19,2},{4,21},{5,... | collective-permute-start | bytes 786440 | tf_op jit(solution)/shard_map/ppermute | solution.py:393
  17.4 2.6 %collective-permute-done.5 = bf16[96,1024]{1,0:T(8,128)(2,1)S(1)} collective-permute-done((bf16[96,1024]{1,0:T(8,128)(2,1)S(1)}, bf16[96,1024]{1,0:T(8,128)(2,1)S(1)}, u32[]{:S(2)}, u32[]{:S(2)}) %collective-permute-start.5) | collective-permute-done | bytes 196640 | tf_op jit(solution)/shard_map/ppermute | solution.py:393
  20.1 2.2 %collective-permute-done.6 = bf16[96,1024]{1,0:T(8,128)(2,1)S(1)} collective-permute-done((bf16[96,1024]{1,0:T(8,128)(2,1)S(1)}, bf16[96,1024]{1,0:T(8,128)(2,1)S(1)}, u32[]{:S(2)}, u32[]{:S(2)}) %collective-permute-start.6) | collective-permute-done | bytes 196640 | tf_op jit(solution)/shard_map/ppermute | solution.py:393
  22.3 4.3 %collective-permute-done.7 = bf16[128,1024]{1,0:T(8,128)(2,1)S(1)} collective-permute-done((bf16[128,1024]{1,0:T(8,128)(2,1)S(1)}, bf16[128,1024]{1,0:T(8,128)(2,1)S(1)}, u32[]{:S(2)}, u32[]{:S(2)}) %collective-permute-start.7) | collective-permute-done | bytes 262176 | tf_op jit(solution)/shard_map/ppermute | solution.py:393
  26.5 0.1 collective-permute-start.8
  27.3 2.0 %collective-permute-done.8.other = bf16[2,2,128,1024]{3,2,1,0:T(8,128)(2,1)S(1)} collective-permute-done((bf16[2,2,128,1024]{3,2,1,0:T(8,128)(2,1)S(1)}, bf16[2,2,128,1024]{3,2,1,0:T(8,128)(2,1)S(1)}, u32[]{:S(2)}, u32[]{:S(2)}) %collective-permute-start.8) | collective-permute-done | bytes 1048608 | tf_op jit(solution)/shard_map/ppermute | solution.py:396
  29.3 8.6 %shard_map.110 = (bf16[4,256,1024]{2,1,0:T(8,128)(2,1)S(1)}, bf16[4,256,1024]{2,1,0:T(8,128)(2,1)S(1)}, bf16[2,256,1024]{2,1,0:T(8,128)(2,1)S(1)}, bf16[2,2,4,27...) custom-call(s32[128]{0:T(128)S(1)} %copy-done.3, s32[4]{0:T(128)S(1)} %copy-done.2, ...), custom_call_target="tpu_custom_call" | custom-call | flops 2147483648 | bytes 12582912 | tf_op jit(solution)/shard_map/pallas_call | solution.py:304
  37.9 0.2 collective-permute-start.9
  38.1 2.6 %collective-permute-done.9 = bf16[2,2,4,272,128]{4,3,2,1,0:T(8,128)(2,1)S(1)} collective-permute-done((bf16[2,2,4,272,128]{4,3,2,1,0:T(8,128)(2,1)S(1)}, bf16[2,2,4,272,128]{4,3,2,1,0:T(8,128)(2,1)S(1)}, u32[]{:S(2)}, u32[]{:S(2)}) %collective-permute-start.9) | collective-permute-done | bytes 1114144 | tf_op jit(solution)/shard_map/ppermute | solution.py:396
  40.7 0.3 add_convert_fusion
  41.1 2.4 %collective-permute-start.12 = (bf16[3,272,128]{2,1,0:T(8,128)(2,1)S(1)}, bf16[3,272,128]{2,1,0:T(8,128)(2,1)S(1)}, u32[]{:S(2)}, u32[]{:S(2)}) collective-permute-start(bf16[3,272,128]{2,1,0:T(8,128)(2,1)S(1)} %get-tuple-element.50), channel_id=1, source_target_pairs={{0,17},{1,16},{16,1},{17,0},{2,19},{3,18},{18,3},{19,2},{4,21},{5,... | collective-permute-start | bytes 626696 | tf_op jit(solution)/shard_map/ppermute | solution.py:393
  43.5 0.5 collective-permute-start.11
  44.0 0.7 %collective-permute-start.10 = (bf16[3,272,128]{2,1,0:T(8,128)(2,1)S(1)}, bf16[3,272,128]{2,1,0:T(8,128)(2,1)S(1)}, u32[]{:S(2)}, u32[]{:S(2)}) collective-permute-start(bf16[3,272,128]{2,1,0:T(8,128)(2,1)S(1)} %get-tuple-element.49), channel_id=1, source_target_pairs={{0,1},{1,0},{16,17},{17,16},{2,3},{3,2},{18,19},{19,18},{4,5},{5,4... | collective-permute-start | bytes 626696 | tf_op jit(solution)/shard_map/ppermute | solution.py:393
  44.7 1.4 %collective-permute-start.13 = (bf16[272,128]{1,0:T(8,128)(2,1)S(1)}, bf16[272,128]{1,0:T(8,128)(2,1)S(1)}, u32[]{:S(2)}, u32[]{:S(2)}) collective-permute-start(bf16[272,128]{1,0:T(8,128)(2,1)S(1)} %get-tuple-element.47), channel_id=1, source_target_pairs={{0,1},{1,0},{16,17},{17,16},{2,3},{3,2},{18,19},{19,18},{4,5},{5,4... | collective-permute-start | bytes 208904 | tf_op jit(solution)/shard_map/ppermute | solution.py:393
  46.0 1.5 %collective-permute-start.14 = (bf16[272,128]{1,0:T(8,128)(2,1)S(1)}, bf16[272,128]{1,0:T(8,128)(2,1)S(1)}, u32[]{:S(2)}, u32[]{:S(2)}) collective-permute-start(bf16[272,128]{1,0:T(8,128)(2,1)S(1)} %get-tuple-element.46), channel_id=1, source_target_pairs={{0,16},{1,17},{16,0},{17,1},{2,18},{3,19},{18,2},{19,3},{4,20},{5,... | collective-permute-start | bytes 208904 | tf_op jit(solution)/shard_map/ppermute | solution.py:393
  47.5 4.0 %shard_map.111 = (bf16[128,4096]{1,0:T(8,128)(2,1)}, bf16[128,4096]{1,0:T(8,128)(2,1)}) custom-call(s32[128]{0:T(128)S(1)} %copy-done.3, f32[1]{0:T(128)S(6)} %copy.19.gate_s, s32[1,128]{1,0:T(1,128)S(1)} %bitcast.31, bf16[4,256,1024]{2,1,0:T(8,128)(2,1)S(1)} %get-tuple-element.34.p16, bf16[4,256,1024]{2,1,0:T(8,128)(2,1)S(1)} %get-tuple-element.35.ds16, ...), custom_call_target="tpu_custom_call" | custom-call | flops 5000000000 | bytes 12582912 | tf_op jit(solution)/shard_map/pallas_call | solution.py:61
  51.5 0.0 collective-permute-done.12
  51.5 0.9 %collective-permute-start.15 = (bf16[272,128]{1,0:T(8,128)(2,1)S(1)}, bf16[272,128]{1,0:T(8,128)(2,1)S(1)}, u32[]{:S(2)}, u32[]{:S(2)}) collective-permute-start(bf16[272,128]{1,0:T(8,128)(2,1)S(1)} %get-tuple-element.45), channel_id=1, source_target_pairs={{0,17},{1,16},{16,1},{17,0},{2,19},{3,18},{18,3},{19,2},{4,21},{5,... | collective-permute-start | bytes 208904 | tf_op jit(solution)/shard_map/ppermute | solution.py:393
  52.4 2.1 %collective-permute-done.11 = bf16[3,272,128]{2,1,0:T(8,128)(2,1)S(1)} collective-permute-done((bf16[3,272,128]{2,1,0:T(8,128)(2,1)S(1)}, bf16[3,272,128]{2,1,0:T(8,128)(2,1)S(1)}, u32[]{:S(2)}, u32[]{:S(2)}) %collective-permute-start.11) | collective-permute-done | bytes 208928 | tf_op jit(solution)/shard_map/ppermute | solution.py:393
  54.5 0.0 collective-permute-done.10
  54.5 0.1 fusion.2
  54.7 0.1 collective-permute-start.16
  54.7 2.3 %collective-permute-start.17 = (bf16[272,128]{1,0:T(8,128)(2,1)S(1)}, bf16[272,128]{1,0:T(8,128)(2,1)S(1)}, u32[]{:S(2)}, u32[]{:S(2)}) collective-permute-start(bf16[272,128]{1,0:T(8,128)(2,1)S(1)} %get-tuple-element.53), channel_id=1, source_target_pairs={{0,4},{2,6},{4,0},{6,2},{1,5},{3,7},{5,1},{7,3},{8,12},{10,14},{12... | collective-permute-start | bytes 208904 | tf_op jit(solution)/shard_map/ppermute | solution.py:390
  57.0 0.0 collective-permute-done.13.refs_1_
  57.0 2.1 %collective-permute-start.18 = (bf16[272,128]{1,0:T(8,128)(2,1)S(1)}, bf16[272,128]{1,0:T(8,128)(2,1)S(1)}, u32[]{:S(2)}, u32[]{:S(2)}) collective-permute-start(bf16[272,128]{1,0:T(8,128)(2,1)S(1)} %get-tuple-element.52), channel_id=1, source_target_pairs={{0,6},{2,4},{4,2},{6,0},{1,7},{3,5},{5,3},{7,1},{8,14},{10,12},{12... | collective-permute-start | bytes 208904 | tf_op jit(solution)/shard_map/ppermute | solution.py:390
  59.1 0.0 collective-permute-done.14.refs_2_
  59.1 0.0 collective-permute-done.15.refs_3_
  59.1 0.0 collective-permute-done.16.refs_4_
  59.1 4.0 %collective-permute-done.17.refs_5_ = bf16[272,128]{1,0:T(8,128)(2,1)S(1)} collective-permute-done((bf16[272,128]{1,0:T(8,128)(2,1)S(1)}, bf16[272,128]{1,0:T(8,128)(2,1)S(1)}, u32[]{:S(2)}, u32[]{:S(2)}) %collective-permute-start.17) | collective-permute-done | bytes 69664 | tf_op jit(solution)/shard_map/ppermute | solution.py:390
  63.2 0.0 collective-permute-done.18.refs_6_
  63.2 0.7 %shard_map.112 = (f32[32,512]{1,0:T(8,128)}, f32[32,512]{1,0:T(8,128)}, f32[1]{0:T(128)}) custom-call(f32[8,128]{1,0:T(8,128)S(1)} %get-tuple-element.40.gate, bf16[272,128]{1,0:T(8,128)(2,1)S(1)} %get-tuple-element.48.refs_0_, bf16[272,128]{1,0:T(8,128)(2,1)S(1)} %collective-permute-done.13.refs_1_, bf16[272,128]{1,0:T(8,128)(2,1)S(1)} %collective-permute-done.14.refs_2_, ...), custom_call_target="tpu_custom_call" | custom-call | tf_op jit(solution)/shard_map/pallas_call | solution.py:372
  (17 shorter events, 0.2 us)
Async XLA Ops:
  2.2 8.9 %collective-permute-start.2 = (bf16[32,1024]{1,0:T(8,128)(2,1)S(1)}, bf16[32,1024]{1,0:T(8,128)(2,1)S(1)}, u32[]{:S(2)}, u32[]{:S(2)}) collective-permute-start(bf16[32,1024]{1,0:T(8,128)(2,1)S(1)} %constant_dynamic-update-slice_fusion), channel_id=1, source_target_pairs={{0,6},{2,4},{4,2},{6,0},{1,7},{3,5},{5,3},{7,1},{8,14},{10,12},{12... | collective-permute-start | bytes 196616 | tf_op jit(solution)/shard_map/ppermute | solution.py:390
  7.2 5.6 %collective-permute-start.1 = (bf16[32,1024]{1,0:T(8,128)(2,1)S(1)}, bf16[32,1024]{1,0:T(8,128)(2,1)S(1)}, u32[]{:S(2)}, u32[]{:S(2)}) collective-permute-start(bf16[32,1024]{1,0:T(8,128)(2,1)S(1)} %constant_dynamic-update-slice_fusion), channel_id=1, source_target_pairs={{0,4},{2,6},{4,0},{6,2},{1,5},{3,7},{5,1},{7,3},{8,12},{10,14},{12... | collective-permute-start | bytes 196616 | tf_op jit(solution)/shard_map/ppermute | solution.py:390
  7.2 5.6 %collective-permute-start = (bf16[32,1024]{1,0:T(8,128)(2,1)S(1)}, bf16[32,1024]{1,0:T(8,128)(2,1)S(1)}, u32[]{:S(2)}, u32[]{:S(2)}) collective-permute-start(bf16[32,1024]{1,0:T(8,128)(2,1)S(1)} %constant_dynamic-update-slice_fusion), channel_id=1, source_target_pairs={{0,2},{2,0},{4,6},{6,4},{1,3},{3,1},{5,7},{7,5},{8,10},{10,8},{12,... | collective-permute-start | bytes 196616 | tf_op jit(solution)/shard_map/ppermute | solution.py:390
  7.8 5.1 %collective-permute-start.3 = (bf16[32,1024]{1,0:T(8,128)(2,1)S(1)}, bf16[32,1024]{1,0:T(8,128)(2,1)S(1)}, u32[]{:S(2)}, u32[]{:S(2)}) collective-permute-start(bf16[32,1024]{1,0:T(8,128)(2,1)S(1)} %constant_dynamic-update-slice_fusion), channel_id=1, source_target_pairs={{0,1},{1,0},{16,17},{17,16},{2,3},{3,2},{18,19},{19,18},{4,5},{5,4... | collective-permute-start | bytes 196616 | tf_op jit(solution)/shard_map/ppermute | solution.py:393
  9.5 4.3 %collective-permute-start.4 = (bf16[32,1024]{1,0:T(8,128)(2,1)S(1)}, bf16[32,1024]{1,0:T(8,128)(2,1)S(1)}, u32[]{:S(2)}, u32[]{:S(2)}) collective-permute-start(bf16[32,1024]{1,0:T(8,128)(2,1)S(1)} %constant_dynamic-update-slice_fusion), channel_id=1, source_target_pairs={{0,16},{1,17},{16,0},{17,1},{2,18},{3,19},{18,2},{19,3},{4,20},{5,... | collective-permute-start | bytes 196616 | tf_op jit(solution)/shard_map/ppermute | solution.py:393
  13.8 6.3 %collective-permute-start.5 = (bf16[96,1024]{1,0:T(8,128)(2,1)S(1)}, bf16[96,1024]{1,0:T(8,128)(2,1)S(1)}, u32[]{:S(2)}, u32[]{:S(2)}) collective-permute-start(bf16[96,1024]{1,0:T(8,128)(2,1)S(1)} %pad_maximum_fusion.1), channel_id=1, source_target_pairs={{0,1},{1,0},{16,17},{17,16},{2,3},{3,2},{18,19},{19,18},{4,5},{5,4... | collective-permute-start | bytes 589832 | tf_op jit(solution)/shard_map/ppermute | solution.py:393
  14.4 7.8 %collective-permute-start.6 = (bf16[96,1024]{1,0:T(8,128)(2,1)S(1)}, bf16[96,1024]{1,0:T(8,128)(2,1)S(1)}, u32[]{:S(2)}, u32[]{:S(2)}) collective-permute-start(bf16[96,1024]{1,0:T(8,128)(2,1)S(1)} %pad_maximum_fusion.1), channel_id=1, source_target_pairs={{0,16},{1,17},{16,0},{17,1},{2,18},{3,19},{18,2},{19,3},{4,20},{5,... | collective-permute-start | bytes 589832 | tf_op jit(solution)/shard_map/ppermute | solution.py:393
  15.9 13.3 %copy-start.1 = (bf16[128,4096]{1,0:T(8,128)(2,1)S(1)}, bf16[128,4096]{1,0:T(8,128)(2,1)}, u32[]{:S(2)}) copy-start(bf16[128,4096]{1,0:T(8,128)(2,1)} %dy_ref.1) | copy-start | bytes 3145732
  16.0 13.3 %copy-start = (bf16[128,4096]{1,0:T(8,128)(2,1)S(1)}, bf16[128,4096]{1,0:T(8,128)(2,1)}, u32[]{:S(2)}) copy-start(bf16[128,4096]{1,0:T(8,128)(2,1)} %q_ref.1) | copy-start | bytes 3145732
  16.0 13.3 %copy-start.2 = (s32[4]{0:T(128)S(1)}, s32[4]{0:T(128)}, u32[]{:S(2)}) copy-start(s32[4]{0:T(128)} %cnt_s.1) | copy-start | bytes 52
  16.0 13.3 %copy-start.3 = (s32[128]{0:T(128)S(1)}, s32[128]{0:T(128)}, u32[]{:S(2)}) copy-start(s32[128]{0:T(128)} %seg_s.3) | copy-start | bytes 1540
  16.0 10.5 %collective-permute-start.7 = (bf16[128,1024]{1,0:T(8,128)(2,1)S(1)}, bf16[128,1024]{1,0:T(8,128)(2,1)S(1)}, u32[]{:S(2)}, u32[]{:S(2)}) collective-permute-start(bf16[128,1024]{1,0:T(8,128)(2,1)S(1)} %pad_maximum_fusion), channel_id=1, source_target_pairs={{0,17},{1,16},{16,1},{17,0},{2,19},{3,18},{18,3},{19,2},{4,21},{5,... | collective-permute-start | bytes 786440 | tf_op jit(solution)/shard_map/ppermute | solution.py:393
  26.5 2.7 %collective-permute-start.8 = (bf16[2,2,128,1024]{3,2,1,0:T(8,128)(2,1)S(1)}, bf16[2,2,128,1024]{3,2,1,0:T(8,128)(2,1)S(1)}, u32[]{:S(2)}, u32[]{:S(2)}) collective-permute-start(bf16[2,2,128,1024]{3,2,1,0:T(8,128)(2,1)S(1)} %bitcast.28), channel_id=1, source_target_pairs={{0,8},{8,0},{1,9},{9,1},{2,10},{10,2},{3,11},{11,3},{4,12},{12,4},... | collective-permute-start | bytes 3145736 | tf_op jit(solution)/shard_map/ppermute | solution.py:396
  37.9 2.8 %collective-permute-start.9 = (bf16[2,2,4,272,128]{4,3,2,1,0:T(8,128)(2,1)S(1)}, bf16[2,2,4,272,128]{4,3,2,1,0:T(8,128)(2,1)S(1)}, u32[]{:S(2)}, u32[]{:S(2)}) collective-permute-start(bf16[2,2,4,272,128]{4,3,2,1,0:T(8,128)(2,1)S(1)} %get-tuple-element.31), channel_id=1, source_target_pairs={{0,8},{8,0},{1,9},{9,1},{2,10},{10,2},{3,11},{11,3},{4,12},{12,4},... | collective-permute-start | bytes 3342344 | tf_op jit(solution)/shard_map/ppermute | solution.py:396
  41.1 10.4 %collective-permute-start.12 = (bf16[3,272,128]{2,1,0:T(8,128)(2,1)S(1)}, bf16[3,272,128]{2,1,0:T(8,128)(2,1)S(1)}, u32[]{:S(2)}, u32[]{:S(2)}) collective-permute-start(bf16[3,272,128]{2,1,0:T(8,128)(2,1)S(1)} %get-tuple-element.50), channel_id=1, source_target_pairs={{0,17},{1,16},{16,1},{17,0},{2,19},{3,18},{18,3},{19,2},{4,21},{5,... | collective-permute-start | bytes 626696 | tf_op jit(solution)/shard_map/ppermute | solution.py:393
  43.5 11.0 %collective-permute-start.11 = (bf16[3,272,128]{2,1,0:T(8,128)(2,1)S(1)}, bf16[3,272,128]{2,1,0:T(8,128)(2,1)S(1)}, u32[]{:S(2)}, u32[]{:S(2)}) collective-permute-start(bf16[3,272,128]{2,1,0:T(8,128)(2,1)S(1)} %get-tuple-element.51), channel_id=1, source_target_pairs={{0,16},{1,17},{16,0},{17,1},{2,18},{3,19},{18,2},{19,3},{4,20},{5,... | collective-permute-start | bytes 626696 | tf_op jit(solution)/shard_map/ppermute | solution.py:393
  44.0 10.5 %collective-permute-start.10 = (bf16[3,272,128]{2,1,0:T(8,128)(2,1)S(1)}, bf16[3,272,128]{2,1,0:T(8,128)(2,1)S(1)}, u32[]{:S(2)}, u32[]{:S(2)}) collective-permute-start(bf16[3,272,128]{2,1,0:T(8,128)(2,1)S(1)} %get-tuple-element.49), channel_id=1, source_target_pairs={{0,1},{1,0},{16,17},{17,16},{2,3},{3,2},{18,19},{19,18},{4,5},{5,4... | collective-permute-start | bytes 626696 | tf_op jit(solution)/shard_map/ppermute | solution.py:393
  44.7 12.3 %collective-permute-start.13 = (bf16[272,128]{1,0:T(8,128)(2,1)S(1)}, bf16[272,128]{1,0:T(8,128)(2,1)S(1)}, u32[]{:S(2)}, u32[]{:S(2)}) collective-permute-start(bf16[272,128]{1,0:T(8,128)(2,1)S(1)} %get-tuple-element.47), channel_id=1, source_target_pairs={{0,1},{1,0},{16,17},{17,16},{2,3},{3,2},{18,19},{19,18},{4,5},{5,4... | collective-permute-start | bytes 208904 | tf_op jit(solution)/shard_map/ppermute | solution.py:393
  46.0 13.1 %collective-permute-start.14 = (bf16[272,128]{1,0:T(8,128)(2,1)S(1)}, bf16[272,128]{1,0:T(8,128)(2,1)S(1)}, u32[]{:S(2)}, u32[]{:S(2)}) collective-permute-start(bf16[272,128]{1,0:T(8,128)(2,1)S(1)} %get-tuple-element.46), channel_id=1, source_target_pairs={{0,16},{1,17},{16,0},{17,1},{2,18},{3,19},{18,2},{19,3},{4,20},{5,... | collective-permute-start | bytes 208904 | tf_op jit(solution)/shard_map/ppermute | solution.py:393
  51.5 7.6 %collective-permute-start.15 = (bf16[272,128]{1,0:T(8,128)(2,1)S(1)}, bf16[272,128]{1,0:T(8,128)(2,1)S(1)}, u32[]{:S(2)}, u32[]{:S(2)}) collective-permute-start(bf16[272,128]{1,0:T(8,128)(2,1)S(1)} %get-tuple-element.45), channel_id=1, source_target_pairs={{0,17},{1,16},{16,1},{17,0},{2,19},{3,18},{18,3},{19,2},{4,21},{5,... | collective-permute-start | bytes 208904 | tf_op jit(solution)/shard_map/ppermute | solution.py:393
  54.7 4.5 %collective-permute-start.16 = (bf16[272,128]{1,0:T(8,128)(2,1)S(1)}, bf16[272,128]{1,0:T(8,128)(2,1)S(1)}, u32[]{:S(2)}, u32[]{:S(2)}) collective-permute-start(bf16[272,128]{1,0:T(8,128)(2,1)S(1)} %get-tuple-element.54), channel_id=1, source_target_pairs={{0,2},{2,0},{4,6},{6,4},{1,3},{3,1},{5,7},{7,5},{8,10},{10,8},{12,... | collective-permute-start | bytes 208904 | tf_op jit(solution)/shard_map/ppermute | solution.py:390
  54.7 8.4 %collective-permute-start.17 = (bf16[272,128]{1,0:T(8,128)(2,1)S(1)}, bf16[272,128]{1,0:T(8,128)(2,1)S(1)}, u32[]{:S(2)}, u32[]{:S(2)}) collective-permute-start(bf16[272,128]{1,0:T(8,128)(2,1)S(1)} %get-tuple-element.53), channel_id=1, source_target_pairs={{0,4},{2,6},{4,0},{6,2},{1,5},{3,7},{5,1},{7,3},{8,12},{10,14},{12... | collective-permute-start | bytes 208904 | tf_op jit(solution)/shard_map/ppermute | solution.py:390
  57.0 6.1 %collective-permute-start.18 = (bf16[272,128]{1,0:T(8,128)(2,1)S(1)}, bf16[272,128]{1,0:T(8,128)(2,1)S(1)}, u32[]{:S(2)}, u32[]{:S(2)}) collective-permute-start(bf16[272,128]{1,0:T(8,128)(2,1)S(1)} %get-tuple-element.52), channel_id=1, source_target_pairs={{0,6},{2,4},{4,2},{6,0},{1,7},{3,5},{5,3},{7,1},{8,14},{10,12},{12... | collective-permute-start | bytes 208904 | tf_op jit(solution)/shard_map/ppermute | solution.py:390

commit v12 on v10

--- a/solution.py
+++ b/solution.py
@@ -187,48 +187,42 @@
     def fold8(x):
         return jnp.sum(x.reshape(x.shape[0] // 8, 8, x.shape[1]), axis=0)
 
-    def products(h):
-        i = h % 2
-        rows = slice(h * span, (h + 1) * span)
-        s = mm(kcat, qc[rows, :], NT)
-        top = jnp.full((8, span), NEG, jnp.float32)
-        for strip in strips:
-            x = s[strip] + jnp.concatenate([bias[strip], bias[strip]], axis=1)
-            sbuf[i, strip] = x
-            top = jnp.maximum(top, jnp.max(x.reshape(STRIP // 8, 8, span), axis=0))
-        dbuf[i] = mm(vcat, dc[rows, :], NT)
-        return top
-
-    def softmax(h, top):
-        i = h % 2
-        rows = slice(h * span, (h + 1) * span)
-        top = jnp.max(top, axis=0, keepdims=True) * (scale * LOG2E)
-        norm = jnp.zeros((8, span), jnp.float32)
-        dots = jnp.zeros((8, span), jnp.float32)
-        for strip in strips:
-            e = jnp.exp2(sbuf[i, strip] * (scale * LOG2E) - top)
-            sbuf[i, strip] = e
-            norm = norm + fold8(e)
-            dots = dots + fold8(e * dbuf[i, strip])
-        inv = 1.0 / jnp.sum(norm, axis=0, keepdims=True)
-        delta = inv * jnp.sum(dots, axis=0, keepdims=True)
-        for strip in strips:
-            p = sbuf[i, strip] * inv
-            p16[0, strip, rows] = p.astype(jnp.bfloat16)
-            ds16[0, strip, rows] = (p * (dbuf[i, strip] - delta)).astype(jnp.bfloat16)
-
     def slot_grads(lo, hi):
         rows = slice(lo * span, hi * span)
         return mm(ds16[0, :, rows], qc[rows, :], NN), mm(p16[0, :, rows], dc[rows, :], NN)
 
-    top = products(0)
     dk = dv = 0.0
-    for h in range(blocks):
-        ahead = products(h + 1) if h + 1 < blocks else None
-        softmax(h, top)
-        top = ahead
-        if h % 2:
-            more = slot_grads(h - 1, h + 1)
+    tops, invs, deltas = {}, {}, {}
+    for t in range(blocks + 2):
+        new, mid, old = t, t - 1, t - 2
+        if new < blocks:
+            rows = slice(new * span, (new + 1) * span)
+            s = mm(kcat, qc[rows, :], NT)
+            dbuf[new % 3] = mm(vcat, dc[rows, :], NT)
+            top = jnp.full((8, span), NEG, jnp.float32)
+        norm = dots = jnp.zeros((8, span), jnp.float32)
+        for strip in strips:
+            if old >= 0:
+                rows = slice(old * span, (old + 1) * span)
+                p = sbuf[old % 3, strip] * invs[old]
+                p16[0, strip, rows] = p.astype(jnp.bfloat16)
+                ds16[0, strip, rows] = (p * (dbuf[old % 3, strip] - deltas[old])).astype(jnp.bfloat16)
+            if 0 <= mid < blocks:
+                e = jnp.exp2(sbuf[mid % 3, strip] * (scale * LOG2E) - tops[mid])
+                sbuf[mid % 3, strip] = e
+                norm = norm + fold8(e)
+                dots = dots + fold8(e * dbuf[mid % 3, strip])
+            if new < blocks:
+                x = s[strip] + jnp.concatenate([bias[strip], bias[strip]], axis=1)
+                sbuf[new % 3, strip] = x
+                top = jnp.maximum(top, jnp.max(x.reshape(STRIP // 8, 8, span), axis=0))
+        if new < blocks:
+            tops[new] = jnp.max(top, axis=0, keepdims=True) * (scale * LOG2E)
+        if 0 <= mid < blocks:
+            invs[mid] = 1.0 / jnp.sum(norm, axis=0, keepdims=True)
+            deltas[mid] = invs[mid] * jnp.sum(dots, axis=0, keepdims=True)
+        if old >= 0 and old % 2:
+            more = slot_grads(old - 1, old + 1)
             dk, dv = dk + more[0], dv + more[1]
     dk = (scale * tg2 * dk).astype(jnp.bfloat16)
     g_ref[...] += fold8((dv * vcat.astype(jnp.float32))[:, :hd] + (dv * vcat.astype(jnp.float32))[:, hd:])
@@ -327,8 +321,8 @@
             pltpu.VMEM((rows, 2 * hd), jnp.bfloat16),
             pltpu.VMEM((rows, 2 * hd), jnp.bfloat16),
             pltpu.VMEM((2, tokens, hd), jnp.bfloat16),
-            pltpu.VMEM((2, slots, 2 * tokens), jnp.float32),
-            pltpu.VMEM((2, slots, 2 * tokens), jnp.float32),
+            pltpu.VMEM((3, slots, 2 * tokens), jnp.float32),
+            pltpu.VMEM((3, slots, 2 * tokens), jnp.float32),
             pltpu.VMEM((slots, tokens), jnp.float32),
             pltpu.SemaphoreType.DMA((5 + 4 * KV_HEADS,)),
             pltpu.SemaphoreType.DMA((KV_HEADS,)),

time: 63.3 us -> 63.3 us (level)
  no operation moved by 1% of the time
where the time goes in v12:
time: 63.3 us; the launch traced here: 63.1 us
  starting transfers between devices  24.4 us (39%)
  waiting for transfers between devices  22.6 us (36%)
  Pallas kernels  12.5 us (20%)
  local copies, waits for them, and re-layouts  1.7 us (3%)
  between operations  1.44 us (2%)
    ppermute x11, starting transfers between devices, send_xy(): return lax.ppermute(x, ('x', 'y'), [(i, i ^ p) for i in range(4)])  14.1 us
    ppermute x11, waiting for transfers between devices, send_xy(): return lax.ppermute(x, ('x', 'y'), [(i, i ^ p) for i in range(4)])  12.1 us
    ppermute x6, starting transfers between devices, send_z(): return lax.ppermute(x, 'z', [(i, i ^ k) for i in range(cols)])  10.1 us
    pallas_call x1, Pallas kernels, scores(): pl.pallas_call(functools.partial(scores_kernel, mine, cols, folded), grid...  7.81 us
    ppermute x6, waiting for transfers between devices, send_z(): return lax.ppermute(x, 'z', [(i, i ^ k) for i in range(cols)])  5.84 us
    ppermute x2, waiting for transfers between devices, send_core(): return lax.ppermute(x, 'core', [(0, 1), (1, 0)])  4.63 us
    pallas_call x1, Pallas kernels, outputs(): pl.pallas_call(outputs_kernel, grid=(KV_HEADS,), in_specs=[smem, smem, pl...  4.01 us
  transfers between devices with their start and end apart: 19, of which 9 were waited for; matrix products, arithmetic and copies ran while one was open for 0% of the time, Pallas kernels for 6%

profile of v12, /device:TPU:0, one launch (start us, length us, event | category | flops | bytes accessed | tf_op | source)
XLA Modules:
  0.0 63.1 jit_solution(8880020685952134585)
XLA Ops:
  0.6 0.8 %constant_dynamic-update-slice_fusion.1 = bf16[32,1024]{1,0:T(8,128)(2,1)S(1)} fusion(bf16[32,512]{1,0:T(8,128)(2,1)} %param.8), kind=kLoop, calls=%fused_computation.19 | loop fusion | bytes 65536
  1.4 0.8 %constant_dynamic-update-slice_fusion = bf16[32,1024]{1,0:T(8,128)(2,1)S(1)} fusion(bf16[32,1024]{1,0:T(8,128)(2,1)S(1)} %constant_dynamic-update-slice_fusion.1, bf16[32,512]{1,0:T(8,128)(2,1)} %param.9), kind=kLoop, calls=%fused_computation.18 | loop fusion | bytes 65536 | tf_op jit(solution)/shard_map/concatenate | solution.py:392
  2.2 5.0 %collective-permute-start.2 = (bf16[32,1024]{1,0:T(8,128)(2,1)S(1)}, bf16[32,1024]{1,0:T(8,128)(2,1)S(1)}, u32[]{:S(2)}, u32[]{:S(2)}) collective-permute-start(bf16[32,1024]{1,0:T(8,128)(2,1)S(1)} %constant_dynamic-update-slice_fusion), channel_id=1, source_target_pairs={{0,6},{2,4},{4,2},{6,0},{1,7},{3,5},{5,3},{7,1},{8,14},{10,12},{12... | collective-permute-start | bytes 196616 | tf_op jit(solution)/shard_map/ppermute | solution.py:384
  7.2 0.0 collective-permute-start.1
  7.2 0.6 collective-permute-start
  7.8 1.7 %collective-permute-start.3 = (bf16[32,1024]{1,0:T(8,128)(2,1)S(1)}, bf16[32,1024]{1,0:T(8,128)(2,1)S(1)}, u32[]{:S(2)}, u32[]{:S(2)}) collective-permute-start(bf16[32,1024]{1,0:T(8,128)(2,1)S(1)} %constant_dynamic-update-slice_fusion), channel_id=1, source_target_pairs={{0,1},{1,0},{16,17},{17,16},{2,3},{3,2},{18,19},{19,18},{4,5},{5,4... | collective-permute-start | bytes 196616 | tf_op jit(solution)/shard_map/ppermute | solution.py:387
  9.5 1.5 %collective-permute-start.4 = (bf16[32,1024]{1,0:T(8,128)(2,1)S(1)}, bf16[32,1024]{1,0:T(8,128)(2,1)S(1)}, u32[]{:S(2)}, u32[]{:S(2)}) collective-permute-start(bf16[32,1024]{1,0:T(8,128)(2,1)S(1)} %constant_dynamic-update-slice_fusion), channel_id=1, source_target_pairs={{0,16},{1,17},{16,0},{17,1},{2,18},{3,19},{18,2},{19,3},{4,20},{5,... | collective-permute-start | bytes 196616 | tf_op jit(solution)/shard_map/ppermute | solution.py:387
  11.0 0.0 collective-permute-done.2
  11.0 1.8 %collective-permute-done.1 = bf16[32,1024]{1,0:T(8,128)(2,1)S(1)} collective-permute-done((bf16[32,1024]{1,0:T(8,128)(2,1)S(1)}, bf16[32,1024]{1,0:T(8,128)(2,1)S(1)}, u32[]{:S(2)}, u32[]{:S(2)}) %collective-permute-start.1) | collective-permute-done | bytes 65568 | tf_op jit(solution)/shard_map/ppermute | solution.py:384
  12.8 0.0 collective-permute-done
  12.8 0.0 collective-permute-done.3
  12.8 0.9 %collective-permute-done.4 = bf16[32,1024]{1,0:T(8,128)(2,1)S(1)} collective-permute-done((bf16[32,1024]{1,0:T(8,128)(2,1)S(1)}, bf16[32,1024]{1,0:T(8,128)(2,1)S(1)}, u32[]{:S(2)}, u32[]{:S(2)}) %collective-permute-start.4) | collective-permute-done | bytes 65568 | tf_op jit(solution)/shard_map/ppermute | solution.py:387
  13.8 0.7 %collective-permute-start.5 = (bf16[96,1024]{1,0:T(8,128)(2,1)S(1)}, bf16[96,1024]{1,0:T(8,128)(2,1)S(1)}, u32[]{:S(2)}, u32[]{:S(2)}) collective-permute-start(bf16[96,1024]{1,0:T(8,128)(2,1)S(1)} %pad_maximum_fusion.1), channel_id=1, source_target_pairs={{0,1},{1,0},{16,17},{17,16},{2,3},{3,2},{18,19},{19,18},{4,5},{5,4... | collective-permute-start | bytes 589832 | tf_op jit(solution)/shard_map/ppermute | solution.py:387
  14.4 1.5 %collective-permute-start.6 = (bf16[96,1024]{1,0:T(8,128)(2,1)S(1)}, bf16[96,1024]{1,0:T(8,128)(2,1)S(1)}, u32[]{:S(2)}, u32[]{:S(2)}) collective-permute-start(bf16[96,1024]{1,0:T(8,128)(2,1)S(1)} %pad_maximum_fusion.1), channel_id=1, source_target_pairs={{0,16},{1,17},{16,0},{17,1},{2,18},{3,19},{18,2},{19,3},{4,20},{5,... | collective-permute-start | bytes 589832 | tf_op jit(solution)/shard_map/ppermute | solution.py:387
  16.0 0.0 copy-start
  16.0 0.0 copy-start.2
  16.0 0.0 copy-start.3
  16.0 1.4 %collective-permute-start.7 = (bf16[128,1024]{1,0:T(8,128)(2,1)S(1)}, bf16[128,1024]{1,0:T(8,128)(2,1)S(1)}, u32[]{:S(2)}, u32[]{:S(2)}) collective-permute-start(bf16[128,1024]{1,0:T(8,128)(2,1)S(1)} %pad_maximum_fusion), channel_id=1, source_target_pairs={{0,17},{1,16},{16,1},{17,0},{2,19},{3,18},{18,3},{19,2},{4,21},{5,... | collective-permute-start | bytes 786440 | tf_op jit(solution)/shard_map/ppermute | solution.py:387
  17.4 2.6 %collective-permute-done.5 = bf16[96,1024]{1,0:T(8,128)(2,1)S(1)} collective-permute-done((bf16[96,1024]{1,0:T(8,128)(2,1)S(1)}, bf16[96,1024]{1,0:T(8,128)(2,1)S(1)}, u32[]{:S(2)}, u32[]{:S(2)}) %collective-permute-start.5) | collective-permute-done | bytes 196640 | tf_op jit(solution)/shard_map/ppermute | solution.py:387
  20.1 2.2 %collective-permute-done.6 = bf16[96,1024]{1,0:T(8,128)(2,1)S(1)} collective-permute-done((bf16[96,1024]{1,0:T(8,128)(2,1)S(1)}, bf16[96,1024]{1,0:T(8,128)(2,1)S(1)}, u32[]{:S(2)}, u32[]{:S(2)}) %collective-permute-start.6) | collective-permute-done | bytes 196640 | tf_op jit(solution)/shard_map/ppermute | solution.py:387
  22.3 4.3 %collective-permute-done.7 = bf16[128,1024]{1,0:T(8,128)(2,1)S(1)} collective-permute-done((bf16[128,1024]{1,0:T(8,128)(2,1)S(1)}, bf16[128,1024]{1,0:T(8,128)(2,1)S(1)}, u32[]{:S(2)}, u32[]{:S(2)}) %collective-permute-start.7) | collective-permute-done | bytes 262176 | tf_op jit(solution)/shard_map/ppermute | solution.py:387
  26.5 0.1 collective-permute-start.8
  27.3 2.0 %collective-permute-done.8.other = bf16[2,2,128,1024]{3,2,1,0:T(8,128)(2,1)S(1)} collective-permute-done((bf16[2,2,128,1024]{3,2,1,0:T(8,128)(2,1)S(1)}, bf16[2,2,128,1024]{3,2,1,0:T(8,128)(2,1)S(1)}, u32[]{:S(2)}, u32[]{:S(2)}) %collective-permute-start.8) | collective-permute-done | bytes 1048608 | tf_op jit(solution)/shard_map/ppermute | solution.py:390
  29.3 7.8 %shard_map.110 = (bf16[4,256,1024]{2,1,0:T(8,128)(2,1)S(1)}, bf16[4,256,1024]{2,1,0:T(8,128)(2,1)S(1)}, bf16[2,256,1024]{2,1,0:T(8,128)(2,1)S(1)}, bf16[2,2,4,27...) custom-call(s32[128]{0:T(128)S(1)} %copy-done.3, s32[4]{0:T(128)S(1)} %copy-done.2, ...), custom_call_target="tpu_custom_call" | custom-call | flops 2147483648 | bytes 12582912 | tf_op jit(solution)/shard_map/pallas_call | solution.py:298
  37.1 0.2 collective-permute-start.9
  37.3 2.6 %collective-permute-done.9 = bf16[2,2,4,272,128]{4,3,2,1,0:T(8,128)(2,1)S(1)} collective-permute-done((bf16[2,2,4,272,128]{4,3,2,1,0:T(8,128)(2,1)S(1)}, bf16[2,2,4,272,128]{4,3,2,1,0:T(8,128)(2,1)S(1)}, u32[]{:S(2)}, u32[]{:S(2)}) %collective-permute-start.9) | collective-permute-done | bytes 1114144 | tf_op jit(solution)/shard_map/ppermute | solution.py:390
  39.9 0.3 add_convert_fusion
  40.3 2.3 %collective-permute-start.12 = (bf16[3,272,128]{2,1,0:T(8,128)(2,1)S(1)}, bf16[3,272,128]{2,1,0:T(8,128)(2,1)S(1)}, u32[]{:S(2)}, u32[]{:S(2)}) collective-permute-start(bf16[3,272,128]{2,1,0:T(8,128)(2,1)S(1)} %get-tuple-element.50), channel_id=1, source_target_pairs={{0,17},{1,16},{16,1},{17,0},{2,19},{3,18},{18,3},{19,2},{4,21},{5,... | collective-permute-start | bytes 626696 | tf_op jit(solution)/shard_map/ppermute | solution.py:387
  42.7 0.5 collective-permute-start.11
  43.2 0.7 %collective-permute-start.10 = (bf16[3,272,128]{2,1,0:T(8,128)(2,1)S(1)}, bf16[3,272,128]{2,1,0:T(8,128)(2,1)S(1)}, u32[]{:S(2)}, u32[]{:S(2)}) collective-permute-start(bf16[3,272,128]{2,1,0:T(8,128)(2,1)S(1)} %get-tuple-element.49), channel_id=1, source_target_pairs={{0,1},{1,0},{16,17},{17,16},{2,3},{3,2},{18,19},{19,18},{4,5},{5,4... | collective-permute-start | bytes 626696 | tf_op jit(solution)/shard_map/ppermute | solution.py:387
  43.9 1.4 %collective-permute-start.13 = (bf16[272,128]{1,0:T(8,128)(2,1)S(1)}, bf16[272,128]{1,0:T(8,128)(2,1)S(1)}, u32[]{:S(2)}, u32[]{:S(2)}) collective-permute-start(bf16[272,128]{1,0:T(8,128)(2,1)S(1)} %get-tuple-element.47), channel_id=1, source_target_pairs={{0,1},{1,0},{16,17},{17,16},{2,3},{3,2},{18,19},{19,18},{4,5},{5,4... | collective-permute-start | bytes 208904 | tf_op jit(solution)/shard_map/ppermute | solution.py:387
  45.2 1.5 %collective-permute-start.14 = (bf16[272,128]{1,0:T(8,128)(2,1)S(1)}, bf16[272,128]{1,0:T(8,128)(2,1)S(1)}, u32[]{:S(2)}, u32[]{:S(2)}) collective-permute-start(bf16[272,128]{1,0:T(8,128)(2,1)S(1)} %get-tuple-element.46), channel_id=1, source_target_pairs={{0,16},{1,17},{16,0},{17,1},{2,18},{3,19},{18,2},{19,3},{4,20},{5,... | collective-permute-start | bytes 208904 | tf_op jit(solution)/shard_map/ppermute | solution.py:387
  46.7 4.0 %shard_map.111 = (bf16[128,4096]{1,0:T(8,128)(2,1)}, bf16[128,4096]{1,0:T(8,128)(2,1)}) custom-call(s32[128]{0:T(128)S(1)} %copy-done.3, f32[1]{0:T(128)S(6)} %copy.19.gate_s, s32[1,128]{1,0:T(1,128)S(1)} %bitcast.31, bf16[4,256,1024]{2,1,0:T(8,128)(2,1)S(1)} %get-tuple-element.34.p16, bf16[4,256,1024]{2,1,0:T(8,128)(2,1)S(1)} %get-tuple-element.35.ds16, ...), custom_call_target="tpu_custom_call" | custom-call | flops 5000000000 | bytes 12582912 | tf_op jit(solution)/shard_map/pallas_call | solution.py:61
  50.7 0.0 collective-permute-done.12
  50.7 0.9 %collective-permute-start.15 = (bf16[272,128]{1,0:T(8,128)(2,1)S(1)}, bf16[272,128]{1,0:T(8,128)(2,1)S(1)}, u32[]{:S(2)}, u32[]{:S(2)}) collective-permute-start(bf16[272,128]{1,0:T(8,128)(2,1)S(1)} %get-tuple-element.45), channel_id=1, source_target_pairs={{0,17},{1,16},{16,1},{17,0},{2,19},{3,18},{18,3},{19,2},{4,21},{5,... | collective-permute-start | bytes 208904 | tf_op jit(solution)/shard_map/ppermute | solution.py:387
  51.6 2.1 %collective-permute-done.11 = bf16[3,272,128]{2,1,0:T(8,128)(2,1)S(1)} collective-permute-done((bf16[3,272,128]{2,1,0:T(8,128)(2,1)S(1)}, bf16[3,272,128]{2,1,0:T(8,128)(2,1)S(1)}, u32[]{:S(2)}, u32[]{:S(2)}) %collective-permute-start.11) | collective-permute-done | bytes 208928 | tf_op jit(solution)/shard_map/ppermute | solution.py:387
  53.7 0.0 collective-permute-done.10
  53.7 0.1 fusion.2
  53.8 0.1 collective-permute-start.16
  53.9 2.3 %collective-permute-start.17 = (bf16[272,128]{1,0:T(8,128)(2,1)S(1)}, bf16[272,128]{1,0:T(8,128)(2,1)S(1)}, u32[]{:S(2)}, u32[]{:S(2)}) collective-permute-start(bf16[272,128]{1,0:T(8,128)(2,1)S(1)} %get-tuple-element.53), channel_id=1, source_target_pairs={{0,4},{2,6},{4,0},{6,2},{1,5},{3,7},{5,1},{7,3},{8,12},{10,14},{12... | collective-permute-start | bytes 208904 | tf_op jit(solution)/shard_map/ppermute | solution.py:384
  56.2 0.0 collective-permute-done.13.refs_1_
  56.2 2.1 %collective-permute-start.18 = (bf16[272,128]{1,0:T(8,128)(2,1)S(1)}, bf16[272,128]{1,0:T(8,128)(2,1)S(1)}, u32[]{:S(2)}, u32[]{:S(2)}) collective-permute-start(bf16[272,128]{1,0:T(8,128)(2,1)S(1)} %get-tuple-element.52), channel_id=1, source_target_pairs={{0,6},{2,4},{4,2},{6,0},{1,7},{3,5},{5,3},{7,1},{8,14},{10,12},{12... | collective-permute-start | bytes 208904 | tf_op jit(solution)/shard_map/ppermute | solution.py:384
  58.3 0.0 collective-permute-done.14.refs_2_
  58.3 0.0 collective-permute-done.15.refs_3_
  58.3 0.0 collective-permute-done.16.refs_4_
  58.3 4.0 %collective-permute-done.17.refs_5_ = bf16[272,128]{1,0:T(8,128)(2,1)S(1)} collective-permute-done((bf16[272,128]{1,0:T(8,128)(2,1)S(1)}, bf16[272,128]{1,0:T(8,128)(2,1)S(1)}, u32[]{:S(2)}, u32[]{:S(2)}) %collective-permute-start.17) | collective-permute-done | bytes 69664 | tf_op jit(solution)/shard_map/ppermute | solution.py:384
  62.3 0.0 collective-permute-done.18.refs_6_
  62.3 0.7 %shard_map.112 = (f32[32,512]{1,0:T(8,128)}, f32[32,512]{1,0:T(8,128)}, f32[1]{0:T(128)}) custom-call(f32[8,128]{1,0:T(8,128)S(1)} %get-tuple-element.40.gate, bf16[272,128]{1,0:T(8,128)(2,1)S(1)} %get-tuple-element.48.refs_0_, bf16[272,128]{1,0:T(8,128)(2,1)S(1)} %collective-permute-done.13.refs_1_, bf16[272,128]{1,0:T(8,128)(2,1)S(1)} %collective-permute-done.14.refs_2_, ...), custom_call_target="tpu_custom_call" | custom-call | tf_op jit(solution)/shard_map/pallas_call | solution.py:366
  (17 shorter events, 0.2 us)
Async XLA Ops:
  2.2 8.9 %collective-permute-start.2 = (bf16[32,1024]{1,0:T(8,128)(2,1)S(1)}, bf16[32,1024]{1,0:T(8,128)(2,1)S(1)}, u32[]{:S(2)}, u32[]{:S(2)}) collective-permute-start(bf16[32,1024]{1,0:T(8,128)(2,1)S(1)} %constant_dynamic-update-slice_fusion), channel_id=1, source_target_pairs={{0,6},{2,4},{4,2},{6,0},{1,7},{3,5},{5,3},{7,1},{8,14},{10,12},{12... | collective-permute-start | bytes 196616 | tf_op jit(solution)/shard_map/ppermute | solution.py:384
  7.2 5.6 %collective-permute-start.1 = (bf16[32,1024]{1,0:T(8,128)(2,1)S(1)}, bf16[32,1024]{1,0:T(8,128)(2,1)S(1)}, u32[]{:S(2)}, u32[]{:S(2)}) collective-permute-start(bf16[32,1024]{1,0:T(8,128)(2,1)S(1)} %constant_dynamic-update-slice_fusion), channel_id=1, source_target_pairs={{0,4},{2,6},{4,0},{6,2},{1,5},{3,7},{5,1},{7,3},{8,12},{10,14},{12... | collective-permute-start | bytes 196616 | tf_op jit(solution)/shard_map/ppermute | solution.py:384
  7.2 5.6 %collective-permute-start = (bf16[32,1024]{1,0:T(8,128)(2,1)S(1)}, bf16[32,1024]{1,0:T(8,128)(2,1)S(1)}, u32[]{:S(2)}, u32[]{:S(2)}) collective-permute-start(bf16[32,1024]{1,0:T(8,128)(2,1)S(1)} %constant_dynamic-update-slice_fusion), channel_id=1, source_target_pairs={{0,2},{2,0},{4,6},{6,4},{1,3},{3,1},{5,7},{7,5},{8,10},{10,8},{12,... | collective-permute-start | bytes 196616 | tf_op jit(solution)/shard_map/ppermute | solution.py:384
  7.8 5.1 %collective-permute-start.3 = (bf16[32,1024]{1,0:T(8,128)(2,1)S(1)}, bf16[32,1024]{1,0:T(8,128)(2,1)S(1)}, u32[]{:S(2)}, u32[]{:S(2)}) collective-permute-start(bf16[32,1024]{1,0:T(8,128)(2,1)S(1)} %constant_dynamic-update-slice_fusion), channel_id=1, source_target_pairs={{0,1},{1,0},{16,17},{17,16},{2,3},{3,2},{18,19},{19,18},{4,5},{5,4... | collective-permute-start | bytes 196616 | tf_op jit(solution)/shard_map/ppermute | solution.py:387
  9.5 4.3 %collective-permute-start.4 = (bf16[32,1024]{1,0:T(8,128)(2,1)S(1)}, bf16[32,1024]{1,0:T(8,128)(2,1)S(1)}, u32[]{:S(2)}, u32[]{:S(2)}) collective-permute-start(bf16[32,1024]{1,0:T(8,128)(2,1)S(1)} %constant_dynamic-update-slice_fusion), channel_id=1, source_target_pairs={{0,16},{1,17},{16,0},{17,1},{2,18},{3,19},{18,2},{19,3},{4,20},{5,... | collective-permute-start | bytes 196616 | tf_op jit(solution)/shard_map/ppermute | solution.py:387
  13.8 6.3 %collective-permute-start.5 = (bf16[96,1024]{1,0:T(8,128)(2,1)S(1)}, bf16[96,1024]{1,0:T(8,128)(2,1)S(1)}, u32[]{:S(2)}, u32[]{:S(2)}) collective-permute-start(bf16[96,1024]{1,0:T(8,128)(2,1)S(1)} %pad_maximum_fusion.1), channel_id=1, source_target_pairs={{0,1},{1,0},{16,17},{17,16},{2,3},{3,2},{18,19},{19,18},{4,5},{5,4... | collective-permute-start | bytes 589832 | tf_op jit(solution)/shard_map/ppermute | solution.py:387
  14.4 7.8 %collective-permute-start.6 = (bf16[96,1024]{1,0:T(8,128)(2,1)S(1)}, bf16[96,1024]{1,0:T(8,128)(2,1)S(1)}, u32[]{:S(2)}, u32[]{:S(2)}) collective-permute-start(bf16[96,1024]{1,0:T(8,128)(2,1)S(1)} %pad_maximum_fusion.1), channel_id=1, source_target_pairs={{0,16},{1,17},{16,0},{17,1},{2,18},{3,19},{18,2},{19,3},{4,20},{5,... | collective-permute-start | bytes 589832 | tf_op jit(solution)/shard_map/ppermute | solution.py:387
  15.9 13.3 %copy-start.1 = (bf16[128,4096]{1,0:T(8,128)(2,1)S(1)}, bf16[128,4096]{1,0:T(8,128)(2,1)}, u32[]{:S(2)}) copy-start(bf16[128,4096]{1,0:T(8,128)(2,1)} %dy_ref.1) | copy-start | bytes 3145732
  16.0 13.3 %copy-start = (bf16[128,4096]{1,0:T(8,128)(2,1)S(1)}, bf16[128,4096]{1,0:T(8,128)(2,1)}, u32[]{:S(2)}) copy-start(bf16[128,4096]{1,0:T(8,128)(2,1)} %q_ref.1) | copy-start | bytes 3145732
  16.0 13.3 %copy-start.2 = (s32[4]{0:T(128)S(1)}, s32[4]{0:T(128)}, u32[]{:S(2)}) copy-start(s32[4]{0:T(128)} %cnt_s.1) | copy-start | bytes 52
  16.0 13.3 %copy-start.3 = (s32[128]{0:T(128)S(1)}, s32[128]{0:T(128)}, u32[]{:S(2)}) copy-start(s32[128]{0:T(128)} %seg_s.3) | copy-start | bytes 1540
  16.0 10.5 %collective-permute-start.7 = (bf16[128,1024]{1,0:T(8,128)(2,1)S(1)}, bf16[128,1024]{1,0:T(8,128)(2,1)S(1)}, u32[]{:S(2)}, u32[]{:S(2)}) collective-permute-start(bf16[128,1024]{1,0:T(8,128)(2,1)S(1)} %pad_maximum_fusion), channel_id=1, source_target_pairs={{0,17},{1,16},{16,1},{17,0},{2,19},{3,18},{18,3},{19,2},{4,21},{5,... | collective-permute-start | bytes 786440 | tf_op jit(solution)/shard_map/ppermute | solution.py:387
  26.5 2.7 %collective-permute-start.8 = (bf16[2,2,128,1024]{3,2,1,0:T(8,128)(2,1)S(1)}, bf16[2,2,128,1024]{3,2,1,0:T(8,128)(2,1)S(1)}, u32[]{:S(2)}, u32[]{:S(2)}) collective-permute-start(bf16[2,2,128,1024]{3,2,1,0:T(8,128)(2,1)S(1)} %bitcast.28), channel_id=1, source_target_pairs={{0,8},{8,0},{1,9},{9,1},{2,10},{10,2},{3,11},{11,3},{4,12},{12,4},... | collective-permute-start | bytes 3145736 | tf_op jit(solution)/shard_map/ppermute | solution.py:390
  37.1 2.8 %collective-permute-start.9 = (bf16[2,2,4,272,128]{4,3,2,1,0:T(8,128)(2,1)S(1)}, bf16[2,2,4,272,128]{4,3,2,1,0:T(8,128)(2,1)S(1)}, u32[]{:S(2)}, u32[]{:S(2)}) collective-permute-start(bf16[2,2,4,272,128]{4,3,2,1,0:T(8,128)(2,1)S(1)} %get-tuple-element.31), channel_id=1, source_target_pairs={{0,8},{8,0},{1,9},{9,1},{2,10},{10,2},{3,11},{11,3},{4,12},{12,4},... | collective-permute-start | bytes 3342344 | tf_op jit(solution)/shard_map/ppermute | solution.py:390
  40.3 10.4 %collective-permute-start.12 = (bf16[3,272,128]{2,1,0:T(8,128)(2,1)S(1)}, bf16[3,272,128]{2,1,0:T(8,128)(2,1)S(1)}, u32[]{:S(2)}, u32[]{:S(2)}) collective-permute-start(bf16[3,272,128]{2,1,0:T(8,128)(2,1)S(1)} %get-tuple-element.50), channel_id=1, source_target_pairs={{0,17},{1,16},{16,1},{17,0},{2,19},{3,18},{18,3},{19,2},{4,21},{5,... | collective-permute-start | bytes 626696 | tf_op jit(solution)/shard_map/ppermute | solution.py:387
  42.7 11.0 %collective-permute-start.11 = (bf16[3,272,128]{2,1,0:T(8,128)(2,1)S(1)}, bf16[3,272,128]{2,1,0:T(8,128)(2,1)S(1)}, u32[]{:S(2)}, u32[]{:S(2)}) collective-permute-start(bf16[3,272,128]{2,1,0:T(8,128)(2,1)S(1)} %get-tuple-element.51), channel_id=1, source_target_pairs={{0,16},{1,17},{16,0},{17,1},{2,18},{3,19},{18,2},{19,3},{4,20},{5,... | collective-permute-start | bytes 626696 | tf_op jit(solution)/shard_map/ppermute | solution.py:387
  43.2 10.5 %collective-permute-start.10 = (bf16[3,272,128]{2,1,0:T(8,128)(2,1)S(1)}, bf16[3,272,128]{2,1,0:T(8,128)(2,1)S(1)}, u32[]{:S(2)}, u32[]{:S(2)}) collective-permute-start(bf16[3,272,128]{2,1,0:T(8,128)(2,1)S(1)} %get-tuple-element.49), channel_id=1, source_target_pairs={{0,1},{1,0},{16,17},{17,16},{2,3},{3,2},{18,19},{19,18},{4,5},{5,4... | collective-permute-start | bytes 626696 | tf_op jit(solution)/shard_map/ppermute | solution.py:387
  43.9 12.3 %collective-permute-start.13 = (bf16[272,128]{1,0:T(8,128)(2,1)S(1)}, bf16[272,128]{1,0:T(8,128)(2,1)S(1)}, u32[]{:S(2)}, u32[]{:S(2)}) collective-permute-start(bf16[272,128]{1,0:T(8,128)(2,1)S(1)} %get-tuple-element.47), channel_id=1, source_target_pairs={{0,1},{1,0},{16,17},{17,16},{2,3},{3,2},{18,19},{19,18},{4,5},{5,4... | collective-permute-start | bytes 208904 | tf_op jit(solution)/shard_map/ppermute | solution.py:387
  45.2 13.1 %collective-permute-start.14 = (bf16[272,128]{1,0:T(8,128)(2,1)S(1)}, bf16[272,128]{1,0:T(8,128)(2,1)S(1)}, u32[]{:S(2)}, u32[]{:S(2)}) collective-permute-start(bf16[272,128]{1,0:T(8,128)(2,1)S(1)} %get-tuple-element.46), channel_id=1, source_target_pairs={{0,16},{1,17},{16,0},{17,1},{2,18},{3,19},{18,2},{19,3},{4,20},{5,... | collective-permute-start | bytes 208904 | tf_op jit(solution)/shard_map/ppermute | solution.py:387
  50.7 7.6 %collective-permute-start.15 = (bf16[272,128]{1,0:T(8,128)(2,1)S(1)}, bf16[272,128]{1,0:T(8,128)(2,1)S(1)}, u32[]{:S(2)}, u32[]{:S(2)}) collective-permute-start(bf16[272,128]{1,0:T(8,128)(2,1)S(1)} %get-tuple-element.45), channel_id=1, source_target_pairs={{0,17},{1,16},{16,1},{17,0},{2,19},{3,18},{18,3},{19,2},{4,21},{5,... | collective-permute-start | bytes 208904 | tf_op jit(solution)/shard_map/ppermute | solution.py:387
  53.8 4.5 %collective-permute-start.16 = (bf16[272,128]{1,0:T(8,128)(2,1)S(1)}, bf16[272,128]{1,0:T(8,128)(2,1)S(1)}, u32[]{:S(2)}, u32[]{:S(2)}) collective-permute-start(bf16[272,128]{1,0:T(8,128)(2,1)S(1)} %get-tuple-element.54), channel_id=1, source_target_pairs={{0,2},{2,0},{4,6},{6,4},{1,3},{3,1},{5,7},{7,5},{8,10},{10,8},{12,... | collective-permute-start | bytes 208904 | tf_op jit(solution)/shard_map/ppermute | solution.py:384
  53.9 8.4 %collective-permute-start.17 = (bf16[272,128]{1,0:T(8,128)(2,1)S(1)}, bf16[272,128]{1,0:T(8,128)(2,1)S(1)}, u32[]{:S(2)}, u32[]{:S(2)}) collective-permute-start(bf16[272,128]{1,0:T(8,128)(2,1)S(1)} %get-tuple-element.53), channel_id=1, source_target_pairs={{0,4},{2,6},{4,0},{6,2},{1,5},{3,7},{5,1},{7,3},{8,12},{10,14},{12... | collective-permute-start | bytes 208904 | tf_op jit(solution)/shard_map/ppermute | solution.py:384
  56.2 6.2 %collective-permute-start.18 = (bf16[272,128]{1,0:T(8,128)(2,1)S(1)}, bf16[272,128]{1,0:T(8,128)(2,1)S(1)}, u32[]{:S(2)}, u32[]{:S(2)}) collective-permute-start(bf16[272,128]{1,0:T(8,128)(2,1)S(1)} %get-tuple-element.52), channel_id=1, source_target_pairs={{0,6},{2,4},{4,2},{6,0},{1,7},{3,5},{5,3},{7,1},{8,14},{10,12},{12... | collective-permute-start | bytes 208904 | tf_op jit(solution)/shard_map/ppermute | solution.py:384

commit v13 on v12

--- a/solution.py
+++ b/solution.py
@@ -25,6 +25,31 @@
 
 def mm(a, b, dims):
     return lax.dot_general(a, b, dims, preferred_element_type=jnp.float32)
+
+
+def join_kernel(k_ref, v_ref, out, sems):
+    width = k_ref.shape[1]
+    copies = [
+        pltpu.make_async_copy(src, out.at[:, pl.ds(i * width, width)], sems.at[i])
+        for i, src in enumerate((k_ref, v_ref))
+    ]
+    for c in copies:
+        c.start()
+    for c in copies:
+        c.wait()
+
+
+def join(keys, values):
+    rows, width = keys.shape
+    hbm = pl.BlockSpec(memory_space=pl.ANY)
+    return pl.pallas_call(
+        join_kernel,
+        in_specs=[hbm, hbm],
+        out_specs=hbm,
+        out_shape=jax.ShapeDtypeStruct((rows, 2 * width), keys.dtype),
+        scratch_shapes=[pltpu.SemaphoreType.DMA((2,))],
+        compiler_params=pltpu.CompilerParams(vmem_limit_bytes=60 * 1024 * 1024),
+    )(keys, values)
 
 
 def outputs_kernel(seg_s, gate_s, seg_v, p16, ds16, k_ref, v_ref, y_ref, dq_ref):
@@ -389,7 +414,7 @@
     def send_core(x):
         return lax.ppermute(x, "core", [(0, 1), (1, 0)])
 
-    kv = jnp.concatenate([keys, values], axis=1)
+    kv = join(keys, values) if folded else jnp.concatenate([keys, values], axis=1)
     if folded:
         near = [send_xy(kv, p) for p in (1, 2)]
         line = [send_z(kv, k) for k in LINE]

time: 63.3 us -> 66.2 us (1.046)
  Pallas kernels: 12.5 us -> 15.6 us
  other arithmetic: 0.45 us -> 1.38 us
  waiting for transfers between devices: 22.6 us -> 21.9 us
  local copies, waits for them, and re-layouts: 1.7 us -> 1.02 us
    pallas_call x0 -> x1, Pallas kernels: none -> 3.1 us  [join(): pl.pallas_call(join_kernel, in_specs=[hbm, hbm], out_specs=hbm, out_shape...]
    ppermute x11, waiting for transfers between devices: 12.1 us -> 10.3 us  [send_xy(): return lax.ppermute(x, ('x', 'y'), [(i, i ^ p) for i in range(4)])]
    ppermute x6, waiting for transfers between devices: 5.84 us -> 6.98 us  [send_z(): return lax.ppermute(x, 'z', [(i, i ^ k) for i in range(cols)])]
    concatenate x1, other arithmetic: 0.02 us -> 0.95 us  [local(): block = jnp.concatenate([kv, line], axis=0)]
    concatenate x1 -> x0, local copies, waits for them, and re-layouts: 0.76 us -> none  [local(): kv = jnp.concatenate([keys, values], axis=1)]
  transfers between devices with their start and end apart: 19 -> 19, of which waited for: 9 -> 11; matrix products, arithmetic and copies ran while one was open for 0% -> 3% of each run, Pallas kernels for 6% -> 6%
where the time goes in v13:
time: 66.2 us; the launch traced here: 66 us
  starting transfers between devices  24.6 us (37%)
  waiting for transfers between devices  21.9 us (33%)
  Pallas kernels  15.6 us (24%)
  between operations  1.43 us (2%)
  other arithmetic  1.38 us (2%)
  local copies, waits for them, and re-layouts  1.02 us (2%)
    ppermute x11, starting transfers between devices, send_xy(): return lax.ppermute(x, ('x', 'y'), [(i, i ^ p) for i in range(4)])  14 us
    ppermute x6, starting transfers between devices, send_z(): return lax.ppermute(x, 'z', [(i, i ^ k) for i in range(cols)])  10.4 us
    ppermute x11, waiting for transfers between devices, send_xy(): return lax.ppermute(x, ('x', 'y'), [(i, i ^ p) for i in range(4)])  10.3 us
    pallas_call x1, Pallas kernels, scores(): pl.pallas_call(functools.partial(scores_kernel, mine, cols, folded), grid...  7.81 us
    ppermute x6, waiting for transfers between devices, send_z(): return lax.ppermute(x, 'z', [(i, i ^ k) for i in range(cols)])  6.98 us
    ppermute x2, waiting for transfers between devices, send_core(): return lax.ppermute(x, 'core', [(0, 1), (1, 0)])  4.63 us
    pallas_call x1, Pallas kernels, outputs(): pl.pallas_call(outputs_kernel, grid=(KV_HEADS,), in_specs=[smem, smem, pl...  4 us
    pallas_call x1, Pallas kernels, join(): pl.pallas_call(join_kernel, in_specs=[hbm, hbm], out_specs=hbm, out_shape...  3.1 us
  transfers between devices with their start and end apart: 19, of which 11 were waited for; matrix products, arithmetic and copies ran while one was open for 3% of the time, Pallas kernels for 6%

profile of v13, /device:TPU:0, one launch (start us, length us, event | category | flops | bytes accessed | tf_op | source)
XLA Modules:
  0.0 66.0 jit_solution(3537108703674250457)
XLA Ops:
  0.6 3.1 %shard_map.110 = bf16[32,1024]{1,0:T(8,128)(2,1)} custom-call(bf16[32,512]{1,0:T(8,128)(2,1)} %k_ref.1, bf16[32,512]{1,0:T(8,128)(2,1)} %v_ref.1), custom_call_target="tpu_custom_call" | custom-call | tf_op jit(solution)/shard_map/pallas_call | solution.py:45
  3.7 5.1 %collective-permute-start.2 = (bf16[32,1024]{1,0:T(8,128)(2,1)}, bf16[32,1024]{1,0:T(8,128)(2,1)S(1)}, u32[]{:S(2)}, u32[]{:S(2)}) collective-permute-start(bf16[32,1024]{1,0:T(8,128)(2,1)} %shard_map.110), channel_id=1, source_target_pairs={{0,6},{2,4},{4,2},{6,0},{1,7},{3,5},{5,3},{7,1},{8,14},{10,12},{12... | collective-permute-start | bytes 196616 | tf_op jit(solution)/shard_map/ppermute | solution.py:409
  8.9 0.0 collective-permute-start.1
  8.9 0.6 collective-permute-start
  9.5 1.7 %collective-permute-start.3 = (bf16[32,1024]{1,0:T(8,128)(2,1)}, bf16[32,1024]{1,0:T(8,128)(2,1)S(1)}, u32[]{:S(2)}, u32[]{:S(2)}) collective-permute-start(bf16[32,1024]{1,0:T(8,128)(2,1)} %shard_map.110), channel_id=1, source_target_pairs={{0,1},{1,0},{16,17},{17,16},{2,3},{3,2},{18,19},{19,18},{4,5},{5,4... | collective-permute-start | bytes 196616 | tf_op jit(solution)/shard_map/ppermute | solution.py:412
  11.2 1.5 %collective-permute-start.4 = (bf16[32,1024]{1,0:T(8,128)(2,1)}, bf16[32,1024]{1,0:T(8,128)(2,1)S(1)}, u32[]{:S(2)}, u32[]{:S(2)}) collective-permute-start(bf16[32,1024]{1,0:T(8,128)(2,1)} %shard_map.110), channel_id=1, source_target_pairs={{0,16},{1,17},{16,0},{17,1},{2,18},{3,19},{18,2},{19,3},{4,20},{5,... | collective-permute-start | bytes 196616 | tf_op jit(solution)/shard_map/ppermute | solution.py:412
  12.7 0.0 collective-permute-done.2
  12.7 2.0 %collective-permute-done.1 = bf16[32,1024]{1,0:T(8,128)(2,1)S(1)} collective-permute-done((bf16[32,1024]{1,0:T(8,128)(2,1)}, bf16[32,1024]{1,0:T(8,128)(2,1)S(1)}, u32[]{:S(2)}, u32[]{:S(2)}) %collective-permute-start.1) | collective-permute-done | bytes 65568 | tf_op jit(solution)/shard_map/ppermute | solution.py:409
  14.7 0.0 collective-permute-done
  14.7 0.0 collective-permute-done.3
  14.7 0.9 %collective-permute-done.4 = bf16[32,1024]{1,0:T(8,128)(2,1)S(1)} collective-permute-done((bf16[32,1024]{1,0:T(8,128)(2,1)}, bf16[32,1024]{1,0:T(8,128)(2,1)S(1)}, u32[]{:S(2)}, u32[]{:S(2)}) %collective-permute-start.4) | collective-permute-done | bytes 65568 | tf_op jit(solution)/shard_map/ppermute | solution.py:412
  15.6 0.7 collective-permute-start.5
  16.3 1.5 %collective-permute-start.6 = (bf16[96,1024]{1,0:T(8,128)(2,1)S(1)}, bf16[96,1024]{1,0:T(8,128)(2,1)S(1)}, u32[]{:S(2)}, u32[]{:S(2)}) collective-permute-start(bf16[96,1024]{1,0:T(8,128)(2,1)S(1)} %pad_maximum_fusion.1), channel_id=1, source_target_pairs={{0,16},{1,17},{16,0},{17,1},{2,18},{3,19},{18,2},{19,3},{4,20},{5,... | collective-permute-start | bytes 589832 | tf_op jit(solution)/shard_map/ppermute | solution.py:412
  17.8 0.8 %constant_dynamic-update-slice_fusion.6 = bf16[512,1024]{1,0:T(8,128)(2,1)S(1)} fusion(bf16[32,1024]{1,0:T(8,128)(2,1)} %shard_map.110), kind=kLoop, calls=%fused_computation.24 | loop fusion | bytes 131072
  18.6 1.0 %pad_maximum_fusion = bf16[128,1024]{1,0:T(8,128)(2,1)S(1)} fusion(bf16[96,1024]{1,0:T(8,128)(2,1)S(1)} %pad_maximum_fusion.1, bf16[32,1024]{1,0:T(8,128)(2,1)} %shard_map.110), kind=kLoop, calls=%fused_computation.5 | loop fusion | flops 524288 | bytes 524288 | tf_op jit(solution)/shard_map/concatenate | solution.py:423
  19.6 0.0 copy-start
  19.6 0.0 copy-start.2
  19.6 0.0 copy-start.3
  19.6 1.4 %collective-permute-start.7 = (bf16[128,1024]{1,0:T(8,128)(2,1)S(1)}, bf16[128,1024]{1,0:T(8,128)(2,1)S(1)}, u32[]{:S(2)}, u32[]{:S(2)}) collective-permute-start(bf16[128,1024]{1,0:T(8,128)(2,1)S(1)} %pad_maximum_fusion), channel_id=1, source_target_pairs={{0,17},{1,16},{16,1},{17,0},{2,19},{3,18},{18,3},{19,2},{4,21},{5,... | collective-permute-start | bytes 786440 | tf_op jit(solution)/shard_map/ppermute | solution.py:412
  21.1 0.2 collective-permute-done.5
  21.3 2.4 %collective-permute-done.6 = bf16[96,1024]{1,0:T(8,128)(2,1)S(1)} collective-permute-done((bf16[96,1024]{1,0:T(8,128)(2,1)S(1)}, bf16[96,1024]{1,0:T(8,128)(2,1)S(1)}, u32[]{:S(2)}, u32[]{:S(2)}) %collective-permute-start.6) | collective-permute-done | bytes 196640 | tf_op jit(solution)/shard_map/ppermute | solution.py:412
  23.8 4.6 %collective-permute-done.7 = bf16[128,1024]{1,0:T(8,128)(2,1)S(1)} collective-permute-done((bf16[128,1024]{1,0:T(8,128)(2,1)S(1)}, bf16[128,1024]{1,0:T(8,128)(2,1)S(1)}, u32[]{:S(2)}, u32[]{:S(2)}) %collective-permute-start.7) | collective-permute-done | bytes 262176 | tf_op jit(solution)/shard_map/ppermute | solution.py:412
  28.4 0.1 collective-permute-start.8
  29.1 2.0 %collective-permute-done.8.other = bf16[2,2,128,1024]{3,2,1,0:T(8,128)(2,1)S(1)} collective-permute-done((bf16[2,2,128,1024]{3,2,1,0:T(8,128)(2,1)S(1)}, bf16[2,2,128,1024]{3,2,1,0:T(8,128)(2,1)S(1)}, u32[]{:S(2)}, u32[]{:S(2)}) %collective-permute-start.8) | collective-permute-done | bytes 1048608 | tf_op jit(solution)/shard_map/ppermute | solution.py:415
  31.2 7.8 %shard_map.111 = (bf16[4,256,1024]{2,1,0:T(8,128)(2,1)S(1)}, bf16[4,256,1024]{2,1,0:T(8,128)(2,1)S(1)}, bf16[2,256,1024]{2,1,0:T(8,128)(2,1)S(1)}, bf16[2,2,4,27...) custom-call(s32[128]{0:T(128)S(1)} %copy-done.3, s32[4]{0:T(128)S(1)} %copy-done.2, ...), custom_call_target="tpu_custom_call" | custom-call | flops 2147483648 | bytes 12582912 | tf_op jit(solution)/shard_map/pallas_call | solution.py:323
  39.0 0.2 collective-permute-start.9
  39.2 2.6 %collective-permute-done.9 = bf16[2,2,4,272,128]{4,3,2,1,0:T(8,128)(2,1)S(1)} collective-permute-done((bf16[2,2,4,272,128]{4,3,2,1,0:T(8,128)(2,1)S(1)}, bf16[2,2,4,272,128]{4,3,2,1,0:T(8,128)(2,1)S(1)}, u32[]{:S(2)}, u32[]{:S(2)}) %collective-permute-start.9) | collective-permute-done | bytes 1114144 | tf_op jit(solution)/shard_map/ppermute | solution.py:415
  41.8 0.3 add_convert_fusion
  42.2 2.3 %collective-permute-start.12 = (bf16[3,272,128]{2,1,0:T(8,128)(2,1)S(1)}, bf16[3,272,128]{2,1,0:T(8,128)(2,1)S(1)}, u32[]{:S(2)}, u32[]{:S(2)}) collective-permute-start(bf16[3,272,128]{2,1,0:T(8,128)(2,1)S(1)} %get-tuple-element.50), channel_id=1, source_target_pairs={{0,17},{1,16},{16,1},{17,0},{2,19},{3,18},{18,3},{19,2},{4,21},{5,... | collective-permute-start | bytes 626696 | tf_op jit(solution)/shard_map/ppermute | solution.py:412
  44.5 0.5 collective-permute-start.11
  45.1 0.7 %collective-permute-start.10 = (bf16[3,272,128]{2,1,0:T(8,128)(2,1)S(1)}, bf16[3,272,128]{2,1,0:T(8,128)(2,1)S(1)}, u32[]{:S(2)}, u32[]{:S(2)}) collective-permute-start(bf16[3,272,128]{2,1,0:T(8,128)(2,1)S(1)} %get-tuple-element.49), channel_id=1, source_target_pairs={{0,1},{1,0},{16,17},{17,16},{2,3},{3,2},{18,19},{19,18},{4,5},{5,4... | collective-permute-start | bytes 626696 | tf_op jit(solution)/shard_map/ppermute | solution.py:412
  45.7 1.4 %collective-permute-start.13 = (bf16[272,128]{1,0:T(8,128)(2,1)S(1)}, bf16[272,128]{1,0:T(8,128)(2,1)S(1)}, u32[]{:S(2)}, u32[]{:S(2)}) collective-permute-start(bf16[272,128]{1,0:T(8,128)(2,1)S(1)} %get-tuple-element.47), channel_id=1, source_target_pairs={{0,1},{1,0},{16,17},{17,16},{2,3},{3,2},{18,19},{19,18},{4,5},{5,4... | collective-permute-start | bytes 208904 | tf_op jit(solution)/shard_map/ppermute | solution.py:412
  47.1 1.5 %collective-permute-start.14 = (bf16[272,128]{1,0:T(8,128)(2,1)S(1)}, bf16[272,128]{1,0:T(8,128)(2,1)S(1)}, u32[]{:S(2)}, u32[]{:S(2)}) collective-permute-start(bf16[272,128]{1,0:T(8,128)(2,1)S(1)} %get-tuple-element.46), channel_id=1, source_target_pairs={{0,16},{1,17},{16,0},{17,1},{2,18},{3,19},{18,2},{19,3},{4,20},{5,... | collective-permute-start | bytes 208904 | tf_op jit(solution)/shard_map/ppermute | solution.py:412
  48.6 4.0 %shard_map.112 = (bf16[128,4096]{1,0:T(8,128)(2,1)}, bf16[128,4096]{1,0:T(8,128)(2,1)}) custom-call(s32[128]{0:T(128)S(1)} %copy-done.3, f32[1]{0:T(128)S(6)} %copy.18.gate_s, s32[1,128]{1,0:T(1,128)S(1)} %bitcast.31, bf16[4,256,1024]{2,1,0:T(8,128)(2,1)S(1)} %get-tuple-element.34.p16, bf16[4,256,1024]{2,1,0:T(8,128)(2,1)S(1)} %get-tuple-element.35.ds16, ...), custom_call_target="tpu_custom_call" | custom-call | flops 5000000000 | bytes 12582912 | tf_op jit(solution)/shard_map/pallas_call | solution.py:86
  52.6 0.0 collective-permute-done.12
  52.6 0.9 %collective-permute-start.15 = (bf16[272,128]{1,0:T(8,128)(2,1)S(1)}, bf16[272,128]{1,0:T(8,128)(2,1)S(1)}, u32[]{:S(2)}, u32[]{:S(2)}) collective-permute-start(bf16[272,128]{1,0:T(8,128)(2,1)S(1)} %get-tuple-element.45), channel_id=1, source_target_pairs={{0,17},{1,16},{16,1},{17,0},{2,19},{3,18},{18,3},{19,2},{4,21},{5,... | collective-permute-start | bytes 208904 | tf_op jit(solution)/shard_map/ppermute | solution.py:412
  53.5 2.1 %collective-permute-done.11 = bf16[3,272,128]{2,1,0:T(8,128)(2,1)S(1)} collective-permute-done((bf16[3,272,128]{2,1,0:T(8,128)(2,1)S(1)}, bf16[3,272,128]{2,1,0:T(8,128)(2,1)S(1)}, u32[]{:S(2)}, u32[]{:S(2)}) %collective-permute-start.11) | collective-permute-done | bytes 208928 | tf_op jit(solution)/shard_map/ppermute | solution.py:412
  55.6 0.0 collective-permute-done.10
  55.6 0.1 fusion.2
  55.7 0.7 %collective-permute-start.16 = (bf16[272,128]{1,0:T(8,128)(2,1)S(1)}, bf16[272,128]{1,0:T(8,128)(2,1)S(1)}, u32[]{:S(2)}, u32[]{:S(2)}) collective-permute-start(bf16[272,128]{1,0:T(8,128)(2,1)S(1)} %get-tuple-element.54), channel_id=1, source_target_pairs={{0,2},{2,0},{4,6},{6,4},{1,3},{3,1},{5,7},{7,5},{8,10},{10,8},{12,... | collective-permute-start | bytes 208904 | tf_op jit(solution)/shard_map/ppermute | solution.py:409
  56.4 2.7 %collective-permute-start.17 = (bf16[272,128]{1,0:T(8,128)(2,1)S(1)}, bf16[272,128]{1,0:T(8,128)(2,1)S(1)}, u32[]{:S(2)}, u32[]{:S(2)}) collective-permute-start(bf16[272,128]{1,0:T(8,128)(2,1)S(1)} %get-tuple-element.53), channel_id=1, source_target_pairs={{0,4},{2,6},{4,0},{6,2},{1,5},{3,7},{5,1},{7,3},{8,12},{10,14},{12... | collective-permute-start | bytes 208904 | tf_op jit(solution)/shard_map/ppermute | solution.py:409
  59.1 1.2 %collective-permute-start.18 = (bf16[272,128]{1,0:T(8,128)(2,1)S(1)}, bf16[272,128]{1,0:T(8,128)(2,1)S(1)}, u32[]{:S(2)}, u32[]{:S(2)}) collective-permute-start(bf16[272,128]{1,0:T(8,128)(2,1)S(1)} %get-tuple-element.52), channel_id=1, source_target_pairs={{0,6},{2,4},{4,2},{6,0},{1,7},{3,5},{5,3},{7,1},{8,14},{10,12},{12... | collective-permute-start | bytes 208904 | tf_op jit(solution)/shard_map/ppermute | solution.py:409
  60.3 0.0 collective-permute-done.14.refs_2_
  60.3 0.0 collective-permute-done.15.refs_3_
  60.3 0.4 collective-permute-done.16.refs_4_
  60.8 3.2 %collective-permute-done.17.refs_5_ = bf16[272,128]{1,0:T(8,128)(2,1)S(1)} collective-permute-done((bf16[272,128]{1,0:T(8,128)(2,1)S(1)}, bf16[272,128]{1,0:T(8,128)(2,1)S(1)}, u32[]{:S(2)}, u32[]{:S(2)}) %collective-permute-start.17) | collective-permute-done | bytes 69664 | tf_op jit(solution)/shard_map/ppermute | solution.py:409
  64.0 1.3 %collective-permute-done.18.refs_6_ = bf16[272,128]{1,0:T(8,128)(2,1)S(1)} collective-permute-done((bf16[272,128]{1,0:T(8,128)(2,1)S(1)}, bf16[272,128]{1,0:T(8,128)(2,1)S(1)}, u32[]{:S(2)}, u32[]{:S(2)}) %collective-permute-start.18) | collective-permute-done | bytes 69664 | tf_op jit(solution)/shard_map/ppermute | solution.py:409
  65.3 0.7 %shard_map.113 = (f32[32,512]{1,0:T(8,128)}, f32[32,512]{1,0:T(8,128)}, f32[1]{0:T(128)}) custom-call(f32[8,128]{1,0:T(8,128)S(1)} %get-tuple-element.40.gate, bf16[272,128]{1,0:T(8,128)(2,1)S(1)} %get-tuple-element.48.refs_0_, bf16[272,128]{1,0:T(8,128)(2,1)S(1)} %collective-permute-done.13.refs_1_, bf16[272,128]{1,0:T(8,128)(2,1)S(1)} %collective-permute-done.14.refs_2_, ...), custom_call_target="tpu_custom_call" | custom-call | tf_op jit(solution)/shard_map/pallas_call | solution.py:391
  (16 shorter events, 0.2 us)
Async XLA Ops:
  3.7 8.9 %collective-permute-start.2 = (bf16[32,1024]{1,0:T(8,128)(2,1)}, bf16[32,1024]{1,0:T(8,128)(2,1)S(1)}, u32[]{:S(2)}, u32[]{:S(2)}) collective-permute-start(bf16[32,1024]{1,0:T(8,128)(2,1)} %shard_map.110), channel_id=1, source_target_pairs={{0,6},{2,4},{4,2},{6,0},{1,7},{3,5},{5,3},{7,1},{8,14},{10,12},{12... | collective-permute-start | bytes 196616 | tf_op jit(solution)/shard_map/ppermute | solution.py:409
  8.9 5.8 %collective-permute-start.1 = (bf16[32,1024]{1,0:T(8,128)(2,1)}, bf16[32,1024]{1,0:T(8,128)(2,1)S(1)}, u32[]{:S(2)}, u32[]{:S(2)}) collective-permute-start(bf16[32,1024]{1,0:T(8,128)(2,1)} %shard_map.110), channel_id=1, source_target_pairs={{0,4},{2,6},{4,0},{6,2},{1,5},{3,7},{5,1},{7,3},{8,12},{10,14},{12... | collective-permute-start | bytes 196616 | tf_op jit(solution)/shard_map/ppermute | solution.py:409
  8.9 5.8 %collective-permute-start = (bf16[32,1024]{1,0:T(8,128)(2,1)}, bf16[32,1024]{1,0:T(8,128)(2,1)S(1)}, u32[]{:S(2)}, u32[]{:S(2)}) collective-permute-start(bf16[32,1024]{1,0:T(8,128)(2,1)} %shard_map.110), channel_id=1, source_target_pairs={{0,2},{2,0},{4,6},{6,4},{1,3},{3,1},{5,7},{7,5},{8,10},{10,8},{12,... | collective-permute-start | bytes 196616 | tf_op jit(solution)/shard_map/ppermute | solution.py:409
  9.5 5.2 %collective-permute-start.3 = (bf16[32,1024]{1,0:T(8,128)(2,1)}, bf16[32,1024]{1,0:T(8,128)(2,1)S(1)}, u32[]{:S(2)}, u32[]{:S(2)}) collective-permute-start(bf16[32,1024]{1,0:T(8,128)(2,1)} %shard_map.110), channel_id=1, source_target_pairs={{0,1},{1,0},{16,17},{17,16},{2,3},{3,2},{18,19},{19,18},{4,5},{5,4... | collective-permute-start | bytes 196616 | tf_op jit(solution)/shard_map/ppermute | solution.py:412
  11.2 4.5 %collective-permute-start.4 = (bf16[32,1024]{1,0:T(8,128)(2,1)}, bf16[32,1024]{1,0:T(8,128)(2,1)S(1)}, u32[]{:S(2)}, u32[]{:S(2)}) collective-permute-start(bf16[32,1024]{1,0:T(8,128)(2,1)} %shard_map.110), channel_id=1, source_target_pairs={{0,16},{1,17},{16,0},{17,1},{2,18},{3,19},{18,2},{19,3},{4,20},{5,... | collective-permute-start | bytes 196616 | tf_op jit(solution)/shard_map/ppermute | solution.py:412
  15.6 5.7 %collective-permute-start.5 = (bf16[96,1024]{1,0:T(8,128)(2,1)S(1)}, bf16[96,1024]{1,0:T(8,128)(2,1)S(1)}, u32[]{:S(2)}, u32[]{:S(2)}) collective-permute-start(bf16[96,1024]{1,0:T(8,128)(2,1)S(1)} %pad_maximum_fusion.1), channel_id=1, source_target_pairs={{0,1},{1,0},{16,17},{17,16},{2,3},{3,2},{18,19},{19,18},{4,5},{5,4... | collective-permute-start | bytes 589832 | tf_op jit(solution)/shard_map/ppermute | solution.py:412
  16.3 7.5 %collective-permute-start.6 = (bf16[96,1024]{1,0:T(8,128)(2,1)S(1)}, bf16[96,1024]{1,0:T(8,128)(2,1)S(1)}, u32[]{:S(2)}, u32[]{:S(2)}) collective-permute-start(bf16[96,1024]{1,0:T(8,128)(2,1)S(1)} %pad_maximum_fusion.1), channel_id=1, source_target_pairs={{0,16},{1,17},{16,0},{17,1},{2,18},{3,19},{18,2},{19,3},{4,20},{5,... | collective-permute-start | bytes 589832 | tf_op jit(solution)/shard_map/ppermute | solution.py:412
  18.6 12.5 %copy-start.1 = (bf16[128,4096]{1,0:T(8,128)(2,1)S(1)}, bf16[128,4096]{1,0:T(8,128)(2,1)}, u32[]{:S(2)}) copy-start(bf16[128,4096]{1,0:T(8,128)(2,1)} %dy_ref.1) | copy-start | bytes 3145732
  19.6 11.6 %copy-start = (bf16[128,4096]{1,0:T(8,128)(2,1)S(1)}, bf16[128,4096]{1,0:T(8,128)(2,1)}, u32[]{:S(2)}) copy-start(bf16[128,4096]{1,0:T(8,128)(2,1)} %q_ref.1) | copy-start | bytes 3145732
  19.6 11.5 %copy-start.2 = (s32[4]{0:T(128)S(1)}, s32[4]{0:T(128)}, u32[]{:S(2)}) copy-start(s32[4]{0:T(128)} %cnt_s.1) | copy-start | bytes 52
  19.6 11.5 %copy-start.3 = (s32[128]{0:T(128)S(1)}, s32[128]{0:T(128)}, u32[]{:S(2)}) copy-start(s32[128]{0:T(128)} %seg_s.3) | copy-start | bytes 1540
  19.6 8.8 %collective-permute-start.7 = (bf16[128,1024]{1,0:T(8,128)(2,1)S(1)}, bf16[128,1024]{1,0:T(8,128)(2,1)S(1)}, u32[]{:S(2)}, u32[]{:S(2)}) collective-permute-start(bf16[128,1024]{1,0:T(8,128)(2,1)S(1)} %pad_maximum_fusion), channel_id=1, source_target_pairs={{0,17},{1,16},{16,1},{17,0},{2,19},{3,18},{18,3},{19,2},{4,21},{5,... | collective-permute-start | bytes 786440 | tf_op jit(solution)/shard_map/ppermute | solution.py:412
  28.4 2.7 %collective-permute-start.8 = (bf16[2,2,128,1024]{3,2,1,0:T(8,128)(2,1)S(1)}, bf16[2,2,128,1024]{3,2,1,0:T(8,128)(2,1)S(1)}, u32[]{:S(2)}, u32[]{:S(2)}) collective-permute-start(bf16[2,2,128,1024]{3,2,1,0:T(8,128)(2,1)S(1)} %bitcast.28), channel_id=1, source_target_pairs={{0,8},{8,0},{1,9},{9,1},{2,10},{10,2},{3,11},{11,3},{4,12},{12,4},... | collective-permute-start | bytes 3145736 | tf_op jit(solution)/shard_map/ppermute | solution.py:415
  39.0 2.8 %collective-permute-start.9 = (bf16[2,2,4,272,128]{4,3,2,1,0:T(8,128)(2,1)S(1)}, bf16[2,2,4,272,128]{4,3,2,1,0:T(8,128)(2,1)S(1)}, u32[]{:S(2)}, u32[]{:S(2)}) collective-permute-start(bf16[2,2,4,272,128]{4,3,2,1,0:T(8,128)(2,1)S(1)} %get-tuple-element.31), channel_id=1, source_target_pairs={{0,8},{8,0},{1,9},{9,1},{2,10},{10,2},{3,11},{11,3},{4,12},{12,4},... | collective-permute-start | bytes 3342344 | tf_op jit(solution)/shard_map/ppermute | solution.py:415
  42.2 10.4 %collective-permute-start.12 = (bf16[3,272,128]{2,1,0:T(8,128)(2,1)S(1)}, bf16[3,272,128]{2,1,0:T(8,128)(2,1)S(1)}, u32[]{:S(2)}, u32[]{:S(2)}) collective-permute-start(bf16[3,272,128]{2,1,0:T(8,128)(2,1)S(1)} %get-tuple-element.50), channel_id=1, source_target_pairs={{0,17},{1,16},{16,1},{17,0},{2,19},{3,18},{18,3},{19,2},{4,21},{5,... | collective-permute-start | bytes 626696 | tf_op jit(solution)/shard_map/ppermute | solution.py:412
  44.5 11.0 %collective-permute-start.11 = (bf16[3,272,128]{2,1,0:T(8,128)(2,1)S(1)}, bf16[3,272,128]{2,1,0:T(8,128)(2,1)S(1)}, u32[]{:S(2)}, u32[]{:S(2)}) collective-permute-start(bf16[3,272,128]{2,1,0:T(8,128)(2,1)S(1)} %get-tuple-element.51), channel_id=1, source_target_pairs={{0,16},{1,17},{16,0},{17,1},{2,18},{3,19},{18,2},{19,3},{4,20},{5,... | collective-permute-start | bytes 626696 | tf_op jit(solution)/shard_map/ppermute | solution.py:412
  45.1 10.5 %collective-permute-start.10 = (bf16[3,272,128]{2,1,0:T(8,128)(2,1)S(1)}, bf16[3,272,128]{2,1,0:T(8,128)(2,1)S(1)}, u32[]{:S(2)}, u32[]{:S(2)}) collective-permute-start(bf16[3,272,128]{2,1,0:T(8,128)(2,1)S(1)} %get-tuple-element.49), channel_id=1, source_target_pairs={{0,1},{1,0},{16,17},{17,16},{2,3},{3,2},{18,19},{19,18},{4,5},{5,4... | collective-permute-start | bytes 626696 | tf_op jit(solution)/shard_map/ppermute | solution.py:412
  45.7 13.4 %collective-permute-start.13 = (bf16[272,128]{1,0:T(8,128)(2,1)S(1)}, bf16[272,128]{1,0:T(8,128)(2,1)S(1)}, u32[]{:S(2)}, u32[]{:S(2)}) collective-permute-start(bf16[272,128]{1,0:T(8,128)(2,1)S(1)} %get-tuple-element.47), channel_id=1, source_target_pairs={{0,1},{1,0},{16,17},{17,16},{2,3},{3,2},{18,19},{19,18},{4,5},{5,4... | collective-permute-start | bytes 208904 | tf_op jit(solution)/shard_map/ppermute | solution.py:412
  47.1 13.2 %collective-permute-start.14 = (bf16[272,128]{1,0:T(8,128)(2,1)S(1)}, bf16[272,128]{1,0:T(8,128)(2,1)S(1)}, u32[]{:S(2)}, u32[]{:S(2)}) collective-permute-start(bf16[272,128]{1,0:T(8,128)(2,1)S(1)} %get-tuple-element.46), channel_id=1, source_target_pairs={{0,16},{1,17},{16,0},{17,1},{2,18},{3,19},{18,2},{19,3},{4,20},{5,... | collective-permute-start | bytes 208904 | tf_op jit(solution)/shard_map/ppermute | solution.py:412
  52.6 7.7 %collective-permute-start.15 = (bf16[272,128]{1,0:T(8,128)(2,1)S(1)}, bf16[272,128]{1,0:T(8,128)(2,1)S(1)}, u32[]{:S(2)}, u32[]{:S(2)}) collective-permute-start(bf16[272,128]{1,0:T(8,128)(2,1)S(1)} %get-tuple-element.45), channel_id=1, source_target_pairs={{0,17},{1,16},{16,1},{17,0},{2,19},{3,18},{18,3},{19,2},{4,21},{5,... | collective-permute-start | bytes 208904 | tf_op jit(solution)/shard_map/ppermute | solution.py:412
  55.7 5.1 %collective-permute-start.16 = (bf16[272,128]{1,0:T(8,128)(2,1)S(1)}, bf16[272,128]{1,0:T(8,128)(2,1)S(1)}, u32[]{:S(2)}, u32[]{:S(2)}) collective-permute-start(bf16[272,128]{1,0:T(8,128)(2,1)S(1)} %get-tuple-element.54), channel_id=1, source_target_pairs={{0,2},{2,0},{4,6},{6,4},{1,3},{3,1},{5,7},{7,5},{8,10},{10,8},{12,... | collective-permute-start | bytes 208904 | tf_op jit(solution)/shard_map/ppermute | solution.py:409
  56.4 7.6 %collective-permute-start.17 = (bf16[272,128]{1,0:T(8,128)(2,1)S(1)}, bf16[272,128]{1,0:T(8,128)(2,1)S(1)}, u32[]{:S(2)}, u32[]{:S(2)}) collective-permute-start(bf16[272,128]{1,0:T(8,128)(2,1)S(1)} %get-tuple-element.53), channel_id=1, source_target_pairs={{0,4},{2,6},{4,0},{6,2},{1,5},{3,7},{5,1},{7,3},{8,12},{10,14},{12... | collective-permute-start | bytes 208904 | tf_op jit(solution)/shard_map/ppermute | solution.py:409
  59.1 6.2 %collective-permute-start.18 = (bf16[272,128]{1,0:T(8,128)(2,1)S(1)}, bf16[272,128]{1,0:T(8,128)(2,1)S(1)}, u32[]{:S(2)}, u32[]{:S(2)}) collective-permute-start(bf16[272,128]{1,0:T(8,128)(2,1)S(1)} %get-tuple-element.52), channel_id=1, source_target_pairs={{0,6},{2,4},{4,2},{6,0},{1,7},{3,5},{5,3},{7,1},{8,14},{10,12},{12... | collective-permute-start | bytes 208904 | tf_op jit(solution)/shard_map/ppermute | solution.py:409

commit v14 on v12

--- a/solution.py
+++ b/solution.py
@@ -417,7 +417,7 @@
         for p in PEERS:
             line = line + send_xy(part[p, 1:], p).astype(f32)
         line, y = lax.optimization_barrier((line.astype(bf16), y))
-        parts += [send_z(line[k - 1], k) for k in LINE]
+        parts += [send_z(line[k - 1], k) for k in LINE[::-1]]
     else:
         line = part[0, 0].astype(f32)
         for p in PEERS:

time: 63.3 us -> 63.1 us (level)
  transfers between devices with their start and end apart: 19 -> 19, of which waited for: 9 -> 10; matrix products, arithmetic and copies ran while one was open for 0% -> 0% of each run, Pallas kernels for 6% -> 6%
where the time goes in v14:
time: 63.1 us; the launch traced here: 62.8 us
  starting transfers between devices  24.4 us (39%)
  waiting for transfers between devices  22.3 us (35%)
  Pallas kernels  12.5 us (20%)
  local copies, waits for them, and re-layouts  1.7 us (3%)
  between operations  1.43 us (2%)
    ppermute x11, starting transfers between devices, send_xy(): return lax.ppermute(x, ('x', 'y'), [(i, i ^ p) for i in range(4)])  14.1 us
    ppermute x11, waiting for transfers between devices, send_xy(): return lax.ppermute(x, ('x', 'y'), [(i, i ^ p) for i in range(4)])  12.1 us
    ppermute x6, starting transfers between devices, send_z(): return lax.ppermute(x, 'z', [(i, i ^ k) for i in range(cols)])  10.1 us
    pallas_call x1, Pallas kernels, scores(): pl.pallas_call(functools.partial(scores_kernel, mine, cols, folded), grid...  7.8 us
    ppermute x6, waiting for transfers between devices, send_z(): return lax.ppermute(x, 'z', [(i, i ^ k) for i in range(cols)])  5.58 us
    ppermute x2, waiting for transfers between devices, send_core(): return lax.ppermute(x, 'core', [(0, 1), (1, 0)])  4.62 us
    pallas_call x1, Pallas kernels, outputs(): pl.pallas_call(outputs_kernel, grid=(KV_HEADS,), in_specs=[smem, smem, pl...  4.01 us
  transfers between devices with their start and end apart: 19, of which 10 were waited for; matrix products, arithmetic and copies ran while one was open for 0% of the time, Pallas kernels for 6%

profile of v14, /device:TPU:0, one launch (start us, length us, event | category | flops | bytes accessed | tf_op | source)
XLA Modules:
  0.0 62.8 jit_solution(4072335504715683550)
XLA Ops:
  0.6 0.8 %constant_dynamic-update-slice_fusion.1 = bf16[32,1024]{1,0:T(8,128)(2,1)S(1)} fusion(bf16[32,512]{1,0:T(8,128)(2,1)} %param.8), kind=kLoop, calls=%fused_computation.19 | loop fusion | bytes 65536
  1.4 0.8 %constant_dynamic-update-slice_fusion = bf16[32,1024]{1,0:T(8,128)(2,1)S(1)} fusion(bf16[32,1024]{1,0:T(8,128)(2,1)S(1)} %constant_dynamic-update-slice_fusion.1, bf16[32,512]{1,0:T(8,128)(2,1)} %param.9), kind=kLoop, calls=%fused_computation.18 | loop fusion | bytes 65536 | tf_op jit(solution)/shard_map/concatenate | solution.py:392
  2.2 5.0 %collective-permute-start.2 = (bf16[32,1024]{1,0:T(8,128)(2,1)S(1)}, bf16[32,1024]{1,0:T(8,128)(2,1)S(1)}, u32[]{:S(2)}, u32[]{:S(2)}) collective-permute-start(bf16[32,1024]{1,0:T(8,128)(2,1)S(1)} %constant_dynamic-update-slice_fusion), channel_id=1, source_target_pairs={{0,6},{2,4},{4,2},{6,0},{1,7},{3,5},{5,3},{7,1},{8,14},{10,12},{12... | collective-permute-start | bytes 196616 | tf_op jit(solution)/shard_map/ppermute | solution.py:384
  7.2 0.0 collective-permute-start.1
  7.2 0.6 collective-permute-start
  7.8 1.7 %collective-permute-start.3 = (bf16[32,1024]{1,0:T(8,128)(2,1)S(1)}, bf16[32,1024]{1,0:T(8,128)(2,1)S(1)}, u32[]{:S(2)}, u32[]{:S(2)}) collective-permute-start(bf16[32,1024]{1,0:T(8,128)(2,1)S(1)} %constant_dynamic-update-slice_fusion), channel_id=1, source_target_pairs={{0,1},{1,0},{16,17},{17,16},{2,3},{3,2},{18,19},{19,18},{4,5},{5,4... | collective-permute-start | bytes 196616 | tf_op jit(solution)/shard_map/ppermute | solution.py:387
  9.5 1.5 %collective-permute-start.4 = (bf16[32,1024]{1,0:T(8,128)(2,1)S(1)}, bf16[32,1024]{1,0:T(8,128)(2,1)S(1)}, u32[]{:S(2)}, u32[]{:S(2)}) collective-permute-start(bf16[32,1024]{1,0:T(8,128)(2,1)S(1)} %constant_dynamic-update-slice_fusion), channel_id=1, source_target_pairs={{0,16},{1,17},{16,0},{17,1},{2,18},{3,19},{18,2},{19,3},{4,20},{5,... | collective-permute-start | bytes 196616 | tf_op jit(solution)/shard_map/ppermute | solution.py:387
  11.0 0.0 collective-permute-done.2
  11.0 1.8 %collective-permute-done.1 = bf16[32,1024]{1,0:T(8,128)(2,1)S(1)} collective-permute-done((bf16[32,1024]{1,0:T(8,128)(2,1)S(1)}, bf16[32,1024]{1,0:T(8,128)(2,1)S(1)}, u32[]{:S(2)}, u32[]{:S(2)}) %collective-permute-start.1) | collective-permute-done | bytes 65568 | tf_op jit(solution)/shard_map/ppermute | solution.py:384
  12.8 0.0 collective-permute-done
  12.8 0.0 collective-permute-done.3
  12.8 0.9 %collective-permute-done.4 = bf16[32,1024]{1,0:T(8,128)(2,1)S(1)} collective-permute-done((bf16[32,1024]{1,0:T(8,128)(2,1)S(1)}, bf16[32,1024]{1,0:T(8,128)(2,1)S(1)}, u32[]{:S(2)}, u32[]{:S(2)}) %collective-permute-start.4) | collective-permute-done | bytes 65568 | tf_op jit(solution)/shard_map/ppermute | solution.py:387
  13.8 0.7 %collective-permute-start.5 = (bf16[96,1024]{1,0:T(8,128)(2,1)S(1)}, bf16[96,1024]{1,0:T(8,128)(2,1)S(1)}, u32[]{:S(2)}, u32[]{:S(2)}) collective-permute-start(bf16[96,1024]{1,0:T(8,128)(2,1)S(1)} %pad_maximum_fusion.1), channel_id=1, source_target_pairs={{0,1},{1,0},{16,17},{17,16},{2,3},{3,2},{18,19},{19,18},{4,5},{5,4... | collective-permute-start | bytes 589832 | tf_op jit(solution)/shard_map/ppermute | solution.py:387
  14.4 1.5 %collective-permute-start.6 = (bf16[96,1024]{1,0:T(8,128)(2,1)S(1)}, bf16[96,1024]{1,0:T(8,128)(2,1)S(1)}, u32[]{:S(2)}, u32[]{:S(2)}) collective-permute-start(bf16[96,1024]{1,0:T(8,128)(2,1)S(1)} %pad_maximum_fusion.1), channel_id=1, source_target_pairs={{0,16},{1,17},{16,0},{17,1},{2,18},{3,19},{18,2},{19,3},{4,20},{5,... | collective-permute-start | bytes 589832 | tf_op jit(solution)/shard_map/ppermute | solution.py:387
  16.0 0.0 copy-start
  16.0 0.0 copy-start.2
  16.0 0.0 copy-start.3
  16.0 1.4 %collective-permute-start.7 = (bf16[128,1024]{1,0:T(8,128)(2,1)S(1)}, bf16[128,1024]{1,0:T(8,128)(2,1)S(1)}, u32[]{:S(2)}, u32[]{:S(2)}) collective-permute-start(bf16[128,1024]{1,0:T(8,128)(2,1)S(1)} %pad_maximum_fusion), channel_id=1, source_target_pairs={{0,17},{1,16},{16,1},{17,0},{2,19},{3,18},{18,3},{19,2},{4,21},{5,... | collective-permute-start | bytes 786440 | tf_op jit(solution)/shard_map/ppermute | solution.py:387
  17.4 2.6 %collective-permute-done.5 = bf16[96,1024]{1,0:T(8,128)(2,1)S(1)} collective-permute-done((bf16[96,1024]{1,0:T(8,128)(2,1)S(1)}, bf16[96,1024]{1,0:T(8,128)(2,1)S(1)}, u32[]{:S(2)}, u32[]{:S(2)}) %collective-permute-start.5) | collective-permute-done | bytes 196640 | tf_op jit(solution)/shard_map/ppermute | solution.py:387
  20.1 2.2 %collective-permute-done.6 = bf16[96,1024]{1,0:T(8,128)(2,1)S(1)} collective-permute-done((bf16[96,1024]{1,0:T(8,128)(2,1)S(1)}, bf16[96,1024]{1,0:T(8,128)(2,1)S(1)}, u32[]{:S(2)}, u32[]{:S(2)}) %collective-permute-start.6) | collective-permute-done | bytes 196640 | tf_op jit(solution)/shard_map/ppermute | solution.py:387
  22.3 4.3 %collective-permute-done.7 = bf16[128,1024]{1,0:T(8,128)(2,1)S(1)} collective-permute-done((bf16[128,1024]{1,0:T(8,128)(2,1)S(1)}, bf16[128,1024]{1,0:T(8,128)(2,1)S(1)}, u32[]{:S(2)}, u32[]{:S(2)}) %collective-permute-start.7) | collective-permute-done | bytes 262176 | tf_op jit(solution)/shard_map/ppermute | solution.py:387
  26.5 0.1 collective-permute-start.8
  27.3 2.0 %collective-permute-done.8.other = bf16[2,2,128,1024]{3,2,1,0:T(8,128)(2,1)S(1)} collective-permute-done((bf16[2,2,128,1024]{3,2,1,0:T(8,128)(2,1)S(1)}, bf16[2,2,128,1024]{3,2,1,0:T(8,128)(2,1)S(1)}, u32[]{:S(2)}, u32[]{:S(2)}) %collective-permute-start.8) | collective-permute-done | bytes 1048608 | tf_op jit(solution)/shard_map/ppermute | solution.py:390
  29.3 7.8 %shard_map.110 = (bf16[4,256,1024]{2,1,0:T(8,128)(2,1)S(1)}, bf16[4,256,1024]{2,1,0:T(8,128)(2,1)S(1)}, bf16[2,256,1024]{2,1,0:T(8,128)(2,1)S(1)}, bf16[2,2,4,27...) custom-call(s32[128]{0:T(128)S(1)} %copy-done.3, s32[4]{0:T(128)S(1)} %copy-done.2, ...), custom_call_target="tpu_custom_call" | custom-call | flops 2147483648 | bytes 12582912 | tf_op jit(solution)/shard_map/pallas_call | solution.py:298
  37.1 0.2 collective-permute-start.9
  37.3 2.6 %collective-permute-done.9 = bf16[2,2,4,272,128]{4,3,2,1,0:T(8,128)(2,1)S(1)} collective-permute-done((bf16[2,2,4,272,128]{4,3,2,1,0:T(8,128)(2,1)S(1)}, bf16[2,2,4,272,128]{4,3,2,1,0:T(8,128)(2,1)S(1)}, u32[]{:S(2)}, u32[]{:S(2)}) %collective-permute-start.9) | collective-permute-done | bytes 1114144 | tf_op jit(solution)/shard_map/ppermute | solution.py:390
  39.9 0.3 add_convert_fusion
  40.3 2.3 %collective-permute-start.12 = (bf16[3,272,128]{2,1,0:T(8,128)(2,1)S(1)}, bf16[3,272,128]{2,1,0:T(8,128)(2,1)S(1)}, u32[]{:S(2)}, u32[]{:S(2)}) collective-permute-start(bf16[3,272,128]{2,1,0:T(8,128)(2,1)S(1)} %get-tuple-element.50), channel_id=1, source_target_pairs={{0,17},{1,16},{16,1},{17,0},{2,19},{3,18},{18,3},{19,2},{4,21},{5,... | collective-permute-start | bytes 626696 | tf_op jit(solution)/shard_map/ppermute | solution.py:387
  42.7 0.5 collective-permute-start.11
  43.2 0.7 %collective-permute-start.10 = (bf16[3,272,128]{2,1,0:T(8,128)(2,1)S(1)}, bf16[3,272,128]{2,1,0:T(8,128)(2,1)S(1)}, u32[]{:S(2)}, u32[]{:S(2)}) collective-permute-start(bf16[3,272,128]{2,1,0:T(8,128)(2,1)S(1)} %get-tuple-element.49), channel_id=1, source_target_pairs={{0,1},{1,0},{16,17},{17,16},{2,3},{3,2},{18,19},{19,18},{4,5},{5,4... | collective-permute-start | bytes 626696 | tf_op jit(solution)/shard_map/ppermute | solution.py:387
  43.9 1.4 %collective-permute-start.13 = (bf16[272,128]{1,0:T(8,128)(2,1)S(1)}, bf16[272,128]{1,0:T(8,128)(2,1)S(1)}, u32[]{:S(2)}, u32[]{:S(2)}) collective-permute-start(bf16[272,128]{1,0:T(8,128)(2,1)S(1)} %get-tuple-element.47), channel_id=1, source_target_pairs={{0,1},{1,0},{16,17},{17,16},{2,3},{3,2},{18,19},{19,18},{4,5},{5,4... | collective-permute-start | bytes 208904 | tf_op jit(solution)/shard_map/ppermute | solution.py:387
  45.2 1.5 %collective-permute-start.14 = (bf16[272,128]{1,0:T(8,128)(2,1)S(1)}, bf16[272,128]{1,0:T(8,128)(2,1)S(1)}, u32[]{:S(2)}, u32[]{:S(2)}) collective-permute-start(bf16[272,128]{1,0:T(8,128)(2,1)S(1)} %get-tuple-element.46), channel_id=1, source_target_pairs={{0,16},{1,17},{16,0},{17,1},{2,18},{3,19},{18,2},{19,3},{4,20},{5,... | collective-permute-start | bytes 208904 | tf_op jit(solution)/shard_map/ppermute | solution.py:387
  46.7 4.0 %shard_map.111 = (bf16[128,4096]{1,0:T(8,128)(2,1)}, bf16[128,4096]{1,0:T(8,128)(2,1)}) custom-call(s32[128]{0:T(128)S(1)} %copy-done.3, f32[1]{0:T(128)S(6)} %copy.19.gate_s, s32[1,128]{1,0:T(1,128)S(1)} %bitcast.31, bf16[4,256,1024]{2,1,0:T(8,128)(2,1)S(1)} %get-tuple-element.34.p16, bf16[4,256,1024]{2,1,0:T(8,128)(2,1)S(1)} %get-tuple-element.35.ds16, ...), custom_call_target="tpu_custom_call" | custom-call | flops 5000000000 | bytes 12582912 | tf_op jit(solution)/shard_map/pallas_call | solution.py:61
  50.7 0.0 collective-permute-done.12
  50.7 0.9 %collective-permute-start.15 = (bf16[272,128]{1,0:T(8,128)(2,1)S(1)}, bf16[272,128]{1,0:T(8,128)(2,1)S(1)}, u32[]{:S(2)}, u32[]{:S(2)}) collective-permute-start(bf16[272,128]{1,0:T(8,128)(2,1)S(1)} %get-tuple-element.45), channel_id=1, source_target_pairs={{0,17},{1,16},{16,1},{17,0},{2,19},{3,18},{18,3},{19,2},{4,21},{5,... | collective-permute-start | bytes 208904 | tf_op jit(solution)/shard_map/ppermute | solution.py:387
  51.6 2.1 %collective-permute-done.11 = bf16[3,272,128]{2,1,0:T(8,128)(2,1)S(1)} collective-permute-done((bf16[3,272,128]{2,1,0:T(8,128)(2,1)S(1)}, bf16[3,272,128]{2,1,0:T(8,128)(2,1)S(1)}, u32[]{:S(2)}, u32[]{:S(2)}) %collective-permute-start.11) | collective-permute-done | bytes 208928 | tf_op jit(solution)/shard_map/ppermute | solution.py:387
  53.7 0.0 collective-permute-done.10
  53.7 0.1 fusion.2
  53.8 1.8 %collective-permute-start.16 = (bf16[272,128]{1,0:T(8,128)(2,1)S(1)}, bf16[272,128]{1,0:T(8,128)(2,1)S(1)}, u32[]{:S(2)}, u32[]{:S(2)}) collective-permute-start(bf16[272,128]{1,0:T(8,128)(2,1)S(1)} %get-tuple-element.54), channel_id=1, source_target_pairs={{0,6},{2,4},{4,2},{6,0},{1,7},{3,5},{5,3},{7,1},{8,14},{10,12},{12... | collective-permute-start | bytes 208904 | tf_op jit(solution)/shard_map/ppermute | solution.py:384
  55.6 0.0 collective-permute-start.17
  55.6 0.0 collective-permute-done.13.refs_1_
  55.6 2.7 %collective-permute-start.18 = (bf16[272,128]{1,0:T(8,128)(2,1)S(1)}, bf16[272,128]{1,0:T(8,128)(2,1)S(1)}, u32[]{:S(2)}, u32[]{:S(2)}) collective-permute-start(bf16[272,128]{1,0:T(8,128)(2,1)S(1)} %get-tuple-element.52), channel_id=1, source_target_pairs={{0,2},{2,0},{4,6},{6,4},{1,3},{3,1},{5,7},{7,5},{8,10},{10,8},{12,... | collective-permute-start | bytes 208904 | tf_op jit(solution)/shard_map/ppermute | solution.py:384
  58.3 0.0 collective-permute-done.14.refs_2_
  58.3 0.0 collective-permute-done.15.refs_3_
  58.3 1.9 %collective-permute-done.16.refs_4_ = bf16[272,128]{1,0:T(8,128)(2,1)S(1)} collective-permute-done((bf16[272,128]{1,0:T(8,128)(2,1)S(1)}, bf16[272,128]{1,0:T(8,128)(2,1)S(1)}, u32[]{:S(2)}, u32[]{:S(2)}) %collective-permute-start.16) | collective-permute-done | bytes 69664 | tf_op jit(solution)/shard_map/ppermute | solution.py:384
  60.2 1.9 %collective-permute-done.17.refs_5_ = bf16[272,128]{1,0:T(8,128)(2,1)S(1)} collective-permute-done((bf16[272,128]{1,0:T(8,128)(2,1)S(1)}, bf16[272,128]{1,0:T(8,128)(2,1)S(1)}, u32[]{:S(2)}, u32[]{:S(2)}) %collective-permute-start.17) | collective-permute-done | bytes 69664 | tf_op jit(solution)/shard_map/ppermute | solution.py:384
  62.1 0.0 collective-permute-done.18.refs_6_
  62.1 0.7 %shard_map.112 = (f32[32,512]{1,0:T(8,128)}, f32[32,512]{1,0:T(8,128)}, f32[1]{0:T(128)}) custom-call(f32[8,128]{1,0:T(8,128)S(1)} %get-tuple-element.40.gate, bf16[272,128]{1,0:T(8,128)(2,1)S(1)} %get-tuple-element.48.refs_0_, bf16[272,128]{1,0:T(8,128)(2,1)S(1)} %collective-permute-done.13.refs_1_, bf16[272,128]{1,0:T(8,128)(2,1)S(1)} %collective-permute-done.14.refs_2_, ...), custom_call_target="tpu_custom_call" | custom-call | tf_op jit(solution)/shard_map/pallas_call | solution.py:366
  (17 shorter events, 0.2 us)
Async XLA Ops:
  2.2 8.9 %collective-permute-start.2 = (bf16[32,1024]{1,0:T(8,128)(2,1)S(1)}, bf16[32,1024]{1,0:T(8,128)(2,1)S(1)}, u32[]{:S(2)}, u32[]{:S(2)}) collective-permute-start(bf16[32,1024]{1,0:T(8,128)(2,1)S(1)} %constant_dynamic-update-slice_fusion), channel_id=1, source_target_pairs={{0,6},{2,4},{4,2},{6,0},{1,7},{3,5},{5,3},{7,1},{8,14},{10,12},{12... | collective-permute-start | bytes 196616 | tf_op jit(solution)/shard_map/ppermute | solution.py:384
  7.2 5.6 %collective-permute-start.1 = (bf16[32,1024]{1,0:T(8,128)(2,1)S(1)}, bf16[32,1024]{1,0:T(8,128)(2,1)S(1)}, u32[]{:S(2)}, u32[]{:S(2)}) collective-permute-start(bf16[32,1024]{1,0:T(8,128)(2,1)S(1)} %constant_dynamic-update-slice_fusion), channel_id=1, source_target_pairs={{0,4},{2,6},{4,0},{6,2},{1,5},{3,7},{5,1},{7,3},{8,12},{10,14},{12... | collective-permute-start | bytes 196616 | tf_op jit(solution)/shard_map/ppermute | solution.py:384
  7.2 5.6 %collective-permute-start = (bf16[32,1024]{1,0:T(8,128)(2,1)S(1)}, bf16[32,1024]{1,0:T(8,128)(2,1)S(1)}, u32[]{:S(2)}, u32[]{:S(2)}) collective-permute-start(bf16[32,1024]{1,0:T(8,128)(2,1)S(1)} %constant_dynamic-update-slice_fusion), channel_id=1, source_target_pairs={{0,2},{2,0},{4,6},{6,4},{1,3},{3,1},{5,7},{7,5},{8,10},{10,8},{12,... | collective-permute-start | bytes 196616 | tf_op jit(solution)/shard_map/ppermute | solution.py:384
  7.8 5.1 %collective-permute-start.3 = (bf16[32,1024]{1,0:T(8,128)(2,1)S(1)}, bf16[32,1024]{1,0:T(8,128)(2,1)S(1)}, u32[]{:S(2)}, u32[]{:S(2)}) collective-permute-start(bf16[32,1024]{1,0:T(8,128)(2,1)S(1)} %constant_dynamic-update-slice_fusion), channel_id=1, source_target_pairs={{0,1},{1,0},{16,17},{17,16},{2,3},{3,2},{18,19},{19,18},{4,5},{5,4... | collective-permute-start | bytes 196616 | tf_op jit(solution)/shard_map/ppermute | solution.py:387
  9.5 4.3 %collective-permute-start.4 = (bf16[32,1024]{1,0:T(8,128)(2,1)S(1)}, bf16[32,1024]{1,0:T(8,128)(2,1)S(1)}, u32[]{:S(2)}, u32[]{:S(2)}) collective-permute-start(bf16[32,1024]{1,0:T(8,128)(2,1)S(1)} %constant_dynamic-update-slice_fusion), channel_id=1, source_target_pairs={{0,16},{1,17},{16,0},{17,1},{2,18},{3,19},{18,2},{19,3},{4,20},{5,... | collective-permute-start | bytes 196616 | tf_op jit(solution)/shard_map/ppermute | solution.py:387
  13.8 6.3 %collective-permute-start.5 = (bf16[96,1024]{1,0:T(8,128)(2,1)S(1)}, bf16[96,1024]{1,0:T(8,128)(2,1)S(1)}, u32[]{:S(2)}, u32[]{:S(2)}) collective-permute-start(bf16[96,1024]{1,0:T(8,128)(2,1)S(1)} %pad_maximum_fusion.1), channel_id=1, source_target_pairs={{0,1},{1,0},{16,17},{17,16},{2,3},{3,2},{18,19},{19,18},{4,5},{5,4... | collective-permute-start | bytes 589832 | tf_op jit(solution)/shard_map/ppermute | solution.py:387
  14.4 7.8 %collective-permute-start.6 = (bf16[96,1024]{1,0:T(8,128)(2,1)S(1)}, bf16[96,1024]{1,0:T(8,128)(2,1)S(1)}, u32[]{:S(2)}, u32[]{:S(2)}) collective-permute-start(bf16[96,1024]{1,0:T(8,128)(2,1)S(1)} %pad_maximum_fusion.1), channel_id=1, source_target_pairs={{0,16},{1,17},{16,0},{17,1},{2,18},{3,19},{18,2},{19,3},{4,20},{5,... | collective-permute-start | bytes 589832 | tf_op jit(solution)/shard_map/ppermute | solution.py:387
  15.9 13.3 %copy-start.1 = (bf16[128,4096]{1,0:T(8,128)(2,1)S(1)}, bf16[128,4096]{1,0:T(8,128)(2,1)}, u32[]{:S(2)}) copy-start(bf16[128,4096]{1,0:T(8,128)(2,1)} %dy_ref.1) | copy-start | bytes 3145732
  16.0 13.3 %copy-start = (bf16[128,4096]{1,0:T(8,128)(2,1)S(1)}, bf16[128,4096]{1,0:T(8,128)(2,1)}, u32[]{:S(2)}) copy-start(bf16[128,4096]{1,0:T(8,128)(2,1)} %q_ref.1) | copy-start | bytes 3145732
  16.0 13.3 %copy-start.2 = (s32[4]{0:T(128)S(1)}, s32[4]{0:T(128)}, u32[]{:S(2)}) copy-start(s32[4]{0:T(128)} %cnt_s.1) | copy-start | bytes 52
  16.0 13.3 %copy-start.3 = (s32[128]{0:T(128)S(1)}, s32[128]{0:T(128)}, u32[]{:S(2)}) copy-start(s32[128]{0:T(128)} %seg_s.3) | copy-start | bytes 1540
  16.0 10.5 %collective-permute-start.7 = (bf16[128,1024]{1,0:T(8,128)(2,1)S(1)}, bf16[128,1024]{1,0:T(8,128)(2,1)S(1)}, u32[]{:S(2)}, u32[]{:S(2)}) collective-permute-start(bf16[128,1024]{1,0:T(8,128)(2,1)S(1)} %pad_maximum_fusion), channel_id=1, source_target_pairs={{0,17},{1,16},{16,1},{17,0},{2,19},{3,18},{18,3},{19,2},{4,21},{5,... | collective-permute-start | bytes 786440 | tf_op jit(solution)/shard_map/ppermute | solution.py:387
  26.5 2.7 %collective-permute-start.8 = (bf16[2,2,128,1024]{3,2,1,0:T(8,128)(2,1)S(1)}, bf16[2,2,128,1024]{3,2,1,0:T(8,128)(2,1)S(1)}, u32[]{:S(2)}, u32[]{:S(2)}) collective-permute-start(bf16[2,2,128,1024]{3,2,1,0:T(8,128)(2,1)S(1)} %bitcast.28), channel_id=1, source_target_pairs={{0,8},{8,0},{1,9},{9,1},{2,10},{10,2},{3,11},{11,3},{4,12},{12,4},... | collective-permute-start | bytes 3145736 | tf_op jit(solution)/shard_map/ppermute | solution.py:390
  37.1 2.8 %collective-permute-start.9 = (bf16[2,2,4,272,128]{4,3,2,1,0:T(8,128)(2,1)S(1)}, bf16[2,2,4,272,128]{4,3,2,1,0:T(8,128)(2,1)S(1)}, u32[]{:S(2)}, u32[]{:S(2)}) collective-permute-start(bf16[2,2,4,272,128]{4,3,2,1,0:T(8,128)(2,1)S(1)} %get-tuple-element.31), channel_id=1, source_target_pairs={{0,8},{8,0},{1,9},{9,1},{2,10},{10,2},{3,11},{11,3},{4,12},{12,4},... | collective-permute-start | bytes 3342344 | tf_op jit(solution)/shard_map/ppermute | solution.py:390
  40.3 10.4 %collective-permute-start.12 = (bf16[3,272,128]{2,1,0:T(8,128)(2,1)S(1)}, bf16[3,272,128]{2,1,0:T(8,128)(2,1)S(1)}, u32[]{:S(2)}, u32[]{:S(2)}) collective-permute-start(bf16[3,272,128]{2,1,0:T(8,128)(2,1)S(1)} %get-tuple-element.50), channel_id=1, source_target_pairs={{0,17},{1,16},{16,1},{17,0},{2,19},{3,18},{18,3},{19,2},{4,21},{5,... | collective-permute-start | bytes 626696 | tf_op jit(solution)/shard_map/ppermute | solution.py:387
  42.7 11.0 %collective-permute-start.11 = (bf16[3,272,128]{2,1,0:T(8,128)(2,1)S(1)}, bf16[3,272,128]{2,1,0:T(8,128)(2,1)S(1)}, u32[]{:S(2)}, u32[]{:S(2)}) collective-permute-start(bf16[3,272,128]{2,1,0:T(8,128)(2,1)S(1)} %get-tuple-element.51), channel_id=1, source_target_pairs={{0,16},{1,17},{16,0},{17,1},{2,18},{3,19},{18,2},{19,3},{4,20},{5,... | collective-permute-start | bytes 626696 | tf_op jit(solution)/shard_map/ppermute | solution.py:387
  43.2 10.5 %collective-permute-start.10 = (bf16[3,272,128]{2,1,0:T(8,128)(2,1)S(1)}, bf16[3,272,128]{2,1,0:T(8,128)(2,1)S(1)}, u32[]{:S(2)}, u32[]{:S(2)}) collective-permute-start(bf16[3,272,128]{2,1,0:T(8,128)(2,1)S(1)} %get-tuple-element.49), channel_id=1, source_target_pairs={{0,1},{1,0},{16,17},{17,16},{2,3},{3,2},{18,19},{19,18},{4,5},{5,4... | collective-permute-start | bytes 626696 | tf_op jit(solution)/shard_map/ppermute | solution.py:387
  43.9 11.8 %collective-permute-start.13 = (bf16[272,128]{1,0:T(8,128)(2,1)S(1)}, bf16[272,128]{1,0:T(8,128)(2,1)S(1)}, u32[]{:S(2)}, u32[]{:S(2)}) collective-permute-start(bf16[272,128]{1,0:T(8,128)(2,1)S(1)} %get-tuple-element.47), channel_id=1, source_target_pairs={{0,1},{1,0},{16,17},{17,16},{2,3},{3,2},{18,19},{19,18},{4,5},{5,4... | collective-permute-start | bytes 208904 | tf_op jit(solution)/shard_map/ppermute | solution.py:387
  45.2 13.1 %collective-permute-start.14 = (bf16[272,128]{1,0:T(8,128)(2,1)S(1)}, bf16[272,128]{1,0:T(8,128)(2,1)S(1)}, u32[]{:S(2)}, u32[]{:S(2)}) collective-permute-start(bf16[272,128]{1,0:T(8,128)(2,1)S(1)} %get-tuple-element.46), channel_id=1, source_target_pairs={{0,16},{1,17},{16,0},{17,1},{2,18},{3,19},{18,2},{19,3},{4,20},{5,... | collective-permute-start | bytes 208904 | tf_op jit(solution)/shard_map/ppermute | solution.py:387
  50.7 7.6 %collective-permute-start.15 = (bf16[272,128]{1,0:T(8,128)(2,1)S(1)}, bf16[272,128]{1,0:T(8,128)(2,1)S(1)}, u32[]{:S(2)}, u32[]{:S(2)}) collective-permute-start(bf16[272,128]{1,0:T(8,128)(2,1)S(1)} %get-tuple-element.45), channel_id=1, source_target_pairs={{0,17},{1,16},{16,1},{17,0},{2,19},{3,18},{18,3},{19,2},{4,21},{5,... | collective-permute-start | bytes 208904 | tf_op jit(solution)/shard_map/ppermute | solution.py:387
  53.8 6.3 %collective-permute-start.16 = (bf16[272,128]{1,0:T(8,128)(2,1)S(1)}, bf16[272,128]{1,0:T(8,128)(2,1)S(1)}, u32[]{:S(2)}, u32[]{:S(2)}) collective-permute-start(bf16[272,128]{1,0:T(8,128)(2,1)S(1)} %get-tuple-element.54), channel_id=1, source_target_pairs={{0,6},{2,4},{4,2},{6,0},{1,7},{3,5},{5,3},{7,1},{8,14},{10,12},{12... | collective-permute-start | bytes 208904 | tf_op jit(solution)/shard_map/ppermute | solution.py:384
  55.6 6.5 %collective-permute-start.17 = (bf16[272,128]{1,0:T(8,128)(2,1)S(1)}, bf16[272,128]{1,0:T(8,128)(2,1)S(1)}, u32[]{:S(2)}, u32[]{:S(2)}) collective-permute-start(bf16[272,128]{1,0:T(8,128)(2,1)S(1)} %get-tuple-element.53), channel_id=1, source_target_pairs={{0,4},{2,6},{4,0},{6,2},{1,5},{3,7},{5,1},{7,3},{8,12},{10,14},{12... | collective-permute-start | bytes 208904 | tf_op jit(solution)/shard_map/ppermute | solution.py:384
  55.6 6.5 %collective-permute-start.18 = (bf16[272,128]{1,0:T(8,128)(2,1)S(1)}, bf16[272,128]{1,0:T(8,128)(2,1)S(1)}, u32[]{:S(2)}, u32[]{:S(2)}) collective-permute-start(bf16[272,128]{1,0:T(8,128)(2,1)S(1)} %get-tuple-element.52), channel_id=1, source_target_pairs={{0,2},{2,0},{4,6},{6,4},{1,3},{3,1},{5,7},{7,5},{8,10},{10,8},{12,... | collective-permute-start | bytes 208904 | tf_op jit(solution)/shard_map/ppermute | solution.py:384

commit v15 on v14

--- a/solution.py
+++ b/solution.py
@@ -391,13 +391,12 @@
 
     kv = jnp.concatenate([keys, values], axis=1)
     if folded:
-        near = [send_xy(kv, p) for p in (1, 2)]
+        near = [send_xy(kv, p) for p in (2, 3)]
         line = [send_z(kv, k) for k in LINE]
         line, near = lax.optimization_barrier((jnp.concatenate(line, axis=0), near))
         kv, line = lax.optimization_barrier((kv, line))
         block = jnp.concatenate([kv, line], axis=0)
-        diag = send_xy(block, 3)
-        own = [block, near[0], send_xy(line, 1), near[1], send_xy(line, 2), diag]
+        own = [block, send_xy(block, 1), near[0], send_xy(line, 2), near[1], send_xy(line, 3)]
     else:
         line = lax.all_gather(kv, "z", axis=0, tiled=True)
         own = [line] + [send_xy(line, p) for p in PEERS]

time: 63.1 us -> 63.2 us (level)
    ppermute x6, waiting for transfers between devices: 5.58 us -> 6.63 us  [send_z(): return lax.ppermute(x, 'z', [(i, i ^ k) for i in range(cols)])]
    ppermute x11, waiting for transfers between devices: 12.1 us -> 11.1 us  [send_xy(): return lax.ppermute(x, ('x', 'y'), [(i, i ^ p) for i in range(4)])]
  transfers between devices with their start and end apart: 19 -> 19, of which waited for: 10 -> 9; matrix products, arithmetic and copies ran while one was open for 0% -> 0% of each run, Pallas kernels for 6% -> 6%
where the time goes in v15:
time: 63.2 us; the launch traced here: 62.9 us
  starting transfers between devices  24.4 us (39%)
  waiting for transfers between devices  22.3 us (35%)
  Pallas kernels  12.5 us (20%)
  local copies, waits for them, and re-layouts  1.71 us (3%)
  between operations  1.46 us (2%)
    ppermute x11, starting transfers between devices, send_xy(): return lax.ppermute(x, ('x', 'y'), [(i, i ^ p) for i in range(4)])  14.1 us
    ppermute x11, waiting for transfers between devices, send_xy(): return lax.ppermute(x, ('x', 'y'), [(i, i ^ p) for i in range(4)])  11.1 us
    ppermute x6, starting transfers between devices, send_z(): return lax.ppermute(x, 'z', [(i, i ^ k) for i in range(cols)])  10.1 us
    pallas_call x1, Pallas kernels, scores(): pl.pallas_call(functools.partial(scores_kernel, mine, cols, folded), grid...  7.8 us
    ppermute x6, waiting for transfers between devices, send_z(): return lax.ppermute(x, 'z', [(i, i ^ k) for i in range(cols)])  6.63 us
    ppermute x2, waiting for transfers between devices, send_core(): return lax.ppermute(x, 'core', [(0, 1), (1, 0)])  4.62 us
    pallas_call x1, Pallas kernels, outputs(): pl.pallas_call(outputs_kernel, grid=(KV_HEADS,), in_specs=[smem, smem, pl...  4.01 us
  transfers between devices with their start and end apart: 19, of which 9 were waited for; matrix products, arithmetic and copies ran while one was open for 0% of the time, Pallas kernels for 6%

profile of v15, /device:TPU:0, one launch (start us, length us, event | category | flops | bytes accessed | tf_op | source)
XLA Modules:
  0.0 62.9 jit_solution(2933724645819321556)
XLA Ops:
  0.6 0.8 %constant_dynamic-update-slice_fusion.1 = bf16[32,1024]{1,0:T(8,128)(2,1)S(1)} fusion(bf16[32,512]{1,0:T(8,128)(2,1)} %param.8), kind=kLoop, calls=%fused_computation.19 | loop fusion | bytes 65536
  1.4 0.8 %constant_dynamic-update-slice_fusion = bf16[32,1024]{1,0:T(8,128)(2,1)S(1)} fusion(bf16[32,1024]{1,0:T(8,128)(2,1)S(1)} %constant_dynamic-update-slice_fusion.1, bf16[32,512]{1,0:T(8,128)(2,1)} %param.9), kind=kLoop, calls=%fused_computation.18 | loop fusion | bytes 65536 | tf_op jit(solution)/shard_map/concatenate | solution.py:392
  2.2 5.0 %collective-permute-start.2 = (bf16[32,1024]{1,0:T(8,128)(2,1)S(1)}, bf16[32,1024]{1,0:T(8,128)(2,1)S(1)}, u32[]{:S(2)}, u32[]{:S(2)}) collective-permute-start(bf16[32,1024]{1,0:T(8,128)(2,1)S(1)} %constant_dynamic-update-slice_fusion), channel_id=1, source_target_pairs={{0,6},{2,4},{4,2},{6,0},{1,7},{3,5},{5,3},{7,1},{8,14},{10,12},{12... | collective-permute-start | bytes 196616 | tf_op jit(solution)/shard_map/ppermute | solution.py:384
  7.2 0.0 collective-permute-start.1
  7.2 0.6 collective-permute-start
  7.8 1.7 %collective-permute-start.3 = (bf16[32,1024]{1,0:T(8,128)(2,1)S(1)}, bf16[32,1024]{1,0:T(8,128)(2,1)S(1)}, u32[]{:S(2)}, u32[]{:S(2)}) collective-permute-start(bf16[32,1024]{1,0:T(8,128)(2,1)S(1)} %constant_dynamic-update-slice_fusion), channel_id=1, source_target_pairs={{0,16},{1,17},{16,0},{17,1},{2,18},{3,19},{18,2},{19,3},{4,20},{5,... | collective-permute-start | bytes 196616 | tf_op jit(solution)/shard_map/ppermute | solution.py:387
  9.5 1.5 %collective-permute-start.4 = (bf16[32,1024]{1,0:T(8,128)(2,1)S(1)}, bf16[32,1024]{1,0:T(8,128)(2,1)S(1)}, u32[]{:S(2)}, u32[]{:S(2)}) collective-permute-start(bf16[32,1024]{1,0:T(8,128)(2,1)S(1)} %constant_dynamic-update-slice_fusion), channel_id=1, source_target_pairs={{0,17},{1,16},{16,1},{17,0},{2,19},{3,18},{18,3},{19,2},{4,21},{5,... | collective-permute-start | bytes 196616 | tf_op jit(solution)/shard_map/ppermute | solution.py:387
  11.0 0.0 collective-permute-done.2
  11.0 1.8 %collective-permute-done.1 = bf16[32,1024]{1,0:T(8,128)(2,1)S(1)} collective-permute-done((bf16[32,1024]{1,0:T(8,128)(2,1)S(1)}, bf16[32,1024]{1,0:T(8,128)(2,1)S(1)}, u32[]{:S(2)}, u32[]{:S(2)}) %collective-permute-start.1) | collective-permute-done | bytes 65568 | tf_op jit(solution)/shard_map/ppermute | solution.py:384
  12.8 0.0 collective-permute-done
  12.8 0.0 collective-permute-done.3
  12.8 1.8 %collective-permute-done.4 = bf16[32,1024]{1,0:T(8,128)(2,1)S(1)} collective-permute-done((bf16[32,1024]{1,0:T(8,128)(2,1)S(1)}, bf16[32,1024]{1,0:T(8,128)(2,1)S(1)}, u32[]{:S(2)}, u32[]{:S(2)}) %collective-permute-start.4) | collective-permute-done | bytes 65568 | tf_op jit(solution)/shard_map/ppermute | solution.py:387
  14.7 0.0 copy-start
  14.7 0.0 copy-start.1
  14.7 0.0 copy-start.2
  14.7 0.0 copy-start.3
  14.7 1.6 %collective-permute-start.5 = (bf16[128,1024]{1,0:T(8,128)(2,1)S(1)}, bf16[128,1024]{1,0:T(8,128)(2,1)S(1)}, u32[]{:S(2)}, u32[]{:S(2)}) collective-permute-start(bf16[128,1024]{1,0:T(8,128)(2,1)S(1)} %pad_maximum_fusion), channel_id=1, source_target_pairs={{0,1},{1,0},{16,17},{17,16},{2,3},{3,2},{18,19},{19,18},{4,5},{5,4... | collective-permute-start | bytes 786440 | tf_op jit(solution)/shard_map/ppermute | solution.py:387
  16.3 0.5 collective-permute-start.6
  16.8 1.4 %collective-permute-start.7 = (bf16[96,1024]{1,0:T(8,128)(2,1)S(1)}, bf16[96,1024]{1,0:T(8,128)(2,1)S(1)}, u32[]{:S(2)}, u32[]{:S(2)}) collective-permute-start(bf16[96,1024]{1,0:T(8,128)(2,1)S(1)} %pad_maximum_fusion.1), channel_id=1, source_target_pairs={{0,17},{1,16},{16,1},{17,0},{2,19},{3,18},{18,3},{19,2},{4,21},{5,... | collective-permute-start | bytes 589832 | tf_op jit(solution)/shard_map/ppermute | solution.py:387
  18.3 7.1 %collective-permute-done.5 = bf16[128,1024]{1,0:T(8,128)(2,1)S(1)} collective-permute-done((bf16[128,1024]{1,0:T(8,128)(2,1)S(1)}, bf16[128,1024]{1,0:T(8,128)(2,1)S(1)}, u32[]{:S(2)}, u32[]{:S(2)}) %collective-permute-start.5) | collective-permute-done | bytes 262176 | tf_op jit(solution)/shard_map/ppermute | solution.py:387
  25.4 0.0 collective-permute-done.6
  25.5 0.0 collective-permute-done.7
  25.5 0.1 collective-permute-start.8
  26.2 2.0 %collective-permute-done.8.other = bf16[2,2,128,1024]{3,2,1,0:T(8,128)(2,1)S(1)} collective-permute-done((bf16[2,2,128,1024]{3,2,1,0:T(8,128)(2,1)S(1)}, bf16[2,2,128,1024]{3,2,1,0:T(8,128)(2,1)S(1)}, u32[]{:S(2)}, u32[]{:S(2)}) %collective-permute-start.8) | collective-permute-done | bytes 1048608 | tf_op jit(solution)/shard_map/ppermute | solution.py:390
  28.2 7.8 %shard_map.110 = (bf16[4,256,1024]{2,1,0:T(8,128)(2,1)S(1)}, bf16[4,256,1024]{2,1,0:T(8,128)(2,1)S(1)}, bf16[2,256,1024]{2,1,0:T(8,128)(2,1)S(1)}, bf16[2,2,4,27...) custom-call(s32[128]{0:T(128)S(1)} %copy-done.3, s32[4]{0:T(128)S(1)} %copy-done.2, ...), custom_call_target="tpu_custom_call" | custom-call | flops 2147483648 | bytes 12582912 | tf_op jit(solution)/shard_map/pallas_call | solution.py:298
  36.0 0.2 collective-permute-start.9
  36.2 2.6 %collective-permute-done.9 = bf16[2,2,4,272,128]{4,3,2,1,0:T(8,128)(2,1)S(1)} collective-permute-done((bf16[2,2,4,272,128]{4,3,2,1,0:T(8,128)(2,1)S(1)}, bf16[2,2,4,272,128]{4,3,2,1,0:T(8,128)(2,1)S(1)}, u32[]{:S(2)}, u32[]{:S(2)}) %collective-permute-start.9) | collective-permute-done | bytes 1114144 | tf_op jit(solution)/shard_map/ppermute | solution.py:390
  38.9 0.3 add_convert_fusion
  39.2 2.4 %collective-permute-start.12 = (bf16[3,272,128]{2,1,0:T(8,128)(2,1)S(1)}, bf16[3,272,128]{2,1,0:T(8,128)(2,1)S(1)}, u32[]{:S(2)}, u32[]{:S(2)}) collective-permute-start(bf16[3,272,128]{2,1,0:T(8,128)(2,1)S(1)} %get-tuple-element.50), channel_id=1, source_target_pairs={{0,17},{1,16},{16,1},{17,0},{2,19},{3,18},{18,3},{19,2},{4,21},{5,... | collective-permute-start | bytes 626696 | tf_op jit(solution)/shard_map/ppermute | solution.py:387
  41.7 0.6 %collective-permute-start.11 = (bf16[3,272,128]{2,1,0:T(8,128)(2,1)S(1)}, bf16[3,272,128]{2,1,0:T(8,128)(2,1)S(1)}, u32[]{:S(2)}, u32[]{:S(2)}) collective-permute-start(bf16[3,272,128]{2,1,0:T(8,128)(2,1)S(1)} %get-tuple-element.51), channel_id=1, source_target_pairs={{0,16},{1,17},{16,0},{17,1},{2,18},{3,19},{18,2},{19,3},{4,20},{5,... | collective-permute-start | bytes 626696 | tf_op jit(solution)/shard_map/ppermute | solution.py:387
  42.3 0.5 collective-permute-start.10
  42.8 1.5 %collective-permute-start.13 = (bf16[272,128]{1,0:T(8,128)(2,1)S(1)}, bf16[272,128]{1,0:T(8,128)(2,1)S(1)}, u32[]{:S(2)}, u32[]{:S(2)}) collective-permute-start(bf16[272,128]{1,0:T(8,128)(2,1)S(1)} %get-tuple-element.47), channel_id=1, source_target_pairs={{0,1},{1,0},{16,17},{17,16},{2,3},{3,2},{18,19},{19,18},{4,5},{5,4... | collective-permute-start | bytes 208904 | tf_op jit(solution)/shard_map/ppermute | solution.py:387
  44.3 1.4 %collective-permute-start.14 = (bf16[272,128]{1,0:T(8,128)(2,1)S(1)}, bf16[272,128]{1,0:T(8,128)(2,1)S(1)}, u32[]{:S(2)}, u32[]{:S(2)}) collective-permute-start(bf16[272,128]{1,0:T(8,128)(2,1)S(1)} %get-tuple-element.46), channel_id=1, source_target_pairs={{0,16},{1,17},{16,0},{17,1},{2,18},{3,19},{18,2},{19,3},{4,20},{5,... | collective-permute-start | bytes 208904 | tf_op jit(solution)/shard_map/ppermute | solution.py:387
  45.7 4.0 %shard_map.111 = (bf16[128,4096]{1,0:T(8,128)(2,1)}, bf16[128,4096]{1,0:T(8,128)(2,1)}) custom-call(s32[128]{0:T(128)S(1)} %copy-done.3, f32[1]{0:T(128)S(6)} %copy.19.gate_s, s32[1,128]{1,0:T(1,128)S(1)} %bitcast.31, bf16[4,256,1024]{2,1,0:T(8,128)(2,1)S(1)} %get-tuple-element.34.p16, bf16[4,256,1024]{2,1,0:T(8,128)(2,1)S(1)} %get-tuple-element.35.ds16, ...), custom_call_target="tpu_custom_call" | custom-call | flops 5000000000 | bytes 12582912 | tf_op jit(solution)/shard_map/pallas_call | solution.py:61
  49.7 0.0 collective-permute-done.12
  49.7 0.9 %collective-permute-start.15 = (bf16[272,128]{1,0:T(8,128)(2,1)S(1)}, bf16[272,128]{1,0:T(8,128)(2,1)S(1)}, u32[]{:S(2)}, u32[]{:S(2)}) collective-permute-start(bf16[272,128]{1,0:T(8,128)(2,1)S(1)} %get-tuple-element.45), channel_id=1, source_target_pairs={{0,17},{1,16},{16,1},{17,0},{2,19},{3,18},{18,3},{19,2},{4,21},{5,... | collective-permute-start | bytes 208904 | tf_op jit(solution)/shard_map/ppermute | solution.py:387
  50.6 2.2 %collective-permute-done.11 = bf16[3,272,128]{2,1,0:T(8,128)(2,1)S(1)} collective-permute-done((bf16[3,272,128]{2,1,0:T(8,128)(2,1)S(1)}, bf16[3,272,128]{2,1,0:T(8,128)(2,1)S(1)}, u32[]{:S(2)}, u32[]{:S(2)}) %collective-permute-start.11) | collective-permute-done | bytes 208928 | tf_op jit(solution)/shard_map/ppermute | solution.py:387
  52.8 0.0 collective-permute-done.10
  52.8 0.1 fusion.2
  52.9 3.7 %collective-permute-start.16 = (bf16[272,128]{1,0:T(8,128)(2,1)S(1)}, bf16[272,128]{1,0:T(8,128)(2,1)S(1)}, u32[]{:S(2)}, u32[]{:S(2)}) collective-permute-start(bf16[272,128]{1,0:T(8,128)(2,1)S(1)} %get-tuple-element.54), channel_id=1, source_target_pairs={{0,6},{2,4},{4,2},{6,0},{1,7},{3,5},{5,3},{7,1},{8,14},{10,12},{12... | collective-permute-start | bytes 208904 | tf_op jit(solution)/shard_map/ppermute | solution.py:384
  56.6 0.0 collective-permute-start.17
  56.6 0.0 collective-permute-done.13.refs_1_
  56.6 0.8 %collective-permute-start.18 = (bf16[272,128]{1,0:T(8,128)(2,1)S(1)}, bf16[272,128]{1,0:T(8,128)(2,1)S(1)}, u32[]{:S(2)}, u32[]{:S(2)}) collective-permute-start(bf16[272,128]{1,0:T(8,128)(2,1)S(1)} %get-tuple-element.52), channel_id=1, source_target_pairs={{0,2},{2,0},{4,6},{6,4},{1,3},{3,1},{5,7},{7,5},{8,10},{10,8},{12,... | collective-permute-start | bytes 208904 | tf_op jit(solution)/shard_map/ppermute | solution.py:384
  57.4 0.0 collective-permute-done.14.refs_2_
  57.4 1.8 %collective-permute-done.16.refs_4_ = bf16[272,128]{1,0:T(8,128)(2,1)S(1)} collective-permute-done((bf16[272,128]{1,0:T(8,128)(2,1)S(1)}, bf16[272,128]{1,0:T(8,128)(2,1)S(1)}, u32[]{:S(2)}, u32[]{:S(2)}) %collective-permute-start.16) | collective-permute-done | bytes 69664 | tf_op jit(solution)/shard_map/ppermute | solution.py:384
  59.2 2.7 %collective-permute-done.17.refs_5_ = bf16[272,128]{1,0:T(8,128)(2,1)S(1)} collective-permute-done((bf16[272,128]{1,0:T(8,128)(2,1)S(1)}, bf16[272,128]{1,0:T(8,128)(2,1)S(1)}, u32[]{:S(2)}, u32[]{:S(2)}) %collective-permute-start.17) | collective-permute-done | bytes 69664 | tf_op jit(solution)/shard_map/ppermute | solution.py:384
  61.9 0.3 collective-permute-done.18.refs_6_
  62.2 0.7 %shard_map.112 = (f32[32,512]{1,0:T(8,128)}, f32[32,512]{1,0:T(8,128)}, f32[1]{0:T(128)}) custom-call(f32[8,128]{1,0:T(8,128)S(1)} %get-tuple-element.40.gate, bf16[272,128]{1,0:T(8,128)(2,1)S(1)} %get-tuple-element.48.refs_0_, bf16[272,128]{1,0:T(8,128)(2,1)S(1)} %collective-permute-done.13.refs_1_, bf16[272,128]{1,0:T(8,128)(2,1)S(1)} %collective-permute-done.14.refs_2_, ...), custom_call_target="tpu_custom_call" | custom-call | tf_op jit(solution)/shard_map/pallas_call | solution.py:366
  (17 shorter events, 0.2 us)
Async XLA Ops:
  2.2 8.8 %collective-permute-start.2 = (bf16[32,1024]{1,0:T(8,128)(2,1)S(1)}, bf16[32,1024]{1,0:T(8,128)(2,1)S(1)}, u32[]{:S(2)}, u32[]{:S(2)}) collective-permute-start(bf16[32,1024]{1,0:T(8,128)(2,1)S(1)} %constant_dynamic-update-slice_fusion), channel_id=1, source_target_pairs={{0,6},{2,4},{4,2},{6,0},{1,7},{3,5},{5,3},{7,1},{8,14},{10,12},{12... | collective-permute-start | bytes 196616 | tf_op jit(solution)/shard_map/ppermute | solution.py:384
  7.2 5.6 %collective-permute-start.1 = (bf16[32,1024]{1,0:T(8,128)(2,1)S(1)}, bf16[32,1024]{1,0:T(8,128)(2,1)S(1)}, u32[]{:S(2)}, u32[]{:S(2)}) collective-permute-start(bf16[32,1024]{1,0:T(8,128)(2,1)S(1)} %constant_dynamic-update-slice_fusion), channel_id=1, source_target_pairs={{0,4},{2,6},{4,0},{6,2},{1,5},{3,7},{5,1},{7,3},{8,12},{10,14},{12... | collective-permute-start | bytes 196616 | tf_op jit(solution)/shard_map/ppermute | solution.py:384
  7.2 5.6 %collective-permute-start = (bf16[32,1024]{1,0:T(8,128)(2,1)S(1)}, bf16[32,1024]{1,0:T(8,128)(2,1)S(1)}, u32[]{:S(2)}, u32[]{:S(2)}) collective-permute-start(bf16[32,1024]{1,0:T(8,128)(2,1)S(1)} %constant_dynamic-update-slice_fusion), channel_id=1, source_target_pairs={{0,2},{2,0},{4,6},{6,4},{1,3},{3,1},{5,7},{7,5},{8,10},{10,8},{12,... | collective-permute-start | bytes 196616 | tf_op jit(solution)/shard_map/ppermute | solution.py:384
  7.8 5.1 %collective-permute-start.3 = (bf16[32,1024]{1,0:T(8,128)(2,1)S(1)}, bf16[32,1024]{1,0:T(8,128)(2,1)S(1)}, u32[]{:S(2)}, u32[]{:S(2)}) collective-permute-start(bf16[32,1024]{1,0:T(8,128)(2,1)S(1)} %constant_dynamic-update-slice_fusion), channel_id=1, source_target_pairs={{0,16},{1,17},{16,0},{17,1},{2,18},{3,19},{18,2},{19,3},{4,20},{5,... | collective-permute-start | bytes 196616 | tf_op jit(solution)/shard_map/ppermute | solution.py:387
  9.5 5.2 %collective-permute-start.4 = (bf16[32,1024]{1,0:T(8,128)(2,1)S(1)}, bf16[32,1024]{1,0:T(8,128)(2,1)S(1)}, u32[]{:S(2)}, u32[]{:S(2)}) collective-permute-start(bf16[32,1024]{1,0:T(8,128)(2,1)S(1)} %constant_dynamic-update-slice_fusion), channel_id=1, source_target_pairs={{0,17},{1,16},{16,1},{17,0},{2,19},{3,18},{18,3},{19,2},{4,21},{5,... | collective-permute-start | bytes 196616 | tf_op jit(solution)/shard_map/ppermute | solution.py:387
  14.7 13.5 %copy-start = (bf16[128,4096]{1,0:T(8,128)(2,1)S(1)}, bf16[128,4096]{1,0:T(8,128)(2,1)}, u32[]{:S(2)}) copy-start(bf16[128,4096]{1,0:T(8,128)(2,1)} %q_ref.1) | copy-start | bytes 3145732
  14.7 13.5 %copy-start.1 = (bf16[128,4096]{1,0:T(8,128)(2,1)S(1)}, bf16[128,4096]{1,0:T(8,128)(2,1)}, u32[]{:S(2)}) copy-start(bf16[128,4096]{1,0:T(8,128)(2,1)} %dy_ref.1) | copy-start | bytes 3145732
  14.7 13.5 %copy-start.2 = (s32[4]{0:T(128)S(1)}, s32[4]{0:T(128)}, u32[]{:S(2)}) copy-start(s32[4]{0:T(128)} %cnt_s.1) | copy-start | bytes 52
  14.7 13.5 %copy-start.3 = (s32[128]{0:T(128)S(1)}, s32[128]{0:T(128)}, u32[]{:S(2)}) copy-start(s32[128]{0:T(128)} %seg_s.3) | copy-start | bytes 1540
  14.7 10.7 %collective-permute-start.5 = (bf16[128,1024]{1,0:T(8,128)(2,1)S(1)}, bf16[128,1024]{1,0:T(8,128)(2,1)S(1)}, u32[]{:S(2)}, u32[]{:S(2)}) collective-permute-start(bf16[128,1024]{1,0:T(8,128)(2,1)S(1)} %pad_maximum_fusion), channel_id=1, source_target_pairs={{0,1},{1,0},{16,17},{17,16},{2,3},{3,2},{18,19},{19,18},{4,5},{5,4... | collective-permute-start | bytes 786440 | tf_op jit(solution)/shard_map/ppermute | solution.py:387
  16.3 9.1 %collective-permute-start.6 = (bf16[96,1024]{1,0:T(8,128)(2,1)S(1)}, bf16[96,1024]{1,0:T(8,128)(2,1)S(1)}, u32[]{:S(2)}, u32[]{:S(2)}) collective-permute-start(bf16[96,1024]{1,0:T(8,128)(2,1)S(1)} %pad_maximum_fusion.1), channel_id=1, source_target_pairs={{0,16},{1,17},{16,0},{17,1},{2,18},{3,19},{18,2},{19,3},{4,20},{5,... | collective-permute-start | bytes 589832 | tf_op jit(solution)/shard_map/ppermute | solution.py:387
  16.8 8.6 %collective-permute-start.7 = (bf16[96,1024]{1,0:T(8,128)(2,1)S(1)}, bf16[96,1024]{1,0:T(8,128)(2,1)S(1)}, u32[]{:S(2)}, u32[]{:S(2)}) collective-permute-start(bf16[96,1024]{1,0:T(8,128)(2,1)S(1)} %pad_maximum_fusion.1), channel_id=1, source_target_pairs={{0,17},{1,16},{16,1},{17,0},{2,19},{3,18},{18,3},{19,2},{4,21},{5,... | collective-permute-start | bytes 589832 | tf_op jit(solution)/shard_map/ppermute | solution.py:387
  25.5 2.7 %collective-permute-start.8 = (bf16[2,2,128,1024]{3,2,1,0:T(8,128)(2,1)S(1)}, bf16[2,2,128,1024]{3,2,1,0:T(8,128)(2,1)S(1)}, u32[]{:S(2)}, u32[]{:S(2)}) collective-permute-start(bf16[2,2,128,1024]{3,2,1,0:T(8,128)(2,1)S(1)} %bitcast.28), channel_id=1, source_target_pairs={{0,8},{8,0},{1,9},{9,1},{2,10},{10,2},{3,11},{11,3},{4,12},{12,4},... | collective-permute-start | bytes 3145736 | tf_op jit(solution)/shard_map/ppermute | solution.py:390
  36.0 2.8 %collective-permute-start.9 = (bf16[2,2,4,272,128]{4,3,2,1,0:T(8,128)(2,1)S(1)}, bf16[2,2,4,272,128]{4,3,2,1,0:T(8,128)(2,1)S(1)}, u32[]{:S(2)}, u32[]{:S(2)}) collective-permute-start(bf16[2,2,4,272,128]{4,3,2,1,0:T(8,128)(2,1)S(1)} %get-tuple-element.31), channel_id=1, source_target_pairs={{0,8},{8,0},{1,9},{9,1},{2,10},{10,2},{3,11},{11,3},{4,12},{12,4},... | collective-permute-start | bytes 3342344 | tf_op jit(solution)/shard_map/ppermute | solution.py:390
  39.2 10.5 %collective-permute-start.12 = (bf16[3,272,128]{2,1,0:T(8,128)(2,1)S(1)}, bf16[3,272,128]{2,1,0:T(8,128)(2,1)S(1)}, u32[]{:S(2)}, u32[]{:S(2)}) collective-permute-start(bf16[3,272,128]{2,1,0:T(8,128)(2,1)S(1)} %get-tuple-element.50), channel_id=1, source_target_pairs={{0,17},{1,16},{16,1},{17,0},{2,19},{3,18},{18,3},{19,2},{4,21},{5,... | collective-permute-start | bytes 626696 | tf_op jit(solution)/shard_map/ppermute | solution.py:387
  41.7 11.1 %collective-permute-start.11 = (bf16[3,272,128]{2,1,0:T(8,128)(2,1)S(1)}, bf16[3,272,128]{2,1,0:T(8,128)(2,1)S(1)}, u32[]{:S(2)}, u32[]{:S(2)}) collective-permute-start(bf16[3,272,128]{2,1,0:T(8,128)(2,1)S(1)} %get-tuple-element.51), channel_id=1, source_target_pairs={{0,16},{1,17},{16,0},{17,1},{2,18},{3,19},{18,2},{19,3},{4,20},{5,... | collective-permute-start | bytes 626696 | tf_op jit(solution)/shard_map/ppermute | solution.py:387
  42.3 10.5 %collective-permute-start.10 = (bf16[3,272,128]{2,1,0:T(8,128)(2,1)S(1)}, bf16[3,272,128]{2,1,0:T(8,128)(2,1)S(1)}, u32[]{:S(2)}, u32[]{:S(2)}) collective-permute-start(bf16[3,272,128]{2,1,0:T(8,128)(2,1)S(1)} %get-tuple-element.49), channel_id=1, source_target_pairs={{0,1},{1,0},{16,17},{17,16},{2,3},{3,2},{18,19},{19,18},{4,5},{5,4... | collective-permute-start | bytes 626696 | tf_op jit(solution)/shard_map/ppermute | solution.py:387
  42.8 13.8 %collective-permute-start.13 = (bf16[272,128]{1,0:T(8,128)(2,1)S(1)}, bf16[272,128]{1,0:T(8,128)(2,1)S(1)}, u32[]{:S(2)}, u32[]{:S(2)}) collective-permute-start(bf16[272,128]{1,0:T(8,128)(2,1)S(1)} %get-tuple-element.47), channel_id=1, source_target_pairs={{0,1},{1,0},{16,17},{17,16},{2,3},{3,2},{18,19},{19,18},{4,5},{5,4... | collective-permute-start | bytes 208904 | tf_op jit(solution)/shard_map/ppermute | solution.py:387
  44.3 13.1 %collective-permute-start.14 = (bf16[272,128]{1,0:T(8,128)(2,1)S(1)}, bf16[272,128]{1,0:T(8,128)(2,1)S(1)}, u32[]{:S(2)}, u32[]{:S(2)}) collective-permute-start(bf16[272,128]{1,0:T(8,128)(2,1)S(1)} %get-tuple-element.46), channel_id=1, source_target_pairs={{0,16},{1,17},{16,0},{17,1},{2,18},{3,19},{18,2},{19,3},{4,20},{5,... | collective-permute-start | bytes 208904 | tf_op jit(solution)/shard_map/ppermute | solution.py:387
  49.7 7.7 %collective-permute-start.15 = (bf16[272,128]{1,0:T(8,128)(2,1)S(1)}, bf16[272,128]{1,0:T(8,128)(2,1)S(1)}, u32[]{:S(2)}, u32[]{:S(2)}) collective-permute-start(bf16[272,128]{1,0:T(8,128)(2,1)S(1)} %get-tuple-element.45), channel_id=1, source_target_pairs={{0,17},{1,16},{16,1},{17,0},{2,19},{3,18},{18,3},{19,2},{4,21},{5,... | collective-permute-start | bytes 208904 | tf_op jit(solution)/shard_map/ppermute | solution.py:387
  52.9 6.3 %collective-permute-start.16 = (bf16[272,128]{1,0:T(8,128)(2,1)S(1)}, bf16[272,128]{1,0:T(8,128)(2,1)S(1)}, u32[]{:S(2)}, u32[]{:S(2)}) collective-permute-start(bf16[272,128]{1,0:T(8,128)(2,1)S(1)} %get-tuple-element.54), channel_id=1, source_target_pairs={{0,6},{2,4},{4,2},{6,0},{1,7},{3,5},{5,3},{7,1},{8,14},{10,12},{12... | collective-permute-start | bytes 208904 | tf_op jit(solution)/shard_map/ppermute | solution.py:384
  56.6 5.3 %collective-permute-start.17 = (bf16[272,128]{1,0:T(8,128)(2,1)S(1)}, bf16[272,128]{1,0:T(8,128)(2,1)S(1)}, u32[]{:S(2)}, u32[]{:S(2)}) collective-permute-start(bf16[272,128]{1,0:T(8,128)(2,1)S(1)} %get-tuple-element.53), channel_id=1, source_target_pairs={{0,4},{2,6},{4,0},{6,2},{1,5},{3,7},{5,1},{7,3},{8,12},{10,14},{12... | collective-permute-start | bytes 208904 | tf_op jit(solution)/shard_map/ppermute | solution.py:384
  56.6 5.6 %collective-permute-start.18 = (bf16[272,128]{1,0:T(8,128)(2,1)S(1)}, bf16[272,128]{1,0:T(8,128)(2,1)S(1)}, u32[]{:S(2)}, u32[]{:S(2)}) collective-permute-start(bf16[272,128]{1,0:T(8,128)(2,1)S(1)} %get-tuple-element.52), channel_id=1, source_target_pairs={{0,2},{2,0},{4,6},{6,4},{1,3},{3,1},{5,7},{7,5},{8,10},{10,8},{12,... | collective-permute-start | bytes 208904 | tf_op jit(solution)/shard_map/ppermute | solution.py:384

commit v16 on v14

--- a/solution.py
+++ b/solution.py
@@ -16,7 +16,7 @@
 LOG2E = 1.4426950408889634
 GROWS = 16
 GTOP = 8
-STRIP = 32
+STRIP = 16
 LINE = PEERS = (1, 2, 3)
 
 NT = (((1,), (1,)), ((), ()))
@@ -179,8 +179,8 @@
             qc[rows, side] = q * rowsel[i]
             dc[rows, side] = dy * rowsel[i]
 
-    span = 2 * tokens
-    blocks = group // 2
+    span = 4 * tokens
+    blocks = group // 4
     strips = [slice(i, i + STRIP) for i in range(0, slots, STRIP)]
     tg2 = jnp.concatenate([tg, tg], axis=1)
 
@@ -213,7 +213,7 @@
                 norm = norm + fold8(e)
                 dots = dots + fold8(e * dbuf[mid % 3, strip])
             if new < blocks:
-                x = s[strip] + jnp.concatenate([bias[strip], bias[strip]], axis=1)
+                x = s[strip] + jnp.concatenate([bias[strip]] * 4, axis=1)
                 sbuf[new % 3, strip] = x
                 top = jnp.maximum(top, jnp.max(x.reshape(STRIP // 8, 8, span), axis=0))
         if new < blocks:
@@ -221,8 +221,8 @@
         if 0 <= mid < blocks:
             invs[mid] = 1.0 / jnp.sum(norm, axis=0, keepdims=True)
             deltas[mid] = invs[mid] * jnp.sum(dots, axis=0, keepdims=True)
-        if old >= 0 and old % 2:
-            more = slot_grads(old - 1, old + 1)
+        if old >= 0:
+            more = slot_grads(old, old + 1)
             dk, dv = dk + more[0], dv + more[1]
     dk = (scale * tg2 * dk).astype(jnp.bfloat16)
     g_ref[...] += fold8((dv * vcat.astype(jnp.float32))[:, :hd] + (dv * vcat.astype(jnp.float32))[:, hd:])
@@ -321,8 +321,8 @@
             pltpu.VMEM((rows, 2 * hd), jnp.bfloat16),
             pltpu.VMEM((rows, 2 * hd), jnp.bfloat16),
             pltpu.VMEM((2, tokens, hd), jnp.bfloat16),
-            pltpu.VMEM((3, slots, 2 * tokens), jnp.float32),
-            pltpu.VMEM((3, slots, 2 * tokens), jnp.float32),
+            pltpu.VMEM((3, slots, 4 * tokens), jnp.float32),
+            pltpu.VMEM((3, slots, 4 * tokens), jnp.float32),
             pltpu.VMEM((slots, tokens), jnp.float32),
             pltpu.SemaphoreType.DMA((5 + 4 * KV_HEADS,)),
             pltpu.SemaphoreType.DMA((KV_HEADS,)),

time: 63.1 us -> 63 us (level)
  no operation moved by 1% of the time
where the time goes in v16:
time: 63 us; the launch traced here: 62.7 us
  starting transfers between devices  24.4 us (39%)
  waiting for transfers between devices  22.3 us (35%)
  Pallas kernels  12.4 us (20%)
  local copies, waits for them, and re-layouts  1.7 us (3%)
  between operations  1.43 us (2%)
    ppermute x11, starting transfers between devices, send_xy(): return lax.ppermute(x, ('x', 'y'), [(i, i ^ p) for i in range(4)])  14.1 us
    ppermute x11, waiting for transfers between devices, send_xy(): return lax.ppermute(x, ('x', 'y'), [(i, i ^ p) for i in range(4)])  12.1 us
    ppermute x6, starting transfers between devices, send_z(): return lax.ppermute(x, 'z', [(i, i ^ k) for i in range(cols)])  10.1 us
    pallas_call x1, Pallas kernels, scores(): pl.pallas_call(functools.partial(scores_kernel, mine, cols, folded), grid...  7.71 us
    ppermute x6, waiting for transfers between devices, send_z(): return lax.ppermute(x, 'z', [(i, i ^ k) for i in range(cols)])  5.58 us
    ppermute x2, waiting for transfers between devices, send_core(): return lax.ppermute(x, 'core', [(0, 1), (1, 0)])  4.63 us
    pallas_call x1, Pallas kernels, outputs(): pl.pallas_call(outputs_kernel, grid=(KV_HEADS,), in_specs=[smem, smem, pl...  4.01 us
  transfers between devices with their start and end apart: 19, of which 10 were waited for; matrix products, arithmetic and copies ran while one was open for 0% of the time, Pallas kernels for 6%

profile of v16, /device:TPU:0, one launch (start us, length us, event | category | flops | bytes accessed | tf_op | source)
XLA Modules:
  0.0 62.7 jit_solution(9623538139145632349)
XLA Ops:
  0.6 0.8 %constant_dynamic-update-slice_fusion.1 = bf16[32,1024]{1,0:T(8,128)(2,1)S(1)} fusion(bf16[32,512]{1,0:T(8,128)(2,1)} %param.8), kind=kLoop, calls=%fused_computation.19 | loop fusion | bytes 65536
  1.4 0.8 %constant_dynamic-update-slice_fusion = bf16[32,1024]{1,0:T(8,128)(2,1)S(1)} fusion(bf16[32,1024]{1,0:T(8,128)(2,1)S(1)} %constant_dynamic-update-slice_fusion.1, bf16[32,512]{1,0:T(8,128)(2,1)} %param.9), kind=kLoop, calls=%fused_computation.18 | loop fusion | bytes 65536 | tf_op jit(solution)/shard_map/concatenate | solution.py:392
  2.2 5.0 %collective-permute-start.2 = (bf16[32,1024]{1,0:T(8,128)(2,1)S(1)}, bf16[32,1024]{1,0:T(8,128)(2,1)S(1)}, u32[]{:S(2)}, u32[]{:S(2)}) collective-permute-start(bf16[32,1024]{1,0:T(8,128)(2,1)S(1)} %constant_dynamic-update-slice_fusion), channel_id=1, source_target_pairs={{0,6},{2,4},{4,2},{6,0},{1,7},{3,5},{5,3},{7,1},{8,14},{10,12},{12... | collective-permute-start | bytes 196616 | tf_op jit(solution)/shard_map/ppermute | solution.py:384
  7.2 0.0 collective-permute-start.1
  7.2 0.6 collective-permute-start
  7.8 1.7 %collective-permute-start.3 = (bf16[32,1024]{1,0:T(8,128)(2,1)S(1)}, bf16[32,1024]{1,0:T(8,128)(2,1)S(1)}, u32[]{:S(2)}, u32[]{:S(2)}) collective-permute-start(bf16[32,1024]{1,0:T(8,128)(2,1)S(1)} %constant_dynamic-update-slice_fusion), channel_id=1, source_target_pairs={{0,1},{1,0},{16,17},{17,16},{2,3},{3,2},{18,19},{19,18},{4,5},{5,4... | collective-permute-start | bytes 196616 | tf_op jit(solution)/shard_map/ppermute | solution.py:387
  9.5 1.5 %collective-permute-start.4 = (bf16[32,1024]{1,0:T(8,128)(2,1)S(1)}, bf16[32,1024]{1,0:T(8,128)(2,1)S(1)}, u32[]{:S(2)}, u32[]{:S(2)}) collective-permute-start(bf16[32,1024]{1,0:T(8,128)(2,1)S(1)} %constant_dynamic-update-slice_fusion), channel_id=1, source_target_pairs={{0,16},{1,17},{16,0},{17,1},{2,18},{3,19},{18,2},{19,3},{4,20},{5,... | collective-permute-start | bytes 196616 | tf_op jit(solution)/shard_map/ppermute | solution.py:387
  11.0 0.0 collective-permute-done.2
  11.0 1.8 %collective-permute-done.1 = bf16[32,1024]{1,0:T(8,128)(2,1)S(1)} collective-permute-done((bf16[32,1024]{1,0:T(8,128)(2,1)S(1)}, bf16[32,1024]{1,0:T(8,128)(2,1)S(1)}, u32[]{:S(2)}, u32[]{:S(2)}) %collective-permute-start.1) | collective-permute-done | bytes 65568 | tf_op jit(solution)/shard_map/ppermute | solution.py:384
  12.8 0.0 collective-permute-done
  12.8 0.0 collective-permute-done.3
  12.8 0.9 %collective-permute-done.4 = bf16[32,1024]{1,0:T(8,128)(2,1)S(1)} collective-permute-done((bf16[32,1024]{1,0:T(8,128)(2,1)S(1)}, bf16[32,1024]{1,0:T(8,128)(2,1)S(1)}, u32[]{:S(2)}, u32[]{:S(2)}) %collective-permute-start.4) | collective-permute-done | bytes 65568 | tf_op jit(solution)/shard_map/ppermute | solution.py:387
  13.8 0.7 %collective-permute-start.5 = (bf16[96,1024]{1,0:T(8,128)(2,1)S(1)}, bf16[96,1024]{1,0:T(8,128)(2,1)S(1)}, u32[]{:S(2)}, u32[]{:S(2)}) collective-permute-start(bf16[96,1024]{1,0:T(8,128)(2,1)S(1)} %pad_maximum_fusion.1), channel_id=1, source_target_pairs={{0,1},{1,0},{16,17},{17,16},{2,3},{3,2},{18,19},{19,18},{4,5},{5,4... | collective-permute-start | bytes 589832 | tf_op jit(solution)/shard_map/ppermute | solution.py:387
  14.4 1.5 %collective-permute-start.6 = (bf16[96,1024]{1,0:T(8,128)(2,1)S(1)}, bf16[96,1024]{1,0:T(8,128)(2,1)S(1)}, u32[]{:S(2)}, u32[]{:S(2)}) collective-permute-start(bf16[96,1024]{1,0:T(8,128)(2,1)S(1)} %pad_maximum_fusion.1), channel_id=1, source_target_pairs={{0,16},{1,17},{16,0},{17,1},{2,18},{3,19},{18,2},{19,3},{4,20},{5,... | collective-permute-start | bytes 589832 | tf_op jit(solution)/shard_map/ppermute | solution.py:387
  16.0 0.0 copy-start
  16.0 0.0 copy-start.2
  16.0 0.0 copy-start.3
  16.0 1.4 %collective-permute-start.7 = (bf16[128,1024]{1,0:T(8,128)(2,1)S(1)}, bf16[128,1024]{1,0:T(8,128)(2,1)S(1)}, u32[]{:S(2)}, u32[]{:S(2)}) collective-permute-start(bf16[128,1024]{1,0:T(8,128)(2,1)S(1)} %pad_maximum_fusion), channel_id=1, source_target_pairs={{0,17},{1,16},{16,1},{17,0},{2,19},{3,18},{18,3},{19,2},{4,21},{5,... | collective-permute-start | bytes 786440 | tf_op jit(solution)/shard_map/ppermute | solution.py:387
  17.4 2.6 %collective-permute-done.5 = bf16[96,1024]{1,0:T(8,128)(2,1)S(1)} collective-permute-done((bf16[96,1024]{1,0:T(8,128)(2,1)S(1)}, bf16[96,1024]{1,0:T(8,128)(2,1)S(1)}, u32[]{:S(2)}, u32[]{:S(2)}) %collective-permute-start.5) | collective-permute-done | bytes 196640 | tf_op jit(solution)/shard_map/ppermute | solution.py:387
  20.1 2.2 %collective-permute-done.6 = bf16[96,1024]{1,0:T(8,128)(2,1)S(1)} collective-permute-done((bf16[96,1024]{1,0:T(8,128)(2,1)S(1)}, bf16[96,1024]{1,0:T(8,128)(2,1)S(1)}, u32[]{:S(2)}, u32[]{:S(2)}) %collective-permute-start.6) | collective-permute-done | bytes 196640 | tf_op jit(solution)/shard_map/ppermute | solution.py:387
  22.3 4.3 %collective-permute-done.7 = bf16[128,1024]{1,0:T(8,128)(2,1)S(1)} collective-permute-done((bf16[128,1024]{1,0:T(8,128)(2,1)S(1)}, bf16[128,1024]{1,0:T(8,128)(2,1)S(1)}, u32[]{:S(2)}, u32[]{:S(2)}) %collective-permute-start.7) | collective-permute-done | bytes 262176 | tf_op jit(solution)/shard_map/ppermute | solution.py:387
  26.5 0.1 collective-permute-start.8
  27.3 2.0 %collective-permute-done.8.other = bf16[2,2,128,1024]{3,2,1,0:T(8,128)(2,1)S(1)} collective-permute-done((bf16[2,2,128,1024]{3,2,1,0:T(8,128)(2,1)S(1)}, bf16[2,2,128,1024]{3,2,1,0:T(8,128)(2,1)S(1)}, u32[]{:S(2)}, u32[]{:S(2)}) %collective-permute-start.8) | collective-permute-done | bytes 1048608 | tf_op jit(solution)/shard_map/ppermute | solution.py:390
  29.3 7.7 %shard_map.110 = (bf16[4,256,1024]{2,1,0:T(8,128)(2,1)S(1)}, bf16[4,256,1024]{2,1,0:T(8,128)(2,1)S(1)}, bf16[2,256,1024]{2,1,0:T(8,128)(2,1)S(1)}, bf16[2,2,4,27...) custom-call(s32[128]{0:T(128)S(1)} %copy-done.3, s32[4]{0:T(128)S(1)} %copy-done.2, ...), custom_call_target="tpu_custom_call" | custom-call | flops 2147483648 | bytes 12582912 | tf_op jit(solution)/shard_map/pallas_call | solution.py:298
  37.0 0.2 collective-permute-start.9
  37.2 2.6 %collective-permute-done.9 = bf16[2,2,4,272,128]{4,3,2,1,0:T(8,128)(2,1)S(1)} collective-permute-done((bf16[2,2,4,272,128]{4,3,2,1,0:T(8,128)(2,1)S(1)}, bf16[2,2,4,272,128]{4,3,2,1,0:T(8,128)(2,1)S(1)}, u32[]{:S(2)}, u32[]{:S(2)}) %collective-permute-start.9) | collective-permute-done | bytes 1114144 | tf_op jit(solution)/shard_map/ppermute | solution.py:390
  39.8 0.3 add_convert_fusion
  40.2 2.3 %collective-permute-start.12 = (bf16[3,272,128]{2,1,0:T(8,128)(2,1)S(1)}, bf16[3,272,128]{2,1,0:T(8,128)(2,1)S(1)}, u32[]{:S(2)}, u32[]{:S(2)}) collective-permute-start(bf16[3,272,128]{2,1,0:T(8,128)(2,1)S(1)} %get-tuple-element.50), channel_id=1, source_target_pairs={{0,17},{1,16},{16,1},{17,0},{2,19},{3,18},{18,3},{19,2},{4,21},{5,... | collective-permute-start | bytes 626696 | tf_op jit(solution)/shard_map/ppermute | solution.py:387
  42.6 0.5 collective-permute-start.11
  43.1 0.7 %collective-permute-start.10 = (bf16[3,272,128]{2,1,0:T(8,128)(2,1)S(1)}, bf16[3,272,128]{2,1,0:T(8,128)(2,1)S(1)}, u32[]{:S(2)}, u32[]{:S(2)}) collective-permute-start(bf16[3,272,128]{2,1,0:T(8,128)(2,1)S(1)} %get-tuple-element.49), channel_id=1, source_target_pairs={{0,1},{1,0},{16,17},{17,16},{2,3},{3,2},{18,19},{19,18},{4,5},{5,4... | collective-permute-start | bytes 626696 | tf_op jit(solution)/shard_map/ppermute | solution.py:387
  43.8 1.4 %collective-permute-start.13 = (bf16[272,128]{1,0:T(8,128)(2,1)S(1)}, bf16[272,128]{1,0:T(8,128)(2,1)S(1)}, u32[]{:S(2)}, u32[]{:S(2)}) collective-permute-start(bf16[272,128]{1,0:T(8,128)(2,1)S(1)} %get-tuple-element.47), channel_id=1, source_target_pairs={{0,1},{1,0},{16,17},{17,16},{2,3},{3,2},{18,19},{19,18},{4,5},{5,4... | collective-permute-start | bytes 208904 | tf_op jit(solution)/shard_map/ppermute | solution.py:387
  45.1 1.5 %collective-permute-start.14 = (bf16[272,128]{1,0:T(8,128)(2,1)S(1)}, bf16[272,128]{1,0:T(8,128)(2,1)S(1)}, u32[]{:S(2)}, u32[]{:S(2)}) collective-permute-start(bf16[272,128]{1,0:T(8,128)(2,1)S(1)} %get-tuple-element.46), channel_id=1, source_target_pairs={{0,16},{1,17},{16,0},{17,1},{2,18},{3,19},{18,2},{19,3},{4,20},{5,... | collective-permute-start | bytes 208904 | tf_op jit(solution)/shard_map/ppermute | solution.py:387
  46.6 4.0 %shard_map.111 = (bf16[128,4096]{1,0:T(8,128)(2,1)}, bf16[128,4096]{1,0:T(8,128)(2,1)}) custom-call(s32[128]{0:T(128)S(1)} %copy-done.3, f32[1]{0:T(128)S(6)} %copy.19.gate_s, s32[1,128]{1,0:T(1,128)S(1)} %bitcast.31, bf16[4,256,1024]{2,1,0:T(8,128)(2,1)S(1)} %get-tuple-element.34.p16, bf16[4,256,1024]{2,1,0:T(8,128)(2,1)S(1)} %get-tuple-element.35.ds16, ...), custom_call_target="tpu_custom_call" | custom-call | flops 5000000000 | bytes 12582912 | tf_op jit(solution)/shard_map/pallas_call | solution.py:61
  50.6 0.0 collective-permute-done.12
  50.6 0.9 %collective-permute-start.15 = (bf16[272,128]{1,0:T(8,128)(2,1)S(1)}, bf16[272,128]{1,0:T(8,128)(2,1)S(1)}, u32[]{:S(2)}, u32[]{:S(2)}) collective-permute-start(bf16[272,128]{1,0:T(8,128)(2,1)S(1)} %get-tuple-element.45), channel_id=1, source_target_pairs={{0,17},{1,16},{16,1},{17,0},{2,19},{3,18},{18,3},{19,2},{4,21},{5,... | collective-permute-start | bytes 208904 | tf_op jit(solution)/shard_map/ppermute | solution.py:387
  51.5 2.1 %collective-permute-done.11 = bf16[3,272,128]{2,1,0:T(8,128)(2,1)S(1)} collective-permute-done((bf16[3,272,128]{2,1,0:T(8,128)(2,1)S(1)}, bf16[3,272,128]{2,1,0:T(8,128)(2,1)S(1)}, u32[]{:S(2)}, u32[]{:S(2)}) %collective-permute-start.11) | collective-permute-done | bytes 208928 | tf_op jit(solution)/shard_map/ppermute | solution.py:387
  53.6 0.0 collective-permute-done.10
  53.6 0.1 fusion.2
  53.7 1.8 %collective-permute-start.16 = (bf16[272,128]{1,0:T(8,128)(2,1)S(1)}, bf16[272,128]{1,0:T(8,128)(2,1)S(1)}, u32[]{:S(2)}, u32[]{:S(2)}) collective-permute-start(bf16[272,128]{1,0:T(8,128)(2,1)S(1)} %get-tuple-element.54), channel_id=1, source_target_pairs={{0,6},{2,4},{4,2},{6,0},{1,7},{3,5},{5,3},{7,1},{8,14},{10,12},{12... | collective-permute-start | bytes 208904 | tf_op jit(solution)/shard_map/ppermute | solution.py:384
  55.5 0.0 collective-permute-start.17
  55.5 0.0 collective-permute-done.13.refs_1_
  55.5 2.7 %collective-permute-start.18 = (bf16[272,128]{1,0:T(8,128)(2,1)S(1)}, bf16[272,128]{1,0:T(8,128)(2,1)S(1)}, u32[]{:S(2)}, u32[]{:S(2)}) collective-permute-start(bf16[272,128]{1,0:T(8,128)(2,1)S(1)} %get-tuple-element.52), channel_id=1, source_target_pairs={{0,2},{2,0},{4,6},{6,4},{1,3},{3,1},{5,7},{7,5},{8,10},{10,8},{12,... | collective-permute-start | bytes 208904 | tf_op jit(solution)/shard_map/ppermute | solution.py:384
  58.2 0.0 collective-permute-done.14.refs_2_
  58.2 0.0 collective-permute-done.15.refs_3_
  58.2 1.9 %collective-permute-done.16.refs_4_ = bf16[272,128]{1,0:T(8,128)(2,1)S(1)} collective-permute-done((bf16[272,128]{1,0:T(8,128)(2,1)S(1)}, bf16[272,128]{1,0:T(8,128)(2,1)S(1)}, u32[]{:S(2)}, u32[]{:S(2)}) %collective-permute-start.16) | collective-permute-done | bytes 69664 | tf_op jit(solution)/shard_map/ppermute | solution.py:384
  60.1 1.9 %collective-permute-done.17.refs_5_ = bf16[272,128]{1,0:T(8,128)(2,1)S(1)} collective-permute-done((bf16[272,128]{1,0:T(8,128)(2,1)S(1)}, bf16[272,128]{1,0:T(8,128)(2,1)S(1)}, u32[]{:S(2)}, u32[]{:S(2)}) %collective-permute-start.17) | collective-permute-done | bytes 69664 | tf_op jit(solution)/shard_map/ppermute | solution.py:384
  62.0 0.0 collective-permute-done.18.refs_6_
  62.0 0.7 %shard_map.112 = (f32[32,512]{1,0:T(8,128)}, f32[32,512]{1,0:T(8,128)}, f32[1]{0:T(128)}) custom-call(f32[8,128]{1,0:T(8,128)S(1)} %get-tuple-element.40.gate, bf16[272,128]{1,0:T(8,128)(2,1)S(1)} %get-tuple-element.48.refs_0_, bf16[272,128]{1,0:T(8,128)(2,1)S(1)} %collective-permute-done.13.refs_1_, bf16[272,128]{1,0:T(8,128)(2,1)S(1)} %collective-permute-done.14.refs_2_, ...), custom_call_target="tpu_custom_call" | custom-call | tf_op jit(solution)/shard_map/pallas_call | solution.py:366
  (17 shorter events, 0.2 us)
Async XLA Ops:
  2.2 8.9 %collective-permute-start.2 = (bf16[32,1024]{1,0:T(8,128)(2,1)S(1)}, bf16[32,1024]{1,0:T(8,128)(2,1)S(1)}, u32[]{:S(2)}, u32[]{:S(2)}) collective-permute-start(bf16[32,1024]{1,0:T(8,128)(2,1)S(1)} %constant_dynamic-update-slice_fusion), channel_id=1, source_target_pairs={{0,6},{2,4},{4,2},{6,0},{1,7},{3,5},{5,3},{7,1},{8,14},{10,12},{12... | collective-permute-start | bytes 196616 | tf_op jit(solution)/shard_map/ppermute | solution.py:384
  7.2 5.6 %collective-permute-start.1 = (bf16[32,1024]{1,0:T(8,128)(2,1)S(1)}, bf16[32,1024]{1,0:T(8,128)(2,1)S(1)}, u32[]{:S(2)}, u32[]{:S(2)}) collective-permute-start(bf16[32,1024]{1,0:T(8,128)(2,1)S(1)} %constant_dynamic-update-slice_fusion), channel_id=1, source_target_pairs={{0,4},{2,6},{4,0},{6,2},{1,5},{3,7},{5,1},{7,3},{8,12},{10,14},{12... | collective-permute-start | bytes 196616 | tf_op jit(solution)/shard_map/ppermute | solution.py:384
  7.2 5.6 %collective-permute-start = (bf16[32,1024]{1,0:T(8,128)(2,1)S(1)}, bf16[32,1024]{1,0:T(8,128)(2,1)S(1)}, u32[]{:S(2)}, u32[]{:S(2)}) collective-permute-start(bf16[32,1024]{1,0:T(8,128)(2,1)S(1)} %constant_dynamic-update-slice_fusion), channel_id=1, source_target_pairs={{0,2},{2,0},{4,6},{6,4},{1,3},{3,1},{5,7},{7,5},{8,10},{10,8},{12,... | collective-permute-start | bytes 196616 | tf_op jit(solution)/shard_map/ppermute | solution.py:384
  7.8 5.1 %collective-permute-start.3 = (bf16[32,1024]{1,0:T(8,128)(2,1)S(1)}, bf16[32,1024]{1,0:T(8,128)(2,1)S(1)}, u32[]{:S(2)}, u32[]{:S(2)}) collective-permute-start(bf16[32,1024]{1,0:T(8,128)(2,1)S(1)} %constant_dynamic-update-slice_fusion), channel_id=1, source_target_pairs={{0,1},{1,0},{16,17},{17,16},{2,3},{3,2},{18,19},{19,18},{4,5},{5,4... | collective-permute-start | bytes 196616 | tf_op jit(solution)/shard_map/ppermute | solution.py:387
  9.5 4.3 %collective-permute-start.4 = (bf16[32,1024]{1,0:T(8,128)(2,1)S(1)}, bf16[32,1024]{1,0:T(8,128)(2,1)S(1)}, u32[]{:S(2)}, u32[]{:S(2)}) collective-permute-start(bf16[32,1024]{1,0:T(8,128)(2,1)S(1)} %constant_dynamic-update-slice_fusion), channel_id=1, source_target_pairs={{0,16},{1,17},{16,0},{17,1},{2,18},{3,19},{18,2},{19,3},{4,20},{5,... | collective-permute-start | bytes 196616 | tf_op jit(solution)/shard_map/ppermute | solution.py:387
  13.8 6.3 %collective-permute-start.5 = (bf16[96,1024]{1,0:T(8,128)(2,1)S(1)}, bf16[96,1024]{1,0:T(8,128)(2,1)S(1)}, u32[]{:S(2)}, u32[]{:S(2)}) collective-permute-start(bf16[96,1024]{1,0:T(8,128)(2,1)S(1)} %pad_maximum_fusion.1), channel_id=1, source_target_pairs={{0,1},{1,0},{16,17},{17,16},{2,3},{3,2},{18,19},{19,18},{4,5},{5,4... | collective-permute-start | bytes 589832 | tf_op jit(solution)/shard_map/ppermute | solution.py:387
  14.4 7.8 %collective-permute-start.6 = (bf16[96,1024]{1,0:T(8,128)(2,1)S(1)}, bf16[96,1024]{1,0:T(8,128)(2,1)S(1)}, u32[]{:S(2)}, u32[]{:S(2)}) collective-permute-start(bf16[96,1024]{1,0:T(8,128)(2,1)S(1)} %pad_maximum_fusion.1), channel_id=1, source_target_pairs={{0,16},{1,17},{16,0},{17,1},{2,18},{3,19},{18,2},{19,3},{4,20},{5,... | collective-permute-start | bytes 589832 | tf_op jit(solution)/shard_map/ppermute | solution.py:387
  15.9 13.3 %copy-start.1 = (bf16[128,4096]{1,0:T(8,128)(2,1)S(1)}, bf16[128,4096]{1,0:T(8,128)(2,1)}, u32[]{:S(2)}) copy-start(bf16[128,4096]{1,0:T(8,128)(2,1)} %dy_ref.1) | copy-start | bytes 3145732
  16.0 13.3 %copy-start = (bf16[128,4096]{1,0:T(8,128)(2,1)S(1)}, bf16[128,4096]{1,0:T(8,128)(2,1)}, u32[]{:S(2)}) copy-start(bf16[128,4096]{1,0:T(8,128)(2,1)} %q_ref.1) | copy-start | bytes 3145732
  16.0 13.3 %copy-start.2 = (s32[4]{0:T(128)S(1)}, s32[4]{0:T(128)}, u32[]{:S(2)}) copy-start(s32[4]{0:T(128)} %cnt_s.1) | copy-start | bytes 52
  16.0 13.3 %copy-start.3 = (s32[128]{0:T(128)S(1)}, s32[128]{0:T(128)}, u32[]{:S(2)}) copy-start(s32[128]{0:T(128)} %seg_s.3) | copy-start | bytes 1540
  16.0 10.5 %collective-permute-start.7 = (bf16[128,1024]{1,0:T(8,128)(2,1)S(1)}, bf16[128,1024]{1,0:T(8,128)(2,1)S(1)}, u32[]{:S(2)}, u32[]{:S(2)}) collective-permute-start(bf16[128,1024]{1,0:T(8,128)(2,1)S(1)} %pad_maximum_fusion), channel_id=1, source_target_pairs={{0,17},{1,16},{16,1},{17,0},{2,19},{3,18},{18,3},{19,2},{4,21},{5,... | collective-permute-start | bytes 786440 | tf_op jit(solution)/shard_map/ppermute | solution.py:387
  26.5 2.7 %collective-permute-start.8 = (bf16[2,2,128,1024]{3,2,1,0:T(8,128)(2,1)S(1)}, bf16[2,2,128,1024]{3,2,1,0:T(8,128)(2,1)S(1)}, u32[]{:S(2)}, u32[]{:S(2)}) collective-permute-start(bf16[2,2,128,1024]{3,2,1,0:T(8,128)(2,1)S(1)} %bitcast.28), channel_id=1, source_target_pairs={{0,8},{8,0},{1,9},{9,1},{2,10},{10,2},{3,11},{11,3},{4,12},{12,4},... | collective-permute-start | bytes 3145736 | tf_op jit(solution)/shard_map/ppermute | solution.py:390
  37.0 2.8 %collective-permute-start.9 = (bf16[2,2,4,272,128]{4,3,2,1,0:T(8,128)(2,1)S(1)}, bf16[2,2,4,272,128]{4,3,2,1,0:T(8,128)(2,1)S(1)}, u32[]{:S(2)}, u32[]{:S(2)}) collective-permute-start(bf16[2,2,4,272,128]{4,3,2,1,0:T(8,128)(2,1)S(1)} %get-tuple-element.31), channel_id=1, source_target_pairs={{0,8},{8,0},{1,9},{9,1},{2,10},{10,2},{3,11},{11,3},{4,12},{12,4},... | collective-permute-start | bytes 3342344 | tf_op jit(solution)/shard_map/ppermute | solution.py:390
  40.2 10.4 %collective-permute-start.12 = (bf16[3,272,128]{2,1,0:T(8,128)(2,1)S(1)}, bf16[3,272,128]{2,1,0:T(8,128)(2,1)S(1)}, u32[]{:S(2)}, u32[]{:S(2)}) collective-permute-start(bf16[3,272,128]{2,1,0:T(8,128)(2,1)S(1)} %get-tuple-element.50), channel_id=1, source_target_pairs={{0,17},{1,16},{16,1},{17,0},{2,19},{3,18},{18,3},{19,2},{4,21},{5,... | collective-permute-start | bytes 626696 | tf_op jit(solution)/shard_map/ppermute | solution.py:387
  42.6 11.0 %collective-permute-start.11 = (bf16[3,272,128]{2,1,0:T(8,128)(2,1)S(1)}, bf16[3,272,128]{2,1,0:T(8,128)(2,1)S(1)}, u32[]{:S(2)}, u32[]{:S(2)}) collective-permute-start(bf16[3,272,128]{2,1,0:T(8,128)(2,1)S(1)} %get-tuple-element.51), channel_id=1, source_target_pairs={{0,16},{1,17},{16,0},{17,1},{2,18},{3,19},{18,2},{19,3},{4,20},{5,... | collective-permute-start | bytes 626696 | tf_op jit(solution)/shard_map/ppermute | solution.py:387
  43.1 10.5 %collective-permute-start.10 = (bf16[3,272,128]{2,1,0:T(8,128)(2,1)S(1)}, bf16[3,272,128]{2,1,0:T(8,128)(2,1)S(1)}, u32[]{:S(2)}, u32[]{:S(2)}) collective-permute-start(bf16[3,272,128]{2,1,0:T(8,128)(2,1)S(1)} %get-tuple-element.49), channel_id=1, source_target_pairs={{0,1},{1,0},{16,17},{17,16},{2,3},{3,2},{18,19},{19,18},{4,5},{5,4... | collective-permute-start | bytes 626696 | tf_op jit(solution)/shard_map/ppermute | solution.py:387
  43.8 11.8 %collective-permute-start.13 = (bf16[272,128]{1,0:T(8,128)(2,1)S(1)}, bf16[272,128]{1,0:T(8,128)(2,1)S(1)}, u32[]{:S(2)}, u32[]{:S(2)}) collective-permute-start(bf16[272,128]{1,0:T(8,128)(2,1)S(1)} %get-tuple-element.47), channel_id=1, source_target_pairs={{0,1},{1,0},{16,17},{17,16},{2,3},{3,2},{18,19},{19,18},{4,5},{5,4... | collective-permute-start | bytes 208904 | tf_op jit(solution)/shard_map/ppermute | solution.py:387
  45.1 13.1 %collective-permute-start.14 = (bf16[272,128]{1,0:T(8,128)(2,1)S(1)}, bf16[272,128]{1,0:T(8,128)(2,1)S(1)}, u32[]{:S(2)}, u32[]{:S(2)}) collective-permute-start(bf16[272,128]{1,0:T(8,128)(2,1)S(1)} %get-tuple-element.46), channel_id=1, source_target_pairs={{0,16},{1,17},{16,0},{17,1},{2,18},{3,19},{18,2},{19,3},{4,20},{5,... | collective-permute-start | bytes 208904 | tf_op jit(solution)/shard_map/ppermute | solution.py:387
  50.6 7.6 %collective-permute-start.15 = (bf16[272,128]{1,0:T(8,128)(2,1)S(1)}, bf16[272,128]{1,0:T(8,128)(2,1)S(1)}, u32[]{:S(2)}, u32[]{:S(2)}) collective-permute-start(bf16[272,128]{1,0:T(8,128)(2,1)S(1)} %get-tuple-element.45), channel_id=1, source_target_pairs={{0,17},{1,16},{16,1},{17,0},{2,19},{3,18},{18,3},{19,2},{4,21},{5,... | collective-permute-start | bytes 208904 | tf_op jit(solution)/shard_map/ppermute | solution.py:387
  53.7 6.3 %collective-permute-start.16 = (bf16[272,128]{1,0:T(8,128)(2,1)S(1)}, bf16[272,128]{1,0:T(8,128)(2,1)S(1)}, u32[]{:S(2)}, u32[]{:S(2)}) collective-permute-start(bf16[272,128]{1,0:T(8,128)(2,1)S(1)} %get-tuple-element.54), channel_id=1, source_target_pairs={{0,6},{2,4},{4,2},{6,0},{1,7},{3,5},{5,3},{7,1},{8,14},{10,12},{12... | collective-permute-start | bytes 208904 | tf_op jit(solution)/shard_map/ppermute | solution.py:384
  55.5 6.5 %collective-permute-start.17 = (bf16[272,128]{1,0:T(8,128)(2,1)S(1)}, bf16[272,128]{1,0:T(8,128)(2,1)S(1)}, u32[]{:S(2)}, u32[]{:S(2)}) collective-permute-start(bf16[272,128]{1,0:T(8,128)(2,1)S(1)} %get-tuple-element.53), channel_id=1, source_target_pairs={{0,4},{2,6},{4,0},{6,2},{1,5},{3,7},{5,1},{7,3},{8,12},{10,14},{12... | collective-permute-start | bytes 208904 | tf_op jit(solution)/shard_map/ppermute | solution.py:384
  55.5 6.5 %collective-permute-start.18 = (bf16[272,128]{1,0:T(8,128)(2,1)S(1)}, bf16[272,128]{1,0:T(8,128)(2,1)S(1)}, u32[]{:S(2)}, u32[]{:S(2)}) collective-permute-start(bf16[272,128]{1,0:T(8,128)(2,1)S(1)} %get-tuple-element.52), channel_id=1, source_target_pairs={{0,2},{2,0},{4,6},{6,4},{1,3},{3,1},{5,7},{7,5},{8,10},{10,8},{12,... | collective-permute-start | bytes 208904 | tf_op jit(solution)/shard_map/ppermute | solution.py:384
